TPU v7x, 32 devices: a whole 2x2x4 slice. The times are simulated.
32 devices in a mesh: left: 4 (over z), right: 4 (over y, x), occ: 2 (over core).
Axes of the slice: x: 2, y: 2, z: 4, core: 2. Of those that a mesh axis runs over, the one named last changes fastest.
Arguments:
- chol: bfloat16 [16, 1024, 2048], P('right', 'occ', 'left'), may hold values from -0.125 to 0.125
- amps: bfloat16 [4, 4, 1024, 512], P('left', None, 'occ', 'right'), may hold values from -1.5 to 1.5
- listed: int32 [4, 4, 4, 4], replicated, may hold values 0 or 1
Outputs:
- residual: float32 [4, 4, 1024, 512], P('left', None, 'occ', 'right')
All inputs are finite; a program needn't handle non-finite values.
Results may differ from a plain program's by a relative error of at most 0.0029.
Values may be sent and summed in bfloat16 or wider, within the bound.
No kernel may reach another device: no remote copies, remote signals or barrier semaphores. Data moves between devices by JAX's collectives and lax.ppermute only.
A program may use at most 192 MiB of HBM per device.

v0:
```python
import functools

import jax
import jax.numpy as jnp
from jax import lax
from jax.experimental import pallas as pl
from jax.experimental.pallas import tpu as pltpu
from jax.sharding import PartitionSpec as P

TV = 32
NTV = 4
NOP = 512
PAIR = 1024
GROUPS = 4


def ladder_kernel(steps, count, first, half_ref, live_ref, pick_ref, tile_ref, *refs):
    lefts = [refs[s * count:(s + 1) * count] for s in range(steps)]
    rights = [refs[steps * count + 2 * s: steps * count + 2 * s + 2] for s in range(steps)]
    rest = refs[steps * (count + 2):]
    amp_ref = rest[0]
    before_ref = None if first else rest[1]
    out_ref, products, ready = rest[-3:]
    step = pl.program_id(0)
    group_rows = lefts[0][0].shape[1]
    c_part = TV // GROUPS
    a_count = group_rows // c_part
    wide = 2 * GROUPS * TV
    half_blocks = rights[0][0].shape[1] // wide

    @pl.when(step < GROUPS)
    def _():
        for half in range(2):
            start = (half_ref[0] if half == 0 else 1 - half_ref[0]) * half_blocks
            for p in range(half_blocks):
                left = jnp.concatenate(
                    [jnp.concatenate([part[t][0] for part in lefts], axis=1) for t in range(count)], axis=0
                )
                right = jnp.concatenate(
                    [
                        jnp.concatenate(
                            [
                                part[half][
                                    0,
                                    pl.ds(
                                        pl.multiple_of(
                                            p * wide + (g // GROUPS * GROUPS + (g + step) % GROUPS) * TV, TV
                                        ),
                                        TV,
                                    ),
                                    :,
                                ]
                                for g in range(2 * GROUPS)
                            ],
                            axis=0,
                        )
                        for part in rights
                    ],
                    axis=1,
                )
                total = lax.dot_general(
                    left, right, (((1,), (1,)), ((), ())), preferred_element_type=jnp.float32
                )
                products[step, start + p] = total.astype(jnp.bfloat16)

    @pl.when(step >= GROUPS)
    def _():
        k = step - GROUPS
        lane_group = lax.broadcasted_iota(jnp.int32, (count * group_rows, wide), 1) // TV % GROUPS
        for p in range(2 * half_blocks):
            mixed = products[k, p]
            for g in range(1, GROUPS):
                mixed = jnp.where(lane_group == g, products[(k + GROUPS - g) % GROUPS, p], mixed)
            mixed = mixed.reshape(count, c_part, a_count, wide)
            for b in range(2):
                for c in range(c_part):
                    ready[:, 2 * p + b, :, c * GROUPS * TV:(c + 1) * GROUPS * TV] = mixed[
                        :, c, :, b * GROUPS * TV:(b + 1) * GROUPS * TV
                    ]
        amp = jnp.concatenate(
            [
                amp_ref[0, pl.ds(pl.multiple_of(((k + GROUPS - g) % GROUPS * c_part + c) * TV, TV), TV), :]
                for c in range(c_part)
                for g in range(GROUPS)
            ],
            axis=0,
        )
        block_rows = TV // GROUPS * a_count
        terms = jnp.dot(
            ready[...].reshape(count * block_rows, TV * TV), amp, preferred_element_type=jnp.float32
        ).reshape(count, block_rows, amp.shape[1])
        for t in range(count):
            term = terms[t] * live_ref[t].astype(jnp.float32)
            if not first:
                term = before_ref[t, 0] + term
            out_ref[t, 0] = term.astype(out_ref.dtype)


def ladder(half, live, pick, tile, lefts, rights, amp, before, part=None, kind=jnp.float32):
    steps = len(lefts)
    rows, depth = lefts[0].shape[1:]
    columns = amp.shape[2]
    a_count = rows // TV
    b_blocks = TV // GROUPS
    wide = 2 * GROUPS * TV
    count = NTV if part is None else NTV // 2
    base = 0 if part is None else part * count
    one = pl.Buffered(1)

    def left_spec(t):
        return pl.BlockSpec(
            (1, rows // GROUPS, depth), lambda i, h, v, k, d: (k[t], jnp.minimum(i, GROUPS - 1), 0)
        )

    def right_spec(place):
        return pl.BlockSpec(
            (1, rows, depth),
            lambda i, h, v, k, d: (d[0] if place is None else place, 0, 0),
            pipeline_mode=one,
        )

    amp_spec = pl.BlockSpec((1, 2 * rows, columns), lambda i, h, v, k, d: (d[0], 0, 0), pipeline_mode=one)

    def sum_spec(place):
        return pl.BlockSpec(
            (count, 1, b_blocks * a_count, columns),
            lambda i, h, v, k, d: (place, jnp.maximum(i - GROUPS, 0), 0, 0),
        )

    first = before is None
    flops = 2 * count * rows * 2 * rows * (steps * depth + columns)
    operands = [half, live[base:base + count], pick[base:base + count], tile]
    operands += [x for x in lefts for _ in range(count)] + [x for own, other, _ in rights for x in (own, other)] + [amp]
    return pl.pallas_call(
        functools.partial(ladder_kernel, steps, count, first),
        grid_spec=pltpu.PrefetchScalarGridSpec(
            num_scalar_prefetch=4,
            grid=(2 * GROUPS,),
            in_specs=[left_spec(t) for _ in lefts for t in range(count)]
            + [right_spec(place) for _, _, place in rights for _ in range(2)]
            + [amp_spec]
            + [sum_spec(base // count)] * (not first),
            out_specs=sum_spec(0),
            scratch_shapes=[
                pltpu.VMEM((GROUPS, 2 * rows // wide, count * rows // GROUPS, wide), jnp.bfloat16),
                pltpu.VMEM((count, b_blocks, a_count, TV * TV), jnp.bfloat16),
            ],
        ),
        out_shape=jax.ShapeDtypeStruct((count, GROUPS, b_blocks * a_count, columns), kind),
        input_output_aliases={} if first or part is not None else {len(operands): 0},
        compiler_params=pltpu.CompilerParams(vmem_limit_bytes=40 * 2**20),
        cost_estimate=pl.CostEstimate(flops=flops, bytes_accessed=20 * 2**20, transcendentals=0),
    )(*operands, *([] if first else [before]))


def partner(value, axis, size, flip):
    return lax.ppermute(value, axis, [(i, i ^ flip) for i in range(size)])


def shift(value, axis, size, step):
    return lax.ppermute(value, axis, [(i, (i + step) % size) for i in range(size)])


def ring_order(size):
    return list(range(0, size, 2)) + list(range(size - 1, 0, -2))


HOPS = (
    (1, 2), (1, 1), (1, 0), (2, 1), (2, 0), (3, 0),
    (1, 3), (2, 3), (2, 2), (3, 2), (3, 1), (3, 3),
)
AMP = "amp"
NEAR = {0: 0, 2: AMP, 4: 1, 6: 2, 8: 3}
FAR = {1: 0, 3: AMP, 5: 1, 7: 2, 9: 3}
STACK = {2: 0, 4: AMP, 6: 1, 8: 2, 10: 3}
CONTRACT = {10: 0, 11: 2, 12: 1}


def on_square(chol, amps, listed):
    row_count, depth = chol.shape[1:]
    columns = amps.shape[3]
    a_count = row_count // TV
    left_index = lax.axis_index("left")
    right_index = lax.axis_index("right")
    occ_index = lax.axis_index("occ")
    order = ring_order(NTV)
    ring = [(order[p], order[(p + 1) % NTV]) for p in range(NTV)]
    near = [[order[(order.index(level) + i) % NTV] for level in range(NTV)] for i in range(NTV)]

    def at_level(table):
        value = jnp.int32(table[0])
        for level in range(1, NTV):
            value = jnp.where(left_index == level, jnp.int32(table[level]), value)
        return value

    d_tiles = [at_level(table) for table in near]
    tiles = jnp.arange(NTV)
    targets = (left_index + 1 + tiles) % NTV
    pick = (targets ^ right_index).astype(jnp.int32)
    own_c = lax.dynamic_index_in_dim(listed, left_index, 1, keepdims=False)
    live = lax.dynamic_index_in_dim(own_c, right_index, 1, keepdims=False)[targets]
    half = occ_index.reshape(1)

    held = {("block", 0, i): lax.dynamic_slice_in_dim(chol, d_tiles[i], 1, 0) for i in (3, 2, 0, 1)}
    held["chol"] = chol
    held["left", AMP, 0] = amps[0]
    last = len(HOPS)
    waiting = {slot: [] for slot in range(last + 4)}

    def meet(keys):
        keys = list(dict.fromkeys(keys))
        for key, value in zip(keys, lax.optimization_barrier([held[key] for key in keys])):
            held[key] = value

    def contract(i, before, part=None, kind=jnp.float32):
        sides = [(held["chol"], held["other", "chol"], None)]
        sides += [(held["block", s, i], held["other", s, i], 0) for s in range(1, NTV)]
        return ladder(
            half,
            lax.dynamic_index_in_dim(live, d_tiles[i], 1, keepdims=False),
            pick,
            d_tiles[i].reshape(1),
            [held["lefts", s] for s in range(NTV)],
            sides,
            held["amp"],
            before,
            part,
            kind,
        )

    for slot in range(last + 1):
        hops = [0, 1] if slot == 0 else [slot + 1] if slot + 1 < last else []
        near_block, far_block, stack_block = NEAR.get(slot), FAR.get(slot), STACK.get(slot)
        now = waiting[slot]
        if slot >= 1:
            now.append(("block", *HOPS[slot - 1]))
        if near_block is not None:
            if near_block != AMP:
                own = held["block", near_block, 0].reshape(a_count, TV, depth)
                held["left", near_block, 0] = own.transpose(1, 0, 2).reshape(row_count, depth)
            now.append(("left", near_block, 0))
        if far_block is not None:
            now += [("left", far_block, flip) for flip in range(3)]
        if stack_block is not None:
            now.append(("left", stack_block, 3))
        now += [("block", HOPS[u][0] - 1, (HOPS[u][1] + 1) % NTV) for u in hops]
        if slot == 1:
            now.append("chol")
        meet(now)
        for u in hops:
            s, i = HOPS[u]
            held["block", s, i] = lax.ppermute(held["block", s - 1, (i + 1) % NTV], "left", ring)
        if near_block is not None:
            for flip in (1, 2):
                held["left", near_block, flip] = partner(held["left", near_block, 0], "right", NTV, flip)
        if far_block is not None:
            held["left", far_block, 3] = partner(held["left", far_block, 0], "right", NTV, 3)
        if slot == 1:
            held["other", "chol"] = partner(held["chol"], "occ", 2, 1)
            waiting[slot + 1].append(("other", "chol"))
        if slot >= 1:
            unit = HOPS[slot - 1]
            held["other", *unit] = partner(held["block", *unit], "occ", 2, 1)
            waiting[slot + 1].append(("other", *unit))
        if stack_block is not None:
            every = [held["left", stack_block, flip] for flip in range(NTV)]
            if stack_block == AMP:
                held["amp"] = lax.all_gather(jnp.concatenate(every, axis=2), "occ", axis=1, tiled=True)
                waiting[slot + 3].append("amp")
            else:
                held["lefts", stack_block] = jnp.stack(every)
                waiting[slot + 1].append(("lefts", stack_block))
        if slot in CONTRACT:
            held["sum"] = contract(CONTRACT[slot], held.get("sum"))
            waiting[slot + 1].append("sum")
    partials = held["sum"]
    early = contract(3, partials, 0, jnp.bfloat16)
    moved = [shift(early[t], "left", NTV, t + 1) for t in range(NTV // 2)]
    late = contract(3, partials, 1)
    moved += [
        shift(late[t].astype(jnp.bfloat16), "left", NTV, NTV // 2 + t + 1) for t in range(NTV // 2 - 1)
    ]
    summed = late[NTV // 2 - 1]
    for piece in moved:
        summed = summed + piece.astype(jnp.float32)
    pieces = []
    for flip in range(NTV):
        piece = summed[:, :, flip * columns:(flip + 1) * columns]
        pieces.append(partner(piece, "right", NTV, flip) if flip else piece)
    result = jnp.stack(pieces)[tiles ^ right_index]
    result = result.reshape(NTV, GROUPS, TV // GROUPS, a_count, columns).transpose(0, 3, 2, 1, 4)
    return result.reshape(1, NTV, row_count, columns)


def broadcast(value, axis, source):
    kept = jnp.where(lax.axis_index(axis) == source, value, 0).astype(value.dtype)
    return lax.psum(kept, axis)


def on_device(sizes, chol, amps, listed):
    tile_count = chol.shape[0]
    if sizes == (NTV, NTV, 2) and tile_count == NTV:
        return on_square(chol, amps, listed)
    row_count = chol.shape[1]
    a_local = row_count // TV
    left_index = lax.axis_index("left")
    right_index = lax.axis_index("right")
    first_tile = right_index * tile_count
    full_vectors = lax.all_gather(chol, "left", axis=2, tiled=True)
    collected = []
    for a_tile in range(NTV):
        wanted = a_tile * NTV + left_index
        holder = wanted // tile_count
        holder_slot = wanted % tile_count
        offered = lax.dynamic_index_in_dim(full_vectors, holder_slot, 0, keepdims=False)
        collected.append(broadcast(offered, "right", holder))
    left_rows = jnp.stack(collected)
    own_c = lax.dynamic_index_in_dim(listed, left_index, 1, keepdims=False).reshape(NTV, NTV * NTV)
    live = lax.dynamic_slice_in_dim(own_c, first_tile, tile_count, 1).T.astype(jnp.float32)
    products = jnp.einsum(
        "xrq,tkq->txrk",
        left_rows,
        lax.all_gather(full_vectors, "occ", axis=1, tiled=True),
        preferred_element_type=jnp.float32,
    )
    inner = (products * live[:, :, None, None]).astype(jnp.bfloat16)
    swapped = inner.reshape(tile_count, NTV, a_local, TV, TV, TV).transpose(0, 1, 2, 4, 3, 5)
    swapped = swapped.reshape(tile_count, NTV * a_local * TV, PAIR)
    amp_columns = lax.all_gather(amps, "right", axis=3, tiled=True)
    d_first = first_tile % NTV
    own_amps = lax.dynamic_slice_in_dim(amp_columns[0], d_first, tile_count, 0)
    partial_sum = jnp.einsum(
        "trk,tkn->rn",
        swapped,
        lax.all_gather(own_amps, "occ", axis=1, tiled=True),
        preferred_element_type=jnp.float32,
    )
    partial_sum = partial_sum.reshape(NTV, row_count, NOP)
    owned_a = lax.psum_scatter(partial_sum, "left", scatter_dimension=0, tiled=True)
    b_tile = first_tile // NTV
    placed = lax.dynamic_update_slice_in_dim(
        jnp.zeros((NTV, row_count, NOP), jnp.float32), owned_a, b_tile, 0
    )
    summed = lax.psum_scatter(placed, "right", scatter_dimension=2, tiled=True)
    return summed.reshape(1, NTV, row_count, summed.shape[2])


def solution(mesh):
    placed = (P("right", "occ", "left"), P("left", None, "occ", "right"), P())
    return jax.shard_map(
        functools.partial(on_device, tuple(mesh.shape[axis] for axis in ("left", "right", "occ"))),
        mesh=mesh,
        in_specs=placed,
        out_specs=P("left", None, "occ", "right"),
        check_vma=False,
    )
```

profile of v0, /device:TPU:8, one launch (start us, length us, event | category | flops | bytes accessed | tf_op | source)
XLA Modules:
  0.0 307.6 jit_solution(8400558123981298013)
XLA Ops:
  6.5 1.8 constant_dynamic-slice_fusion.3
  8.7 1.9 collective-permute-start.1
  10.7 1.5 collective-permute-start.2
  12.2 11.1 %collective-permute-done.refs_18_ = bf16[1,512,512]{2,1,0:T(8,128)(2,1)S(1)} collective-permute-done((bf16[1,512,512]{2,1,0:T(8,128)(2,1)S(1)}, bf16[1,512,512]{2,1,0:T(8,128)(2,1)S(1)}, u32[]{:S(2)}, u32[]{:S(2)}) %collective-permute-start) | collective-permute-done | bytes 524320 | tf_op jit(solution)/shard_map/ppermute | solution.py:252
  23.8 2.6 collective-permute-start.5
  26.6 1.5 collective-permute-start.6
  28.1 1.6 collective-permute-start.8
  29.7 9.7 %collective-permute-done.5.refs_18_ = bf16[1,512,512]{2,1,0:T(8,128)(2,1)S(1)} collective-permute-done((bf16[1,512,512]{2,1,0:T(8,128)(2,1)S(1)}, bf16[1,512,512]{2,1,0:T(8,128)(2,1)S(1)}, u32[]{:S(2)}, u32[]{:S(2)}) %collective-permute-start.5) | collective-permute-done | bytes 524320 | tf_op jit(solution)/shard_map/ppermute | solution.py:252
  40.2 1.4 collective-permute-done.6
  41.6 1.6 collective-permute-start.10
  43.7 1.6 collective-permute-start.12
  45.6 5.0 %collective-permute-done.8.refs_18_ = bf16[1,512,512]{2,1,0:T(8,128)(2,1)S(1)} collective-permute-done((bf16[1,512,512]{2,1,0:T(8,128)(2,1)S(1)}, bf16[1,512,512]{2,1,0:T(8,128)(2,1)S(1)}, u32[]{:S(2)}, u32[]{:S(2)}) %collective-permute-start.8) | collective-permute-done | bytes 524320 | tf_op jit(solution)/shard_map/ppermute | solution.py:252
  50.6 4.3 %collective-permute-done.10 = bf16[4,512,128]{2,1,0:T(8,128)(2,1)S(1)} collective-permute-done((bf16[4,512,128]{2,1,0:T(8,128)(2,1)S(1)}, bf16[4,512,128]{2,1,0:T(8,128)(2,1)S(1)}, u32[]{:S(2)}, u32[]{:S(2)}) %collective-permute-start.10) | collective-permute-done | bytes 524320 | tf_op jit(solution)/shard_map/ppermute | solution.py:157
  55.0 2.6 collective-permute-done.9
  59.1 2.4 collective-permute-done.12.refs_20_
  62.3 10.5 %collective-permute-done.13 = bf16[4,512,128]{2,1,0:T(8,128)(2,1)S(1)} collective-permute-done((bf16[4,512,128]{2,1,0:T(8,128)(2,1)S(1)}, bf16[4,512,128]{2,1,0:T(8,128)(2,1)S(1)}, u32[]{:S(2)}, u32[]{:S(2)}) %collective-permute-start.13) | collective-permute-done | bytes 524320 | tf_op jit(solution)/shard_map/ppermute | solution.py:157
  72.8 1.6 pad_maximum_fusion.1
  74.5 1.6 collective-permute-start.15
  77.1 1.2 collective-permute-start.19
  79.2 11.1 %collective-permute-done.15.refs_20_ = bf16[1,512,512]{2,1,0:T(8,128)(2,1)S(1)} collective-permute-done((bf16[1,512,512]{2,1,0:T(8,128)(2,1)S(1)}, bf16[1,512,512]{2,1,0:T(8,128)(2,1)S(1)}, u32[]{:S(2)}, u32[]{:S(2)}) %collective-permute-start.15) | collective-permute-done | bytes 524320 | tf_op jit(solution)/shard_map/ppermute | solution.py:252
  91.1 1.3 collective-permute-start.20
  92.6 1.3 collective-permute-start.22
  93.9 7.6 %collective-permute-done.19.refs_22_ = bf16[1,512,512]{2,1,0:T(8,128)(2,1)S(1)} collective-permute-done((bf16[1,512,512]{2,1,0:T(8,128)(2,1)S(1)}, bf16[1,512,512]{2,1,0:T(8,128)(2,1)S(1)}, u32[]{:S(2)}, u32[]{:S(2)}) %collective-permute-start.19) | collective-permute-done | bytes 524320 | tf_op jit(solution)/shard_map/ppermute | solution.py:252
  102.3 4.2 %collective-permute-done.20 = bf16[512,512]{1,0:T(8,128)(2,1)S(1)} collective-permute-done((bf16[512,512]{1,0:T(8,128)(2,1)}, bf16[512,512]{1,0:T(8,128)(2,1)S(1)}, u32[]{:S(2)}, u32[]{:S(2)}) %collective-permute-start.20) | collective-permute-done | bytes 524320 | tf_op jit(solution)/shard_map/ppermute | solution.py:157
  106.5 1.3 collective-permute-start.23
  109.6 2.6 pad_maximum_fusion.2.refs_4_.refs_5_.refs_6_.refs_7_.refs_2_.refs_3_
  113.0 7.8 %collective-permute-done.23 = bf16[512,512]{1,0:T(8,128)(2,1)S(1)} collective-permute-done((bf16[512,512]{1,0:T(8,128)(2,1)S(1)}, bf16[512,512]{1,0:T(8,128)(2,1)S(1)}, u32[]{:S(2)}, u32[]{:S(2)}) %collective-permute-start.23) | collective-permute-done | bytes 524320 | tf_op jit(solution)/shard_map/ppermute | solution.py:157
  123.0 2.2 copy.13
  126.4 11.2 %collective-permute-done.27 = bf16[512,512]{1,0:T(8,128)(2,1)} collective-permute-done((bf16[512,512]{1,0:T(8,128)(2,1)}, bf16[512,512]{1,0:T(8,128)(2,1)}, u32[]{:S(2)}, u32[]{:S(2)}) %collective-permute-start.27) | collective-permute-done | bytes 524320 | tf_op jit(solution)/shard_map/ppermute | solution.py:157
  139.6 1.3 collective-permute-start.33
  140.9 1.9 pad_maximum_fusion.3.refs_8_.refs_9_.refs_10_.refs_11_.refs_4_.refs_5_
  142.9 8.5 %collective-permute-done.30 = bf16[512,512]{1,0:T(8,128)(2,1)} collective-permute-done((bf16[512,512]{1,0:T(8,128)(2,1)}, bf16[512,512]{1,0:T(8,128)(2,1)}, u32[]{:S(2)}, u32[]{:S(2)}) %collective-permute-start.30) | collective-permute-done | bytes 524320 | tf_op jit(solution)/shard_map/ppermute | solution.py:157
  153.6 1.2 collective-permute-start.36
  154.9 12.5 %collective-permute-done.34 = bf16[512,512]{1,0:T(8,128)(2,1)S(1)} collective-permute-done((bf16[512,512]{1,0:T(8,128)(2,1)}, bf16[512,512]{1,0:T(8,128)(2,1)S(1)}, u32[]{:S(2)}, u32[]{:S(2)}) %collective-permute-start.34) | collective-permute-done | bytes 524320 | tf_op jit(solution)/shard_map/ppermute | solution.py:157
  167.5 1.2 collective-permute-start.38
  168.7 1.8 pad_maximum_fusion.4.refs_12_.refs_13_.refs_14_.refs_15_.refs_6_.refs_7_
  171.4 16.0 %shard_map.37.refs_25_ = f32[4,4,128,512]{3,2,1,0:T(8,128)} custom-call(s32[1]{0:T(128)} %bitcast.half_ref, s32[4]{0:T(128)S(1)} %get-tuple-element.139.live_ref, s32[4]{0:T(128)S(1)} %fusion.7.pick_ref, s32[1]{0:T(128)} %bitcast.33.tile_ref, bf16[4,512,512]{2,1,0:T(8,128)(2,1)S(1)} %pad_maximum_fusion.refs_0_.refs_1_.refs_2_.refs_3_, ...), custom_call_target="tpu_custom_call" | custom-call | flops 10737418240 | bytes 20971520 | tf_op jit(solution)/shard_map/pallas_call | solution.py:134
  187.8 17.7 %shard_map.38.refs_25_ = f32[4,4,128,512]{3,2,1,0:T(8,128)} custom-call(s32[1]{0:T(128)} %bitcast.half_ref, s32[4]{0:T(128)S(1)} %get-tuple-element.138.live_ref, s32[4]{0:T(128)S(1)} %fusion.7.pick_ref, s32[1]{0:T(128)} %bitcast.34.tile_ref, ...), custom_call_target="tpu_custom_call", output_to_operand_aliasing={{}: (29, {})} | custom-call | flops 10737418240 | bytes 20971520 | tf_op jit(solution)/shard_map/pallas_call | solution.py:134
  205.8 17.5 %shard_map.39.refs_17_ = f32[4,4,128,512]{3,2,1,0:T(8,128)} custom-call(s32[1]{0:T(128)} %bitcast.half_ref, s32[4]{0:T(128)S(1)} %get-tuple-element.137.live_ref, s32[4]{0:T(128)S(1)} %fusion.7.pick_ref, s32[1]{0:T(128)} %bitcast.35.tile_ref, ...), custom_call_target="tpu_custom_call", output_to_operand_aliasing={{}: (29, {})} | custom-call | flops 10737418240 | bytes 20971520 | tf_op jit(solution)/shard_map/pallas_call | solution.py:134
  223.4 11.1 %shard_map.41 = bf16[2,4,128,512]{3,2,1,0:T(8,128)(2,1)S(1)} custom-call(s32[1]{0:T(128)} %bitcast.half_ref, s32[2]{0:T(128)S(1)} %get-tuple-element.135.live_ref, s32[2]{0:T(128)S(1)} %get-tuple-element.151.pick_ref, s32[1]{0:T(128)} %bitcast.3.tile_ref, bf16[4,512,512]{2,1,0:T(8,128)(2,1)S(1)} %pad_maximum_fusion.refs_0_.refs_1_.refs_2_.refs_3_, ...), custom_call_target="tpu_custom_call" | custom-call | flops 5368709120 | bytes 20971520 | tf_op jit(solution)/shard_map/pallas_call | solution.py:134
  235.3 3.1 collective-permute-start.41
  238.4 11.2 %shard_map.40 = f32[2,4,128,512]{3,2,1,0:T(8,128)S(1)} custom-call(s32[1]{0:T(128)} %bitcast.half_ref, s32[2]{0:T(128)S(1)} %get-tuple-element.136.live_ref, s32[2]{0:T(128)S(1)} %get-tuple-element.152.pick_ref, s32[1]{0:T(128)} %bitcast.3.tile_ref, bf16[4,512,512]{2,1,0:T(8,128)(2,1)S(1)} %pad_maximum_fusion.refs_0_.refs_1_.refs_2_.refs_3_, ...), custom_call_target="tpu_custom_call" | custom-call | flops 5368709120 | bytes 20971520 | tf_op jit(solution)/shard_map/pallas_call | solution.py:134
  249.7 30.9 %collective-permute-done.41 = bf16[4,128,512]{2,1,0:T(8,128)(2,1)S(1)} collective-permute-done((bf16[4,128,512]{2,1,0:T(8,128)(2,1)S(1)}, bf16[4,128,512]{2,1,0:T(8,128)(2,1)S(1)}, u32[]{:S(2)}, u32[]{:S(2)}) %collective-permute-start.41) | collective-permute-done | bytes 524320 | tf_op jit(solution)/shard_map/ppermute | solution.py:161
  280.6 3.0 collective-permute-done.42
  285.7 1.8 collective-permute-start.45
  287.6 5.7 %collective-permute-done.43 = f32[4,128,128]{2,1,0:T(8,128)S(1)} collective-permute-done((f32[4,128,128]{2,1,0:T(8,128)S(1)}, f32[4,128,128]{2,1,0:T(8,128)S(1)}, u32[]{:S(2)}, u32[]{:S(2)}) %collective-permute-start.43) | collective-permute-done | bytes 262176 | tf_op jit(solution)/shard_map/ppermute | solution.py:157
  293.3 5.1 %collective-permute-done.44 = f32[4,128,128]{2,1,0:T(8,128)S(1)} collective-permute-done((f32[4,128,128]{2,1,0:T(8,128)S(1)}, f32[4,128,128]{2,1,0:T(8,128)S(1)}, u32[]{:S(2)}, u32[]{:S(2)}) %collective-permute-start.44) | collective-permute-done | bytes 262176 | tf_op jit(solution)/shard_map/ppermute | solution.py:157
  299.1 1.6 copy.14
  (145 shorter events, 24.5 us)
Async XLA Ops:
  6.5 132.5 %copy-start = (s32[4,4,4,4]{3,2,1,0:T(4,128)S(1)}, s32[4,4,4,4]{3,2,1,0:T(4,128)}, u32[]{:S(2)}) copy-start(s32[4,4,4,4]{3,2,1,0:T(4,128)} %param.5) | copy-start | bytes 3076
  6.5 115.5 %all-gather.2.cloned.1.call-start = ((), (), s32[]{:S(2)}) async-start(), calls=%async_computation | async-start | bytes 6291456 | tf_op jit(solution)/shard_map/all_gather | solution.py:268
  8.7 14.6 %collective-permute-start = (bf16[1,512,512]{2,1,0:T(8,128)(2,1)S(1)}, bf16[1,512,512]{2,1,0:T(8,128)(2,1)S(1)}, u32[]{:S(2)}, u32[]{:S(2)}) collective-permute-start(bf16[1,512,512]{2,1,0:T(8,128)(2,1)S(1)} %get-tuple-element.70), channel_id=1, source_target_pairs={{0,16},{16,24},{24,8},{8,0},{1,17},{17,25},{25,9},{9,1},{2,18},{18... | collective-permute-start | bytes 1572872 | tf_op jit(solution)/shard_map/ppermute | solution.py:252
  8.7 14.6 %collective-permute-start.1 = (bf16[512,512]{1,0:T(8,128)(2,1)S(1)}, bf16[512,512]{1,0:T(8,128)(2,1)S(1)}, u32[]{:S(2)}, u32[]{:S(2)}) collective-permute-start(bf16[512,512]{1,0:T(8,128)(2,1)S(1)} %bitcast.79), channel_id=1, source_target_pairs={{0,2},{2,0},{4,6},{6,4},{1,3},{3,1},{5,7},{7,5},{8,10},{10,8},{12,... | collective-permute-start | bytes 1572872 | tf_op jit(solution)/shard_map/ppermute | solution.py:157
  10.7 13.1 %collective-permute-start.2 = (bf16[512,512]{1,0:T(8,128)(2,1)S(1)}, bf16[512,512]{1,0:T(8,128)(2,1)S(1)}, u32[]{:S(2)}, u32[]{:S(2)}) collective-permute-start(bf16[512,512]{1,0:T(8,128)(2,1)S(1)} %bitcast.80), channel_id=1, source_target_pairs={{0,4},{2,6},{4,0},{6,2},{1,5},{3,7},{5,1},{7,3},{8,12},{10,14},{12... | collective-permute-start | bytes 1572872 | tf_op jit(solution)/shard_map/ppermute | solution.py:157
  23.8 17.8 %collective-permute-start.3 = (bf16[4,512,512]{2,1,0:T(8,128)(2,1)S(1)}, bf16[4,512,512]{2,1,0:T(8,128)(2,1)S(1)}, u32[]{:S(2)}, u32[]{:S(2)}) collective-permute-start(bf16[4,512,512]{2,1,0:T(8,128)(2,1)S(1)} %copy-done.2), channel_id=1, source_target_pairs={{0,1},{1,0},{2,3},{3,2},{4,5},{5,4},{6,7},{7,6},{8,9},{9,8},{10,11... | collective-permute-start | bytes 6291464 | tf_op jit(solution)/shard_map/ppermute | solution.py:157
  23.8 15.6 %collective-permute-start.5 = (bf16[1,512,512]{2,1,0:T(8,128)(2,1)S(1)}, bf16[1,512,512]{2,1,0:T(8,128)(2,1)S(1)}, u32[]{:S(2)}, u32[]{:S(2)}) collective-permute-start(bf16[1,512,512]{2,1,0:T(8,128)(2,1)S(1)} %get-tuple-element.74), channel_id=1, source_target_pairs={{0,16},{16,24},{24,8},{8,0},{1,17},{17,25},{25,9},{9,1},{2,18},{18... | collective-permute-start | bytes 1572872 | tf_op jit(solution)/shard_map/ppermute | solution.py:252
  26.4 13.0 %collective-permute-start.4 = (bf16[1,512,512]{2,1,0:T(8,128)(2,1)S(1)}, bf16[1,512,512]{2,1,0:T(8,128)(2,1)S(1)}, u32[]{:S(2)}, u32[]{:S(2)}) collective-permute-start(bf16[1,512,512]{2,1,0:T(8,128)(2,1)S(1)} %collective-permute-done.refs_18_), channel_id=1, source_target_pairs={{0,1},{1,0},{2,3},{3,2},{4,5},{5,4},{6,7},{7,6},{8,9},{9,8},{10,11... | collective-permute-start | bytes 1572872 | tf_op jit(solution)/shard_map/ppermute | solution.py:157
  26.6 15.0 %collective-permute-start.6 = (bf16[512,512]{1,0:T(8,128)(2,1)S(1)}, bf16[512,512]{1,0:T(8,128)(2,1)S(1)}, u32[]{:S(2)}, u32[]{:S(2)}) collective-permute-start(bf16[512,512]{1,0:T(8,128)(2,1)S(1)} %bitcast.81), channel_id=1, source_target_pairs={{0,6},{2,4},{4,2},{6,0},{1,7},{3,5},{5,3},{7,1},{8,14},{10,12},{12... | collective-permute-start | bytes 1572872 | tf_op jit(solution)/shard_map/ppermute | solution.py:157
  28.1 22.5 %collective-permute-start.8 = (bf16[1,512,512]{2,1,0:T(8,128)(2,1)S(1)}, bf16[1,512,512]{2,1,0:T(8,128)(2,1)S(1)}, u32[]{:S(2)}, u32[]{:S(2)}) collective-permute-start(bf16[1,512,512]{2,1,0:T(8,128)(2,1)S(1)} %get-tuple-element.80), channel_id=1, source_target_pairs={{0,16},{16,24},{24,8},{8,0},{1,17},{17,25},{25,9},{9,1},{2,18},{18... | collective-permute-start | bytes 1572872 | tf_op jit(solution)/shard_map/ppermute | solution.py:252
  41.6 13.4 %collective-permute-start.10 = (bf16[4,512,128]{2,1,0:T(8,128)(2,1)S(1)}, bf16[4,512,128]{2,1,0:T(8,128)(2,1)S(1)}, u32[]{:S(2)}, u32[]{:S(2)}) collective-permute-start(bf16[4,512,128]{2,1,0:T(8,128)(2,1)S(1)} %bitcast.83), channel_id=1, source_target_pairs={{0,4},{2,6},{4,0},{6,2},{1,5},{3,7},{5,1},{7,3},{8,12},{10,14},{12... | collective-permute-start | bytes 1572872 | tf_op jit(solution)/shard_map/ppermute | solution.py:157
  43.2 11.8 %collective-permute-start.7 = (bf16[1,512,512]{2,1,0:T(8,128)(2,1)S(1)}, bf16[1,512,512]{2,1,0:T(8,128)(2,1)S(1)}, u32[]{:S(2)}, u32[]{:S(2)}) collective-permute-start(bf16[1,512,512]{2,1,0:T(8,128)(2,1)S(1)} %collective-permute-done.5.refs_18_), channel_id=1, source_target_pairs={{0,1},{1,0},{2,3},{3,2},{4,5},{5,4},{6,7},{7,6},{8,9},{9,8},{10,11... | collective-permute-start | bytes 1572872 | tf_op jit(solution)/shard_map/ppermute | solution.py:157
  43.2 14.3 %collective-permute-start.9 = (bf16[4,512,128]{2,1,0:T(8,128)(2,1)S(1)}, bf16[4,512,128]{2,1,0:T(8,128)(2,1)S(1)}, u32[]{:S(2)}, u32[]{:S(2)}) collective-permute-start(bf16[4,512,128]{2,1,0:T(8,128)(2,1)S(1)} %bitcast.84), channel_id=1, source_target_pairs={{0,2},{2,0},{4,6},{6,4},{1,3},{3,1},{5,7},{7,5},{8,10},{10,8},{12,... | collective-permute-start | bytes 1572872 | tf_op jit(solution)/shard_map/ppermute | solution.py:157
  43.7 17.7 %collective-permute-start.12 = (bf16[1,512,512]{2,1,0:T(8,128)(2,1)S(1)}, bf16[1,512,512]{2,1,0:T(8,128)(2,1)S(1)}, u32[]{:S(2)}, u32[]{:S(2)}) collective-permute-start(bf16[1,512,512]{2,1,0:T(8,128)(2,1)S(1)} %collective-permute-done.refs_18_), channel_id=1, source_target_pairs={{0,16},{16,24},{24,8},{8,0},{1,17},{17,25},{25,9},{9,1},{2,18},{18... | collective-permute-start | bytes 1572872 | tf_op jit(solution)/shard_map/ppermute | solution.py:252
  57.5 3.9 %collective-permute-start.11 = (bf16[1,512,512]{2,1,0:T(8,128)(2,1)S(1)}, bf16[1,512,512]{2,1,0:T(8,128)(2,1)S(1)}, u32[]{:S(2)}, u32[]{:S(2)}) collective-permute-start(bf16[1,512,512]{2,1,0:T(8,128)(2,1)S(1)} %collective-permute-done.8.refs_18_), channel_id=1, source_target_pairs={{0,1},{1,0},{2,3},{3,2},{4,5},{5,4},{6,7},{7,6},{8,9},{9,8},{10,11... | collective-permute-start | bytes 1572872 | tf_op jit(solution)/shard_map/ppermute | solution.py:157
  57.5 15.2 %collective-permute-start.13 = (bf16[4,512,128]{2,1,0:T(8,128)(2,1)S(1)}, bf16[4,512,128]{2,1,0:T(8,128)(2,1)S(1)}, u32[]{:S(2)}, u32[]{:S(2)}) collective-permute-start(bf16[4,512,128]{2,1,0:T(8,128)(2,1)S(1)} %bitcast.85), channel_id=1, source_target_pairs={{0,6},{2,4},{4,2},{6,0},{1,7},{3,5},{5,3},{7,1},{8,14},{10,12},{12... | collective-permute-start | bytes 1572872 | tf_op jit(solution)/shard_map/ppermute | solution.py:157
  74.5 15.8 %collective-permute-start.15 = (bf16[1,512,512]{2,1,0:T(8,128)(2,1)S(1)}, bf16[1,512,512]{2,1,0:T(8,128)(2,1)S(1)}, u32[]{:S(2)}, u32[]{:S(2)}) collective-permute-start(bf16[1,512,512]{2,1,0:T(8,128)(2,1)S(1)} %collective-permute-done.5.refs_18_), channel_id=1, source_target_pairs={{0,16},{16,24},{24,8},{8,0},{1,17},{17,25},{25,9},{9,1},{2,18},{18... | collective-permute-start | bytes 1572872 | tf_op jit(solution)/shard_map/ppermute | solution.py:252
  76.1 14.2 %collective-permute-start.14 = (bf16[1,512,512]{2,1,0:T(8,128)(2,1)S(1)}, bf16[1,512,512]{2,1,0:T(8,128)(2,1)S(1)}, u32[]{:S(2)}, u32[]{:S(2)}) collective-permute-start(bf16[1,512,512]{2,1,0:T(8,128)(2,1)S(1)} %collective-permute-done.12.refs_20_), channel_id=1, source_target_pairs={{0,1},{1,0},{2,3},{3,2},{4,5},{5,4},{6,7},{7,6},{8,9},{9,8},{10,11... | collective-permute-start | bytes 1572872 | tf_op jit(solution)/shard_map/ppermute | solution.py:157
  76.1 15.0 %collective-permute-start.16 = (bf16[512,512]{1,0:T(8,128)(2,1)}, bf16[512,512]{1,0:T(8,128)(2,1)S(1)}, u32[]{:S(2)}, u32[]{:S(2)}) collective-permute-start(bf16[512,512]{1,0:T(8,128)(2,1)} %bitcast.75), channel_id=1, source_target_pairs={{0,2},{2,0},{4,6},{6,4},{1,3},{3,1},{5,7},{7,5},{8,10},{10,8},{12,... | collective-permute-start | bytes 1572872 | tf_op jit(solution)/shard_map/ppermute | solution.py:157
  76.6 14.4 %collective-permute-start.17 = (bf16[512,512]{1,0:T(8,128)(2,1)}, bf16[512,512]{1,0:T(8,128)(2,1)S(1)}, u32[]{:S(2)}, u32[]{:S(2)}) collective-permute-start(bf16[512,512]{1,0:T(8,128)(2,1)} %bitcast.76), channel_id=1, source_target_pairs={{0,4},{2,6},{4,0},{6,2},{1,5},{3,7},{5,1},{7,3},{8,12},{10,14},{12... | collective-permute-start | bytes 1572872 | tf_op jit(solution)/shard_map/ppermute | solution.py:157
  77.1 24.3 %collective-permute-start.19 = (bf16[1,512,512]{2,1,0:T(8,128)(2,1)S(1)}, bf16[1,512,512]{2,1,0:T(8,128)(2,1)S(1)}, u32[]{:S(2)}, u32[]{:S(2)}) collective-permute-start(bf16[1,512,512]{2,1,0:T(8,128)(2,1)S(1)} %collective-permute-done.12.refs_20_), channel_id=1, source_target_pairs={{0,16},{16,24},{24,8},{8,0},{1,17},{17,25},{25,9},{9,1},{2,18},{18... | collective-permute-start | bytes 1572872 | tf_op jit(solution)/shard_map/ppermute | solution.py:252
  91.1 10.4 %collective-permute-start.18 = (bf16[1,512,512]{2,1,0:T(8,128)(2,1)S(1)}, bf16[1,512,512]{2,1,0:T(8,128)(2,1)S(1)}, u32[]{:S(2)}, u32[]{:S(2)}) collective-permute-start(bf16[1,512,512]{2,1,0:T(8,128)(2,1)S(1)} %collective-permute-done.15.refs_20_), channel_id=1, source_target_pairs={{0,1},{1,0},{2,3},{3,2},{4,5},{5,4},{6,7},{7,6},{8,9},{9,8},{10,11... | collective-permute-start | bytes 1572872 | tf_op jit(solution)/shard_map/ppermute | solution.py:157
  91.1 15.4 %collective-permute-start.20 = (bf16[512,512]{1,0:T(8,128)(2,1)}, bf16[512,512]{1,0:T(8,128)(2,1)S(1)}, u32[]{:S(2)}, u32[]{:S(2)}) collective-permute-start(bf16[512,512]{1,0:T(8,128)(2,1)} %bitcast.77), channel_id=1, source_target_pairs={{0,6},{2,4},{4,2},{6,0},{1,7},{3,5},{5,3},{7,1},{8,14},{10,12},{12... | collective-permute-start | bytes 1572872 | tf_op jit(solution)/shard_map/ppermute | solution.py:157
  92.6 19.6 %collective-permute-start.22 = (bf16[1,512,512]{2,1,0:T(8,128)(2,1)}, bf16[1,512,512]{2,1,0:T(8,128)(2,1)S(1)}, u32[]{:S(2)}, u32[]{:S(2)}) collective-permute-start(bf16[1,512,512]{2,1,0:T(8,128)(2,1)} %copy-done.29), channel_id=1, source_target_pairs={{0,16},{16,24},{24,8},{8,0},{1,17},{17,25},{25,9},{9,1},{2,18},{18... | collective-permute-start | bytes 1572872 | tf_op jit(solution)/shard_map/ppermute | solution.py:252
  106.5 5.7 %collective-permute-start.21 = (bf16[1,512,512]{2,1,0:T(8,128)(2,1)S(1)}, bf16[1,512,512]{2,1,0:T(8,128)(2,1)S(1)}, u32[]{:S(2)}, u32[]{:S(2)}) collective-permute-start(bf16[1,512,512]{2,1,0:T(8,128)(2,1)S(1)} %collective-permute-done.19.refs_22_), channel_id=1, source_target_pairs={{0,1},{1,0},{2,3},{3,2},{4,5},{5,4},{6,7},{7,6},{8,9},{9,8},{10,11... | collective-permute-start | bytes 1572872 | tf_op jit(solution)/shard_map/ppermute | solution.py:157
  106.5 14.3 %collective-permute-start.23 = (bf16[512,512]{1,0:T(8,128)(2,1)S(1)}, bf16[512,512]{1,0:T(8,128)(2,1)S(1)}, u32[]{:S(2)}, u32[]{:S(2)}) collective-permute-start(bf16[512,512]{1,0:T(8,128)(2,1)S(1)} %bitcast.71), channel_id=1, source_target_pairs={{0,2},{2,0},{4,6},{6,4},{1,3},{3,1},{5,7},{7,5},{8,10},{10,8},{12,... | collective-permute-start | bytes 1572872 | tf_op jit(solution)/shard_map/ppermute | solution.py:157
  107.8 14.2 %collective-permute-start.24 = (bf16[512,512]{1,0:T(8,128)(2,1)S(1)}, bf16[512,512]{1,0:T(8,128)(2,1)}, u32[]{:S(2)}, u32[]{:S(2)}) collective-permute-start(bf16[512,512]{1,0:T(8,128)(2,1)S(1)} %bitcast.72), channel_id=1, source_target_pairs={{0,4},{2,6},{4,0},{6,2},{1,5},{3,7},{5,1},{7,3},{8,12},{10,14},{12... | collective-permute-start | bytes 1572872 | tf_op jit(solution)/shard_map/ppermute | solution.py:157
  108.3 18.0 %collective-permute-start.26 = (bf16[1,512,512]{2,1,0:T(8,128)(2,1)}, bf16[1,512,512]{2,1,0:T(8,128)(2,1)S(1)}, u32[]{:S(2)}, u32[]{:S(2)}) collective-permute-start(bf16[1,512,512]{2,1,0:T(8,128)(2,1)} %copy-done.4), channel_id=1, source_target_pairs={{0,16},{16,24},{24,8},{8,0},{1,17},{17,25},{25,9},{9,1},{2,18},{18... | collective-permute-start | bytes 1572872 | tf_op jit(solution)/shard_map/ppermute | solution.py:252
  122.0 4.4 %collective-permute-start.25 = (bf16[1,512,512]{2,1,0:T(8,128)(2,1)S(1)}, bf16[1,512,512]{2,1,0:T(8,128)(2,1)}, u32[]{:S(2)}, u32[]{:S(2)}) collective-permute-start(bf16[1,512,512]{2,1,0:T(8,128)(2,1)S(1)} %collective-permute-done.22.refs_10_), channel_id=1, source_target_pairs={{0,1},{1,0},{2,3},{3,2},{4,5},{5,4},{6,7},{7,6},{8,9},{9,8},{10,11... | collective-permute-start | bytes 1572872 | tf_op jit(solution)/shard_map/ppermute | solution.py:157
  122.0 15.6 %collective-permute-start.27 = (bf16[512,512]{1,0:T(8,128)(2,1)}, bf16[512,512]{1,0:T(8,128)(2,1)}, u32[]{:S(2)}, u32[]{:S(2)}) collective-permute-start(bf16[512,512]{1,0:T(8,128)(2,1)} %bitcast.73), channel_id=1, source_target_pairs={{0,6},{2,4},{4,2},{6,0},{1,7},{3,5},{5,3},{7,1},{8,14},{10,12},{12... | collective-permute-start | bytes 1572872 | tf_op jit(solution)/shard_map/ppermute | solution.py:157
  125.2 17.7 %collective-permute-start.29 = (bf16[1,512,512]{2,1,0:T(8,128)(2,1)S(1)}, bf16[1,512,512]{2,1,0:T(8,128)(2,1)}, u32[]{:S(2)}, u32[]{:S(2)}) collective-permute-start(bf16[1,512,512]{2,1,0:T(8,128)(2,1)S(1)} %collective-permute-done.22.refs_10_), channel_id=1, source_target_pairs={{0,16},{16,24},{24,8},{8,0},{1,17},{17,25},{25,9},{9,1},{2,18},{18... | collective-permute-start | bytes 1572872 | tf_op jit(solution)/shard_map/ppermute | solution.py:252
  137.6 13.9 %collective-permute-start.30 = (bf16[512,512]{1,0:T(8,128)(2,1)}, bf16[512,512]{1,0:T(8,128)(2,1)}, u32[]{:S(2)}, u32[]{:S(2)}) collective-permute-start(bf16[512,512]{1,0:T(8,128)(2,1)} %bitcast.24), channel_id=1, source_target_pairs={{0,2},{2,0},{4,6},{6,4},{1,3},{3,1},{5,7},{7,5},{8,10},{10,8},{12,... | collective-permute-start | bytes 1572872 | tf_op jit(solution)/shard_map/ppermute | solution.py:157
  138.5 13.5 %collective-permute-start.31 = (bf16[512,512]{1,0:T(8,128)(2,1)}, bf16[512,512]{1,0:T(8,128)(2,1)}, u32[]{:S(2)}, u32[]{:S(2)}) collective-permute-start(bf16[512,512]{1,0:T(8,128)(2,1)} %bitcast.24), channel_id=1, source_target_pairs={{0,4},{2,6},{4,0},{6,2},{1,5},{3,7},{5,1},{7,3},{8,12},{10,14},{12... | collective-permute-start | bytes 1572872 | tf_op jit(solution)/shard_map/ppermute | solution.py:157
  139.0 3.9 %collective-permute-start.28 = (bf16[1,512,512]{2,1,0:T(8,128)(2,1)S(1)}, bf16[1,512,512]{2,1,0:T(8,128)(2,1)}, u32[]{:S(2)}, u32[]{:S(2)}) collective-permute-start(bf16[1,512,512]{2,1,0:T(8,128)(2,1)S(1)} %collective-permute-done.26.refs_12_), channel_id=1, source_target_pairs={{0,1},{1,0},{2,3},{3,2},{4,5},{5,4},{6,7},{7,6},{8,9},{9,8},{10,11... | collective-permute-start | bytes 1572872 | tf_op jit(solution)/shard_map/ppermute | solution.py:157
  139.6 15.3 %collective-permute-start.33 = (bf16[1,512,512]{2,1,0:T(8,128)(2,1)S(1)}, bf16[1,512,512]{2,1,0:T(8,128)(2,1)S(1)}, u32[]{:S(2)}, u32[]{:S(2)}) collective-permute-start(bf16[1,512,512]{2,1,0:T(8,128)(2,1)S(1)} %collective-permute-done.26.refs_12_), channel_id=1, source_target_pairs={{0,16},{16,24},{24,8},{8,0},{1,17},{17,25},{25,9},{9,1},{2,18},{18... | collective-permute-start | bytes 1572872 | tf_op jit(solution)/shard_map/ppermute | solution.py:252
  152.0 2.9 collective-permute-start.32
  152.0 15.4 %collective-permute-start.34 = (bf16[512,512]{1,0:T(8,128)(2,1)}, bf16[512,512]{1,0:T(8,128)(2,1)S(1)}, u32[]{:S(2)}, u32[]{:S(2)}) collective-permute-start(bf16[512,512]{1,0:T(8,128)(2,1)} %bitcast.24), channel_id=1, source_target_pairs={{0,6},{2,4},{4,2},{6,0},{1,7},{3,5},{5,3},{7,1},{8,14},{10,12},{12... | collective-permute-start | bytes 1572872 | tf_op jit(solution)/shard_map/ppermute | solution.py:157
  153.6 33.9 %collective-permute-start.36 = (bf16[1,512,512]{2,1,0:T(8,128)(2,1)}, bf16[1,512,512]{2,1,0:T(8,128)(2,1)S(1)}, u32[]{:S(2)}, u32[]{:S(2)}) collective-permute-start(bf16[1,512,512]{2,1,0:T(8,128)(2,1)} %collective-permute-done.29.refs_20_), channel_id=1, source_target_pairs={{0,16},{16,24},{24,8},{8,0},{1,17},{17,25},{25,9},{9,1},{2,18},{18... | collective-permute-start | bytes 1572872 | tf_op jit(solution)/shard_map/ppermute | solution.py:252
  167.5 19.9 %collective-permute-start.35 = (bf16[1,512,512]{2,1,0:T(8,128)(2,1)S(1)}, bf16[1,512,512]{2,1,0:T(8,128)(2,1)S(1)}, u32[]{:S(2)}, u32[]{:S(2)}) collective-permute-start(bf16[1,512,512]{2,1,0:T(8,128)(2,1)S(1)} %collective-permute-done.33.refs_22_), channel_id=1, source_target_pairs={{0,1},{1,0},{2,3},{3,2},{4,5},{5,4},{6,7},{7,6},{8,9},{9,8},{10,11... | collective-permute-start | bytes 1572872 | tf_op jit(solution)/shard_map/ppermute | solution.py:157
  167.5 38.0 %collective-permute-start.38 = (bf16[1,512,512]{2,1,0:T(8,128)(2,1)S(1)}, bf16[1,512,512]{2,1,0:T(8,128)(2,1)S(1)}, u32[]{:S(2)}, u32[]{:S(2)}) collective-permute-start(bf16[1,512,512]{2,1,0:T(8,128)(2,1)S(1)} %copy-done.7), channel_id=1, source_target_pairs={{0,16},{16,24},{24,8},{8,0},{1,17},{17,25},{25,9},{9,1},{2,18},{18... | collective-permute-start | bytes 1572872 | tf_op jit(solution)/shard_map/ppermute | solution.py:252
  187.4 18.0 %collective-permute-start.37 = (bf16[1,512,512]{2,1,0:T(8,128)(2,1)S(1)}, bf16[1,512,512]{2,1,0:T(8,128)(2,1)S(1)}, u32[]{:S(2)}, u32[]{:S(2)}) collective-permute-start(bf16[1,512,512]{2,1,0:T(8,128)(2,1)S(1)} %collective-permute-done.36.refs_22_), channel_id=1, source_target_pairs={{0,1},{1,0},{2,3},{3,2},{4,5},{5,4},{6,7},{7,6},{8,9},{9,8},{10,11... | collective-permute-start | bytes 1572872 | tf_op jit(solution)/shard_map/ppermute | solution.py:157
  205.5 17.9 %collective-permute-start.39 = (bf16[1,512,512]{2,1,0:T(8,128)(2,1)S(1)}, bf16[1,512,512]{2,1,0:T(8,128)(2,1)S(1)}, u32[]{:S(2)}, u32[]{:S(2)}) collective-permute-start(bf16[1,512,512]{2,1,0:T(8,128)(2,1)S(1)} %collective-permute-done.38.refs_14_), channel_id=1, source_target_pairs={{0,1},{1,0},{2,3},{3,2},{4,5},{5,4},{6,7},{7,6},{8,9},{9,8},{10,11... | collective-permute-start | bytes 1572872 | tf_op jit(solution)/shard_map/ppermute | solution.py:157
  234.6 15.1 %collective-permute-start.40 = (bf16[4,128,512]{2,1,0:T(8,128)(2,1)S(1)}, bf16[4,128,512]{2,1,0:T(8,128)(2,1)S(1)}, u32[]{:S(2)}, u32[]{:S(2)}) collective-permute-start(bf16[4,128,512]{2,1,0:T(8,128)(2,1)S(1)} %get-tuple-element.148), channel_id=1, source_target_pairs={{0,8},{8,16},{16,24},{24,0},{1,9},{9,17},{17,25},{25,1},{2,10},{10... | collective-permute-start | bytes 1572872 | tf_op jit(solution)/shard_map/ppermute | solution.py:161
  235.3 45.3 %collective-permute-start.41 = (bf16[4,128,512]{2,1,0:T(8,128)(2,1)S(1)}, bf16[4,128,512]{2,1,0:T(8,128)(2,1)S(1)}, u32[]{:S(2)}, u32[]{:S(2)}) collective-permute-start(bf16[4,128,512]{2,1,0:T(8,128)(2,1)S(1)} %get-tuple-element.149), channel_id=1, source_target_pairs={{0,16},{8,24},{16,0},{24,8},{1,17},{9,25},{17,1},{25,9},{2,18},{10... | collective-permute-start | bytes 1572872 | tf_op jit(solution)/shard_map/ppermute | solution.py:161
  249.6 34.0 %collective-permute-start.42 = (bf16[4,128,512]{2,1,0:T(8,128)(2,1)S(1)}, bf16[4,128,512]{2,1,0:T(8,128)(2,1)S(1)}, u32[]{:S(2)}, u32[]{:S(2)}) collective-permute-start(bf16[4,128,512]{2,1,0:T(8,128)(2,1)S(1)} %fusion.3), channel_id=1, source_target_pairs={{0,24},{8,0},{16,8},{24,16},{1,25},{9,1},{17,9},{25,17},{2,26},{10... | collective-permute-start | bytes 1572872 | tf_op jit(solution)/shard_map/ppermute | solution.py:161
  284.0 9.3 %collective-permute-start.43 = (f32[4,128,128]{2,1,0:T(8,128)S(1)}, f32[4,128,128]{2,1,0:T(8,128)S(1)}, u32[]{:S(2)}, u32[]{:S(2)}) collective-permute-start(f32[4,128,128]{2,1,0:T(8,128)S(1)} %get-tuple-element.147), channel_id=1, source_target_pairs={{0,2},{2,0},{4,6},{6,4},{1,3},{3,1},{5,7},{7,5},{8,10},{10,8},{12,... | collective-permute-start | bytes 786440 | tf_op jit(solution)/shard_map/ppermute | solution.py:157
  285.2 13.2 %collective-permute-start.44 = (f32[4,128,128]{2,1,0:T(8,128)S(1)}, f32[4,128,128]{2,1,0:T(8,128)S(1)}, u32[]{:S(2)}, u32[]{:S(2)}) collective-permute-start(f32[4,128,128]{2,1,0:T(8,128)S(1)} %get-tuple-element.146), channel_id=1, source_target_pairs={{0,4},{2,6},{4,0},{6,2},{1,5},{3,7},{5,1},{7,3},{8,12},{10,14},{12... | collective-permute-start | bytes 786440 | tf_op jit(solution)/shard_map/ppermute | solution.py:157
  285.7 12.7 %collective-permute-start.45 = (f32[4,128,128]{2,1,0:T(8,128)S(1)}, f32[4,128,128]{2,1,0:T(8,128)S(1)}, u32[]{:S(2)}, u32[]{:S(2)}) collective-permute-start(f32[4,128,128]{2,1,0:T(8,128)S(1)} %get-tuple-element.145), channel_id=1, source_target_pairs={{0,6},{2,4},{4,2},{6,0},{1,7},{3,5},{5,3},{7,1},{8,14},{10,12},{12... | collective-permute-start | bytes 786440 | tf_op jit(solution)/shard_map/ppermute | solution.py:157
  (32 other events, 502.1 us)
Sparse Core Ops, SparseCore 0:
  74.6 11.9 all-gather.1
where the time goes:
time: 308 us
  waiting for transfers between devices  156 us (51%)
  Pallas kernels  73.5 us (24%)
  starting transfers between devices  39.6 us (13%)
  local copies, waits for them, and re-layouts  15.8 us (5%)
  between operations  13.8 us (4%)
  other arithmetic  8.64 us (3%)
    ppermute x31, waiting for transfers between devices, partner(): return lax.ppermute(value, axis, [(i, i ^ flip) for i in range(size)])  75.4 us
    pallas_call x5, Pallas kernels, ladder(): pl.pallas_call(functools.partial(ladder_kernel, steps, count, first), gri...  73.5 us
    ppermute x12, waiting for transfers between devices, on_square(): lax.ppermute(held['block', s - 1, (i + 1) % NTV], 'left', ring)  47 us
    ppermute x3, waiting for transfers between devices, shift(): lax.ppermute(value, axis, [(i, (i + step) % size) for i in range(size)])  33.9 us
    ppermute x31, starting transfers between devices, partner(): return lax.ppermute(value, axis, [(i, i ^ flip) for i in range(size)])  19.6 us
    ppermute x12, starting transfers between devices, on_square(): lax.ppermute(held['block', s - 1, (i + 1) % NTV], 'left', ring)  16.1 us
    unnamed x66, local copies, waits for them, and re-layouts  6.64 us
    another operation x4, other arithmetic, on_square(): held['lefts', stack_block] = jnp.stack(every)  6.61 us
  transfers between devices with their start and end apart: 47, of which 23 were waited for; matrix products, arithmetic and copies ran while one was open for 4% of the time, Pallas kernels for 20%

commit v1 on v0

--- a/solution.py
+++ b/solution.py
@@ -112,10 +112,10 @@
             (1, rows // GROUPS, depth), lambda i, h, v, k, d: (k[t], jnp.minimum(i, GROUPS - 1), 0)
         )
 
-    def right_spec(place):
+    def right_spec(place, other):
         return pl.BlockSpec(
             (1, rows, depth),
-            lambda i, h, v, k, d: (d[0] if place is None else place, 0, 0),
+            lambda i, h, v, k, d: (d[0] if place is None else place, 1 - h[0] if other else 0, 0),
             pipeline_mode=one,
         )
 
@@ -137,7 +137,11 @@
             num_scalar_prefetch=4,
             grid=(2 * GROUPS,),
             in_specs=[left_spec(t) for _ in lefts for t in range(count)]
-            + [right_spec(place) for _, _, place in rights for _ in range(2)]
+            + [
+                right_spec(place, other)
+                for own, both, place in rights
+                for other in (False, both.shape[1] > own.shape[1])
+            ]
             + [amp_spec]
             + [sum_spec(base // count)] * (not first),
             out_specs=sum_spec(0),
@@ -172,7 +176,9 @@
 AMP = "amp"
 NEAR = {0: 0, 2: AMP, 4: 1, 6: 2, 8: 3}
 FAR = {1: 0, 3: AMP, 5: 1, 7: 2, 9: 3}
-STACK = {2: 0, 4: AMP, 6: 1, 8: 2, 10: 3}
+STACK = {3: 0, 5: AMP, 7: 1, 9: 2, 10: 3}
+CROSS = {10: (8, 9), 11: (10,), 12: (11,)}
+GATHERED = 8
 CONTRACT = {10: 0, 11: 2, 12: 1}
 
 
@@ -240,11 +246,11 @@
                 held["left", near_block, 0] = own.transpose(1, 0, 2).reshape(row_count, depth)
             now.append(("left", near_block, 0))
         if far_block is not None:
-            now += [("left", far_block, flip) for flip in range(3)]
+            now.append(("left", far_block, 0))
         if stack_block is not None:
-            now.append(("left", stack_block, 3))
+            now += [("left", stack_block, flip) for flip in range(NTV)]
         now += [("block", HOPS[u][0] - 1, (HOPS[u][1] + 1) % NTV) for u in hops]
-        if slot == 1:
+        if slot == 0:
             now.append("chol")
         meet(now)
         for u in hops:
@@ -253,13 +259,18 @@
         if near_block is not None:
             for flip in (1, 2):
                 held["left", near_block, flip] = partner(held["left", near_block, 0], "right", NTV, flip)
+            waiting[min(slot + 2, last - 2)] += [("left", near_block, 1), ("left", near_block, 2)]
         if far_block is not None:
             held["left", far_block, 3] = partner(held["left", far_block, 0], "right", NTV, 3)
-        if slot == 1:
-            held["other", "chol"] = partner(held["chol"], "occ", 2, 1)
-            waiting[slot + 1].append(("other", "chol"))
-        if slot >= 1:
+        if slot == 0:
+            held["other", "chol"] = lax.all_gather(held["chol"], "occ", axis=1, tiled=True)
+            waiting[slot + 3].append(("other", "chol"))
+        if 1 <= slot <= GATHERED:
             unit = HOPS[slot - 1]
+            held["other", *unit] = lax.all_gather(held["block", *unit], "occ", axis=1, tiled=True)
+            waiting[slot + 3].append(("other", *unit))
+        for u in CROSS.get(slot, ()):
+            unit = HOPS[u]
             held["other", *unit] = partner(held["block", *unit], "occ", 2, 1)
             waiting[slot + 1].append(("other", *unit))
         if stack_block is not None:

time: 308 us -> 315 us (1.023)
  waiting for transfers between devices: 156 us -> 139 us
  local copies, waits for them, and re-layouts: 15.8 us -> 31.2 us
  other arithmetic: 8.64 us -> 13.7 us
    ppermute x31 -> x22, waiting for transfers between devices: 75.4 us -> 54.8 us  [partner(): return lax.ppermute(value, axis, [(i, i ^ flip) for i in range(size)])]
    unnamed x66 -> x78, local copies, waits for them, and re-layouts: 6.64 us -> 20.3 us
    ppermute x12, waiting for transfers between devices: 47 us -> 50.7 us  [on_square(): lax.ppermute(held['block', s - 1, (i + 1) % NTV], 'left', ring)]
    another operation x4, other arithmetic: 6.61 us -> 10.2 us  [on_square(): held['lefts', stack_block] = jnp.stack(every)]
    ppermute x31 -> x22, starting transfers between devices: 19.6 us -> 21.9 us  [partner(): return lax.ppermute(value, axis, [(i, i ^ flip) for i in range(size)])]
  transfers between devices with their start and end apart: 47 -> 47, of which waited for: 23 -> 21; matrix products, arithmetic and copies ran while one was open for 4% -> 6% of each run, Pallas kernels for 20% -> 20%
where the time goes in v1:
time: 315 us; the launch traced here: 313 us
  waiting for transfers between devices  139 us (44%)
  Pallas kernels  75 us (24%)
  starting transfers between devices  40.5 us (13%)
  local copies, waits for them, and re-layouts  31.2 us (10%)
  between operations  13.9 us (4%)
  other arithmetic  13.7 us (4%)
    pallas_call x5, Pallas kernels, ladder(): pl.pallas_call(functools.partial(ladder_kernel, steps, count, first), gri...  75 us
    ppermute x22, waiting for transfers between devices, partner(): return lax.ppermute(value, axis, [(i, i ^ flip) for i in range(size)])  54.8 us
    ppermute x12, waiting for transfers between devices, on_square(): lax.ppermute(held['block', s - 1, (i + 1) % NTV], 'left', ring)  50.7 us
    ppermute x3, waiting for transfers between devices, shift(): lax.ppermute(value, axis, [(i, (i + step) % size) for i in range(size)])  33.5 us
    ppermute x22, starting transfers between devices, partner(): return lax.ppermute(value, axis, [(i, i ^ flip) for i in range(size)])  21.9 us
    unnamed x78, local copies, waits for them, and re-layouts  20.3 us
    ppermute x12, starting transfers between devices, on_square(): lax.ppermute(held['block', s - 1, (i + 1) % NTV], 'left', ring)  14.2 us
    another operation x4, other arithmetic, on_square(): held['lefts', stack_block] = jnp.stack(every)  10.2 us
  transfers between devices with their start and end apart: 47, of which 21 were waited for; matrix products, arithmetic and copies ran while one was open for 6% of the time, Pallas kernels for 20%

profile of v1, /device:TPU:8, one launch (start us, length us, event | category | flops | bytes accessed | tf_op | source)
XLA Modules:
  0.0 313.4 jit_solution(16043849423524572769)
XLA Ops:
  6.5 1.7 constant_dynamic-slice_fusion.3
  9.0 14.6 %collective-permute-done.refs_18_ = bf16[1,512,512]{2,1,0:T(8,128)(2,1)S(1)} collective-permute-done((bf16[1,512,512]{2,1,0:T(8,128)(2,1)S(1)}, bf16[1,512,512]{2,1,0:T(8,128)(2,1)S(1)}, u32[]{:S(2)}, u32[]{:S(2)}) %collective-permute-start) | collective-permute-done | bytes 524320 | tf_op jit(solution)/shard_map/ppermute | solution.py:258
  24.5 1.6 collective-permute-start.1
  26.0 1.5 collective-permute-start.2
  27.6 9.8 %collective-permute-done.1 = bf16[512,512]{1,0:T(8,128)(2,1)S(1)} collective-permute-done((bf16[512,512]{1,0:T(8,128)(2,1)S(1)}, bf16[512,512]{1,0:T(8,128)(2,1)S(1)}, u32[]{:S(2)}, u32[]{:S(2)}) %collective-permute-start.1) | collective-permute-done | bytes 524320 | tf_op jit(solution)/shard_map/ppermute | solution.py:161
  38.6 2.1 collective-permute-done.3.refs_18_
  42.2 11.7 %collective-permute-done.6.refs_18_ = bf16[1,512,512]{2,1,0:T(8,128)(2,1)S(1)} collective-permute-done((bf16[1,512,512]{2,1,0:T(8,128)(2,1)S(1)}, bf16[1,512,512]{2,1,0:T(8,128)(2,1)S(1)}, u32[]{:S(2)}, u32[]{:S(2)}) %collective-permute-start.6) | collective-permute-done | bytes 524320 | tf_op jit(solution)/shard_map/ppermute | solution.py:258
  55.8 2.3 collective-permute-start.8
  58.1 2.1 copy.11
  60.3 2.0 pad_maximum_fusion.refs_0_.refs_1_.refs_2_.refs_3_
  62.3 3.1 collective-permute-done.4
  67.9 2.3 collective-permute-start.10
  70.1 1.3 collective-permute-start.9
  71.5 7.1 %collective-permute-done.10 = bf16[4,512,128]{2,1,0:T(8,128)(2,1)} collective-permute-done((bf16[4,512,128]{2,1,0:T(8,128)(2,1)}, bf16[4,512,128]{2,1,0:T(8,128)(2,1)}, u32[]{:S(2)}, u32[]{:S(2)}) %collective-permute-start.10) | collective-permute-done | bytes 524320 | tf_op jit(solution)/shard_map/ppermute | solution.py:161
  78.6 1.6 collective-permute-done.9.refs_20_
  81.1 3.1 pad_maximum_fusion.1
  87.9 6.1 %collective-permute-done.11 = bf16[512,512]{1,0:T(8,128)(2,1)} collective-permute-done((bf16[512,512]{1,0:T(8,128)(2,1)}, bf16[512,512]{1,0:T(8,128)(2,1)}, u32[]{:S(2)}, u32[]{:S(2)}) %collective-permute-start.11) | collective-permute-done | bytes 524320 | tf_op jit(solution)/shard_map/ppermute | solution.py:161
  94.0 6.0 %collective-permute-done.12 = bf16[512,512]{1,0:T(8,128)(2,1)} collective-permute-done((bf16[512,512]{1,0:T(8,128)(2,1)}, bf16[512,512]{1,0:T(8,128)(2,1)}, u32[]{:S(2)}, u32[]{:S(2)}) %collective-permute-start.12) | collective-permute-done | bytes 524320 | tf_op jit(solution)/shard_map/ppermute | solution.py:161
  100.1 1.8 collective-permute-start.17
  101.9 10.6 %collective-permute-done.16.refs_10_ = bf16[1,512,512]{2,1,0:T(8,128)(2,1)S(1)} collective-permute-done((bf16[1,512,512]{2,1,0:T(8,128)(2,1)}, bf16[1,512,512]{2,1,0:T(8,128)(2,1)S(1)}, u32[]{:S(2)}, u32[]{:S(2)}) %collective-permute-start.16) | collective-permute-done | bytes 524320 | tf_op jit(solution)/shard_map/ppermute | solution.py:258
  112.5 2.7 collective-permute-done.17
  115.4 1.5 collective-permute-start.14
  118.0 3.7 %collective-permute-start.21 = (bf16[1,512,512]{2,1,0:T(8,128)(2,1)}, bf16[1,512,512]{2,1,0:T(8,128)(2,1)}, u32[]{:S(2)}, u32[]{:S(2)}) collective-permute-start(bf16[1,512,512]{2,1,0:T(8,128)(2,1)} %copy-done.8), channel_id=1, source_target_pairs={{0,16},{16,24},{24,8},{8,0},{1,17},{17,25},{25,9},{9,1},{2,18},{18... | collective-permute-start | bytes 1572872 | tf_op jit(solution)/shard_map/ppermute | solution.py:258
  124.0 2.2 copy.13
  126.1 3.2 %pad_maximum_fusion.2.refs_4_.refs_5_.refs_6_.refs_7_.refs_2_.refs_3_ = bf16[4,512,512]{2,1,0:T(8,128)(2,1)} fusion(bf16[1,512,512]{2,1,0:T(8,128)(2,1)} %bitcast.21, bf16[1,512,512]{2,1,0:T(8,128)(2,1)} %bitcast.20, bf16[1,512,512]{2,1,0:T(8,128)(2,1)} %bitcast.19, bf16[1,512,512]{2,1,0:T(8,128)(2,1)} %bitcast.73), kind=kLoop, calls=%fused_computation.4 | loop fusion | flops 3145728 | bytes 4194304 | tf_op jit(solution)/shard_map/stack | solution.py:282
  130.2 10.1 %collective-permute-done.18.refs_12_ = bf16[1,512,512]{2,1,0:T(8,128)(2,1)S(1)} collective-permute-done((bf16[1,512,512]{2,1,0:T(8,128)(2,1)S(1)}, bf16[1,512,512]{2,1,0:T(8,128)(2,1)S(1)}, u32[]{:S(2)}, u32[]{:S(2)}) %collective-permute-start.18) | collective-permute-done | bytes 524320 | tf_op jit(solution)/shard_map/ppermute | solution.py:258
  142.1 1.8 collective-permute-start.24
  143.8 2.1 collective-permute-start.23
  146.1 3.1 pad_maximum_fusion.3.refs_8_.refs_9_.refs_10_.refs_11_.refs_4_.refs_5_
  149.2 6.8 %collective-permute-done.24 = bf16[512,512]{1,0:T(8,128)(2,1)} collective-permute-done((bf16[512,512]{1,0:T(8,128)(2,1)}, bf16[512,512]{1,0:T(8,128)(2,1)}, u32[]{:S(2)}, u32[]{:S(2)}) %collective-permute-start.24) | collective-permute-done | bytes 524320 | tf_op jit(solution)/shard_map/ppermute | solution.py:161
  156.0 2.2 collective-permute-start.27
  159.4 1.9 pad_maximum_fusion.4.refs_12_.refs_13_.refs_14_.refs_15_.refs_6_.refs_7_
  167.0 16.4 %shard_map.37.refs_25_ = f32[4,4,128,512]{3,2,1,0:T(8,128)} custom-call(s32[1]{0:T(128)} %bitcast.half_ref, s32[4]{0:T(128)S(1)} %get-tuple-element.165.live_ref, s32[4]{0:T(128)S(1)} %fusion.7.pick_ref, s32[1]{0:T(128)} %bitcast.33.tile_ref, bf16[4,512,512]{2,1,0:T(8,128)(2,1)S(1)} %pad_maximum_fusion.refs_0_.refs_1_.refs_2_.refs_3_, ...), custom_call_target="tpu_custom_call" | custom-call | flops 10737418240 | bytes 20971520 | tf_op jit(solution)/shard_map/pallas_call | solution.py:134
  183.6 1.6 copy-done.2
  185.1 1.6 copy-done.4
  186.7 1.6 copy-done.6
  188.3 1.6 copy-done.7
  192.2 18.5 %shard_map.38.refs_25_ = f32[4,4,128,512]{3,2,1,0:T(8,128)} custom-call(s32[1]{0:T(128)} %bitcast.half_ref, s32[4]{0:T(128)S(1)} %get-tuple-element.164.live_ref, s32[4]{0:T(128)S(1)} %fusion.7.pick_ref, s32[1]{0:T(128)} %bitcast.34.tile_ref, ...), custom_call_target="tpu_custom_call", output_to_operand_aliasing={{}: (29, {})} | custom-call | flops 10737418240 | bytes 20971520 | tf_op jit(solution)/shard_map/pallas_call | solution.py:134
  211.3 18.1 %shard_map.39.refs_17_ = f32[4,4,128,512]{3,2,1,0:T(8,128)} custom-call(s32[1]{0:T(128)} %bitcast.half_ref, s32[4]{0:T(128)S(1)} %get-tuple-element.163.live_ref, s32[4]{0:T(128)S(1)} %fusion.7.pick_ref, s32[1]{0:T(128)} %bitcast.35.tile_ref, ...), custom_call_target="tpu_custom_call", output_to_operand_aliasing={{}: (29, {})} | custom-call | flops 10737418240 | bytes 20971520 | tf_op jit(solution)/shard_map/pallas_call | solution.py:134
  229.5 10.8 %shard_map.41 = bf16[2,4,128,512]{3,2,1,0:T(8,128)(2,1)S(1)} custom-call(s32[1]{0:T(128)} %bitcast.half_ref, s32[2]{0:T(128)S(1)} %get-tuple-element.161.live_ref, s32[2]{0:T(128)S(1)} %get-tuple-element.177.pick_ref, s32[1]{0:T(128)} %bitcast.3.tile_ref, bf16[4,512,512]{2,1,0:T(8,128)(2,1)S(1)} %pad_maximum_fusion.refs_0_.refs_1_.refs_2_.refs_3_, ...), custom_call_target="tpu_custom_call" | custom-call | flops 5368709120 | bytes 20971520 | tf_op jit(solution)/shard_map/pallas_call | solution.py:134
  240.9 3.0 collective-permute-start.32
  243.8 11.1 %shard_map.40 = f32[2,4,128,512]{3,2,1,0:T(8,128)S(1)} custom-call(s32[1]{0:T(128)} %bitcast.half_ref, s32[2]{0:T(128)S(1)} %get-tuple-element.162.live_ref, s32[2]{0:T(128)S(1)} %get-tuple-element.178.pick_ref, s32[1]{0:T(128)} %bitcast.3.tile_ref, bf16[4,512,512]{2,1,0:T(8,128)(2,1)S(1)} %pad_maximum_fusion.refs_0_.refs_1_.refs_2_.refs_3_, ...), custom_call_target="tpu_custom_call" | custom-call | flops 5368709120 | bytes 20971520 | tf_op jit(solution)/shard_map/pallas_call | solution.py:134
  255.8 30.2 %collective-permute-done.32 = bf16[4,128,512]{2,1,0:T(8,128)(2,1)S(1)} collective-permute-done((bf16[4,128,512]{2,1,0:T(8,128)(2,1)S(1)}, bf16[4,128,512]{2,1,0:T(8,128)(2,1)S(1)}, u32[]{:S(2)}, u32[]{:S(2)}) %collective-permute-start.32) | collective-permute-done | bytes 524320 | tf_op jit(solution)/shard_map/ppermute | solution.py:165
  285.9 3.3 %collective-permute-done.33 = bf16[4,128,512]{2,1,0:T(8,128)(2,1)S(1)} collective-permute-done((bf16[4,128,512]{2,1,0:T(8,128)(2,1)S(1)}, bf16[4,128,512]{2,1,0:T(8,128)(2,1)S(1)}, u32[]{:S(2)}, u32[]{:S(2)}) %collective-permute-start.33) | collective-permute-done | bytes 524320 | tf_op jit(solution)/shard_map/ppermute | solution.py:165
  291.7 1.6 collective-permute-start.36
  293.2 5.7 %collective-permute-done.34 = f32[4,128,128]{2,1,0:T(8,128)S(1)} collective-permute-done((f32[4,128,128]{2,1,0:T(8,128)S(1)}, f32[4,128,128]{2,1,0:T(8,128)S(1)}, u32[]{:S(2)}, u32[]{:S(2)}) %collective-permute-start.34) | collective-permute-done | bytes 262176 | tf_op jit(solution)/shard_map/ppermute | solution.py:161
  298.9 5.3 %collective-permute-done.35 = f32[4,128,128]{2,1,0:T(8,128)S(1)} collective-permute-done((f32[4,128,128]{2,1,0:T(8,128)S(1)}, f32[4,128,128]{2,1,0:T(8,128)S(1)}, u32[]{:S(2)}, u32[]{:S(2)}) %collective-permute-start.35) | collective-permute-done | bytes 262176 | tf_op jit(solution)/shard_map/ppermute | solution.py:161
  305.0 1.6 copy.14
  (166 shorter events, 33.7 us)
Async XLA Ops:
  6.5 116.5 %copy-start = (s32[4,4,4,4]{3,2,1,0:T(4,128)S(1)}, s32[4,4,4,4]{3,2,1,0:T(4,128)}, u32[]{:S(2)}) copy-start(s32[4,4,4,4]{3,2,1,0:T(4,128)} %param.5) | copy-start | bytes 3076
  6.5 47.4 %all-gather.13.cloned.1.call-start = ((), (), s32[]{:S(2)}) async-start(), calls=%async_computation.1 | async-start | bytes 6291456 | tf_op jit(solution)/shard_map/all_gather | solution.py:266
  9.0 58.0 %all-gather.11.cloned.1.call-start = ((), (), s32[]{:S(2)}) async-start(), calls=%async_computation | async-start | bytes 1572864 | tf_op jit(solution)/shard_map/all_gather | solution.py:270
  9.0 14.6 %collective-permute-start = (bf16[1,512,512]{2,1,0:T(8,128)(2,1)S(1)}, bf16[1,512,512]{2,1,0:T(8,128)(2,1)S(1)}, u32[]{:S(2)}, u32[]{:S(2)}) collective-permute-start(bf16[1,512,512]{2,1,0:T(8,128)(2,1)S(1)} %get-tuple-element.83), channel_id=1, source_target_pairs={{0,16},{16,24},{24,8},{8,0},{1,17},{17,25},{25,9},{9,1},{2,18},{18... | collective-permute-start | bytes 1572872 | tf_op jit(solution)/shard_map/ppermute | solution.py:258
  24.4 47.0 %all-gather.15.cloned.1.call-start = ((), (), s32[]{:S(2)}) async-start(), calls=%async_computation.2 | async-start | bytes 1572864 | tf_op jit(solution)/shard_map/all_gather | solution.py:270
  24.5 12.9 %collective-permute-start.1 = (bf16[512,512]{1,0:T(8,128)(2,1)S(1)}, bf16[512,512]{1,0:T(8,128)(2,1)S(1)}, u32[]{:S(2)}, u32[]{:S(2)}) collective-permute-start(bf16[512,512]{1,0:T(8,128)(2,1)S(1)} %bitcast.78), channel_id=1, source_target_pairs={{0,2},{2,0},{4,6},{6,4},{1,3},{3,1},{5,7},{7,5},{8,10},{10,8},{12,... | collective-permute-start | bytes 1572872 | tf_op jit(solution)/shard_map/ppermute | solution.py:161
  26.0 12.5 %collective-permute-start.2 = (bf16[512,512]{1,0:T(8,128)(2,1)S(1)}, bf16[512,512]{1,0:T(8,128)(2,1)S(1)}, u32[]{:S(2)}, u32[]{:S(2)}) collective-permute-start(bf16[512,512]{1,0:T(8,128)(2,1)S(1)} %bitcast.79), channel_id=1, source_target_pairs={{0,4},{2,6},{4,0},{6,2},{1,5},{3,7},{5,1},{7,3},{8,12},{10,14},{12... | collective-permute-start | bytes 1572872 | tf_op jit(solution)/shard_map/ppermute | solution.py:161
  27.6 13.1 %collective-permute-start.3 = (bf16[1,512,512]{2,1,0:T(8,128)(2,1)S(1)}, bf16[1,512,512]{2,1,0:T(8,128)(2,1)S(1)}, u32[]{:S(2)}, u32[]{:S(2)}) collective-permute-start(bf16[1,512,512]{2,1,0:T(8,128)(2,1)S(1)} %get-tuple-element.86), channel_id=1, source_target_pairs={{0,16},{16,24},{24,8},{8,0},{1,17},{17,25},{25,9},{9,1},{2,18},{18... | collective-permute-start | bytes 1572872 | tf_op jit(solution)/shard_map/ppermute | solution.py:258
  41.5 58.5 %all-gather.21.cloned.1.call-start = ((), (), s32[]{:S(2)}) async-start(), calls=%async_computation.5 | async-start | bytes 1572864 | tf_op jit(solution)/shard_map/all_gather | solution.py:270
  41.6 12.3 %collective-permute-start.6 = (bf16[1,512,512]{2,1,0:T(8,128)(2,1)S(1)}, bf16[1,512,512]{2,1,0:T(8,128)(2,1)S(1)}, u32[]{:S(2)}, u32[]{:S(2)}) collective-permute-start(bf16[1,512,512]{2,1,0:T(8,128)(2,1)S(1)} %get-tuple-element.89), channel_id=1, source_target_pairs={{0,16},{16,24},{24,8},{8,0},{1,17},{17,25},{25,9},{9,1},{2,18},{18... | collective-permute-start | bytes 1572872 | tf_op jit(solution)/shard_map/ppermute | solution.py:258
  41.6 12.3 %collective-permute-start.7 = (bf16[512,512]{1,0:T(8,128)(2,1)S(1)}, bf16[512,512]{1,0:T(8,128)(2,1)S(1)}, u32[]{:S(2)}, u32[]{:S(2)}) collective-permute-start(bf16[512,512]{1,0:T(8,128)(2,1)S(1)} %bitcast.80), channel_id=1, source_target_pairs={{0,6},{2,4},{4,2},{6,0},{1,7},{3,5},{5,3},{7,1},{8,14},{10,12},{12... | collective-permute-start | bytes 1572872 | tf_op jit(solution)/shard_map/ppermute | solution.py:161
  54.7 60.6 %all-gather.23.cloned.1.call-start = ((), (), s32[]{:S(2)}) async-start(), calls=%async_computation.6 | async-start | bytes 1572864 | tf_op jit(solution)/shard_map/all_gather | solution.py:270
  54.7 10.7 %collective-permute-start.4 = (bf16[4,512,128]{2,1,0:T(8,128)(2,1)}, bf16[4,512,128]{2,1,0:T(8,128)(2,1)S(1)}, u32[]{:S(2)}, u32[]{:S(2)}) collective-permute-start(bf16[4,512,128]{2,1,0:T(8,128)(2,1)} %bitcast.7), channel_id=1, source_target_pairs={{0,2},{2,0},{4,6},{6,4},{1,3},{3,1},{5,7},{7,5},{8,10},{10,8},{12,... | collective-permute-start | bytes 1572872 | tf_op jit(solution)/shard_map/ppermute | solution.py:161
  55.3 10.9 %collective-permute-start.5 = (bf16[4,512,128]{2,1,0:T(8,128)(2,1)}, bf16[4,512,128]{2,1,0:T(8,128)(2,1)S(1)}, u32[]{:S(2)}, u32[]{:S(2)}) collective-permute-start(bf16[4,512,128]{2,1,0:T(8,128)(2,1)} %bitcast.7), channel_id=1, source_target_pairs={{0,4},{2,6},{4,0},{6,2},{1,5},{3,7},{5,1},{7,3},{8,12},{10,14},{12... | collective-permute-start | bytes 1572872 | tf_op jit(solution)/shard_map/ppermute | solution.py:161
  55.8 11.2 %collective-permute-start.8 = (bf16[1,512,512]{2,1,0:T(8,128)(2,1)}, bf16[1,512,512]{2,1,0:T(8,128)(2,1)S(1)}, u32[]{:S(2)}, u32[]{:S(2)}) collective-permute-start(bf16[1,512,512]{2,1,0:T(8,128)(2,1)} %copy-done.19), channel_id=1, source_target_pairs={{0,16},{16,24},{24,8},{8,0},{1,17},{17,25},{25,9},{9,1},{2,18},{18... | collective-permute-start | bytes 1572872 | tf_op jit(solution)/shard_map/ppermute | solution.py:258
  67.8 72.5 %all-gather.17.cloned.1.call-start = ((), (), s32[]{:S(2)}) async-start(), calls=%async_computation.3 | async-start | bytes 1572864 | tf_op jit(solution)/shard_map/all_gather | solution.py:270
  67.9 10.7 %collective-permute-start.10 = (bf16[4,512,128]{2,1,0:T(8,128)(2,1)}, bf16[4,512,128]{2,1,0:T(8,128)(2,1)}, u32[]{:S(2)}, u32[]{:S(2)}) collective-permute-start(bf16[4,512,128]{2,1,0:T(8,128)(2,1)} %bitcast.7), channel_id=1, source_target_pairs={{0,6},{2,4},{4,2},{6,0},{1,7},{3,5},{5,3},{7,1},{8,14},{10,12},{12... | collective-permute-start | bytes 1572872 | tf_op jit(solution)/shard_map/ppermute | solution.py:161
  70.1 10.1 %collective-permute-start.9 = (bf16[1,512,512]{2,1,0:T(8,128)(2,1)S(1)}, bf16[1,512,512]{2,1,0:T(8,128)(2,1)S(1)}, u32[]{:S(2)}, u32[]{:S(2)}) collective-permute-start(bf16[1,512,512]{2,1,0:T(8,128)(2,1)S(1)} %copy-done.22), channel_id=1, source_target_pairs={{0,16},{16,24},{24,8},{8,0},{1,17},{17,25},{25,9},{9,1},{2,18},{18... | collective-permute-start | bytes 1572872 | tf_op jit(solution)/shard_map/ppermute | solution.py:258
  81.0 59.2 %all-gather.19.cloned.1.call-start = ((), (), s32[]{:S(2)}) async-start(), calls=%async_computation.4 | async-start | bytes 6291456 | tf_op jit(solution)/shard_map/all_gather | solution.py:279
  84.2 57.8 %all-gather.27.cloned.1.call-start = ((), (), s32[]{:S(2)}) async-start(), calls=%async_computation.8 | async-start | bytes 1572864 | tf_op jit(solution)/shard_map/all_gather | solution.py:270
  84.2 9.7 %collective-permute-start.11 = (bf16[512,512]{1,0:T(8,128)(2,1)}, bf16[512,512]{1,0:T(8,128)(2,1)}, u32[]{:S(2)}, u32[]{:S(2)}) collective-permute-start(bf16[512,512]{1,0:T(8,128)(2,1)} %bitcast.70), channel_id=1, source_target_pairs={{0,2},{2,0},{4,6},{6,4},{1,3},{3,1},{5,7},{7,5},{8,10},{10,8},{12,... | collective-permute-start | bytes 1572872 | tf_op jit(solution)/shard_map/ppermute | solution.py:161
  84.8 15.1 %collective-permute-start.12 = (bf16[512,512]{1,0:T(8,128)(2,1)}, bf16[512,512]{1,0:T(8,128)(2,1)}, u32[]{:S(2)}, u32[]{:S(2)}) collective-permute-start(bf16[512,512]{1,0:T(8,128)(2,1)} %bitcast.71), channel_id=1, source_target_pairs={{0,4},{2,6},{4,0},{6,2},{1,5},{3,7},{5,1},{7,3},{8,12},{10,14},{12... | collective-permute-start | bytes 1572872 | tf_op jit(solution)/shard_map/ppermute | solution.py:161
  85.6 14.4 %collective-permute-start.13 = (bf16[1,512,512]{2,1,0:T(8,128)(2,1)}, bf16[1,512,512]{2,1,0:T(8,128)(2,1)}, u32[]{:S(2)}, u32[]{:S(2)}) collective-permute-start(bf16[1,512,512]{2,1,0:T(8,128)(2,1)} %copy-done.24), channel_id=1, source_target_pairs={{0,16},{16,24},{24,8},{8,0},{1,17},{17,25},{25,9},{9,1},{2,18},{18... | collective-permute-start | bytes 1572872 | tf_op jit(solution)/shard_map/ppermute | solution.py:258
  100.0 58.2 %all-gather.25.cloned.1.call-start = ((), (), s32[]{:S(2)}) async-start(), calls=%async_computation.7 | async-start | bytes 1572864 | tf_op jit(solution)/shard_map/all_gather | solution.py:270
  100.0 12.5 %collective-permute-start.16 = (bf16[1,512,512]{2,1,0:T(8,128)(2,1)}, bf16[1,512,512]{2,1,0:T(8,128)(2,1)S(1)}, u32[]{:S(2)}, u32[]{:S(2)}) collective-permute-start(bf16[1,512,512]{2,1,0:T(8,128)(2,1)} %copy-done.32), channel_id=1, source_target_pairs={{0,16},{16,24},{24,8},{8,0},{1,17},{17,25},{25,9},{9,1},{2,18},{18... | collective-permute-start | bytes 1572872 | tf_op jit(solution)/shard_map/ppermute | solution.py:258
  100.1 15.1 %collective-permute-start.17 = (bf16[512,512]{1,0:T(8,128)(2,1)}, bf16[512,512]{1,0:T(8,128)(2,1)}, u32[]{:S(2)}, u32[]{:S(2)}) collective-permute-start(bf16[512,512]{1,0:T(8,128)(2,1)} %bitcast.72), channel_id=1, source_target_pairs={{0,6},{2,4},{4,2},{6,0},{1,7},{3,5},{5,3},{7,1},{8,14},{10,12},{12... | collective-permute-start | bytes 1572872 | tf_op jit(solution)/shard_map/ppermute | solution.py:161
  115.3 68.2 %all-gather.29.cloned.1.call-start = ((), (), s32[]{:S(2)}) async-start(), calls=%async_computation.9 | async-start | bytes 1572864 | tf_op jit(solution)/shard_map/all_gather | solution.py:270
  115.4 14.0 %collective-permute-start.14 = (bf16[512,512]{1,0:T(8,128)(2,1)}, bf16[512,512]{1,0:T(8,128)(2,1)}, u32[]{:S(2)}, u32[]{:S(2)}) collective-permute-start(bf16[512,512]{1,0:T(8,128)(2,1)} %bitcast.74), channel_id=1, source_target_pairs={{0,2},{2,0},{4,6},{6,4},{1,3},{3,1},{5,7},{7,5},{8,10},{10,8},{12,... | collective-permute-start | bytes 1572872 | tf_op jit(solution)/shard_map/ppermute | solution.py:161
  116.9 13.3 %collective-permute-start.15 = (bf16[512,512]{1,0:T(8,128)(2,1)}, bf16[512,512]{1,0:T(8,128)(2,1)}, u32[]{:S(2)}, u32[]{:S(2)}) collective-permute-start(bf16[512,512]{1,0:T(8,128)(2,1)} %bitcast.75), channel_id=1, source_target_pairs={{0,4},{2,6},{4,0},{6,2},{1,5},{3,7},{5,1},{7,3},{8,12},{10,14},{12... | collective-permute-start | bytes 1572872 | tf_op jit(solution)/shard_map/ppermute | solution.py:161
  118.0 24.0 %collective-permute-start.21 = (bf16[1,512,512]{2,1,0:T(8,128)(2,1)}, bf16[1,512,512]{2,1,0:T(8,128)(2,1)}, u32[]{:S(2)}, u32[]{:S(2)}) collective-permute-start(bf16[1,512,512]{2,1,0:T(8,128)(2,1)} %copy-done.8), channel_id=1, source_target_pairs={{0,16},{16,24},{24,8},{8,0},{1,17},{17,25},{25,9},{9,1},{2,18},{18... | collective-permute-start | bytes 1572872 | tf_op jit(solution)/shard_map/ppermute | solution.py:258
  121.7 18.5 %collective-permute-start.18 = (bf16[1,512,512]{2,1,0:T(8,128)(2,1)S(1)}, bf16[1,512,512]{2,1,0:T(8,128)(2,1)S(1)}, u32[]{:S(2)}, u32[]{:S(2)}) collective-permute-start(bf16[1,512,512]{2,1,0:T(8,128)(2,1)S(1)} %copy-done.13), channel_id=1, source_target_pairs={{0,16},{16,24},{24,8},{8,0},{1,17},{17,25},{25,9},{9,1},{2,18},{18... | collective-permute-start | bytes 1572872 | tf_op jit(solution)/shard_map/ppermute | solution.py:258
  121.8 20.3 %collective-permute-start.22 = (bf16[512,512]{1,0:T(8,128)(2,1)}, bf16[512,512]{1,0:T(8,128)(2,1)}, u32[]{:S(2)}, u32[]{:S(2)}) collective-permute-start(bf16[512,512]{1,0:T(8,128)(2,1)} %bitcast.76), channel_id=1, source_target_pairs={{0,6},{2,4},{4,2},{6,0},{1,7},{3,5},{5,3},{7,1},{8,14},{10,12},{12... | collective-permute-start | bytes 1572872 | tf_op jit(solution)/shard_map/ppermute | solution.py:161
  140.3 17.9 %collective-permute-start.19 = (bf16[512,512]{1,0:T(8,128)(2,1)}, bf16[512,512]{1,0:T(8,128)(2,1)}, u32[]{:S(2)}, u32[]{:S(2)}) collective-permute-start(bf16[512,512]{1,0:T(8,128)(2,1)} %bitcast.82), channel_id=1, source_target_pairs={{0,2},{2,0},{4,6},{6,4},{1,3},{3,1},{5,7},{7,5},{8,10},{10,8},{12,... | collective-permute-start | bytes 1572872 | tf_op jit(solution)/shard_map/ppermute | solution.py:161
  140.8 17.4 %collective-permute-start.20 = (bf16[512,512]{1,0:T(8,128)(2,1)}, bf16[512,512]{1,0:T(8,128)(2,1)}, u32[]{:S(2)}, u32[]{:S(2)}) collective-permute-start(bf16[512,512]{1,0:T(8,128)(2,1)} %bitcast.83), channel_id=1, source_target_pairs={{0,4},{2,6},{4,0},{6,2},{1,5},{3,7},{5,1},{7,3},{8,12},{10,14},{12... | collective-permute-start | bytes 1572872 | tf_op jit(solution)/shard_map/ppermute | solution.py:161
  142.1 13.9 %collective-permute-start.24 = (bf16[512,512]{1,0:T(8,128)(2,1)}, bf16[512,512]{1,0:T(8,128)(2,1)}, u32[]{:S(2)}, u32[]{:S(2)}) collective-permute-start(bf16[512,512]{1,0:T(8,128)(2,1)} %bitcast.84), channel_id=1, source_target_pairs={{0,6},{2,4},{4,2},{6,0},{1,7},{3,5},{5,3},{7,1},{8,14},{10,12},{12... | collective-permute-start | bytes 1572872 | tf_op jit(solution)/shard_map/ppermute | solution.py:161
  143.8 14.4 %collective-permute-start.23 = (bf16[1,512,512]{2,1,0:T(8,128)(2,1)S(1)}, bf16[1,512,512]{2,1,0:T(8,128)(2,1)}, u32[]{:S(2)}, u32[]{:S(2)}) collective-permute-start(bf16[1,512,512]{2,1,0:T(8,128)(2,1)S(1)} %collective-permute-done.18.refs_12_), channel_id=1, source_target_pairs={{0,16},{16,24},{24,8},{8,0},{1,17},{17,25},{25,9},{9,1},{2,18},{18... | collective-permute-start | bytes 1572872 | tf_op jit(solution)/shard_map/ppermute | solution.py:258
  146.0 37.4 %collective-permute-start.25 = (bf16[1,512,512]{2,1,0:T(8,128)(2,1)}, bf16[1,512,512]{2,1,0:T(8,128)(2,1)}, u32[]{:S(2)}, u32[]{:S(2)}) collective-permute-start(bf16[1,512,512]{2,1,0:T(8,128)(2,1)} %collective-permute-done.21.refs_20_), channel_id=1, source_target_pairs={{0,1},{1,0},{2,3},{3,2},{4,5},{5,4},{6,7},{7,6},{8,9},{9,8},{10,11... | collective-permute-start | bytes 1572872 | tf_op jit(solution)/shard_map/ppermute | solution.py:161
  156.0 27.4 %collective-permute-start.27 = (bf16[1,512,512]{2,1,0:T(8,128)(2,1)}, bf16[1,512,512]{2,1,0:T(8,128)(2,1)}, u32[]{:S(2)}, u32[]{:S(2)}) collective-permute-start(bf16[1,512,512]{2,1,0:T(8,128)(2,1)} %collective-permute-done.21.refs_20_), channel_id=1, source_target_pairs={{0,16},{16,24},{24,8},{8,0},{1,17},{17,25},{25,9},{9,1},{2,18},{18... | collective-permute-start | bytes 1572872 | tf_op jit(solution)/shard_map/ppermute | solution.py:258
  158.2 25.2 %collective-permute-start.26 = (bf16[1,512,512]{2,1,0:T(8,128)(2,1)}, bf16[1,512,512]{2,1,0:T(8,128)(2,1)}, u32[]{:S(2)}, u32[]{:S(2)}) collective-permute-start(bf16[1,512,512]{2,1,0:T(8,128)(2,1)} %collective-permute-done.23.refs_22_), channel_id=1, source_target_pairs={{0,1},{1,0},{2,3},{3,2},{4,5},{5,4},{6,7},{7,6},{8,9},{9,8},{10,11... | collective-permute-start | bytes 1572872 | tf_op jit(solution)/shard_map/ppermute | solution.py:161
  158.3 52.4 %collective-permute-start.29 = (bf16[1,512,512]{2,1,0:T(8,128)(2,1)}, bf16[1,512,512]{2,1,0:T(8,128)(2,1)S(1)}, u32[]{:S(2)}, u32[]{:S(2)}) collective-permute-start(bf16[1,512,512]{2,1,0:T(8,128)(2,1)} %copy-done.14), channel_id=1, source_target_pairs={{0,16},{16,24},{24,8},{8,0},{1,17},{17,25},{25,9},{9,1},{2,18},{18... | collective-permute-start | bytes 1572872 | tf_op jit(solution)/shard_map/ppermute | solution.py:258
  183.5 27.2 %collective-permute-start.28 = (bf16[1,512,512]{2,1,0:T(8,128)(2,1)}, bf16[1,512,512]{2,1,0:T(8,128)(2,1)S(1)}, u32[]{:S(2)}, u32[]{:S(2)}) collective-permute-start(bf16[1,512,512]{2,1,0:T(8,128)(2,1)} %collective-permute-done.27.refs_22_), channel_id=1, source_target_pairs={{0,1},{1,0},{2,3},{3,2},{4,5},{5,4},{6,7},{7,6},{8,9},{9,8},{10,11... | collective-permute-start | bytes 1572872 | tf_op jit(solution)/shard_map/ppermute | solution.py:161
  210.7 18.8 %collective-permute-start.30 = (bf16[1,512,512]{2,1,0:T(8,128)(2,1)S(1)}, bf16[1,512,512]{2,1,0:T(8,128)(2,1)S(1)}, u32[]{:S(2)}, u32[]{:S(2)}) collective-permute-start(bf16[1,512,512]{2,1,0:T(8,128)(2,1)S(1)} %collective-permute-done.29.refs_14_), channel_id=1, source_target_pairs={{0,1},{1,0},{2,3},{3,2},{4,5},{5,4},{6,7},{7,6},{8,9},{9,8},{10,11... | collective-permute-start | bytes 1572872 | tf_op jit(solution)/shard_map/ppermute | solution.py:161
  240.4 15.4 %collective-permute-start.31 = (bf16[4,128,512]{2,1,0:T(8,128)(2,1)S(1)}, bf16[4,128,512]{2,1,0:T(8,128)(2,1)S(1)}, u32[]{:S(2)}, u32[]{:S(2)}) collective-permute-start(bf16[4,128,512]{2,1,0:T(8,128)(2,1)S(1)} %get-tuple-element.174), channel_id=1, source_target_pairs={{0,8},{8,16},{16,24},{24,0},{1,9},{9,17},{17,25},{25,1},{2,10},{10... | collective-permute-start | bytes 1572872 | tf_op jit(solution)/shard_map/ppermute | solution.py:165
  240.9 45.1 %collective-permute-start.32 = (bf16[4,128,512]{2,1,0:T(8,128)(2,1)S(1)}, bf16[4,128,512]{2,1,0:T(8,128)(2,1)S(1)}, u32[]{:S(2)}, u32[]{:S(2)}) collective-permute-start(bf16[4,128,512]{2,1,0:T(8,128)(2,1)S(1)} %get-tuple-element.175), channel_id=1, source_target_pairs={{0,16},{8,24},{16,0},{24,8},{1,17},{9,25},{17,1},{25,9},{2,18},{10... | collective-permute-start | bytes 1572872 | tf_op jit(solution)/shard_map/ppermute | solution.py:165
  255.1 34.2 %collective-permute-start.33 = (bf16[4,128,512]{2,1,0:T(8,128)(2,1)S(1)}, bf16[4,128,512]{2,1,0:T(8,128)(2,1)S(1)}, u32[]{:S(2)}, u32[]{:S(2)}) collective-permute-start(bf16[4,128,512]{2,1,0:T(8,128)(2,1)S(1)} %fusion.3), channel_id=1, source_target_pairs={{0,24},{8,0},{16,8},{24,16},{1,25},{9,1},{17,9},{25,17},{2,26},{10... | collective-permute-start | bytes 1572872 | tf_op jit(solution)/shard_map/ppermute | solution.py:165
  289.7 9.3 %collective-permute-start.34 = (f32[4,128,128]{2,1,0:T(8,128)S(1)}, f32[4,128,128]{2,1,0:T(8,128)S(1)}, u32[]{:S(2)}, u32[]{:S(2)}) collective-permute-start(f32[4,128,128]{2,1,0:T(8,128)S(1)} %get-tuple-element.173), channel_id=1, source_target_pairs={{0,2},{2,0},{4,6},{6,4},{1,3},{3,1},{5,7},{7,5},{8,10},{10,8},{12,... | collective-permute-start | bytes 786440 | tf_op jit(solution)/shard_map/ppermute | solution.py:161
  290.7 13.6 %collective-permute-start.35 = (f32[4,128,128]{2,1,0:T(8,128)S(1)}, f32[4,128,128]{2,1,0:T(8,128)S(1)}, u32[]{:S(2)}, u32[]{:S(2)}) collective-permute-start(f32[4,128,128]{2,1,0:T(8,128)S(1)} %get-tuple-element.172), channel_id=1, source_target_pairs={{0,4},{2,6},{4,0},{6,2},{1,5},{3,7},{5,1},{7,3},{8,12},{10,14},{12... | collective-permute-start | bytes 786440 | tf_op jit(solution)/shard_map/ppermute | solution.py:161
  291.7 12.6 %collective-permute-start.36 = (f32[4,128,128]{2,1,0:T(8,128)S(1)}, f32[4,128,128]{2,1,0:T(8,128)S(1)}, u32[]{:S(2)}, u32[]{:S(2)}) collective-permute-start(f32[4,128,128]{2,1,0:T(8,128)S(1)} %get-tuple-element.171), channel_id=1, source_target_pairs={{0,6},{2,4},{4,2},{6,0},{1,7},{3,5},{5,3},{7,1},{8,14},{10,12},{12... | collective-permute-start | bytes 786440 | tf_op jit(solution)/shard_map/ppermute | solution.py:161
  (38 other events, 352.4 us)
Sparse Core Ops, SparseCore 0:
  8.9 15.0 all-gather.12
  25.6 10.1 all-gather.10
  41.6 7.5 all-gather.14
  54.8 8.5 all-gather.20
  67.9 9.2 all-gather.22
  81.2 7.6 all-gather.16
  90.4 14.8 all-gather.18
  106.9 10.1 all-gather.26
  118.6 10.1 all-gather.24
  146.2 7.5 all-gather.28

commit v2 on v0

--- a/solution.py
+++ b/solution.py
@@ -20,7 +20,7 @@
     rest = refs[steps * (count + 2):]
     amp_ref = rest[0]
     before_ref = None if first else rest[1]
-    out_ref, products, ready = rest[-3:]
+    out_ref, products, ready, gathered = rest[-4:]
     step = pl.program_id(0)
     group_rows = lefts[0][0].shape[1]
     c_part = TV // GROUPS
@@ -30,12 +30,13 @@
 
     @pl.when(step < GROUPS)
     def _():
+        for t in range(count):
+            for s in range(steps):
+                rows = lefts[s][t][0]
+                gathered[t * group_rows:(t + 1) * group_rows, s * rows.shape[1]:(s + 1) * rows.shape[1]] = rows
         for half in range(2):
             start = (half_ref[0] if half == 0 else 1 - half_ref[0]) * half_blocks
             for p in range(half_blocks):
-                left = jnp.concatenate(
-                    [jnp.concatenate([part[t][0] for part in lefts], axis=1) for t in range(count)], axis=0
-                )
                 right = jnp.concatenate(
                     [
                         jnp.concatenate(
@@ -59,7 +60,7 @@
                     axis=1,
                 )
                 total = lax.dot_general(
-                    left, right, (((1,), (1,)), ((), ())), preferred_element_type=jnp.float32
+                    gathered[...], right, (((1,), (1,)), ((), ())), preferred_element_type=jnp.float32
                 )
                 products[step, start + p] = total.astype(jnp.bfloat16)
 
@@ -144,6 +145,7 @@
             scratch_shapes=[
                 pltpu.VMEM((GROUPS, 2 * rows // wide, count * rows // GROUPS, wide), jnp.bfloat16),
                 pltpu.VMEM((count, b_blocks, a_count, TV * TV), jnp.bfloat16),
+                pltpu.VMEM((count * rows // GROUPS, steps * depth), jnp.bfloat16),
             ],
         ),
         out_shape=jax.ShapeDtypeStruct((count, GROUPS, b_blocks * a_count, columns), kind),
@@ -242,7 +244,7 @@
         if far_block is not None:
             now += [("left", far_block, flip) for flip in range(3)]
         if stack_block is not None:
-            now.append(("left", stack_block, 3))
+            now += [("left", stack_block, "first"), ("left", stack_block, "second")]
         now += [("block", HOPS[u][0] - 1, (HOPS[u][1] + 1) % NTV) for u in hops]
         if slot == 1:
             now.append("chol")
@@ -254,7 +256,9 @@
             for flip in (1, 2):
                 held["left", near_block, flip] = partner(held["left", near_block, 0], "right", NTV, flip)
         if far_block is not None:
-            held["left", far_block, 3] = partner(held["left", far_block, 0], "right", NTV, 3)
+            middle = held["left", far_block, 0].shape[0] // 2
+            held["left", far_block, "first"] = partner(held["left", far_block, 1][:middle], "right", NTV, 2)
+            held["left", far_block, "second"] = partner(held["left", far_block, 2][middle:], "right", NTV, 1)
         if slot == 1:
             held["other", "chol"] = partner(held["chol"], "occ", 2, 1)
             waiting[slot + 1].append(("other", "chol"))
@@ -263,7 +267,8 @@
             held["other", *unit] = partner(held["block", *unit], "occ", 2, 1)
             waiting[slot + 1].append(("other", *unit))
         if stack_block is not None:
-            every = [held["left", stack_block, flip] for flip in range(NTV)]
+            every = [held["left", stack_block, flip] for flip in range(3)]
+            every.append(jnp.concatenate([held["left", stack_block, half_of] for half_of in ("first", "second")]))
             if stack_block == AMP:
                 held["amp"] = lax.all_gather(jnp.concatenate(every, axis=2), "occ", axis=1, tiled=True)
                 waiting[slot + 3].append("amp")

time: 308 us -> 298 us (0.968)
  waiting for transfers between devices: 156 us -> 121 us
  starting transfers between devices: 39.6 us -> 50.8 us
  local copies, waits for them, and re-layouts: 15.8 us -> 26.9 us
    ppermute x31 -> x36, waiting for transfers between devices: 75.4 us -> 32.1 us  [partner(): return lax.ppermute(value, axis, [(i, i ^ flip) for i in range(size)])]
    ppermute x12, waiting for transfers between devices: 47 us -> 55.3 us  [on_square(): lax.ppermute(held['block', s - 1, (i + 1) % NTV], 'left', ring)]
    ppermute x31 -> x36, starting transfers between devices: 19.6 us -> 26.4 us  [partner(): return lax.ppermute(value, axis, [(i, i ^ flip) for i in range(size)])]
    slice x0 -> x10, local copies, waits for them, and re-layouts: none -> 5.4 us  [the longest x5 3.4 us: on_square(): held['left', far_block, 2][middle:]]
    unnamed x66 -> x68, local copies, waits for them, and re-layouts: 6.64 us -> 11.4 us
    ppermute x12, starting transfers between devices: 16.1 us -> 19.9 us  [on_square(): lax.ppermute(held['block', s - 1, (i + 1) % NTV], 'left', ring)]
    another operation x4 -> x8, other arithmetic: 6.61 us -> 8.96 us  [on_square(): held['lefts', stack_block] = jnp.stack(every)]
  transfers between devices with their start and end apart: 47 -> 52, of which waited for: 23 -> 27; matrix products, arithmetic and copies ran while one was open for 4% -> 7% of each run, Pallas kernels for 20% -> 21%
where the time goes in v2:
time: 298 us
  waiting for transfers between devices  121 us (41%)
  Pallas kernels  73.9 us (25%)
  starting transfers between devices  50.8 us (17%)
  local copies, waits for them, and re-layouts  26.9 us (9%)
  between operations  13.8 us (5%)
  other arithmetic  11 us (4%)
    pallas_call x5, Pallas kernels, ladder(): pl.pallas_call(functools.partial(ladder_kernel, steps, count, first), gri...  73.9 us
    ppermute x12, waiting for transfers between devices, on_square(): lax.ppermute(held['block', s - 1, (i + 1) % NTV], 'left', ring)  55.3 us
    ppermute x3, waiting for transfers between devices, shift(): lax.ppermute(value, axis, [(i, (i + step) % size) for i in range(size)])  33.6 us
    ppermute x36, waiting for transfers between devices, partner(): return lax.ppermute(value, axis, [(i, i ^ flip) for i in range(size)])  32.1 us
    ppermute x36, starting transfers between devices, partner(): return lax.ppermute(value, axis, [(i, i ^ flip) for i in range(size)])  26.4 us
    ppermute x12, starting transfers between devices, on_square(): lax.ppermute(held['block', s - 1, (i + 1) % NTV], 'left', ring)  19.9 us
    unnamed x68, local copies, waits for them, and re-layouts  11.4 us
    another operation x8, other arithmetic, on_square(): held['lefts', stack_block] = jnp.stack(every)  8.96 us
  transfers between devices with their start and end apart: 52, of which 27 were waited for; matrix products, arithmetic and copies ran while one was open for 7% of the time, Pallas kernels for 21%

profile of v2, /device:TPU:8, one launch (start us, length us, event | category | flops | bytes accessed | tf_op | source)
XLA Modules:
  0.0 297.5 jit_solution(12845764092486521973)
XLA Ops:
  6.5 1.8 constant_dynamic-slice_fusion.3
  8.7 1.9 collective-permute-start.1
  10.7 1.5 collective-permute-start.2
  12.2 11.1 %collective-permute-done.refs_18_ = bf16[1,512,512]{2,1,0:T(8,128)(2,1)S(1)} collective-permute-done((bf16[1,512,512]{2,1,0:T(8,128)(2,1)S(1)}, bf16[1,512,512]{2,1,0:T(8,128)(2,1)S(1)}, u32[]{:S(2)}, u32[]{:S(2)}) %collective-permute-start) | collective-permute-done | bytes 524320 | tf_op jit(solution)/shard_map/ppermute | solution.py:254
  23.8 2.6 collective-permute-start.5
  26.6 1.6 collective-permute-start.6
  28.8 10.2 %collective-permute-done.5.refs_18_ = bf16[1,512,512]{2,1,0:T(8,128)(2,1)S(1)} collective-permute-done((bf16[1,512,512]{2,1,0:T(8,128)(2,1)S(1)}, bf16[1,512,512]{2,1,0:T(8,128)(2,1)S(1)}, u32[]{:S(2)}, u32[]{:S(2)}) %collective-permute-start.5) | collective-permute-done | bytes 524320 | tf_op jit(solution)/shard_map/ppermute | solution.py:254
  39.0 1.7 collective-permute-start.9
  43.7 2.5 collective-permute-start.13
  46.5 8.4 %collective-permute-done.9.refs_18_ = bf16[1,512,512]{2,1,0:T(8,128)(2,1)} collective-permute-done((bf16[1,512,512]{2,1,0:T(8,128)(2,1)S(1)}, bf16[1,512,512]{2,1,0:T(8,128)(2,1)}, u32[]{:S(2)}, u32[]{:S(2)}) %collective-permute-start.9) | collective-permute-done | bytes 524320 | tf_op jit(solution)/shard_map/ppermute | solution.py:254
  55.2 1.6 collective-permute-start.14
  56.8 1.6 collective-permute-start.15
  58.3 2.1 copy.11
  60.5 4.2 %collective-permute-done.13.refs_20_ = bf16[1,512,512]{2,1,0:T(8,128)(2,1)S(1)} collective-permute-done((bf16[1,512,512]{2,1,0:T(8,128)(2,1)S(1)}, bf16[1,512,512]{2,1,0:T(8,128)(2,1)S(1)}, u32[]{:S(2)}, u32[]{:S(2)}) %collective-permute-start.13) | collective-permute-done | bytes 524320 | tf_op jit(solution)/shard_map/ppermute | solution.py:254
  66.1 1.6 maximum_maximum_fusion
  67.8 2.5 collective-permute-start.17
  74.3 9.3 %collective-permute-done.17.refs_20_ = bf16[1,512,512]{2,1,0:T(8,128)(2,1)S(1)} collective-permute-done((bf16[1,512,512]{2,1,0:T(8,128)(2,1)S(1)}, bf16[1,512,512]{2,1,0:T(8,128)(2,1)S(1)}, u32[]{:S(2)}, u32[]{:S(2)}) %collective-permute-start.17) | collective-permute-done | bytes 524320 | tf_op jit(solution)/shard_map/ppermute | solution.py:254
  87.6 2.2 collective-permute-start.25
  89.8 5.0 %collective-permute-done.21.refs_22_ = bf16[1,512,512]{2,1,0:T(8,128)(2,1)S(1)} collective-permute-done((bf16[1,512,512]{2,1,0:T(8,128)(2,1)S(1)}, bf16[1,512,512]{2,1,0:T(8,128)(2,1)S(1)}, u32[]{:S(2)}, u32[]{:S(2)}) %collective-permute-start.21) | collective-permute-done | bytes 524320 | tf_op jit(solution)/shard_map/ppermute | solution.py:254
  99.6 1.6 pad_maximum_fusion.1.refs_4_.refs_5_.refs_6_.refs_7_.refs_2_.refs_3_
  101.2 4.9 %collective-permute-done.25.refs_10_ = bf16[1,512,512]{2,1,0:T(8,128)(2,1)S(1)} collective-permute-done((bf16[1,512,512]{2,1,0:T(8,128)(2,1)S(1)}, bf16[1,512,512]{2,1,0:T(8,128)(2,1)S(1)}, u32[]{:S(2)}, u32[]{:S(2)}) %collective-permute-start.25) | collective-permute-done | bytes 524320 | tf_op jit(solution)/shard_map/ppermute | solution.py:254
  106.9 3.5 %collective-permute-done.26 = bf16[512,512]{1,0:T(8,128)(2,1)S(1)} collective-permute-done((bf16[512,512]{1,0:T(8,128)(2,1)S(1)}, bf16[512,512]{1,0:T(8,128)(2,1)S(1)}, u32[]{:S(2)}, u32[]{:S(2)}) %collective-permute-start.26) | collective-permute-done | bytes 524320 | tf_op jit(solution)/shard_map/ppermute | solution.py:159
  113.7 1.7 slice.83
  116.4 2.1 copy.13
  119.5 1.7 collective-permute-done.30
  121.2 2.9 collective-permute-done.31
  126.4 1.6 collective-permute-start.37
  129.1 3.0 %pad_maximum_fusion.2.refs_8_.refs_9_.refs_10_.refs_11_.refs_4_.refs_5_ = bf16[4,512,512]{2,1,0:T(8,128)(2,1)} fusion(bf16[1,512,512]{2,1,0:T(8,128)(2,1)S(1)} %maximum_bitcast_fusion.2, bf16[1,512,512]{2,1,0:T(8,128)(2,1)} %bitcast.27, bf16[1,512,512]{2,1,0:T(8,128)(2,1)} %bitcast.83, bf16[1,512,512]{2,1,0:T(8,128)(2,1)} %bitcast.76), kind=kLoop, calls=%fused_computation.5 | loop fusion | flops 3145728 | bytes 4194304 | tf_op jit(solution)/shard_map/stack | solution.py:276
  132.1 2.2 collective-permute-done.33.refs_20_
  134.4 3.3 %collective-permute-done.34 = bf16[512,512]{1,0:T(8,128)(2,1)} collective-permute-done((bf16[512,512]{1,0:T(8,128)(2,1)}, bf16[512,512]{1,0:T(8,128)(2,1)}, u32[]{:S(2)}, u32[]{:S(2)}) %collective-permute-start.34) | collective-permute-done | bytes 524320 | tf_op jit(solution)/shard_map/ppermute | solution.py:159
  140.5 1.7 slice.85
  143.3 1.6 collective-permute-start.41
  144.9 3.8 %collective-permute-done.38 = bf16[256,512]{1,0:T(8,128)(2,1)} collective-permute-done((bf16[256,512]{1,0:T(8,128)(2,1)S(1)}, bf16[256,512]{1,0:T(8,128)(2,1)}, u32[]{:S(2)}, u32[]{:S(2)}) %collective-permute-start.38) | collective-permute-done | bytes 262176 | tf_op jit(solution)/shard_map/ppermute | solution.py:159
  148.7 2.2 collective-permute-done.39
  150.9 1.6 collective-permute-start.43
  153.7 1.8 pad_maximum_fusion.3.refs_12_.refs_13_.refs_14_.refs_15_.refs_6_.refs_7_
  156.4 1.6 copy-done.4
  161.1 16.2 %shard_map.37.refs_25_ = f32[4,4,128,512]{3,2,1,0:T(8,128)} custom-call(s32[1]{0:T(128)} %bitcast.half_ref, s32[4]{0:T(128)S(1)} %get-tuple-element.149.live_ref, s32[4]{0:T(128)S(1)} %fusion.7.pick_ref, s32[1]{0:T(128)} %bitcast.33.tile_ref, bf16[4,512,512]{2,1,0:T(8,128)(2,1)S(1)} %pad_maximum_fusion.refs_0_.refs_1_.refs_2_.refs_3_, ...), custom_call_target="tpu_custom_call" | custom-call | flops 10737418240 | bytes 20971520 | tf_op jit(solution)/shard_map/pallas_call | solution.py:135
  177.6 18.0 %shard_map.38.refs_25_ = f32[4,4,128,512]{3,2,1,0:T(8,128)} custom-call(s32[1]{0:T(128)} %bitcast.half_ref, s32[4]{0:T(128)S(1)} %get-tuple-element.148.live_ref, s32[4]{0:T(128)S(1)} %fusion.7.pick_ref, s32[1]{0:T(128)} %bitcast.34.tile_ref, ...), custom_call_target="tpu_custom_call", output_to_operand_aliasing={{}: (29, {})} | custom-call | flops 10737418240 | bytes 20971520 | tf_op jit(solution)/shard_map/pallas_call | solution.py:135
  196.0 17.5 %shard_map.39.refs_17_ = f32[4,4,128,512]{3,2,1,0:T(8,128)} custom-call(s32[1]{0:T(128)} %bitcast.half_ref, s32[4]{0:T(128)S(1)} %get-tuple-element.147.live_ref, s32[4]{0:T(128)S(1)} %fusion.7.pick_ref, s32[1]{0:T(128)} %bitcast.35.tile_ref, ...), custom_call_target="tpu_custom_call", output_to_operand_aliasing={{}: (29, {})} | custom-call | flops 10737418240 | bytes 20971520 | tf_op jit(solution)/shard_map/pallas_call | solution.py:135
  213.4 11.1 %shard_map.41 = bf16[2,4,128,512]{3,2,1,0:T(8,128)(2,1)S(1)} custom-call(s32[1]{0:T(128)} %bitcast.half_ref, s32[2]{0:T(128)S(1)} %get-tuple-element.145.live_ref, s32[2]{0:T(128)S(1)} %get-tuple-element.161.pick_ref, s32[1]{0:T(128)} %bitcast.3.tile_ref, bf16[4,512,512]{2,1,0:T(8,128)(2,1)S(1)} %pad_maximum_fusion.refs_0_.refs_1_.refs_2_.refs_3_, ...), custom_call_target="tpu_custom_call" | custom-call | flops 5368709120 | bytes 20971520 | tf_op jit(solution)/shard_map/pallas_call | solution.py:135
  225.3 3.8 %collective-permute-start.46 = (bf16[4,128,512]{2,1,0:T(8,128)(2,1)S(1)}, bf16[4,128,512]{2,1,0:T(8,128)(2,1)S(1)}, u32[]{:S(2)}, u32[]{:S(2)}) collective-permute-start(bf16[4,128,512]{2,1,0:T(8,128)(2,1)S(1)} %get-tuple-element.159), channel_id=1, source_target_pairs={{0,16},{8,24},{16,0},{24,8},{1,17},{9,25},{17,1},{25,9},{2,18},{10... | collective-permute-start | bytes 1572872 | tf_op jit(solution)/shard_map/ppermute | solution.py:163
  229.0 11.2 %shard_map.40 = f32[2,4,128,512]{3,2,1,0:T(8,128)S(1)} custom-call(s32[1]{0:T(128)} %bitcast.half_ref, s32[2]{0:T(128)S(1)} %get-tuple-element.146.live_ref, s32[2]{0:T(128)S(1)} %get-tuple-element.162.pick_ref, s32[1]{0:T(128)} %bitcast.3.tile_ref, bf16[4,512,512]{2,1,0:T(8,128)(2,1)S(1)} %pad_maximum_fusion.refs_0_.refs_1_.refs_2_.refs_3_, ...), custom_call_target="tpu_custom_call" | custom-call | flops 5368709120 | bytes 20971520 | tf_op jit(solution)/shard_map/pallas_call | solution.py:135
  240.4 30.4 %collective-permute-done.46 = bf16[4,128,512]{2,1,0:T(8,128)(2,1)S(1)} collective-permute-done((bf16[4,128,512]{2,1,0:T(8,128)(2,1)S(1)}, bf16[4,128,512]{2,1,0:T(8,128)(2,1)S(1)}, u32[]{:S(2)}, u32[]{:S(2)}) %collective-permute-start.46) | collective-permute-done | bytes 524320 | tf_op jit(solution)/shard_map/ppermute | solution.py:163
  270.8 3.2 %collective-permute-done.47 = bf16[4,128,512]{2,1,0:T(8,128)(2,1)S(1)} collective-permute-done((bf16[4,128,512]{2,1,0:T(8,128)(2,1)S(1)}, bf16[4,128,512]{2,1,0:T(8,128)(2,1)S(1)}, u32[]{:S(2)}, u32[]{:S(2)}) %collective-permute-start.47) | collective-permute-done | bytes 524320 | tf_op jit(solution)/shard_map/ppermute | solution.py:163
  278.0 5.7 %collective-permute-done.48 = f32[4,128,128]{2,1,0:T(8,128)S(1)} collective-permute-done((f32[4,128,128]{2,1,0:T(8,128)S(1)}, f32[4,128,128]{2,1,0:T(8,128)S(1)}, u32[]{:S(2)}, u32[]{:S(2)}) %collective-permute-start.48) | collective-permute-done | bytes 262176 | tf_op jit(solution)/shard_map/ppermute | solution.py:159
  283.7 3.4 %collective-permute-done.49 = f32[4,128,128]{2,1,0:T(8,128)S(1)} collective-permute-done((f32[4,128,128]{2,1,0:T(8,128)S(1)}, f32[4,128,128]{2,1,0:T(8,128)S(1)}, u32[]{:S(2)}, u32[]{:S(2)}) %collective-permute-start.49) | collective-permute-done | bytes 262176 | tf_op jit(solution)/shard_map/ppermute | solution.py:159
  289.0 1.6 copy.14
  (171 shorter events, 45.5 us)
Async XLA Ops:
  6.5 104.8 %all-gather.2.cloned.1.call-start = ((), (), s32[]{:S(2)}) async-start(), calls=%async_computation | async-start | bytes 6291456 | tf_op jit(solution)/shard_map/all_gather | solution.py:273
  8.7 14.6 %collective-permute-start = (bf16[1,512,512]{2,1,0:T(8,128)(2,1)S(1)}, bf16[1,512,512]{2,1,0:T(8,128)(2,1)S(1)}, u32[]{:S(2)}, u32[]{:S(2)}) collective-permute-start(bf16[1,512,512]{2,1,0:T(8,128)(2,1)S(1)} %get-tuple-element.75), channel_id=1, source_target_pairs={{0,16},{16,24},{24,8},{8,0},{1,17},{17,25},{25,9},{9,1},{2,18},{18... | collective-permute-start | bytes 1572872 | tf_op jit(solution)/shard_map/ppermute | solution.py:254
  8.7 14.6 %collective-permute-start.1 = (bf16[512,512]{1,0:T(8,128)(2,1)S(1)}, bf16[512,512]{1,0:T(8,128)(2,1)S(1)}, u32[]{:S(2)}, u32[]{:S(2)}) collective-permute-start(bf16[512,512]{1,0:T(8,128)(2,1)S(1)} %bitcast.80), channel_id=1, source_target_pairs={{0,2},{2,0},{4,6},{6,4},{1,3},{3,1},{5,7},{7,5},{8,10},{10,8},{12,... | collective-permute-start | bytes 1572872 | tf_op jit(solution)/shard_map/ppermute | solution.py:159
  10.7 13.1 %collective-permute-start.2 = (bf16[512,512]{1,0:T(8,128)(2,1)S(1)}, bf16[512,512]{1,0:T(8,128)(2,1)S(1)}, u32[]{:S(2)}, u32[]{:S(2)}) collective-permute-start(bf16[512,512]{1,0:T(8,128)(2,1)S(1)} %bitcast.81), channel_id=1, source_target_pairs={{0,4},{2,6},{4,0},{6,2},{1,5},{3,7},{5,1},{7,3},{8,12},{10,14},{12... | collective-permute-start | bytes 1572872 | tf_op jit(solution)/shard_map/ppermute | solution.py:159
  23.8 17.8 %collective-permute-start.3 = (bf16[4,512,512]{2,1,0:T(8,128)(2,1)S(1)}, bf16[4,512,512]{2,1,0:T(8,128)(2,1)S(1)}, u32[]{:S(2)}, u32[]{:S(2)}) collective-permute-start(bf16[4,512,512]{2,1,0:T(8,128)(2,1)S(1)} %copy-done.3), channel_id=1, source_target_pairs={{0,1},{1,0},{2,3},{3,2},{4,5},{5,4},{6,7},{7,6},{8,9},{9,8},{10,11... | collective-permute-start | bytes 6291464 | tf_op jit(solution)/shard_map/ppermute | solution.py:159
  23.8 15.2 %collective-permute-start.5 = (bf16[1,512,512]{2,1,0:T(8,128)(2,1)S(1)}, bf16[1,512,512]{2,1,0:T(8,128)(2,1)S(1)}, u32[]{:S(2)}, u32[]{:S(2)}) collective-permute-start(bf16[1,512,512]{2,1,0:T(8,128)(2,1)S(1)} %get-tuple-element.79), channel_id=1, source_target_pairs={{0,16},{16,24},{24,8},{8,0},{1,17},{17,25},{25,9},{9,1},{2,18},{18... | collective-permute-start | bytes 1572872 | tf_op jit(solution)/shard_map/ppermute | solution.py:254
  26.4 14.3 %collective-permute-start.4 = (bf16[1,512,512]{2,1,0:T(8,128)(2,1)S(1)}, bf16[1,512,512]{2,1,0:T(8,128)(2,1)S(1)}, u32[]{:S(2)}, u32[]{:S(2)}) collective-permute-start(bf16[1,512,512]{2,1,0:T(8,128)(2,1)S(1)} %collective-permute-done.refs_18_), channel_id=1, source_target_pairs={{0,1},{1,0},{2,3},{3,2},{4,5},{5,4},{6,7},{7,6},{8,9},{9,8},{10,11... | collective-permute-start | bytes 1572872 | tf_op jit(solution)/shard_map/ppermute | solution.py:159
  26.6 14.1 %collective-permute-start.6 = (bf16[256,512]{1,0:T(8,128)(2,1)S(1)}, bf16[256,512]{1,0:T(8,128)(2,1)S(1)}, u32[]{:S(2)}, u32[]{:S(2)}) collective-permute-start(bf16[256,512]{1,0:T(8,128)(2,1)S(1)} %slice.76), channel_id=1, source_target_pairs={{0,4},{2,6},{4,0},{6,2},{1,5},{3,7},{5,1},{7,3},{8,12},{10,14},{12... | collective-permute-start | bytes 786440 | tf_op jit(solution)/shard_map/ppermute | solution.py:159
  28.2 12.5 %collective-permute-start.7 = (bf16[256,512]{1,0:T(8,128)(2,1)S(1)}, bf16[256,512]{1,0:T(8,128)(2,1)S(1)}, u32[]{:S(2)}, u32[]{:S(2)}) collective-permute-start(bf16[256,512]{1,0:T(8,128)(2,1)S(1)} %slice.77), channel_id=1, source_target_pairs={{0,2},{2,0},{4,6},{6,4},{1,3},{3,1},{5,7},{7,5},{8,10},{10,8},{12,... | collective-permute-start | bytes 786440 | tf_op jit(solution)/shard_map/ppermute | solution.py:159
  39.0 15.8 %collective-permute-start.9 = (bf16[1,512,512]{2,1,0:T(8,128)(2,1)S(1)}, bf16[1,512,512]{2,1,0:T(8,128)(2,1)}, u32[]{:S(2)}, u32[]{:S(2)}) collective-permute-start(bf16[1,512,512]{2,1,0:T(8,128)(2,1)S(1)} %get-tuple-element.86), channel_id=1, source_target_pairs={{0,16},{16,24},{24,8},{8,0},{1,17},{17,25},{25,9},{9,1},{2,18},{18... | collective-permute-start | bytes 1572872 | tf_op jit(solution)/shard_map/ppermute | solution.py:254
  41.5 13.3 %collective-permute-start.10 = (bf16[4,512,128]{2,1,0:T(8,128)(2,1)S(1)}, bf16[4,512,128]{2,1,0:T(8,128)(2,1)S(1)}, u32[]{:S(2)}, u32[]{:S(2)}) collective-permute-start(bf16[4,512,128]{2,1,0:T(8,128)(2,1)S(1)} %bitcast.88), channel_id=1, source_target_pairs={{0,2},{2,0},{4,6},{6,4},{1,3},{3,1},{5,7},{7,5},{8,10},{10,8},{12,... | collective-permute-start | bytes 1572872 | tf_op jit(solution)/shard_map/ppermute | solution.py:159
  42.1 13.0 %collective-permute-start.11 = (bf16[4,512,128]{2,1,0:T(8,128)(2,1)S(1)}, bf16[4,512,128]{2,1,0:T(8,128)(2,1)S(1)}, u32[]{:S(2)}, u32[]{:S(2)}) collective-permute-start(bf16[4,512,128]{2,1,0:T(8,128)(2,1)S(1)} %bitcast.89), channel_id=1, source_target_pairs={{0,4},{2,6},{4,0},{6,2},{1,5},{3,7},{5,1},{7,3},{8,12},{10,14},{12... | collective-permute-start | bytes 1572872 | tf_op jit(solution)/shard_map/ppermute | solution.py:159
  43.7 11.5 %collective-permute-start.8 = (bf16[1,512,512]{2,1,0:T(8,128)(2,1)S(1)}, bf16[1,512,512]{2,1,0:T(8,128)(2,1)S(1)}, u32[]{:S(2)}, u32[]{:S(2)}) collective-permute-start(bf16[1,512,512]{2,1,0:T(8,128)(2,1)S(1)} %collective-permute-done.5.refs_18_), channel_id=1, source_target_pairs={{0,1},{1,0},{2,3},{3,2},{4,5},{5,4},{6,7},{7,6},{8,9},{9,8},{10,11... | collective-permute-start | bytes 1572872 | tf_op jit(solution)/shard_map/ppermute | solution.py:159
  43.7 21.0 %collective-permute-start.13 = (bf16[1,512,512]{2,1,0:T(8,128)(2,1)S(1)}, bf16[1,512,512]{2,1,0:T(8,128)(2,1)S(1)}, u32[]{:S(2)}, u32[]{:S(2)}) collective-permute-start(bf16[1,512,512]{2,1,0:T(8,128)(2,1)S(1)} %collective-permute-done.refs_18_), channel_id=1, source_target_pairs={{0,16},{16,24},{24,8},{8,0},{1,17},{17,25},{25,9},{9,1},{2,18},{18... | collective-permute-start | bytes 1572872 | tf_op jit(solution)/shard_map/ppermute | solution.py:254
  55.1 10.1 %collective-permute-start.12 = (bf16[1,512,512]{2,1,0:T(8,128)(2,1)}, bf16[1,512,512]{2,1,0:T(8,128)(2,1)S(1)}, u32[]{:S(2)}, u32[]{:S(2)}) collective-permute-start(bf16[1,512,512]{2,1,0:T(8,128)(2,1)} %collective-permute-done.9.refs_18_), channel_id=1, source_target_pairs={{0,1},{1,0},{2,3},{3,2},{4,5},{5,4},{6,7},{7,6},{8,9},{9,8},{10,11... | collective-permute-start | bytes 1572872 | tf_op jit(solution)/shard_map/ppermute | solution.py:159
  55.2 9.5 %collective-permute-start.14 = (bf16[2,512,128]{2,1,0:T(8,128)(2,1)S(1)}, bf16[2,512,128]{2,1,0:T(8,128)(2,1)S(1)}, u32[]{:S(2)}, u32[]{:S(2)}) collective-permute-start(bf16[2,512,128]{2,1,0:T(8,128)(2,1)S(1)} %slice.78), channel_id=1, source_target_pairs={{0,4},{2,6},{4,0},{6,2},{1,5},{3,7},{5,1},{7,3},{8,12},{10,14},{12... | collective-permute-start | bytes 786440 | tf_op jit(solution)/shard_map/ppermute | solution.py:159
  67.8 15.8 %collective-permute-start.17 = (bf16[1,512,512]{2,1,0:T(8,128)(2,1)S(1)}, bf16[1,512,512]{2,1,0:T(8,128)(2,1)S(1)}, u32[]{:S(2)}, u32[]{:S(2)}) collective-permute-start(bf16[1,512,512]{2,1,0:T(8,128)(2,1)S(1)} %collective-permute-done.5.refs_18_), channel_id=1, source_target_pairs={{0,16},{16,24},{24,8},{8,0},{1,17},{17,25},{25,9},{9,1},{2,18},{18... | collective-permute-start | bytes 1572872 | tf_op jit(solution)/shard_map/ppermute | solution.py:254
  70.3 13.3 %collective-permute-start.16 = (bf16[1,512,512]{2,1,0:T(8,128)(2,1)S(1)}, bf16[1,512,512]{2,1,0:T(8,128)(2,1)S(1)}, u32[]{:S(2)}, u32[]{:S(2)}) collective-permute-start(bf16[1,512,512]{2,1,0:T(8,128)(2,1)S(1)} %collective-permute-done.13.refs_20_), channel_id=1, source_target_pairs={{0,1},{1,0},{2,3},{3,2},{4,5},{5,4},{6,7},{7,6},{8,9},{9,8},{10,11... | collective-permute-start | bytes 1572872 | tf_op jit(solution)/shard_map/ppermute | solution.py:159
  70.3 14.5 %collective-permute-start.18 = (bf16[512,512]{1,0:T(8,128)(2,1)}, bf16[512,512]{1,0:T(8,128)(2,1)S(1)}, u32[]{:S(2)}, u32[]{:S(2)}) collective-permute-start(bf16[512,512]{1,0:T(8,128)(2,1)} %bitcast.77), channel_id=1, source_target_pairs={{0,2},{2,0},{4,6},{6,4},{1,3},{3,1},{5,7},{7,5},{8,10},{10,8},{12,... | collective-permute-start | bytes 1572872 | tf_op jit(solution)/shard_map/ppermute | solution.py:159
  71.8 14.3 %collective-permute-start.19 = (bf16[512,512]{1,0:T(8,128)(2,1)}, bf16[512,512]{1,0:T(8,128)(2,1)S(1)}, u32[]{:S(2)}, u32[]{:S(2)}) collective-permute-start(bf16[512,512]{1,0:T(8,128)(2,1)} %bitcast.78), channel_id=1, source_target_pairs={{0,4},{2,6},{4,0},{6,2},{1,5},{3,7},{5,1},{7,3},{8,12},{10,14},{12... | collective-permute-start | bytes 1572872 | tf_op jit(solution)/shard_map/ppermute | solution.py:159
  72.3 22.5 %collective-permute-start.21 = (bf16[1,512,512]{2,1,0:T(8,128)(2,1)S(1)}, bf16[1,512,512]{2,1,0:T(8,128)(2,1)S(1)}, u32[]{:S(2)}, u32[]{:S(2)}) collective-permute-start(bf16[1,512,512]{2,1,0:T(8,128)(2,1)S(1)} %collective-permute-done.13.refs_20_), channel_id=1, source_target_pairs={{0,16},{16,24},{24,8},{8,0},{1,17},{17,25},{25,9},{9,1},{2,18},{18... | collective-permute-start | bytes 1572872 | tf_op jit(solution)/shard_map/ppermute | solution.py:254
  86.1 9.1 %collective-permute-start.20 = (bf16[1,512,512]{2,1,0:T(8,128)(2,1)S(1)}, bf16[1,512,512]{2,1,0:T(8,128)(2,1)S(1)}, u32[]{:S(2)}, u32[]{:S(2)}) collective-permute-start(bf16[1,512,512]{2,1,0:T(8,128)(2,1)S(1)} %collective-permute-done.17.refs_20_), channel_id=1, source_target_pairs={{0,1},{1,0},{2,3},{3,2},{4,5},{5,4},{6,7},{7,6},{8,9},{9,8},{10,11... | collective-permute-start | bytes 1572872 | tf_op jit(solution)/shard_map/ppermute | solution.py:159
  86.1 8.8 %collective-permute-start.22 = (bf16[256,512]{1,0:T(8,128)(2,1)S(1)}, bf16[256,512]{1,0:T(8,128)(2,1)S(1)}, u32[]{:S(2)}, u32[]{:S(2)}) collective-permute-start(bf16[256,512]{1,0:T(8,128)(2,1)S(1)} %slice.80), channel_id=1, source_target_pairs={{0,4},{2,6},{4,0},{6,2},{1,5},{3,7},{5,1},{7,3},{8,12},{10,14},{12... | collective-permute-start | bytes 786440 | tf_op jit(solution)/shard_map/ppermute | solution.py:159
  87.6 18.5 %collective-permute-start.25 = (bf16[1,512,512]{2,1,0:T(8,128)(2,1)S(1)}, bf16[1,512,512]{2,1,0:T(8,128)(2,1)S(1)}, u32[]{:S(2)}, u32[]{:S(2)}) collective-permute-start(bf16[1,512,512]{2,1,0:T(8,128)(2,1)S(1)} %copy-done.29), channel_id=1, source_target_pairs={{0,16},{16,24},{24,8},{8,0},{1,17},{17,25},{25,9},{9,1},{2,18},{18... | collective-permute-start | bytes 1572872 | tf_op jit(solution)/shard_map/ppermute | solution.py:254
  96.0 10.1 %collective-permute-start.24 = (bf16[1,512,512]{2,1,0:T(8,128)(2,1)S(1)}, bf16[1,512,512]{2,1,0:T(8,128)(2,1)S(1)}, u32[]{:S(2)}, u32[]{:S(2)}) collective-permute-start(bf16[1,512,512]{2,1,0:T(8,128)(2,1)S(1)} %collective-permute-done.21.refs_22_), channel_id=1, source_target_pairs={{0,1},{1,0},{2,3},{3,2},{4,5},{5,4},{6,7},{7,6},{8,9},{9,8},{10,11... | collective-permute-start | bytes 1572872 | tf_op jit(solution)/shard_map/ppermute | solution.py:159
  96.0 14.3 %collective-permute-start.26 = (bf16[512,512]{1,0:T(8,128)(2,1)S(1)}, bf16[512,512]{1,0:T(8,128)(2,1)S(1)}, u32[]{:S(2)}, u32[]{:S(2)}) collective-permute-start(bf16[512,512]{1,0:T(8,128)(2,1)S(1)} %bitcast.74), channel_id=1, source_target_pairs={{0,2},{2,0},{4,6},{6,4},{1,3},{3,1},{5,7},{7,5},{8,10},{10,8},{12,... | collective-permute-start | bytes 1572872 | tf_op jit(solution)/shard_map/ppermute | solution.py:159
  97.2 14.2 %collective-permute-start.27 = (bf16[512,512]{1,0:T(8,128)(2,1)S(1)}, bf16[512,512]{1,0:T(8,128)(2,1)}, u32[]{:S(2)}, u32[]{:S(2)}) collective-permute-start(bf16[512,512]{1,0:T(8,128)(2,1)S(1)} %bitcast.75), channel_id=1, source_target_pairs={{0,4},{2,6},{4,0},{6,2},{1,5},{3,7},{5,1},{7,3},{8,12},{10,14},{12... | collective-permute-start | bytes 1572872 | tf_op jit(solution)/shard_map/ppermute | solution.py:159
  98.1 21.5 %collective-permute-start.29 = (bf16[1,512,512]{2,1,0:T(8,128)(2,1)}, bf16[1,512,512]{2,1,0:T(8,128)(2,1)S(1)}, u32[]{:S(2)}, u32[]{:S(2)}) collective-permute-start(bf16[1,512,512]{2,1,0:T(8,128)(2,1)} %collective-permute-done.9.refs_18_), channel_id=1, source_target_pairs={{0,16},{16,24},{24,8},{8,0},{1,17},{17,25},{25,9},{9,1},{2,18},{18... | collective-permute-start | bytes 1572872 | tf_op jit(solution)/shard_map/ppermute | solution.py:254
  111.3 12.8 %collective-permute-start.28 = (bf16[1,512,512]{2,1,0:T(8,128)(2,1)S(1)}, bf16[1,512,512]{2,1,0:T(8,128)(2,1)}, u32[]{:S(2)}, u32[]{:S(2)}) collective-permute-start(bf16[1,512,512]{2,1,0:T(8,128)(2,1)S(1)} %collective-permute-done.25.refs_10_), channel_id=1, source_target_pairs={{0,1},{1,0},{2,3},{3,2},{4,5},{5,4},{6,7},{7,6},{8,9},{9,8},{10,11... | collective-permute-start | bytes 1572872 | tf_op jit(solution)/shard_map/ppermute | solution.py:159
  112.3 8.9 %collective-permute-start.30 = (bf16[256,512]{1,0:T(8,128)(2,1)S(1)}, bf16[256,512]{1,0:T(8,128)(2,1)}, u32[]{:S(2)}, u32[]{:S(2)}) collective-permute-start(bf16[256,512]{1,0:T(8,128)(2,1)S(1)} %slice.82), channel_id=1, source_target_pairs={{0,4},{2,6},{4,0},{6,2},{1,5},{3,7},{5,1},{7,3},{8,12},{10,14},{12... | collective-permute-start | bytes 786440 | tf_op jit(solution)/shard_map/ppermute | solution.py:159
  118.6 15.8 %collective-permute-start.33 = (bf16[1,512,512]{2,1,0:T(8,128)(2,1)S(1)}, bf16[1,512,512]{2,1,0:T(8,128)(2,1)}, u32[]{:S(2)}, u32[]{:S(2)}) collective-permute-start(bf16[1,512,512]{2,1,0:T(8,128)(2,1)S(1)} %collective-permute-done.25.refs_10_), channel_id=1, source_target_pairs={{0,16},{16,24},{24,8},{8,0},{1,17},{17,25},{25,9},{9,1},{2,18},{18... | collective-permute-start | bytes 1572872 | tf_op jit(solution)/shard_map/ppermute | solution.py:254
  124.1 13.6 %collective-permute-start.34 = (bf16[512,512]{1,0:T(8,128)(2,1)}, bf16[512,512]{1,0:T(8,128)(2,1)}, u32[]{:S(2)}, u32[]{:S(2)}) collective-permute-start(bf16[512,512]{1,0:T(8,128)(2,1)} %bitcast.24), channel_id=1, source_target_pairs={{0,2},{2,0},{4,6},{6,4},{1,3},{3,1},{5,7},{7,5},{8,10},{10,8},{12,... | collective-permute-start | bytes 1572872 | tf_op jit(solution)/shard_map/ppermute | solution.py:159
  125.2 13.3 %collective-permute-start.35 = (bf16[512,512]{1,0:T(8,128)(2,1)}, bf16[512,512]{1,0:T(8,128)(2,1)}, u32[]{:S(2)}, u32[]{:S(2)}) collective-permute-start(bf16[512,512]{1,0:T(8,128)(2,1)} %bitcast.24), channel_id=1, source_target_pairs={{0,4},{2,6},{4,0},{6,2},{1,5},{3,7},{5,1},{7,3},{8,12},{10,14},{12... | collective-permute-start | bytes 1572872 | tf_op jit(solution)/shard_map/ppermute | solution.py:159
  126.4 18.5 %collective-permute-start.37 = (bf16[1,512,512]{2,1,0:T(8,128)(2,1)S(1)}, bf16[1,512,512]{2,1,0:T(8,128)(2,1)}, u32[]{:S(2)}, u32[]{:S(2)}) collective-permute-start(bf16[1,512,512]{2,1,0:T(8,128)(2,1)S(1)} %collective-permute-done.29.refs_12_), channel_id=1, source_target_pairs={{0,16},{16,24},{24,8},{8,0},{1,17},{17,25},{25,9},{9,1},{2,18},{18... | collective-permute-start | bytes 1572872 | tf_op jit(solution)/shard_map/ppermute | solution.py:254
  138.5 12.5 %collective-permute-start.36 = (bf16[1,512,512]{2,1,0:T(8,128)(2,1)}, bf16[1,512,512]{2,1,0:T(8,128)(2,1)}, u32[]{:S(2)}, u32[]{:S(2)}) collective-permute-start(bf16[1,512,512]{2,1,0:T(8,128)(2,1)} %collective-permute-done.33.refs_20_), channel_id=1, source_target_pairs={{0,1},{1,0},{2,3},{3,2},{4,5},{5,4},{6,7},{7,6},{8,9},{9,8},{10,11... | collective-permute-start | bytes 1572872 | tf_op jit(solution)/shard_map/ppermute | solution.py:159
  139.8 8.9 %collective-permute-start.38 = (bf16[256,512]{1,0:T(8,128)(2,1)S(1)}, bf16[256,512]{1,0:T(8,128)(2,1)}, u32[]{:S(2)}, u32[]{:S(2)}) collective-permute-start(bf16[256,512]{1,0:T(8,128)(2,1)S(1)} %slice.84), channel_id=1, source_target_pairs={{0,4},{2,6},{4,0},{6,2},{1,5},{3,7},{5,1},{7,3},{8,12},{10,14},{12... | collective-permute-start | bytes 786440 | tf_op jit(solution)/shard_map/ppermute | solution.py:159
  142.2 8.8 %collective-permute-start.39 = (bf16[256,512]{1,0:T(8,128)(2,1)}, bf16[256,512]{1,0:T(8,128)(2,1)}, u32[]{:S(2)}, u32[]{:S(2)}) collective-permute-start(bf16[256,512]{1,0:T(8,128)(2,1)} %slice.85), channel_id=1, source_target_pairs={{0,2},{2,0},{4,6},{6,4},{1,3},{3,1},{5,7},{7,5},{8,10},{10,8},{12,... | collective-permute-start | bytes 786440 | tf_op jit(solution)/shard_map/ppermute | solution.py:159
  143.3 34.0 %collective-permute-start.41 = (bf16[1,512,512]{2,1,0:T(8,128)(2,1)}, bf16[1,512,512]{2,1,0:T(8,128)(2,1)S(1)}, u32[]{:S(2)}, u32[]{:S(2)}) collective-permute-start(bf16[1,512,512]{2,1,0:T(8,128)(2,1)} %collective-permute-done.33.refs_20_), channel_id=1, source_target_pairs={{0,16},{16,24},{24,8},{8,0},{1,17},{17,25},{25,9},{9,1},{2,18},{18... | collective-permute-start | bytes 1572872 | tf_op jit(solution)/shard_map/ppermute | solution.py:254
  150.9 26.4 %collective-permute-start.40 = (bf16[1,512,512]{2,1,0:T(8,128)(2,1)}, bf16[1,512,512]{2,1,0:T(8,128)(2,1)S(1)}, u32[]{:S(2)}, u32[]{:S(2)}) collective-permute-start(bf16[1,512,512]{2,1,0:T(8,128)(2,1)} %collective-permute-done.37.refs_22_), channel_id=1, source_target_pairs={{0,1},{1,0},{2,3},{3,2},{4,5},{5,4},{6,7},{7,6},{8,9},{9,8},{10,11... | collective-permute-start | bytes 1572872 | tf_op jit(solution)/shard_map/ppermute | solution.py:159
  150.9 44.7 %collective-permute-start.43 = (bf16[1,512,512]{2,1,0:T(8,128)(2,1)}, bf16[1,512,512]{2,1,0:T(8,128)(2,1)S(1)}, u32[]{:S(2)}, u32[]{:S(2)}) collective-permute-start(bf16[1,512,512]{2,1,0:T(8,128)(2,1)} %copy-done.5), channel_id=1, source_target_pairs={{0,16},{16,24},{24,8},{8,0},{1,17},{17,25},{25,9},{9,1},{2,18},{18... | collective-permute-start | bytes 1572872 | tf_op jit(solution)/shard_map/ppermute | solution.py:254
  177.3 18.3 %collective-permute-start.42 = (bf16[1,512,512]{2,1,0:T(8,128)(2,1)S(1)}, bf16[1,512,512]{2,1,0:T(8,128)(2,1)S(1)}, u32[]{:S(2)}, u32[]{:S(2)}) collective-permute-start(bf16[1,512,512]{2,1,0:T(8,128)(2,1)S(1)} %collective-permute-done.41.refs_22_), channel_id=1, source_target_pairs={{0,1},{1,0},{2,3},{3,2},{4,5},{5,4},{6,7},{7,6},{8,9},{9,8},{10,11... | collective-permute-start | bytes 1572872 | tf_op jit(solution)/shard_map/ppermute | solution.py:159
  195.6 17.8 %collective-permute-start.44 = (bf16[1,512,512]{2,1,0:T(8,128)(2,1)S(1)}, bf16[1,512,512]{2,1,0:T(8,128)(2,1)S(1)}, u32[]{:S(2)}, u32[]{:S(2)}) collective-permute-start(bf16[1,512,512]{2,1,0:T(8,128)(2,1)S(1)} %collective-permute-done.43.refs_14_), channel_id=1, source_target_pairs={{0,1},{1,0},{2,3},{3,2},{4,5},{5,4},{6,7},{7,6},{8,9},{9,8},{10,11... | collective-permute-start | bytes 1572872 | tf_op jit(solution)/shard_map/ppermute | solution.py:159
  224.7 15.7 %collective-permute-start.45 = (bf16[4,128,512]{2,1,0:T(8,128)(2,1)S(1)}, bf16[4,128,512]{2,1,0:T(8,128)(2,1)S(1)}, u32[]{:S(2)}, u32[]{:S(2)}) collective-permute-start(bf16[4,128,512]{2,1,0:T(8,128)(2,1)S(1)} %get-tuple-element.158), channel_id=1, source_target_pairs={{0,8},{8,16},{16,24},{24,0},{1,9},{9,17},{17,25},{25,1},{2,10},{10... | collective-permute-start | bytes 1572872 | tf_op jit(solution)/shard_map/ppermute | solution.py:163
  225.3 45.5 %collective-permute-start.46 = (bf16[4,128,512]{2,1,0:T(8,128)(2,1)S(1)}, bf16[4,128,512]{2,1,0:T(8,128)(2,1)S(1)}, u32[]{:S(2)}, u32[]{:S(2)}) collective-permute-start(bf16[4,128,512]{2,1,0:T(8,128)(2,1)S(1)} %get-tuple-element.159), channel_id=1, source_target_pairs={{0,16},{8,24},{16,0},{24,8},{1,17},{9,25},{17,1},{25,9},{2,18},{10... | collective-permute-start | bytes 1572872 | tf_op jit(solution)/shard_map/ppermute | solution.py:163
  240.3 33.7 %collective-permute-start.47 = (bf16[4,128,512]{2,1,0:T(8,128)(2,1)S(1)}, bf16[4,128,512]{2,1,0:T(8,128)(2,1)S(1)}, u32[]{:S(2)}, u32[]{:S(2)}) collective-permute-start(bf16[4,128,512]{2,1,0:T(8,128)(2,1)S(1)} %fusion.3), channel_id=1, source_target_pairs={{0,24},{8,0},{16,8},{24,16},{1,25},{9,1},{17,9},{25,17},{2,26},{10... | collective-permute-start | bytes 1572872 | tf_op jit(solution)/shard_map/ppermute | solution.py:163
  274.4 9.3 %collective-permute-start.48 = (f32[4,128,128]{2,1,0:T(8,128)S(1)}, f32[4,128,128]{2,1,0:T(8,128)S(1)}, u32[]{:S(2)}, u32[]{:S(2)}) collective-permute-start(f32[4,128,128]{2,1,0:T(8,128)S(1)} %get-tuple-element.157), channel_id=1, source_target_pairs={{0,2},{2,0},{4,6},{6,4},{1,3},{3,1},{5,7},{7,5},{8,10},{10,8},{12,... | collective-permute-start | bytes 786440 | tf_op jit(solution)/shard_map/ppermute | solution.py:159
  275.4 11.7 %collective-permute-start.49 = (f32[4,128,128]{2,1,0:T(8,128)S(1)}, f32[4,128,128]{2,1,0:T(8,128)S(1)}, u32[]{:S(2)}, u32[]{:S(2)}) collective-permute-start(f32[4,128,128]{2,1,0:T(8,128)S(1)} %get-tuple-element.156), channel_id=1, source_target_pairs={{0,4},{2,6},{4,0},{6,2},{1,5},{3,7},{5,1},{7,3},{8,12},{10,14},{12... | collective-permute-start | bytes 786440 | tf_op jit(solution)/shard_map/ppermute | solution.py:159
  276.6 11.7 %collective-permute-start.50 = (f32[4,128,128]{2,1,0:T(8,128)S(1)}, f32[4,128,128]{2,1,0:T(8,128)S(1)}, u32[]{:S(2)}, u32[]{:S(2)}) collective-permute-start(f32[4,128,128]{2,1,0:T(8,128)S(1)} %get-tuple-element.155), channel_id=1, source_target_pairs={{0,6},{2,4},{4,2},{6,0},{1,7},{3,5},{5,3},{7,1},{8,14},{10,12},{12... | collective-permute-start | bytes 786440 | tf_op jit(solution)/shard_map/ppermute | solution.py:159
  (38 other events, 514.2 us)
Sparse Core Ops, SparseCore 0:
  67.9 13.7 all-gather.1

commit v3 on v0

--- a/solution.py
+++ b/solution.py
@@ -14,34 +14,88 @@
 GROUPS = 4
 
 
-def ladder_kernel(steps, count, first, half_ref, live_ref, pick_ref, tile_ref, *refs):
-    lefts = [refs[s * count:(s + 1) * count] for s in range(steps)]
-    rights = [refs[steps * count + 2 * s: steps * count + 2 * s + 2] for s in range(steps)]
-    rest = refs[steps * (count + 2):]
-    amp_ref = rest[0]
-    before_ref = None if first else rest[1]
-    out_ref, products, ready = rest[-3:]
-    step = pl.program_id(0)
-    group_rows = lefts[0][0].shape[1]
+def ladder_kernel(steps, count, half_ref, live_ref, pick_ref, tile_ref, *refs):
+    kinds = NTV + 1
+    lefts = [refs[s * kinds:(s + 1) * kinds] for s in range(steps)]
+    rest = refs[steps * kinds:]
+    whole, rest = rest[:2], rest[2:]
+    tiles = [rest[2 * n:2 * n + 2] for n in range((steps - 1) * NTV)]
+    amp_ref, out_ref, total_ref, products, ready, left_buf, right_buf, left_sem, right_sem = rest[
+        2 * (steps - 1) * NTV:
+    ]
+    d_tile, step = pl.program_id(0), pl.program_id(1)
+    rows = left_buf.shape[2]
+    group_rows = rows // GROUPS
     c_part = TV // GROUPS
     a_count = group_rows // c_part
     wide = 2 * GROUPS * TV
-    half_blocks = rights[0][0].shape[1] // wide
+    half_blocks = rows // wide
+    block_rows = TV // GROUPS * a_count
+    slot = d_tile % 2
+
+    def right_copies(i):
+        copies = []
+        for s in range(steps):
+            for side in range(2):
+                source = whole[side].at[tile_ref[i]] if s == 0 else tiles[(s - 1) * NTV + i][side].at[0]
+                place = (i % 2, s, side)
+                copies.append(pltpu.make_async_copy(source, right_buf.at[place], right_sem.at[place]))
+        return copies
+
+    @pl.when((d_tile == 0) & (step == 0))
+    def _():
+        for t in range(count):
+            for s in range(steps):
+                for k in range(NTV - 1):
+
+                    @pl.when(pick_ref[t] == k)
+                    def _():
+                        pltpu.make_async_copy(lefts[s][k], left_buf.at[t, s], left_sem.at[t, s]).start()
+
+                @pl.when(pick_ref[t] == NTV - 1)
+                def _():
+                    for part in range(2):
+                        place = pl.ds(part * (rows // 2), rows // 2)
+                        pltpu.make_async_copy(
+                            lefts[s][NTV - 1 + part], left_buf.at[t, s, place], left_sem.at[t, s]
+                        ).start()
+        for copy in right_copies(0):
+            copy.start()
+        for t in range(count):
+            for s in range(steps):
+                pltpu.make_async_copy(lefts[s][0], left_buf.at[t, s], left_sem.at[t, s]).wait()
+
+    for i in range(NTV):
+
+        @pl.when((d_tile == i) & (step == 0))
+        def _():
+            for copy in right_copies(i):
+                copy.wait()
+            if i + 1 < NTV:
+                for copy in right_copies(i + 1):
+                    copy.start()
 
     @pl.when(step < GROUPS)
     def _():
+        group = pl.ds(pl.multiple_of(step * group_rows, group_rows), group_rows)
         for half in range(2):
             start = (half_ref[0] if half == 0 else 1 - half_ref[0]) * half_blocks
             for p in range(half_blocks):
                 left = jnp.concatenate(
-                    [jnp.concatenate([part[t][0] for part in lefts], axis=1) for t in range(count)], axis=0
+                    [
+                        jnp.concatenate([left_buf[t, s, group, :] for s in range(steps)], axis=1)
+                        for t in range(count)
+                    ],
+                    axis=0,
                 )
                 right = jnp.concatenate(
                     [
                         jnp.concatenate(
                             [
-                                part[half][
-                                    0,
+                                right_buf[
+                                    slot,
+                                    s,
+                                    half,
                                     pl.ds(
                                         pl.multiple_of(
                                             p * wide + (g // GROUPS * GROUPS + (g + step) % GROUPS) * TV, TV
@@ -54,14 +108,13 @@
                             ],
                             axis=0,
                         )
-                        for part in rights
+                        for s in range(steps)
                     ],
                     axis=1,
                 )
-                total = lax.dot_general(
+                products[step, start + p] = lax.dot_general(
                     left, right, (((1,), (1,)), ((), ())), preferred_element_type=jnp.float32
-                )
-                products[step, start + p] = total.astype(jnp.bfloat16)
+                ).astype(jnp.bfloat16)
 
     @pl.when(step >= GROUPS)
     def _():
@@ -85,72 +138,60 @@
             ],
             axis=0,
         )
-        block_rows = TV // GROUPS * a_count
         terms = jnp.dot(
             ready[...].reshape(count * block_rows, TV * TV), amp, preferred_element_type=jnp.float32
         ).reshape(count, block_rows, amp.shape[1])
         for t in range(count):
-            term = terms[t] * live_ref[t].astype(jnp.float32)
-            if not first:
-                term = before_ref[t, 0] + term
-            out_ref[t, 0] = term.astype(out_ref.dtype)
-
-
-def ladder(half, live, pick, tile, lefts, rights, amp, before, part=None, kind=jnp.float32):
+            term = terms[t] * live_ref[d_tile, t].astype(jnp.float32)
+
+            @pl.when(d_tile == 0)
+            def _():
+                total_ref[t, k] = term
+
+            @pl.when((d_tile > 0) & (d_tile < NTV - 1))
+            def _():
+                total_ref[t, k] += term
+
+            @pl.when(d_tile == NTV - 1)
+            def _():
+                out_ref[t, k] = (total_ref[t, k] + term).astype(out_ref.dtype)
+
+
+def ladder(half, live, pick, tile, lefts, whole, tiles, amp, part, kind):
     steps = len(lefts)
-    rows, depth = lefts[0].shape[1:]
+    rows, depth = whole[0].shape[1:]
     columns = amp.shape[2]
     a_count = rows // TV
     b_blocks = TV // GROUPS
     wide = 2 * GROUPS * TV
-    count = NTV if part is None else NTV // 2
-    base = 0 if part is None else part * count
-    one = pl.Buffered(1)
-
-    def left_spec(t):
-        return pl.BlockSpec(
-            (1, rows // GROUPS, depth), lambda i, h, v, k, d: (k[t], jnp.minimum(i, GROUPS - 1), 0)
-        )
-
-    def right_spec(place):
-        return pl.BlockSpec(
-            (1, rows, depth),
-            lambda i, h, v, k, d: (d[0] if place is None else place, 0, 0),
-            pipeline_mode=one,
-        )
-
-    amp_spec = pl.BlockSpec((1, 2 * rows, columns), lambda i, h, v, k, d: (d[0], 0, 0), pipeline_mode=one)
-
-    def sum_spec(place):
-        return pl.BlockSpec(
-            (count, 1, b_blocks * a_count, columns),
-            lambda i, h, v, k, d: (place, jnp.maximum(i - GROUPS, 0), 0, 0),
-        )
-
-    first = before is None
-    flops = 2 * count * rows * 2 * rows * (steps * depth + columns)
-    operands = [half, live[base:base + count], pick[base:base + count], tile]
-    operands += [x for x in lefts for _ in range(count)] + [x for own, other, _ in rights for x in (own, other)] + [amp]
+    count = NTV // 2
+    base = part * count
+    result = (count, GROUPS, b_blocks * a_count, columns)
+    flops = 2 * NTV * count * rows * 2 * rows * (steps * depth + columns)
+    anywhere = pl.BlockSpec(memory_space=pl.ANY)
+    copied = [x for step in lefts for x in step] + [*whole] + [x for pair in tiles for x in pair]
     return pl.pallas_call(
-        functools.partial(ladder_kernel, steps, count, first),
+        functools.partial(ladder_kernel, steps, count),
         grid_spec=pltpu.PrefetchScalarGridSpec(
             num_scalar_prefetch=4,
-            grid=(2 * GROUPS,),
-            in_specs=[left_spec(t) for _ in lefts for t in range(count)]
-            + [right_spec(place) for _, _, place in rights for _ in range(2)]
-            + [amp_spec]
-            + [sum_spec(base // count)] * (not first),
-            out_specs=sum_spec(0),
+            grid=(NTV, 2 * GROUPS),
+            in_specs=[anywhere] * len(copied)
+            + [pl.BlockSpec((1, 2 * rows, columns), lambda i, j, h, v, k, d: (d[i], 0, 0))],
+            out_specs=pl.BlockSpec(result, lambda i, j, h, v, k, d: (0, 0, 0, 0)),
             scratch_shapes=[
+                pltpu.VMEM(result, jnp.float32),
                 pltpu.VMEM((GROUPS, 2 * rows // wide, count * rows // GROUPS, wide), jnp.bfloat16),
                 pltpu.VMEM((count, b_blocks, a_count, TV * TV), jnp.bfloat16),
+                pltpu.VMEM((count, steps, rows, depth), jnp.bfloat16),
+                pltpu.VMEM((2, steps, 2, rows, depth), jnp.bfloat16),
+                pltpu.SemaphoreType.DMA((count, steps)),
+                pltpu.SemaphoreType.DMA((2, steps, 2)),
             ],
         ),
-        out_shape=jax.ShapeDtypeStruct((count, GROUPS, b_blocks * a_count, columns), kind),
-        input_output_aliases={} if first or part is not None else {len(operands): 0},
+        out_shape=jax.ShapeDtypeStruct(result, kind),
         compiler_params=pltpu.CompilerParams(vmem_limit_bytes=40 * 2**20),
-        cost_estimate=pl.CostEstimate(flops=flops, bytes_accessed=20 * 2**20, transcendentals=0),
-    )(*operands, *([] if first else [before]))
+        cost_estimate=pl.CostEstimate(flops=flops, bytes_accessed=28 * 2**20, transcendentals=0),
+    )(half, live[:, base:base + count], pick[base:base + count], tile, *copied, amp)
 
 
 def partner(value, axis, size, flip):
@@ -172,8 +213,7 @@
 AMP = "amp"
 NEAR = {0: 0, 2: AMP, 4: 1, 6: 2, 8: 3}
 FAR = {1: 0, 3: AMP, 5: 1, 7: 2, 9: 3}
-STACK = {2: 0, 4: AMP, 6: 1, 8: 2, 10: 3}
-CONTRACT = {10: 0, 11: 2, 12: 1}
+FAR_DONE = {2: 0, 4: AMP, 6: 1, 8: 2, 10: 3}
 
 
 def on_square(chol, amps, listed):
@@ -212,25 +252,9 @@
         for key, value in zip(keys, lax.optimization_barrier([held[key] for key in keys])):
             held[key] = value
 
-    def contract(i, before, part=None, kind=jnp.float32):
-        sides = [(held["chol"], held["other", "chol"], None)]
-        sides += [(held["block", s, i], held["other", s, i], 0) for s in range(1, NTV)]
-        return ladder(
-            half,
-            lax.dynamic_index_in_dim(live, d_tiles[i], 1, keepdims=False),
-            pick,
-            d_tiles[i].reshape(1),
-            [held["lefts", s] for s in range(NTV)],
-            sides,
-            held["amp"],
-            before,
-            part,
-            kind,
-        )
-
     for slot in range(last + 1):
         hops = [0, 1] if slot == 0 else [slot + 1] if slot + 1 < last else []
-        near_block, far_block, stack_block = NEAR.get(slot), FAR.get(slot), STACK.get(slot)
+        near_block, far_block, done_block = NEAR.get(slot), FAR.get(slot), FAR_DONE.get(slot)
         now = waiting[slot]
         if slot >= 1:
             now.append(("block", *HOPS[slot - 1]))
@@ -241,8 +265,8 @@
             now.append(("left", near_block, 0))
         if far_block is not None:
             now += [("left", far_block, flip) for flip in range(3)]
-        if stack_block is not None:
-            now.append(("left", stack_block, 3))
+        if done_block is not None:
+            now += [("left", done_block, "first"), ("left", done_block, "second")]
         now += [("block", HOPS[u][0] - 1, (HOPS[u][1] + 1) % NTV) for u in hops]
         if slot == 1:
             now.append("chol")
@@ -254,7 +278,9 @@
             for flip in (1, 2):
                 held["left", near_block, flip] = partner(held["left", near_block, 0], "right", NTV, flip)
         if far_block is not None:
-            held["left", far_block, 3] = partner(held["left", far_block, 0], "right", NTV, 3)
+            middle = held["left", far_block, 0].shape[0] // 2
+            held["left", far_block, "first"] = partner(held["left", far_block, 1][:middle], "right", NTV, 2)
+            held["left", far_block, "second"] = partner(held["left", far_block, 2][middle:], "right", NTV, 1)
         if slot == 1:
             held["other", "chol"] = partner(held["chol"], "occ", 2, 1)
             waiting[slot + 1].append(("other", "chol"))
@@ -262,21 +288,26 @@
             unit = HOPS[slot - 1]
             held["other", *unit] = partner(held["block", *unit], "occ", 2, 1)
             waiting[slot + 1].append(("other", *unit))
-        if stack_block is not None:
-            every = [held["left", stack_block, flip] for flip in range(NTV)]
-            if stack_block == AMP:
-                held["amp"] = lax.all_gather(jnp.concatenate(every, axis=2), "occ", axis=1, tiled=True)
-                waiting[slot + 3].append("amp")
-            else:
-                held["lefts", stack_block] = jnp.stack(every)
-                waiting[slot + 1].append(("lefts", stack_block))
-        if slot in CONTRACT:
-            held["sum"] = contract(CONTRACT[slot], held.get("sum"))
-            waiting[slot + 1].append("sum")
-    partials = held["sum"]
-    early = contract(3, partials, 0, jnp.bfloat16)
+        if done_block == AMP:
+            far = jnp.concatenate([held["left", AMP, "first"], held["left", AMP, "second"]])
+            every = [held["left", AMP, flip] for flip in range(3)] + [far]
+            held["amp"] = lax.all_gather(jnp.concatenate(every, axis=2), "occ", axis=1, tiled=True)
+            waiting[slot + 3].append("amp")
+    d_order = jnp.stack(d_tiles)
+    contract = functools.partial(
+        ladder,
+        half,
+        live[:, d_order].T,
+        pick,
+        d_order,
+        [[held["left", s, part] for part in (0, 1, 2, "first", "second")] for s in range(NTV)],
+        (held["chol"], held["other", "chol"]),
+        [(held["block", s, i], held["other", s, i]) for s in range(1, NTV) for i in range(NTV)],
+        held["amp"],
+    )
+    early = contract(0, jnp.bfloat16)
     moved = [shift(early[t], "left", NTV, t + 1) for t in range(NTV // 2)]
-    late = contract(3, partials, 1)
+    late = contract(1, jnp.float32)
     moved += [
         shift(late[t].astype(jnp.bfloat16), "left", NTV, NTV // 2 + t + 1) for t in range(NTV // 2 - 1)
     ]

time: 308 us -> 319 us (1.036); the launches traced: 308 us -> 315 us
  local copies, waits for them, and re-layouts: 15.8 us -> 43.9 us
  waiting for transfers between devices: 156 us -> 129 us
  starting transfers between devices: 39.6 us -> 47.8 us
  other arithmetic: 8.64 us -> 3.41 us
  Pallas kernels: 73.5 us -> 76.9 us
    ppermute x31 -> x36, waiting for transfers between devices: 75.4 us -> 39 us  [partner(): return lax.ppermute(value, axis, [(i, i ^ flip) for i in range(size)])]
    ppermute x12, waiting for transfers between devices: 47 us -> 77.1 us  [on_square(): lax.ppermute(held['block', s - 1, (i + 1) % NTV], 'left', ring)]
    unnamed x66 -> x134, local copies, waits for them, and re-layouts: 6.64 us -> 32.3 us
    ppermute x3, waiting for transfers between devices: 33.9 us -> 13.4 us  [shift(): lax.ppermute(value, axis, [(i, (i + step) % size) for i in range(size)])]
    another operation x4 -> x1, other arithmetic: 6.61 us -> 0.08 us  [on_square(): d_order = jnp.stack(d_tiles)]
    ppermute x31 -> x36, starting transfers between devices: 19.6 us -> 26 us  [partner(): return lax.ppermute(value, axis, [(i, i ^ flip) for i in range(size)])]
    pallas_call x5 -> x2, Pallas kernels: 73.5 us -> 76.9 us  [ladder(): pl.pallas_call(functools.partial(ladder_kernel, steps, count), grid_spec=...]
  transfers between devices with their start and end apart: 47 -> 52, of which waited for: 23 -> 29; matrix products, arithmetic and copies ran while one was open for 4% -> 2% of each run, Pallas kernels for 20% -> 12%
where the time goes in v3:
time: 319 us; the launch traced here: 315 us
  waiting for transfers between devices  129 us (40%)
  Pallas kernels  76.9 us (24%)
  starting transfers between devices  47.8 us (15%)
  local copies, waits for them, and re-layouts  43.9 us (14%)
  between operations  13.9 us (4%)
  other arithmetic  3.41 us (1%)
    ppermute x12, waiting for transfers between devices, on_square(): lax.ppermute(held['block', s - 1, (i + 1) % NTV], 'left', ring)  77.1 us
    pallas_call x2, Pallas kernels, ladder(): pl.pallas_call(functools.partial(ladder_kernel, steps, count), grid_spec=...  76.9 us
    ppermute x36, waiting for transfers between devices, partner(): return lax.ppermute(value, axis, [(i, i ^ flip) for i in range(size)])  39 us
    unnamed x134, local copies, waits for them, and re-layouts  32.3 us
    ppermute x36, starting transfers between devices, partner(): return lax.ppermute(value, axis, [(i, i ^ flip) for i in range(size)])  26 us
    ppermute x12, starting transfers between devices, on_square(): lax.ppermute(held['block', s - 1, (i + 1) % NTV], 'left', ring)  18.4 us
    ppermute x3, waiting for transfers between devices, shift(): lax.ppermute(value, axis, [(i, (i + step) % size) for i in range(size)])  13.4 us
  transfers between devices with their start and end apart: 52, of which 29 were waited for; matrix products, arithmetic and copies ran while one was open for 2% of the time, Pallas kernels for 12%

profile of v3, /device:TPU:8, one launch (start us, length us, event | category | flops | bytes accessed | tf_op | source)
XLA Modules:
  0.0 315.4 jit_solution(15858407952420560594)
XLA Ops:
  6.5 1.8 constant_dynamic-slice_fusion
  8.7 1.9 collective-permute-start.1
  10.7 1.5 collective-permute-start.2
  12.2 11.1 %collective-permute-done.refs_26_ = bf16[1,512,512]{2,1,0:T(8,128)(2,1)S(1)} collective-permute-done((bf16[1,512,512]{2,1,0:T(8,128)(2,1)S(1)}, bf16[1,512,512]{2,1,0:T(8,128)(2,1)S(1)}, u32[]{:S(2)}, u32[]{:S(2)}) %collective-permute-start) | collective-permute-done | bytes 524320 | tf_op jit(solution)/shard_map/ppermute | solution.py:276
  23.8 2.6 collective-permute-start.5
  26.6 1.6 collective-permute-start.6
  28.8 10.2 %collective-permute-done.5.refs_24_ = bf16[1,512,512]{2,1,0:T(8,128)(2,1)S(1)} collective-permute-done((bf16[1,512,512]{2,1,0:T(8,128)(2,1)S(1)}, bf16[1,512,512]{2,1,0:T(8,128)(2,1)S(1)}, u32[]{:S(2)}, u32[]{:S(2)}) %collective-permute-start.5) | collective-permute-done | bytes 524320 | tf_op jit(solution)/shard_map/ppermute | solution.py:276
  39.0 1.7 collective-permute-start.9
  42.9 1.5 collective-permute-start.11
  44.4 2.5 collective-permute-start.13
  46.9 7.9 %collective-permute-done.9.refs_22_ = bf16[1,512,512]{2,1,0:T(8,128)(2,1)S(1)} collective-permute-done((bf16[1,512,512]{2,1,0:T(8,128)(2,1)S(1)}, bf16[1,512,512]{2,1,0:T(8,128)(2,1)S(1)}, u32[]{:S(2)}, u32[]{:S(2)}) %collective-permute-start.9) | collective-permute-done | bytes 524320 | tf_op jit(solution)/shard_map/ppermute | solution.py:276
  56.7 1.6 collective-permute-start.14
  58.3 1.6 collective-permute-start.15
  60.1 4.5 %collective-permute-done.13.refs_32_ = bf16[1,512,512]{2,1,0:T(8,128)(2,1)S(1)} collective-permute-done((bf16[1,512,512]{2,1,0:T(8,128)(2,1)S(1)}, bf16[1,512,512]{2,1,0:T(8,128)(2,1)S(1)}, u32[]{:S(2)}, u32[]{:S(2)}) %collective-permute-start.13) | collective-permute-done | bytes 524320 | tf_op jit(solution)/shard_map/ppermute | solution.py:276
  65.4 1.3 collective-permute-done.15
  66.8 1.7 maximum_maximum_fusion
  68.5 2.5 collective-permute-start.17
  71.0 1.5 collective-permute-start.18
  73.4 10.9 %collective-permute-done.17.refs_30_ = bf16[1,512,512]{2,1,0:T(8,128)(2,1)S(1)} collective-permute-done((bf16[1,512,512]{2,1,0:T(8,128)(2,1)S(1)}, bf16[1,512,512]{2,1,0:T(8,128)(2,1)S(1)}, u32[]{:S(2)}, u32[]{:S(2)}) %collective-permute-start.17) | collective-permute-done | bytes 524320 | tf_op jit(solution)/shard_map/ppermute | solution.py:276
  88.8 6.8 %collective-permute-done.21.refs_38_ = bf16[1,512,512]{2,1,0:T(8,128)(2,1)} collective-permute-done((bf16[1,512,512]{2,1,0:T(8,128)(2,1)S(1)}, bf16[1,512,512]{2,1,0:T(8,128)(2,1)}, u32[]{:S(2)}, u32[]{:S(2)}) %collective-permute-start.21) | collective-permute-done | bytes 524320 | tf_op jit(solution)/shard_map/ppermute | solution.py:276
  97.9 1.5 collective-permute-start.26
  99.5 1.9 collective-permute-start.29
  101.4 5.4 %collective-permute-done.25.refs_28_ = bf16[1,512,512]{2,1,0:T(8,128)(2,1)} collective-permute-done((bf16[1,512,512]{2,1,0:T(8,128)(2,1)S(1)}, bf16[1,512,512]{2,1,0:T(8,128)(2,1)}, u32[]{:S(2)}, u32[]{:S(2)}) %collective-permute-start.25) | collective-permute-done | bytes 524320 | tf_op jit(solution)/shard_map/ppermute | solution.py:276
  106.9 5.3 %collective-permute-done.26.refs_11_ = bf16[512,512]{1,0:T(8,128)(2,1)S(1)} collective-permute-done((bf16[512,512]{1,0:T(8,128)(2,1)S(1)}, bf16[512,512]{1,0:T(8,128)(2,1)S(1)}, u32[]{:S(2)}, u32[]{:S(2)}) %collective-permute-start.26) | collective-permute-done | bytes 524320 | tf_op jit(solution)/shard_map/ppermute | solution.py:198
  112.2 1.3 collective-permute-done.27.refs_12_
  116.0 1.3 copy.13
  118.7 3.7 %collective-permute-done.30.refs_13_ = bf16[256,512]{1,0:T(8,128)(2,1)S(1)} collective-permute-done((bf16[256,512]{1,0:T(8,128)(2,1)S(1)}, bf16[256,512]{1,0:T(8,128)(2,1)S(1)}, u32[]{:S(2)}, u32[]{:S(2)}) %collective-permute-start.30) | collective-permute-done | bytes 262176 | tf_op jit(solution)/shard_map/ppermute | solution.py:198
  127.2 1.6 collective-permute-start.37
  128.8 4.6 %collective-permute-done.33.refs_34_ = bf16[1,512,512]{2,1,0:T(8,128)(2,1)} collective-permute-done((bf16[1,512,512]{2,1,0:T(8,128)(2,1)}, bf16[1,512,512]{2,1,0:T(8,128)(2,1)}, u32[]{:S(2)}, u32[]{:S(2)}) %collective-permute-start.33) | collective-permute-done | bytes 524320 | tf_op jit(solution)/shard_map/ppermute | solution.py:276
  133.4 5.9 %collective-permute-done.34.refs_16_ = bf16[512,512]{1,0:T(8,128)(2,1)S(1)} collective-permute-done((bf16[512,512]{1,0:T(8,128)(2,1)S(1)}, bf16[512,512]{1,0:T(8,128)(2,1)S(1)}, u32[]{:S(2)}, u32[]{:S(2)}) %collective-permute-start.34) | collective-permute-done | bytes 524320 | tf_op jit(solution)/shard_map/ppermute | solution.py:198
  142.2 1.6 collective-permute-start.39
  143.8 1.6 collective-permute-start.41
  145.3 4.3 %collective-permute-done.38.refs_18_ = bf16[256,512]{1,0:T(8,128)(2,1)S(1)} collective-permute-done((bf16[256,512]{1,0:T(8,128)(2,1)S(1)}, bf16[256,512]{1,0:T(8,128)(2,1)S(1)}, u32[]{:S(2)}, u32[]{:S(2)}) %collective-permute-start.38) | collective-permute-done | bytes 262176 | tf_op jit(solution)/shard_map/ppermute | solution.py:198
  151.4 1.6 collective-permute-start.43
  152.9 6.8 %collective-permute-done.41.refs_40_ = bf16[1,512,512]{2,1,0:T(8,128)(2,1)} collective-permute-done((bf16[1,512,512]{2,1,0:T(8,128)(2,1)}, bf16[1,512,512]{2,1,0:T(8,128)(2,1)}, u32[]{:S(2)}, u32[]{:S(2)}) %collective-permute-start.41) | collective-permute-done | bytes 524320 | tf_op jit(solution)/shard_map/ppermute | solution.py:276
  161.1 8.8 %collective-permute-done.43.refs_44_ = bf16[1,512,512]{2,1,0:T(8,128)(2,1)} collective-permute-done((bf16[1,512,512]{2,1,0:T(8,128)(2,1)S(1)}, bf16[1,512,512]{2,1,0:T(8,128)(2,1)}, u32[]{:S(2)}, u32[]{:S(2)}) %collective-permute-start.43) | collective-permute-done | bytes 524320 | tf_op jit(solution)/shard_map/ppermute | solution.py:276
  170.1 1.9 collective-permute-done.44.refs_45_
  195.2 38.4 %shard_map.38 = bf16[2,4,128,512]{3,2,1,0:T(8,128)(2,1)} custom-call(s32[1]{0:T(128)} %bitcast.half_ref, s32[4,2]{1,0:T(4,128)S(1)} %get-tuple-element.143.live_ref, s32[2]{0:T(128)S(1)} %get-tuple-element.145.pick_ref, s32[4]{0:T(128)S(1)} %pad_add_fusion.tile_ref, bf16[512,512]{1,0:T(8,128)(2,1)S(1)} %bitcast.58, bf16[512,512]{1,0:T(8,128)(2,1)S(1)} %copy-done.2, ...), custom_call_target="tpu_custom_call" | custom-call | flops 21474836480 | bytes 29360128 | tf_op jit(solution)/shard_map/pallas_call | solution.py:173
  233.6 1.4 slice_bitcast_fusion.2
  235.1 1.6 collective-permute-start.45
  236.7 1.8 collective-permute-start.46
  238.5 38.5 %shard_map.37 = f32[2,4,128,512]{3,2,1,0:T(8,128)} custom-call(s32[1]{0:T(128)} %bitcast.half_ref, s32[4,2]{1,0:T(4,128)S(1)} %get-tuple-element.144.live_ref, s32[2]{0:T(128)S(1)} %get-tuple-element.146.pick_ref, s32[4]{0:T(128)S(1)} %pad_add_fusion.tile_ref, bf16[512,512]{1,0:T(8,128)(2,1)S(1)} %bitcast.59, bf16[512,512]{1,0:T(8,128)(2,1)S(1)} %copy-done.3, ...), custom_call_target="tpu_custom_call" | custom-call | flops 21474836480 | bytes 29360128 | tf_op jit(solution)/shard_map/pallas_call | solution.py:173
  278.4 13.4 %collective-permute-done.47 = bf16[4,128,512]{2,1,0:T(8,128)(2,1)S(1)} collective-permute-done((bf16[4,128,512]{2,1,0:T(8,128)(2,1)S(1)}, bf16[4,128,512]{2,1,0:T(8,128)(2,1)S(1)}, u32[]{:S(2)}, u32[]{:S(2)}) %collective-permute-start.47) | collective-permute-done | bytes 524320 | tf_op jit(solution)/shard_map/ppermute | solution.py:202
  291.8 1.5 fusion.2
  294.5 2.5 collective-permute-start.50
  297.0 5.7 %collective-permute-done.48 = f32[4,128,128]{2,1,0:T(8,128)S(1)} collective-permute-done((f32[4,128,128]{2,1,0:T(8,128)S(1)}, f32[4,128,128]{2,1,0:T(8,128)S(1)}, u32[]{:S(2)}, u32[]{:S(2)}) %collective-permute-start.48) | collective-permute-done | bytes 262176 | tf_op jit(solution)/shard_map/ppermute | solution.py:198
  302.7 3.5 %collective-permute-done.49 = f32[4,128,128]{2,1,0:T(8,128)S(1)} collective-permute-done((f32[4,128,128]{2,1,0:T(8,128)S(1)}, f32[4,128,128]{2,1,0:T(8,128)S(1)}, u32[]{:S(2)}, u32[]{:S(2)}) %collective-permute-start.49) | collective-permute-done | bytes 262176 | tf_op jit(solution)/shard_map/ppermute | solution.py:198
  306.9 1.6 copy.14
  (229 shorter events, 55.8 us)
Async XLA Ops:
  6.5 107.0 %all-gather.2.cloned.1.call-start = ((), (), s32[]{:S(2)}) async-start(), calls=%async_computation | async-start | bytes 6291456 | tf_op jit(solution)/shard_map/all_gather | solution.py:294
  8.7 14.6 %collective-permute-start = (bf16[1,512,512]{2,1,0:T(8,128)(2,1)S(1)}, bf16[1,512,512]{2,1,0:T(8,128)(2,1)S(1)}, u32[]{:S(2)}, u32[]{:S(2)}) collective-permute-start(bf16[1,512,512]{2,1,0:T(8,128)(2,1)S(1)} %get-tuple-element.69), channel_id=1, source_target_pairs={{0,16},{16,24},{24,8},{8,0},{1,17},{17,25},{25,9},{9,1},{2,18},{18... | collective-permute-start | bytes 1572872 | tf_op jit(solution)/shard_map/ppermute | solution.py:276
  8.7 14.6 %collective-permute-start.1 = (bf16[512,512]{1,0:T(8,128)(2,1)S(1)}, bf16[512,512]{1,0:T(8,128)(2,1)S(1)}, u32[]{:S(2)}, u32[]{:S(2)}) collective-permute-start(bf16[512,512]{1,0:T(8,128)(2,1)S(1)} %bitcast.56), channel_id=1, source_target_pairs={{0,2},{2,0},{4,6},{6,4},{1,3},{3,1},{5,7},{7,5},{8,10},{10,8},{12,... | collective-permute-start | bytes 1572872 | tf_op jit(solution)/shard_map/ppermute | solution.py:198
  10.7 13.1 %collective-permute-start.2 = (bf16[512,512]{1,0:T(8,128)(2,1)S(1)}, bf16[512,512]{1,0:T(8,128)(2,1)S(1)}, u32[]{:S(2)}, u32[]{:S(2)}) collective-permute-start(bf16[512,512]{1,0:T(8,128)(2,1)S(1)} %bitcast.57), channel_id=1, source_target_pairs={{0,4},{2,6},{4,0},{6,2},{1,5},{3,7},{5,1},{7,3},{8,12},{10,14},{12... | collective-permute-start | bytes 1572872 | tf_op jit(solution)/shard_map/ppermute | solution.py:198
  23.8 18.5 %collective-permute-start.3 = (bf16[4,512,512]{2,1,0:T(8,128)(2,1)S(1)}, bf16[4,512,512]{2,1,0:T(8,128)(2,1)S(1)}, u32[]{:S(2)}, u32[]{:S(2)}) collective-permute-start(bf16[4,512,512]{2,1,0:T(8,128)(2,1)S(1)} %copy-done.58), channel_id=1, source_target_pairs={{0,1},{1,0},{2,3},{3,2},{4,5},{5,4},{6,7},{7,6},{8,9},{9,8},{10,11... | collective-permute-start | bytes 6291464 | tf_op jit(solution)/shard_map/ppermute | solution.py:198
  23.8 15.2 %collective-permute-start.5 = (bf16[1,512,512]{2,1,0:T(8,128)(2,1)S(1)}, bf16[1,512,512]{2,1,0:T(8,128)(2,1)S(1)}, u32[]{:S(2)}, u32[]{:S(2)}) collective-permute-start(bf16[1,512,512]{2,1,0:T(8,128)(2,1)S(1)} %get-tuple-element.76), channel_id=1, source_target_pairs={{0,16},{16,24},{24,8},{8,0},{1,17},{17,25},{25,9},{9,1},{2,18},{18... | collective-permute-start | bytes 1572872 | tf_op jit(solution)/shard_map/ppermute | solution.py:276
  26.4 15.0 %collective-permute-start.4 = (bf16[1,512,512]{2,1,0:T(8,128)(2,1)S(1)}, bf16[1,512,512]{2,1,0:T(8,128)(2,1)S(1)}, u32[]{:S(2)}, u32[]{:S(2)}) collective-permute-start(bf16[1,512,512]{2,1,0:T(8,128)(2,1)S(1)} %collective-permute-done.refs_26_), channel_id=1, source_target_pairs={{0,1},{1,0},{2,3},{3,2},{4,5},{5,4},{6,7},{7,6},{8,9},{9,8},{10,11... | collective-permute-start | bytes 1572872 | tf_op jit(solution)/shard_map/ppermute | solution.py:198
  26.6 14.1 %collective-permute-start.6 = (bf16[256,512]{1,0:T(8,128)(2,1)S(1)}, bf16[256,512]{1,0:T(8,128)(2,1)S(1)}, u32[]{:S(2)}, u32[]{:S(2)}) collective-permute-start(bf16[256,512]{1,0:T(8,128)(2,1)S(1)} %slice.69), channel_id=1, source_target_pairs={{0,4},{2,6},{4,0},{6,2},{1,5},{3,7},{5,1},{7,3},{8,12},{10,14},{12... | collective-permute-start | bytes 786440 | tf_op jit(solution)/shard_map/ppermute | solution.py:198
  28.2 12.5 %collective-permute-start.7 = (bf16[256,512]{1,0:T(8,128)(2,1)S(1)}, bf16[256,512]{1,0:T(8,128)(2,1)S(1)}, u32[]{:S(2)}, u32[]{:S(2)}) collective-permute-start(bf16[256,512]{1,0:T(8,128)(2,1)S(1)} %slice.70), channel_id=1, source_target_pairs={{0,2},{2,0},{4,6},{6,4},{1,3},{3,1},{5,7},{7,5},{8,10},{10,8},{12,... | collective-permute-start | bytes 786440 | tf_op jit(solution)/shard_map/ppermute | solution.py:198
  39.0 15.7 %collective-permute-start.9 = (bf16[1,512,512]{2,1,0:T(8,128)(2,1)S(1)}, bf16[1,512,512]{2,1,0:T(8,128)(2,1)S(1)}, u32[]{:S(2)}, u32[]{:S(2)}) collective-permute-start(bf16[1,512,512]{2,1,0:T(8,128)(2,1)S(1)} %get-tuple-element.80), channel_id=1, source_target_pairs={{0,16},{16,24},{24,8},{8,0},{1,17},{17,25},{25,9},{9,1},{2,18},{18... | collective-permute-start | bytes 1572872 | tf_op jit(solution)/shard_map/ppermute | solution.py:276
  42.3 13.3 %collective-permute-start.10 = (bf16[4,512,128]{2,1,0:T(8,128)(2,1)S(1)}, bf16[4,512,128]{2,1,0:T(8,128)(2,1)S(1)}, u32[]{:S(2)}, u32[]{:S(2)}) collective-permute-start(bf16[4,512,128]{2,1,0:T(8,128)(2,1)S(1)} %bitcast.76), channel_id=1, source_target_pairs={{0,2},{2,0},{4,6},{6,4},{1,3},{3,1},{5,7},{7,5},{8,10},{10,8},{12,... | collective-permute-start | bytes 1572872 | tf_op jit(solution)/shard_map/ppermute | solution.py:198
  42.9 12.9 %collective-permute-start.11 = (bf16[4,512,128]{2,1,0:T(8,128)(2,1)S(1)}, bf16[4,512,128]{2,1,0:T(8,128)(2,1)S(1)}, u32[]{:S(2)}, u32[]{:S(2)}) collective-permute-start(bf16[4,512,128]{2,1,0:T(8,128)(2,1)S(1)} %bitcast.77), channel_id=1, source_target_pairs={{0,4},{2,6},{4,0},{6,2},{1,5},{3,7},{5,1},{7,3},{8,12},{10,14},{12... | collective-permute-start | bytes 1572872 | tf_op jit(solution)/shard_map/ppermute | solution.py:198
  44.4 11.4 %collective-permute-start.8 = (bf16[1,512,512]{2,1,0:T(8,128)(2,1)S(1)}, bf16[1,512,512]{2,1,0:T(8,128)(2,1)S(1)}, u32[]{:S(2)}, u32[]{:S(2)}) collective-permute-start(bf16[1,512,512]{2,1,0:T(8,128)(2,1)S(1)} %collective-permute-done.5.refs_24_), channel_id=1, source_target_pairs={{0,1},{1,0},{2,3},{3,2},{4,5},{5,4},{6,7},{7,6},{8,9},{9,8},{10,11... | collective-permute-start | bytes 1572872 | tf_op jit(solution)/shard_map/ppermute | solution.py:198
  44.4 20.3 %collective-permute-start.13 = (bf16[1,512,512]{2,1,0:T(8,128)(2,1)S(1)}, bf16[1,512,512]{2,1,0:T(8,128)(2,1)S(1)}, u32[]{:S(2)}, u32[]{:S(2)}) collective-permute-start(bf16[1,512,512]{2,1,0:T(8,128)(2,1)S(1)} %collective-permute-done.refs_26_), channel_id=1, source_target_pairs={{0,16},{16,24},{24,8},{8,0},{1,17},{17,25},{25,9},{9,1},{2,18},{18... | collective-permute-start | bytes 1572872 | tf_op jit(solution)/shard_map/ppermute | solution.py:276
  56.6 10.1 %collective-permute-start.12 = (bf16[1,512,512]{2,1,0:T(8,128)(2,1)S(1)}, bf16[1,512,512]{2,1,0:T(8,128)(2,1)S(1)}, u32[]{:S(2)}, u32[]{:S(2)}) collective-permute-start(bf16[1,512,512]{2,1,0:T(8,128)(2,1)S(1)} %collective-permute-done.9.refs_22_), channel_id=1, source_target_pairs={{0,1},{1,0},{2,3},{3,2},{4,5},{5,4},{6,7},{7,6},{8,9},{9,8},{10,11... | collective-permute-start | bytes 1572872 | tf_op jit(solution)/shard_map/ppermute | solution.py:198
  56.7 8.8 %collective-permute-start.14 = (bf16[2,512,128]{2,1,0:T(8,128)(2,1)S(1)}, bf16[2,512,128]{2,1,0:T(8,128)(2,1)S(1)}, u32[]{:S(2)}, u32[]{:S(2)}) collective-permute-start(bf16[2,512,128]{2,1,0:T(8,128)(2,1)S(1)} %slice.71), channel_id=1, source_target_pairs={{0,4},{2,6},{4,0},{6,2},{1,5},{3,7},{5,1},{7,3},{8,12},{10,14},{12... | collective-permute-start | bytes 786440 | tf_op jit(solution)/shard_map/ppermute | solution.py:198
  58.3 8.5 %collective-permute-start.15 = (bf16[2,512,128]{2,1,0:T(8,128)(2,1)S(1)}, bf16[2,512,128]{2,1,0:T(8,128)(2,1)S(1)}, u32[]{:S(2)}, u32[]{:S(2)}) collective-permute-start(bf16[2,512,128]{2,1,0:T(8,128)(2,1)S(1)} %slice.72), channel_id=1, source_target_pairs={{0,2},{2,0},{4,6},{6,4},{1,3},{3,1},{5,7},{7,5},{8,10},{10,8},{12,... | collective-permute-start | bytes 786440 | tf_op jit(solution)/shard_map/ppermute | solution.py:198
  68.5 15.8 %collective-permute-start.17 = (bf16[1,512,512]{2,1,0:T(8,128)(2,1)S(1)}, bf16[1,512,512]{2,1,0:T(8,128)(2,1)S(1)}, u32[]{:S(2)}, u32[]{:S(2)}) collective-permute-start(bf16[1,512,512]{2,1,0:T(8,128)(2,1)S(1)} %collective-permute-done.5.refs_24_), channel_id=1, source_target_pairs={{0,16},{16,24},{24,8},{8,0},{1,17},{17,25},{25,9},{9,1},{2,18},{18... | collective-permute-start | bytes 1572872 | tf_op jit(solution)/shard_map/ppermute | solution.py:276
  71.0 13.3 %collective-permute-start.16 = (bf16[1,512,512]{2,1,0:T(8,128)(2,1)S(1)}, bf16[1,512,512]{2,1,0:T(8,128)(2,1)S(1)}, u32[]{:S(2)}, u32[]{:S(2)}) collective-permute-start(bf16[1,512,512]{2,1,0:T(8,128)(2,1)S(1)} %collective-permute-done.13.refs_32_), channel_id=1, source_target_pairs={{0,1},{1,0},{2,3},{3,2},{4,5},{5,4},{6,7},{7,6},{8,9},{9,8},{10,11... | collective-permute-start | bytes 1572872 | tf_op jit(solution)/shard_map/ppermute | solution.py:198
  71.0 14.3 %collective-permute-start.18 = (bf16[512,512]{1,0:T(8,128)(2,1)S(1)}, bf16[512,512]{1,0:T(8,128)(2,1)S(1)}, u32[]{:S(2)}, u32[]{:S(2)}) collective-permute-start(bf16[512,512]{1,0:T(8,128)(2,1)S(1)} %bitcast.61), channel_id=1, source_target_pairs={{0,2},{2,0},{4,6},{6,4},{1,3},{3,1},{5,7},{7,5},{8,10},{10,8},{12,... | collective-permute-start | bytes 1572872 | tf_op jit(solution)/shard_map/ppermute | solution.py:198
  72.5 14.1 %collective-permute-start.19 = (bf16[512,512]{1,0:T(8,128)(2,1)S(1)}, bf16[512,512]{1,0:T(8,128)(2,1)S(1)}, u32[]{:S(2)}, u32[]{:S(2)}) collective-permute-start(bf16[512,512]{1,0:T(8,128)(2,1)S(1)} %bitcast.62), channel_id=1, source_target_pairs={{0,4},{2,6},{4,0},{6,2},{1,5},{3,7},{5,1},{7,3},{8,12},{10,14},{12... | collective-permute-start | bytes 1572872 | tf_op jit(solution)/shard_map/ppermute | solution.py:198
  73.0 22.6 %collective-permute-start.21 = (bf16[1,512,512]{2,1,0:T(8,128)(2,1)S(1)}, bf16[1,512,512]{2,1,0:T(8,128)(2,1)}, u32[]{:S(2)}, u32[]{:S(2)}) collective-permute-start(bf16[1,512,512]{2,1,0:T(8,128)(2,1)S(1)} %collective-permute-done.13.refs_32_), channel_id=1, source_target_pairs={{0,16},{16,24},{24,8},{8,0},{1,17},{17,25},{25,9},{9,1},{2,18},{18... | collective-permute-start | bytes 1572872 | tf_op jit(solution)/shard_map/ppermute | solution.py:276
  86.6 10.5 %collective-permute-start.20 = (bf16[1,512,512]{2,1,0:T(8,128)(2,1)S(1)}, bf16[1,512,512]{2,1,0:T(8,128)(2,1)S(1)}, u32[]{:S(2)}, u32[]{:S(2)}) collective-permute-start(bf16[1,512,512]{2,1,0:T(8,128)(2,1)S(1)} %collective-permute-done.17.refs_30_), channel_id=1, source_target_pairs={{0,1},{1,0},{2,3},{3,2},{4,5},{5,4},{6,7},{7,6},{8,9},{9,8},{10,11... | collective-permute-start | bytes 1572872 | tf_op jit(solution)/shard_map/ppermute | solution.py:198
  86.6 9.0 %collective-permute-start.22 = (bf16[256,512]{1,0:T(8,128)(2,1)S(1)}, bf16[256,512]{1,0:T(8,128)(2,1)S(1)}, u32[]{:S(2)}, u32[]{:S(2)}) collective-permute-start(bf16[256,512]{1,0:T(8,128)(2,1)S(1)} %slice.73), channel_id=1, source_target_pairs={{0,4},{2,6},{4,0},{6,2},{1,5},{3,7},{5,1},{7,3},{8,12},{10,14},{12... | collective-permute-start | bytes 786440 | tf_op jit(solution)/shard_map/ppermute | solution.py:198
  87.2 9.2 %collective-permute-start.23 = (bf16[256,512]{1,0:T(8,128)(2,1)S(1)}, bf16[256,512]{1,0:T(8,128)(2,1)S(1)}, u32[]{:S(2)}, u32[]{:S(2)}) collective-permute-start(bf16[256,512]{1,0:T(8,128)(2,1)S(1)} %slice.74), channel_id=1, source_target_pairs={{0,2},{2,0},{4,6},{6,4},{1,3},{3,1},{5,7},{7,5},{8,10},{10,8},{12,... | collective-permute-start | bytes 786440 | tf_op jit(solution)/shard_map/ppermute | solution.py:198
  88.1 18.8 %collective-permute-start.25 = (bf16[1,512,512]{2,1,0:T(8,128)(2,1)S(1)}, bf16[1,512,512]{2,1,0:T(8,128)(2,1)}, u32[]{:S(2)}, u32[]{:S(2)}) collective-permute-start(bf16[1,512,512]{2,1,0:T(8,128)(2,1)S(1)} %copy-done.60), channel_id=1, source_target_pairs={{0,16},{16,24},{24,8},{8,0},{1,17},{17,25},{25,9},{9,1},{2,18},{18... | collective-permute-start | bytes 1572872 | tf_op jit(solution)/shard_map/ppermute | solution.py:276
  97.9 9.0 %collective-permute-start.24 = (bf16[1,512,512]{2,1,0:T(8,128)(2,1)}, bf16[1,512,512]{2,1,0:T(8,128)(2,1)S(1)}, u32[]{:S(2)}, u32[]{:S(2)}) collective-permute-start(bf16[1,512,512]{2,1,0:T(8,128)(2,1)} %collective-permute-done.21.refs_38_), channel_id=1, source_target_pairs={{0,1},{1,0},{2,3},{3,2},{4,5},{5,4},{6,7},{7,6},{8,9},{9,8},{10,11... | collective-permute-start | bytes 1572872 | tf_op jit(solution)/shard_map/ppermute | solution.py:198
  97.9 14.3 %collective-permute-start.26 = (bf16[512,512]{1,0:T(8,128)(2,1)S(1)}, bf16[512,512]{1,0:T(8,128)(2,1)S(1)}, u32[]{:S(2)}, u32[]{:S(2)}) collective-permute-start(bf16[512,512]{1,0:T(8,128)(2,1)S(1)} %bitcast.66), channel_id=1, source_target_pairs={{0,2},{2,0},{4,6},{6,4},{1,3},{3,1},{5,7},{7,5},{8,10},{10,8},{12,... | collective-permute-start | bytes 1572872 | tf_op jit(solution)/shard_map/ppermute | solution.py:198
  99.4 14.2 %collective-permute-start.27 = (bf16[512,512]{1,0:T(8,128)(2,1)S(1)}, bf16[512,512]{1,0:T(8,128)(2,1)}, u32[]{:S(2)}, u32[]{:S(2)}) collective-permute-start(bf16[512,512]{1,0:T(8,128)(2,1)S(1)} %bitcast.67), channel_id=1, source_target_pairs={{0,4},{2,6},{4,0},{6,2},{1,5},{3,7},{5,1},{7,3},{8,12},{10,14},{12... | collective-permute-start | bytes 1572872 | tf_op jit(solution)/shard_map/ppermute | solution.py:198
  99.5 19.1 %collective-permute-start.29 = (bf16[1,512,512]{2,1,0:T(8,128)(2,1)S(1)}, bf16[1,512,512]{2,1,0:T(8,128)(2,1)}, u32[]{:S(2)}, u32[]{:S(2)}) collective-permute-start(bf16[1,512,512]{2,1,0:T(8,128)(2,1)S(1)} %collective-permute-done.9.refs_22_), channel_id=1, source_target_pairs={{0,16},{16,24},{24,8},{8,0},{1,17},{17,25},{25,9},{9,1},{2,18},{18... | collective-permute-start | bytes 1572872 | tf_op jit(solution)/shard_map/ppermute | solution.py:276
  113.5 10.6 %collective-permute-start.28 = (bf16[1,512,512]{2,1,0:T(8,128)(2,1)}, bf16[1,512,512]{2,1,0:T(8,128)(2,1)S(1)}, u32[]{:S(2)}, u32[]{:S(2)}) collective-permute-start(bf16[1,512,512]{2,1,0:T(8,128)(2,1)} %collective-permute-done.25.refs_28_), channel_id=1, source_target_pairs={{0,1},{1,0},{2,3},{3,2},{4,5},{5,4},{6,7},{7,6},{8,9},{9,8},{10,11... | collective-permute-start | bytes 1572872 | tf_op jit(solution)/shard_map/ppermute | solution.py:198
  113.5 8.8 %collective-permute-start.30 = (bf16[256,512]{1,0:T(8,128)(2,1)S(1)}, bf16[256,512]{1,0:T(8,128)(2,1)S(1)}, u32[]{:S(2)}, u32[]{:S(2)}) collective-permute-start(bf16[256,512]{1,0:T(8,128)(2,1)S(1)} %slice.75), channel_id=1, source_target_pairs={{0,4},{2,6},{4,0},{6,2},{1,5},{3,7},{5,1},{7,3},{8,12},{10,14},{12... | collective-permute-start | bytes 786440 | tf_op jit(solution)/shard_map/ppermute | solution.py:198
  114.9 8.5 %collective-permute-start.31 = (bf16[256,512]{1,0:T(8,128)(2,1)S(1)}, bf16[256,512]{1,0:T(8,128)(2,1)S(1)}, u32[]{:S(2)}, u32[]{:S(2)}) collective-permute-start(bf16[256,512]{1,0:T(8,128)(2,1)S(1)} %slice.76), channel_id=1, source_target_pairs={{0,2},{2,0},{4,6},{6,4},{1,3},{3,1},{5,7},{7,5},{8,10},{10,8},{12,... | collective-permute-start | bytes 786440 | tf_op jit(solution)/shard_map/ppermute | solution.py:198
  117.4 16.1 %collective-permute-start.33 = (bf16[1,512,512]{2,1,0:T(8,128)(2,1)}, bf16[1,512,512]{2,1,0:T(8,128)(2,1)}, u32[]{:S(2)}, u32[]{:S(2)}) collective-permute-start(bf16[1,512,512]{2,1,0:T(8,128)(2,1)} %collective-permute-done.25.refs_28_), channel_id=1, source_target_pairs={{0,16},{16,24},{24,8},{8,0},{1,17},{17,25},{25,9},{9,1},{2,18},{18... | collective-permute-start | bytes 1572872 | tf_op jit(solution)/shard_map/ppermute | solution.py:276
  125.0 14.3 %collective-permute-start.34 = (bf16[512,512]{1,0:T(8,128)(2,1)S(1)}, bf16[512,512]{1,0:T(8,128)(2,1)S(1)}, u32[]{:S(2)}, u32[]{:S(2)}) collective-permute-start(bf16[512,512]{1,0:T(8,128)(2,1)S(1)} %bitcast.70), channel_id=1, source_target_pairs={{0,2},{2,0},{4,6},{6,4},{1,3},{3,1},{5,7},{7,5},{8,10},{10,8},{12,... | collective-permute-start | bytes 1572872 | tf_op jit(solution)/shard_map/ppermute | solution.py:198
  126.1 14.1 %collective-permute-start.35 = (bf16[512,512]{1,0:T(8,128)(2,1)S(1)}, bf16[512,512]{1,0:T(8,128)(2,1)S(1)}, u32[]{:S(2)}, u32[]{:S(2)}) collective-permute-start(bf16[512,512]{1,0:T(8,128)(2,1)S(1)} %bitcast.71), channel_id=1, source_target_pairs={{0,4},{2,6},{4,0},{6,2},{1,5},{3,7},{5,1},{7,3},{8,12},{10,14},{12... | collective-permute-start | bytes 1572872 | tf_op jit(solution)/shard_map/ppermute | solution.py:198
  127.2 18.1 %collective-permute-start.37 = (bf16[1,512,512]{2,1,0:T(8,128)(2,1)}, bf16[1,512,512]{2,1,0:T(8,128)(2,1)}, u32[]{:S(2)}, u32[]{:S(2)}) collective-permute-start(bf16[1,512,512]{2,1,0:T(8,128)(2,1)} %collective-permute-done.29.refs_36_), channel_id=1, source_target_pairs={{0,16},{16,24},{24,8},{8,0},{1,17},{17,25},{25,9},{9,1},{2,18},{18... | collective-permute-start | bytes 1572872 | tf_op jit(solution)/shard_map/ppermute | solution.py:276
  140.1 11.2 %collective-permute-start.36 = (bf16[1,512,512]{2,1,0:T(8,128)(2,1)}, bf16[1,512,512]{2,1,0:T(8,128)(2,1)}, u32[]{:S(2)}, u32[]{:S(2)}) collective-permute-start(bf16[1,512,512]{2,1,0:T(8,128)(2,1)} %collective-permute-done.33.refs_34_), channel_id=1, source_target_pairs={{0,1},{1,0},{2,3},{3,2},{4,5},{5,4},{6,7},{7,6},{8,9},{9,8},{10,11... | collective-permute-start | bytes 1572872 | tf_op jit(solution)/shard_map/ppermute | solution.py:198
  141.0 8.7 %collective-permute-start.38 = (bf16[256,512]{1,0:T(8,128)(2,1)S(1)}, bf16[256,512]{1,0:T(8,128)(2,1)S(1)}, u32[]{:S(2)}, u32[]{:S(2)}) collective-permute-start(bf16[256,512]{1,0:T(8,128)(2,1)S(1)} %slice.77), channel_id=1, source_target_pairs={{0,4},{2,6},{4,0},{6,2},{1,5},{3,7},{5,1},{7,3},{8,12},{10,14},{12... | collective-permute-start | bytes 786440 | tf_op jit(solution)/shard_map/ppermute | solution.py:198
  143.8 16.0 %collective-permute-start.41 = (bf16[1,512,512]{2,1,0:T(8,128)(2,1)}, bf16[1,512,512]{2,1,0:T(8,128)(2,1)}, u32[]{:S(2)}, u32[]{:S(2)}) collective-permute-start(bf16[1,512,512]{2,1,0:T(8,128)(2,1)} %collective-permute-done.33.refs_34_), channel_id=1, source_target_pairs={{0,16},{16,24},{24,8},{8,0},{1,17},{17,25},{25,9},{9,1},{2,18},{18... | collective-permute-start | bytes 1572872 | tf_op jit(solution)/shard_map/ppermute | solution.py:276
  151.4 18.6 %collective-permute-start.43 = (bf16[1,512,512]{2,1,0:T(8,128)(2,1)S(1)}, bf16[1,512,512]{2,1,0:T(8,128)(2,1)}, u32[]{:S(2)}, u32[]{:S(2)}) collective-permute-start(bf16[1,512,512]{2,1,0:T(8,128)(2,1)S(1)} %collective-permute-done.17.refs_30_), channel_id=1, source_target_pairs={{0,16},{16,24},{24,8},{8,0},{1,17},{17,25},{25,9},{9,1},{2,18},{18... | collective-permute-start | bytes 1572872 | tf_op jit(solution)/shard_map/ppermute | solution.py:276
  159.8 10.1 %collective-permute-start.42 = (bf16[1,512,512]{2,1,0:T(8,128)(2,1)}, bf16[1,512,512]{2,1,0:T(8,128)(2,1)}, u32[]{:S(2)}, u32[]{:S(2)}) collective-permute-start(bf16[1,512,512]{2,1,0:T(8,128)(2,1)} %collective-permute-done.41.refs_40_), channel_id=1, source_target_pairs={{0,1},{1,0},{2,3},{3,2},{4,5},{5,4},{6,7},{7,6},{8,9},{9,8},{10,11... | collective-permute-start | bytes 1572872 | tf_op jit(solution)/shard_map/ppermute | solution.py:198
  235.1 43.3 %collective-permute-start.45 = (bf16[4,128,512]{2,1,0:T(8,128)(2,1)S(1)}, bf16[4,128,512]{2,1,0:T(8,128)(2,1)S(1)}, u32[]{:S(2)}, u32[]{:S(2)}) collective-permute-start(bf16[4,128,512]{2,1,0:T(8,128)(2,1)S(1)} %get-tuple-element.141), channel_id=1, source_target_pairs={{0,8},{8,16},{16,24},{24,0},{1,9},{9,17},{17,25},{25,1},{2,10},{10... | collective-permute-start | bytes 1572872 | tf_op jit(solution)/shard_map/ppermute | solution.py:202
  236.7 41.7 %collective-permute-start.46 = (bf16[4,128,512]{2,1,0:T(8,128)(2,1)S(1)}, bf16[4,128,512]{2,1,0:T(8,128)(2,1)S(1)}, u32[]{:S(2)}, u32[]{:S(2)}) collective-permute-start(bf16[4,128,512]{2,1,0:T(8,128)(2,1)S(1)} %get-tuple-element.142), channel_id=1, source_target_pairs={{0,16},{8,24},{16,0},{24,8},{1,17},{9,25},{17,1},{25,9},{2,18},{10... | collective-permute-start | bytes 1572872 | tf_op jit(solution)/shard_map/ppermute | solution.py:202
  278.3 13.5 %collective-permute-start.47 = (bf16[4,128,512]{2,1,0:T(8,128)(2,1)S(1)}, bf16[4,128,512]{2,1,0:T(8,128)(2,1)S(1)}, u32[]{:S(2)}, u32[]{:S(2)}) collective-permute-start(bf16[4,128,512]{2,1,0:T(8,128)(2,1)S(1)} %fusion.3), channel_id=1, source_target_pairs={{0,24},{8,0},{16,8},{24,16},{1,25},{9,1},{17,9},{25,17},{2,26},{10... | collective-permute-start | bytes 1572872 | tf_op jit(solution)/shard_map/ppermute | solution.py:202
  293.4 9.3 %collective-permute-start.48 = (f32[4,128,128]{2,1,0:T(8,128)S(1)}, f32[4,128,128]{2,1,0:T(8,128)S(1)}, u32[]{:S(2)}, u32[]{:S(2)}) collective-permute-start(f32[4,128,128]{2,1,0:T(8,128)S(1)} %get-tuple-element.140), channel_id=1, source_target_pairs={{0,2},{2,0},{4,6},{6,4},{1,3},{3,1},{5,7},{7,5},{8,10},{10,8},{12,... | collective-permute-start | bytes 786440 | tf_op jit(solution)/shard_map/ppermute | solution.py:198
  293.9 12.2 %collective-permute-start.49 = (f32[4,128,128]{2,1,0:T(8,128)S(1)}, f32[4,128,128]{2,1,0:T(8,128)S(1)}, u32[]{:S(2)}, u32[]{:S(2)}) collective-permute-start(f32[4,128,128]{2,1,0:T(8,128)S(1)} %get-tuple-element.139), channel_id=1, source_target_pairs={{0,4},{2,6},{4,0},{6,2},{1,5},{3,7},{5,1},{7,3},{8,12},{10,14},{12... | collective-permute-start | bytes 786440 | tf_op jit(solution)/shard_map/ppermute | solution.py:198
  294.5 11.7 %collective-permute-start.50 = (f32[4,128,128]{2,1,0:T(8,128)S(1)}, f32[4,128,128]{2,1,0:T(8,128)S(1)}, u32[]{:S(2)}, u32[]{:S(2)}) collective-permute-start(f32[4,128,128]{2,1,0:T(8,128)S(1)} %get-tuple-element.138), channel_id=1, source_target_pairs={{0,6},{2,4},{4,2},{6,0},{1,7},{3,5},{5,3},{7,1},{8,14},{10,12},{12... | collective-permute-start | bytes 786440 | tf_op jit(solution)/shard_map/ppermute | solution.py:198
  (71 other events, 938.9 us)
Sparse Core Ops, SparseCore 0:
  68.6 13.1 all-gather.1

commit v4 on v3

--- a/solution.py
+++ b/solution.py
@@ -24,7 +24,8 @@
         2 * (steps - 1) * NTV:
     ]
     d_tile, step = pl.program_id(0), pl.program_id(1)
-    rows = left_buf.shape[2]
+    rows = left_buf.shape[0] // count
+    depth = left_buf.shape[1] // steps
     group_rows = rows // GROUPS
     c_part = TV // GROUPS
     a_count = group_rows // c_part
@@ -38,9 +39,12 @@
         for s in range(steps):
             for side in range(2):
                 source = whole[side].at[tile_ref[i]] if s == 0 else tiles[(s - 1) * NTV + i][side].at[0]
-                place = (i % 2, s, side)
-                copies.append(pltpu.make_async_copy(source, right_buf.at[place], right_sem.at[place]))
+                target = right_buf.at[i % 2, side, :, pl.ds(s * depth, depth)]
+                copies.append(pltpu.make_async_copy(source, target, right_sem.at[i % 2, s, side]))
         return copies
+
+    def left_place(t, s, first, size):
+        return left_buf.at[pl.ds(t * rows + first, size), pl.ds(s * depth, depth)]
 
     @pl.when((d_tile == 0) & (step == 0))
     def _():
@@ -50,20 +54,18 @@
 
                     @pl.when(pick_ref[t] == k)
                     def _():
-                        pltpu.make_async_copy(lefts[s][k], left_buf.at[t, s], left_sem.at[t, s]).start()
+                        pltpu.make_async_copy(lefts[s][k], left_place(t, s, 0, rows), left_sem.at[t, s]).start()
 
                 @pl.when(pick_ref[t] == NTV - 1)
                 def _():
                     for part in range(2):
-                        place = pl.ds(part * (rows // 2), rows // 2)
-                        pltpu.make_async_copy(
-                            lefts[s][NTV - 1 + part], left_buf.at[t, s, place], left_sem.at[t, s]
-                        ).start()
+                        target = left_place(t, s, part * (rows // 2), rows // 2)
+                        pltpu.make_async_copy(lefts[s][NTV - 1 + part], target, left_sem.at[t, s]).start()
         for copy in right_copies(0):
             copy.start()
         for t in range(count):
             for s in range(steps):
-                pltpu.make_async_copy(lefts[s][0], left_buf.at[t, s], left_sem.at[t, s]).wait()
+                pltpu.make_async_copy(lefts[s][0], left_place(t, s, 0, rows), left_sem.at[t, s]).wait()
 
     for i in range(NTV):
 
@@ -77,44 +79,25 @@
 
     @pl.when(step < GROUPS)
     def _():
-        group = pl.ds(pl.multiple_of(step * group_rows, group_rows), group_rows)
-        for half in range(2):
-            start = (half_ref[0] if half == 0 else 1 - half_ref[0]) * half_blocks
-            for p in range(half_blocks):
-                left = jnp.concatenate(
-                    [
-                        jnp.concatenate([left_buf[t, s, group, :] for s in range(steps)], axis=1)
-                        for t in range(count)
-                    ],
-                    axis=0,
-                )
-                right = jnp.concatenate(
-                    [
-                        jnp.concatenate(
-                            [
-                                right_buf[
-                                    slot,
-                                    s,
-                                    half,
-                                    pl.ds(
-                                        pl.multiple_of(
-                                            p * wide + (g // GROUPS * GROUPS + (g + step) % GROUPS) * TV, TV
-                                        ),
-                                        TV,
-                                    ),
-                                    :,
-                                ]
-                                for g in range(2 * GROUPS)
-                            ],
-                            axis=0,
-                        )
-                        for s in range(steps)
-                    ],
-                    axis=1,
-                )
-                products[step, start + p] = lax.dot_general(
-                    left, right, (((1,), (1,)), ((), ())), preferred_element_type=jnp.float32
-                ).astype(jnp.bfloat16)
+        half, p = step // half_blocks, step % half_blocks
+        side = jnp.where(half == 0, half_ref[0], 1 - half_ref[0])
+        result = lax.dot_general(
+            left_buf[...],
+            right_buf[slot, half, pl.ds(pl.multiple_of(p * wide, wide), wide), :],
+            (((1,), (1,)), ((), ())),
+            preferred_element_type=jnp.float32,
+        )
+        lanes = GROUPS * TV
+        for j in range(GROUPS):
+            for t in range(count):
+                first = t * rows + j * group_rows
+                for b in range(2):
+                    piece = result[first:first + group_rows, b * lanes:(b + 1) * lanes]
+                    if j:
+                        piece = pltpu.roll(piece, lanes - j * TV, 1)
+                    products[
+                        j, side * half_blocks + p, t * group_rows:(t + 1) * group_rows, b * lanes:(b + 1) * lanes
+                    ] = piece.astype(jnp.bfloat16)
 
     @pl.when(step >= GROUPS)
     def _():
@@ -182,14 +165,14 @@
                 pltpu.VMEM(result, jnp.float32),
                 pltpu.VMEM((GROUPS, 2 * rows // wide, count * rows // GROUPS, wide), jnp.bfloat16),
                 pltpu.VMEM((count, b_blocks, a_count, TV * TV), jnp.bfloat16),
-                pltpu.VMEM((count, steps, rows, depth), jnp.bfloat16),
-                pltpu.VMEM((2, steps, 2, rows, depth), jnp.bfloat16),
+                pltpu.VMEM((count * rows, steps * depth), jnp.bfloat16),
+                pltpu.VMEM((2, 2, rows, steps * depth), jnp.bfloat16),
                 pltpu.SemaphoreType.DMA((count, steps)),
                 pltpu.SemaphoreType.DMA((2, steps, 2)),
             ],
         ),
         out_shape=jax.ShapeDtypeStruct(result, kind),
-        compiler_params=pltpu.CompilerParams(vmem_limit_bytes=40 * 2**20),
+        compiler_params=pltpu.CompilerParams(vmem_limit_bytes=60 * 2**20),
         cost_estimate=pl.CostEstimate(flops=flops, bytes_accessed=28 * 2**20, transcendentals=0),
     )(half, live[:, base:base + count], pick[base:base + count], tile, *copied, amp)
 

time: 319 us -> 298 us (0.934)
  local copies, waits for them, and re-layouts: 43.9 us -> 14.8 us
  Pallas kernels: 76.9 us -> 83.7 us
  starting transfers between devices: 47.8 us -> 52.2 us
    unnamed x134 -> x80, local copies, waits for them, and re-layouts: 32.3 us -> 3.26 us
    pallas_call x2, Pallas kernels: 76.9 us -> 83.7 us  [ladder(): pl.pallas_call(functools.partial(ladder_kernel, steps, count), grid_spec=...]
    ppermute x36, waiting for transfers between devices: 39 us -> 32.7 us  [partner(): return lax.ppermute(value, axis, [(i, i ^ flip) for i in range(size)])]
    ppermute x12, starting transfers between devices: 18.4 us -> 22.3 us  [on_square(): lax.ppermute(held['block', s - 1, (i + 1) % NTV], 'left', ring)]
  transfers between devices with their start and end apart: 52 -> 52, of which waited for: 29 -> 27; matrix products, arithmetic and copies ran while one was open for 2% -> 2% of each run, Pallas kernels for 12% -> 14%
where the time goes in v4:
time: 298 us; the launch traced here: 294 us
  waiting for transfers between devices  126 us (42%)
  Pallas kernels  83.7 us (28%)
  starting transfers between devices  52.2 us (18%)
  local copies, waits for them, and re-layouts  14.8 us (5%)
  between operations  13.9 us (5%)
  other arithmetic  4.03 us (1%)
    pallas_call x2, Pallas kernels, ladder(): pl.pallas_call(functools.partial(ladder_kernel, steps, count), grid_spec=...  83.7 us
    ppermute x12, waiting for transfers between devices, on_square(): lax.ppermute(held['block', s - 1, (i + 1) % NTV], 'left', ring)  79.4 us
    ppermute x36, waiting for transfers between devices, partner(): return lax.ppermute(value, axis, [(i, i ^ flip) for i in range(size)])  32.7 us
    ppermute x36, starting transfers between devices, partner(): return lax.ppermute(value, axis, [(i, i ^ flip) for i in range(size)])  26.1 us
    ppermute x12, starting transfers between devices, on_square(): lax.ppermute(held['block', s - 1, (i + 1) % NTV], 'left', ring)  22.3 us
    ppermute x3, waiting for transfers between devices, shift(): lax.ppermute(value, axis, [(i, (i + step) % size) for i in range(size)])  13.4 us
  transfers between devices with their start and end apart: 52, of which 27 were waited for; matrix products, arithmetic and copies ran while one was open for 2% of the time, Pallas kernels for 14%

profile of v4, /device:TPU:8, one launch (start us, length us, event | category | flops | bytes accessed | tf_op | source)
XLA Modules:
  0.0 294.3 jit_solution(15187772610201297486)
XLA Ops:
  6.5 1.8 constant_dynamic-slice_fusion
  8.7 1.9 collective-permute-start.1
  10.7 1.5 collective-permute-start.2
  12.2 11.1 %collective-permute-done.refs_26_ = bf16[1,512,512]{2,1,0:T(8,128)(2,1)S(1)} collective-permute-done((bf16[1,512,512]{2,1,0:T(8,128)(2,1)S(1)}, bf16[1,512,512]{2,1,0:T(8,128)(2,1)S(1)}, u32[]{:S(2)}, u32[]{:S(2)}) %collective-permute-start) | collective-permute-done | bytes 524320 | tf_op jit(solution)/shard_map/ppermute | solution.py:259
  23.8 2.6 collective-permute-start.5
  26.6 1.6 collective-permute-start.6
  28.8 10.2 %collective-permute-done.5.refs_24_ = bf16[1,512,512]{2,1,0:T(8,128)(2,1)S(1)} collective-permute-done((bf16[1,512,512]{2,1,0:T(8,128)(2,1)S(1)}, bf16[1,512,512]{2,1,0:T(8,128)(2,1)S(1)}, u32[]{:S(2)}, u32[]{:S(2)}) %collective-permute-start.5) | collective-permute-done | bytes 524320 | tf_op jit(solution)/shard_map/ppermute | solution.py:259
  39.0 1.7 collective-permute-start.9
  41.4 1.5 collective-permute-start.11
  43.0 2.5 collective-permute-start.13
  45.4 9.3 %collective-permute-done.9.refs_22_ = bf16[1,512,512]{2,1,0:T(8,128)(2,1)S(1)} collective-permute-done((bf16[1,512,512]{2,1,0:T(8,128)(2,1)S(1)}, bf16[1,512,512]{2,1,0:T(8,128)(2,1)S(1)}, u32[]{:S(2)}, u32[]{:S(2)}) %collective-permute-start.9) | collective-permute-done | bytes 524320 | tf_op jit(solution)/shard_map/ppermute | solution.py:259
  54.9 1.6 collective-permute-start.14
  58.0 6.8 %collective-permute-done.13.refs_32_ = bf16[1,512,512]{2,1,0:T(8,128)(2,1)} collective-permute-done((bf16[1,512,512]{2,1,0:T(8,128)(2,1)S(1)}, bf16[1,512,512]{2,1,0:T(8,128)(2,1)}, u32[]{:S(2)}, u32[]{:S(2)}) %collective-permute-start.13) | collective-permute-done | bytes 524320 | tf_op jit(solution)/shard_map/ppermute | solution.py:259
  65.8 1.6 maximum_maximum_fusion
  67.5 2.4 collective-permute-start.17
  71.6 2.0 collective-permute-start.21
  73.6 9.8 %collective-permute-done.17.refs_30_ = bf16[1,512,512]{2,1,0:T(8,128)(2,1)S(1)} collective-permute-done((bf16[1,512,512]{2,1,0:T(8,128)(2,1)S(1)}, bf16[1,512,512]{2,1,0:T(8,128)(2,1)S(1)}, u32[]{:S(2)}, u32[]{:S(2)}) %collective-permute-start.17) | collective-permute-done | bytes 524320 | tf_op jit(solution)/shard_map/ppermute | solution.py:259
  87.0 2.6 collective-permute-start.25
  89.7 4.9 %collective-permute-done.21.refs_38_ = bf16[1,512,512]{2,1,0:T(8,128)(2,1)S(1)} collective-permute-done((bf16[1,512,512]{2,1,0:T(8,128)(2,1)}, bf16[1,512,512]{2,1,0:T(8,128)(2,1)S(1)}, u32[]{:S(2)}, u32[]{:S(2)}) %collective-permute-start.21) | collective-permute-done | bytes 524320 | tf_op jit(solution)/shard_map/ppermute | solution.py:259
  96.8 1.8 collective-permute-start.29
  98.6 7.3 %collective-permute-done.25.refs_28_ = bf16[1,512,512]{2,1,0:T(8,128)(2,1)} collective-permute-done((bf16[1,512,512]{2,1,0:T(8,128)(2,1)S(1)}, bf16[1,512,512]{2,1,0:T(8,128)(2,1)}, u32[]{:S(2)}, u32[]{:S(2)}) %collective-permute-start.25) | collective-permute-done | bytes 524320 | tf_op jit(solution)/shard_map/ppermute | solution.py:259
  105.9 3.1 %collective-permute-done.26.refs_11_ = bf16[512,512]{1,0:T(8,128)(2,1)S(1)} collective-permute-done((bf16[512,512]{1,0:T(8,128)(2,1)S(1)}, bf16[512,512]{1,0:T(8,128)(2,1)S(1)}, u32[]{:S(2)}, u32[]{:S(2)}) %collective-permute-start.26) | collective-permute-done | bytes 524320 | tf_op jit(solution)/shard_map/ppermute | solution.py:181
  112.0 1.2 collective-permute-start.31
  113.5 1.2 collective-permute-start.33
  115.6 3.2 %collective-permute-done.30.refs_13_ = bf16[256,512]{1,0:T(8,128)(2,1)S(1)} collective-permute-done((bf16[256,512]{1,0:T(8,128)(2,1)S(1)}, bf16[256,512]{1,0:T(8,128)(2,1)S(1)}, u32[]{:S(2)}, u32[]{:S(2)}) %collective-permute-start.30) | collective-permute-done | bytes 262176 | tf_op jit(solution)/shard_map/ppermute | solution.py:181
  118.8 1.7 collective-permute-done.31.refs_14_
  120.6 1.2 collective-permute-start.34
  122.6 1.6 collective-permute-start.37
  124.3 5.2 %collective-permute-done.33.refs_34_ = bf16[1,512,512]{2,1,0:T(8,128)(2,1)S(1)} collective-permute-done((bf16[1,512,512]{2,1,0:T(8,128)(2,1)}, bf16[1,512,512]{2,1,0:T(8,128)(2,1)S(1)}, u32[]{:S(2)}, u32[]{:S(2)}) %collective-permute-start.33) | collective-permute-done | bytes 524320 | tf_op jit(solution)/shard_map/ppermute | solution.py:259
  129.5 5.4 %collective-permute-done.34.refs_16_ = bf16[512,512]{1,0:T(8,128)(2,1)S(1)} collective-permute-done((bf16[512,512]{1,0:T(8,128)(2,1)S(1)}, bf16[512,512]{1,0:T(8,128)(2,1)S(1)}, u32[]{:S(2)}, u32[]{:S(2)}) %collective-permute-start.34) | collective-permute-done | bytes 524320 | tf_op jit(solution)/shard_map/ppermute | solution.py:181
  137.9 2.0 collective-permute-start.41
  140.0 4.6 %collective-permute-done.38.refs_18_ = bf16[256,512]{1,0:T(8,128)(2,1)S(1)} collective-permute-done((bf16[256,512]{1,0:T(8,128)(2,1)S(1)}, bf16[256,512]{1,0:T(8,128)(2,1)S(1)}, u32[]{:S(2)}, u32[]{:S(2)}) %collective-permute-start.38) | collective-permute-done | bytes 262176 | tf_op jit(solution)/shard_map/ppermute | solution.py:181
  146.8 1.6 collective-permute-start.43
  148.4 5.3 %collective-permute-done.41.refs_40_ = bf16[1,512,512]{2,1,0:T(8,128)(2,1)} collective-permute-done((bf16[1,512,512]{2,1,0:T(8,128)(2,1)S(1)}, bf16[1,512,512]{2,1,0:T(8,128)(2,1)}, u32[]{:S(2)}, u32[]{:S(2)}) %collective-permute-start.41) | collective-permute-done | bytes 524320 | tf_op jit(solution)/shard_map/ppermute | solution.py:259
  155.1 8.8 %collective-permute-done.43.refs_44_ = bf16[1,512,512]{2,1,0:T(8,128)(2,1)} collective-permute-done((bf16[1,512,512]{2,1,0:T(8,128)(2,1)S(1)}, bf16[1,512,512]{2,1,0:T(8,128)(2,1)}, u32[]{:S(2)}, u32[]{:S(2)}) %collective-permute-start.43) | collective-permute-done | bytes 524320 | tf_op jit(solution)/shard_map/ppermute | solution.py:259
  166.8 41.6 %shard_map.38 = bf16[2,4,128,512]{3,2,1,0:T(8,128)(2,1)} custom-call(s32[1]{0:T(128)} %bitcast.half_ref, s32[4,2]{1,0:T(4,128)} %get-tuple-element.143.live_ref, s32[2]{0:T(128)} %get-tuple-element.145.pick_ref, s32[4]{0:T(128)} %pad_add_fusion.tile_ref, bf16[512,512]{1,0:T(8,128)(2,1)} %bitcast.60, bf16[512,512]{1,0:T(8,128)(2,1)} %copy-done.10, ...), custom_call_target="tpu_custom_call" | custom-call | flops 21474836480 | bytes 29360128 | tf_op jit(solution)/shard_map/pallas_call | solution.py:156
  208.5 1.3 slice_bitcast_fusion.2
  209.8 2.2 collective-permute-start.45
  211.9 1.4 collective-permute-start.46
  213.3 42.1 %shard_map.37 = f32[2,4,128,512]{3,2,1,0:T(8,128)} custom-call(s32[1]{0:T(128)} %bitcast.half_ref, s32[4,2]{1,0:T(4,128)} %get-tuple-element.144.live_ref, s32[2]{0:T(128)} %get-tuple-element.146.pick_ref, s32[4]{0:T(128)} %pad_add_fusion.tile_ref, bf16[512,512]{1,0:T(8,128)(2,1)} %bitcast.61, bf16[512,512]{1,0:T(8,128)(2,1)} %copy-done.10, ...), custom_call_target="tpu_custom_call" | custom-call | flops 21474836480 | bytes 29360128 | tf_op jit(solution)/shard_map/pallas_call | solution.py:156
  255.4 1.3 fusion.3
  257.0 13.4 %collective-permute-done.47 = bf16[4,128,512]{2,1,0:T(8,128)(2,1)S(1)} collective-permute-done((bf16[4,128,512]{2,1,0:T(8,128)(2,1)S(1)}, bf16[4,128,512]{2,1,0:T(8,128)(2,1)S(1)}, u32[]{:S(2)}, u32[]{:S(2)}) %collective-permute-start.47) | collective-permute-done | bytes 524320 | tf_op jit(solution)/shard_map/ppermute | solution.py:185
  270.3 1.5 fusion.2
  272.6 1.2 collective-permute-start.49
  273.8 1.7 collective-permute-start.50
  275.6 5.7 %collective-permute-done.48 = f32[4,128,128]{2,1,0:T(8,128)S(1)} collective-permute-done((f32[4,128,128]{2,1,0:T(8,128)S(1)}, f32[4,128,128]{2,1,0:T(8,128)S(1)}, u32[]{:S(2)}, u32[]{:S(2)}) %collective-permute-start.48) | collective-permute-done | bytes 262176 | tf_op jit(solution)/shard_map/ppermute | solution.py:181
  281.3 3.8 %collective-permute-done.49 = f32[4,128,128]{2,1,0:T(8,128)S(1)} collective-permute-done((f32[4,128,128]{2,1,0:T(8,128)S(1)}, f32[4,128,128]{2,1,0:T(8,128)S(1)}, u32[]{:S(2)}, u32[]{:S(2)}) %collective-permute-start.49) | collective-permute-done | bytes 262176 | tf_op jit(solution)/shard_map/ppermute | solution.py:181
  285.8 1.6 copy.14
  (175 shorter events, 28.6 us)
Async XLA Ops:
  6.5 103.4 %all-gather.2.cloned.1.call-start = ((), (), s32[]{:S(2)}) async-start(), calls=%async_computation | async-start | bytes 6291456 | tf_op jit(solution)/shard_map/all_gather | solution.py:277
  8.7 14.6 %collective-permute-start = (bf16[1,512,512]{2,1,0:T(8,128)(2,1)S(1)}, bf16[1,512,512]{2,1,0:T(8,128)(2,1)S(1)}, u32[]{:S(2)}, u32[]{:S(2)}) collective-permute-start(bf16[1,512,512]{2,1,0:T(8,128)(2,1)S(1)} %get-tuple-element.69), channel_id=1, source_target_pairs={{0,16},{16,24},{24,8},{8,0},{1,17},{17,25},{25,9},{9,1},{2,18},{18... | collective-permute-start | bytes 1572872 | tf_op jit(solution)/shard_map/ppermute | solution.py:259
  8.7 14.6 %collective-permute-start.1 = (bf16[512,512]{1,0:T(8,128)(2,1)S(1)}, bf16[512,512]{1,0:T(8,128)(2,1)S(1)}, u32[]{:S(2)}, u32[]{:S(2)}) collective-permute-start(bf16[512,512]{1,0:T(8,128)(2,1)S(1)} %bitcast.58), channel_id=1, source_target_pairs={{0,2},{2,0},{4,6},{6,4},{1,3},{3,1},{5,7},{7,5},{8,10},{10,8},{12,... | collective-permute-start | bytes 1572872 | tf_op jit(solution)/shard_map/ppermute | solution.py:181
  10.7 13.1 %collective-permute-start.2 = (bf16[512,512]{1,0:T(8,128)(2,1)S(1)}, bf16[512,512]{1,0:T(8,128)(2,1)S(1)}, u32[]{:S(2)}, u32[]{:S(2)}) collective-permute-start(bf16[512,512]{1,0:T(8,128)(2,1)S(1)} %bitcast.59), channel_id=1, source_target_pairs={{0,4},{2,6},{4,0},{6,2},{1,5},{3,7},{5,1},{7,3},{8,12},{10,14},{12... | collective-permute-start | bytes 1572872 | tf_op jit(solution)/shard_map/ppermute | solution.py:181
  23.8 17.0 %collective-permute-start.3 = (bf16[4,512,512]{2,1,0:T(8,128)(2,1)S(1)}, bf16[4,512,512]{2,1,0:T(8,128)(2,1)S(1)}, u32[]{:S(2)}, u32[]{:S(2)}) collective-permute-start(bf16[4,512,512]{2,1,0:T(8,128)(2,1)S(1)} %copy-done.1), channel_id=1, source_target_pairs={{0,1},{1,0},{2,3},{3,2},{4,5},{5,4},{6,7},{7,6},{8,9},{9,8},{10,11... | collective-permute-start | bytes 6291464 | tf_op jit(solution)/shard_map/ppermute | solution.py:181
  23.8 15.2 %collective-permute-start.5 = (bf16[1,512,512]{2,1,0:T(8,128)(2,1)S(1)}, bf16[1,512,512]{2,1,0:T(8,128)(2,1)S(1)}, u32[]{:S(2)}, u32[]{:S(2)}) collective-permute-start(bf16[1,512,512]{2,1,0:T(8,128)(2,1)S(1)} %get-tuple-element.76), channel_id=1, source_target_pairs={{0,16},{16,24},{24,8},{8,0},{1,17},{17,25},{25,9},{9,1},{2,18},{18... | collective-permute-start | bytes 1572872 | tf_op jit(solution)/shard_map/ppermute | solution.py:259
  26.4 14.3 %collective-permute-start.4 = (bf16[1,512,512]{2,1,0:T(8,128)(2,1)S(1)}, bf16[1,512,512]{2,1,0:T(8,128)(2,1)S(1)}, u32[]{:S(2)}, u32[]{:S(2)}) collective-permute-start(bf16[1,512,512]{2,1,0:T(8,128)(2,1)S(1)} %collective-permute-done.refs_26_), channel_id=1, source_target_pairs={{0,1},{1,0},{2,3},{3,2},{4,5},{5,4},{6,7},{7,6},{8,9},{9,8},{10,11... | collective-permute-start | bytes 1572872 | tf_op jit(solution)/shard_map/ppermute | solution.py:181
  26.6 14.1 %collective-permute-start.6 = (bf16[256,512]{1,0:T(8,128)(2,1)S(1)}, bf16[256,512]{1,0:T(8,128)(2,1)S(1)}, u32[]{:S(2)}, u32[]{:S(2)}) collective-permute-start(bf16[256,512]{1,0:T(8,128)(2,1)S(1)} %slice.69), channel_id=1, source_target_pairs={{0,4},{2,6},{4,0},{6,2},{1,5},{3,7},{5,1},{7,3},{8,12},{10,14},{12... | collective-permute-start | bytes 786440 | tf_op jit(solution)/shard_map/ppermute | solution.py:181
  28.2 12.5 %collective-permute-start.7 = (bf16[256,512]{1,0:T(8,128)(2,1)S(1)}, bf16[256,512]{1,0:T(8,128)(2,1)S(1)}, u32[]{:S(2)}, u32[]{:S(2)}) collective-permute-start(bf16[256,512]{1,0:T(8,128)(2,1)S(1)} %slice.70), channel_id=1, source_target_pairs={{0,2},{2,0},{4,6},{6,4},{1,3},{3,1},{5,7},{7,5},{8,10},{10,8},{12,... | collective-permute-start | bytes 786440 | tf_op jit(solution)/shard_map/ppermute | solution.py:181
  39.0 15.7 %collective-permute-start.9 = (bf16[1,512,512]{2,1,0:T(8,128)(2,1)S(1)}, bf16[1,512,512]{2,1,0:T(8,128)(2,1)S(1)}, u32[]{:S(2)}, u32[]{:S(2)}) collective-permute-start(bf16[1,512,512]{2,1,0:T(8,128)(2,1)S(1)} %get-tuple-element.80), channel_id=1, source_target_pairs={{0,16},{16,24},{24,8},{8,0},{1,17},{17,25},{25,9},{9,1},{2,18},{18... | collective-permute-start | bytes 1572872 | tf_op jit(solution)/shard_map/ppermute | solution.py:259
  40.8 14.0 %collective-permute-start.10 = (bf16[4,512,128]{2,1,0:T(8,128)(2,1)S(1)}, bf16[4,512,128]{2,1,0:T(8,128)(2,1)S(1)}, u32[]{:S(2)}, u32[]{:S(2)}) collective-permute-start(bf16[4,512,128]{2,1,0:T(8,128)(2,1)S(1)} %bitcast.77), channel_id=1, source_target_pairs={{0,2},{2,0},{4,6},{6,4},{1,3},{3,1},{5,7},{7,5},{8,10},{10,8},{12,... | collective-permute-start | bytes 1572872 | tf_op jit(solution)/shard_map/ppermute | solution.py:181
  41.4 13.3 %collective-permute-start.11 = (bf16[4,512,128]{2,1,0:T(8,128)(2,1)S(1)}, bf16[4,512,128]{2,1,0:T(8,128)(2,1)S(1)}, u32[]{:S(2)}, u32[]{:S(2)}) collective-permute-start(bf16[4,512,128]{2,1,0:T(8,128)(2,1)S(1)} %bitcast.78), channel_id=1, source_target_pairs={{0,4},{2,6},{4,0},{6,2},{1,5},{3,7},{5,1},{7,3},{8,12},{10,14},{12... | collective-permute-start | bytes 1572872 | tf_op jit(solution)/shard_map/ppermute | solution.py:181
  43.0 11.8 %collective-permute-start.8 = (bf16[1,512,512]{2,1,0:T(8,128)(2,1)S(1)}, bf16[1,512,512]{2,1,0:T(8,128)(2,1)S(1)}, u32[]{:S(2)}, u32[]{:S(2)}) collective-permute-start(bf16[1,512,512]{2,1,0:T(8,128)(2,1)S(1)} %collective-permute-done.5.refs_24_), channel_id=1, source_target_pairs={{0,1},{1,0},{2,3},{3,2},{4,5},{5,4},{6,7},{7,6},{8,9},{9,8},{10,11... | collective-permute-start | bytes 1572872 | tf_op jit(solution)/shard_map/ppermute | solution.py:181
  43.0 21.8 %collective-permute-start.13 = (bf16[1,512,512]{2,1,0:T(8,128)(2,1)S(1)}, bf16[1,512,512]{2,1,0:T(8,128)(2,1)}, u32[]{:S(2)}, u32[]{:S(2)}) collective-permute-start(bf16[1,512,512]{2,1,0:T(8,128)(2,1)S(1)} %collective-permute-done.refs_26_), channel_id=1, source_target_pairs={{0,16},{16,24},{24,8},{8,0},{1,17},{17,25},{25,9},{9,1},{2,18},{18... | collective-permute-start | bytes 1572872 | tf_op jit(solution)/shard_map/ppermute | solution.py:259
  54.8 10.2 %collective-permute-start.12 = (bf16[1,512,512]{2,1,0:T(8,128)(2,1)S(1)}, bf16[1,512,512]{2,1,0:T(8,128)(2,1)S(1)}, u32[]{:S(2)}, u32[]{:S(2)}) collective-permute-start(bf16[1,512,512]{2,1,0:T(8,128)(2,1)S(1)} %collective-permute-done.9.refs_22_), channel_id=1, source_target_pairs={{0,1},{1,0},{2,3},{3,2},{4,5},{5,4},{6,7},{7,6},{8,9},{9,8},{10,11... | collective-permute-start | bytes 1572872 | tf_op jit(solution)/shard_map/ppermute | solution.py:181
  54.9 9.9 %collective-permute-start.14 = (bf16[2,512,128]{2,1,0:T(8,128)(2,1)S(1)}, bf16[2,512,128]{2,1,0:T(8,128)(2,1)S(1)}, u32[]{:S(2)}, u32[]{:S(2)}) collective-permute-start(bf16[2,512,128]{2,1,0:T(8,128)(2,1)S(1)} %slice.71), channel_id=1, source_target_pairs={{0,4},{2,6},{4,0},{6,2},{1,5},{3,7},{5,1},{7,3},{8,12},{10,14},{12... | collective-permute-start | bytes 786440 | tf_op jit(solution)/shard_map/ppermute | solution.py:181
  67.5 15.8 %collective-permute-start.17 = (bf16[1,512,512]{2,1,0:T(8,128)(2,1)S(1)}, bf16[1,512,512]{2,1,0:T(8,128)(2,1)S(1)}, u32[]{:S(2)}, u32[]{:S(2)}) collective-permute-start(bf16[1,512,512]{2,1,0:T(8,128)(2,1)S(1)} %collective-permute-done.5.refs_24_), channel_id=1, source_target_pairs={{0,16},{16,24},{24,8},{8,0},{1,17},{17,25},{25,9},{9,1},{2,18},{18... | collective-permute-start | bytes 1572872 | tf_op jit(solution)/shard_map/ppermute | solution.py:259
  69.9 13.4 %collective-permute-start.16 = (bf16[1,512,512]{2,1,0:T(8,128)(2,1)}, bf16[1,512,512]{2,1,0:T(8,128)(2,1)S(1)}, u32[]{:S(2)}, u32[]{:S(2)}) collective-permute-start(bf16[1,512,512]{2,1,0:T(8,128)(2,1)} %collective-permute-done.13.refs_32_), channel_id=1, source_target_pairs={{0,1},{1,0},{2,3},{3,2},{4,5},{5,4},{6,7},{7,6},{8,9},{9,8},{10,11... | collective-permute-start | bytes 1572872 | tf_op jit(solution)/shard_map/ppermute | solution.py:181
  69.9 14.3 %collective-permute-start.18 = (bf16[512,512]{1,0:T(8,128)(2,1)S(1)}, bf16[512,512]{1,0:T(8,128)(2,1)S(1)}, u32[]{:S(2)}, u32[]{:S(2)}) collective-permute-start(bf16[512,512]{1,0:T(8,128)(2,1)S(1)} %bitcast.63), channel_id=1, source_target_pairs={{0,2},{2,0},{4,6},{6,4},{1,3},{3,1},{5,7},{7,5},{8,10},{10,8},{12,... | collective-permute-start | bytes 1572872 | tf_op jit(solution)/shard_map/ppermute | solution.py:181
  71.1 14.1 %collective-permute-start.19 = (bf16[512,512]{1,0:T(8,128)(2,1)S(1)}, bf16[512,512]{1,0:T(8,128)(2,1)S(1)}, u32[]{:S(2)}, u32[]{:S(2)}) collective-permute-start(bf16[512,512]{1,0:T(8,128)(2,1)S(1)} %bitcast.64), channel_id=1, source_target_pairs={{0,4},{2,6},{4,0},{6,2},{1,5},{3,7},{5,1},{7,3},{8,12},{10,14},{12... | collective-permute-start | bytes 1572872 | tf_op jit(solution)/shard_map/ppermute | solution.py:181
  71.6 23.0 %collective-permute-start.21 = (bf16[1,512,512]{2,1,0:T(8,128)(2,1)}, bf16[1,512,512]{2,1,0:T(8,128)(2,1)S(1)}, u32[]{:S(2)}, u32[]{:S(2)}) collective-permute-start(bf16[1,512,512]{2,1,0:T(8,128)(2,1)} %collective-permute-done.13.refs_32_), channel_id=1, source_target_pairs={{0,16},{16,24},{24,8},{8,0},{1,17},{17,25},{25,9},{9,1},{2,18},{18... | collective-permute-start | bytes 1572872 | tf_op jit(solution)/shard_map/ppermute | solution.py:259
  85.1 9.5 %collective-permute-start.20 = (bf16[1,512,512]{2,1,0:T(8,128)(2,1)S(1)}, bf16[1,512,512]{2,1,0:T(8,128)(2,1)S(1)}, u32[]{:S(2)}, u32[]{:S(2)}) collective-permute-start(bf16[1,512,512]{2,1,0:T(8,128)(2,1)S(1)} %collective-permute-done.17.refs_30_), channel_id=1, source_target_pairs={{0,1},{1,0},{2,3},{3,2},{4,5},{5,4},{6,7},{7,6},{8,9},{9,8},{10,11... | collective-permute-start | bytes 1572872 | tf_op jit(solution)/shard_map/ppermute | solution.py:181
  85.2 9.4 %collective-permute-start.22 = (bf16[256,512]{1,0:T(8,128)(2,1)S(1)}, bf16[256,512]{1,0:T(8,128)(2,1)S(1)}, u32[]{:S(2)}, u32[]{:S(2)}) collective-permute-start(bf16[256,512]{1,0:T(8,128)(2,1)S(1)} %slice.73), channel_id=1, source_target_pairs={{0,4},{2,6},{4,0},{6,2},{1,5},{3,7},{5,1},{7,3},{8,12},{10,14},{12... | collective-permute-start | bytes 786440 | tf_op jit(solution)/shard_map/ppermute | solution.py:181
  85.8 8.8 %collective-permute-start.23 = (bf16[256,512]{1,0:T(8,128)(2,1)S(1)}, bf16[256,512]{1,0:T(8,128)(2,1)S(1)}, u32[]{:S(2)}, u32[]{:S(2)}) collective-permute-start(bf16[256,512]{1,0:T(8,128)(2,1)S(1)} %slice.74), channel_id=1, source_target_pairs={{0,2},{2,0},{4,6},{6,4},{1,3},{3,1},{5,7},{7,5},{8,10},{10,8},{12,... | collective-permute-start | bytes 786440 | tf_op jit(solution)/shard_map/ppermute | solution.py:181
  87.0 18.9 %collective-permute-start.25 = (bf16[1,512,512]{2,1,0:T(8,128)(2,1)S(1)}, bf16[1,512,512]{2,1,0:T(8,128)(2,1)}, u32[]{:S(2)}, u32[]{:S(2)}) collective-permute-start(bf16[1,512,512]{2,1,0:T(8,128)(2,1)S(1)} %get-tuple-element.99), channel_id=1, source_target_pairs={{0,16},{16,24},{24,8},{8,0},{1,17},{17,25},{25,9},{9,1},{2,18},{18... | collective-permute-start | bytes 1572872 | tf_op jit(solution)/shard_map/ppermute | solution.py:259
  94.6 11.3 %collective-permute-start.24 = (bf16[1,512,512]{2,1,0:T(8,128)(2,1)S(1)}, bf16[1,512,512]{2,1,0:T(8,128)(2,1)S(1)}, u32[]{:S(2)}, u32[]{:S(2)}) collective-permute-start(bf16[1,512,512]{2,1,0:T(8,128)(2,1)S(1)} %collective-permute-done.21.refs_38_), channel_id=1, source_target_pairs={{0,1},{1,0},{2,3},{3,2},{4,5},{5,4},{6,7},{7,6},{8,9},{9,8},{10,11... | collective-permute-start | bytes 1572872 | tf_op jit(solution)/shard_map/ppermute | solution.py:181
  94.7 14.3 %collective-permute-start.26 = (bf16[512,512]{1,0:T(8,128)(2,1)S(1)}, bf16[512,512]{1,0:T(8,128)(2,1)S(1)}, u32[]{:S(2)}, u32[]{:S(2)}) collective-permute-start(bf16[512,512]{1,0:T(8,128)(2,1)S(1)} %bitcast.69), channel_id=1, source_target_pairs={{0,2},{2,0},{4,6},{6,4},{1,3},{3,1},{5,7},{7,5},{8,10},{10,8},{12,... | collective-permute-start | bytes 1572872 | tf_op jit(solution)/shard_map/ppermute | solution.py:181
  95.9 14.1 %collective-permute-start.27 = (bf16[512,512]{1,0:T(8,128)(2,1)S(1)}, bf16[512,512]{1,0:T(8,128)(2,1)}, u32[]{:S(2)}, u32[]{:S(2)}) collective-permute-start(bf16[512,512]{1,0:T(8,128)(2,1)S(1)} %bitcast.70), channel_id=1, source_target_pairs={{0,4},{2,6},{4,0},{6,2},{1,5},{3,7},{5,1},{7,3},{8,12},{10,14},{12... | collective-permute-start | bytes 1572872 | tf_op jit(solution)/shard_map/ppermute | solution.py:181
  96.8 18.8 %collective-permute-start.29 = (bf16[1,512,512]{2,1,0:T(8,128)(2,1)S(1)}, bf16[1,512,512]{2,1,0:T(8,128)(2,1)}, u32[]{:S(2)}, u32[]{:S(2)}) collective-permute-start(bf16[1,512,512]{2,1,0:T(8,128)(2,1)S(1)} %collective-permute-done.9.refs_22_), channel_id=1, source_target_pairs={{0,16},{16,24},{24,8},{8,0},{1,17},{17,25},{25,9},{9,1},{2,18},{18... | collective-permute-start | bytes 1572872 | tf_op jit(solution)/shard_map/ppermute | solution.py:259
  110.0 10.5 %collective-permute-start.28 = (bf16[1,512,512]{2,1,0:T(8,128)(2,1)}, bf16[1,512,512]{2,1,0:T(8,128)(2,1)S(1)}, u32[]{:S(2)}, u32[]{:S(2)}) collective-permute-start(bf16[1,512,512]{2,1,0:T(8,128)(2,1)} %collective-permute-done.25.refs_28_), channel_id=1, source_target_pairs={{0,1},{1,0},{2,3},{3,2},{4,5},{5,4},{6,7},{7,6},{8,9},{9,8},{10,11... | collective-permute-start | bytes 1572872 | tf_op jit(solution)/shard_map/ppermute | solution.py:181
  110.0 8.8 %collective-permute-start.30 = (bf16[256,512]{1,0:T(8,128)(2,1)S(1)}, bf16[256,512]{1,0:T(8,128)(2,1)S(1)}, u32[]{:S(2)}, u32[]{:S(2)}) collective-permute-start(bf16[256,512]{1,0:T(8,128)(2,1)S(1)} %slice.75), channel_id=1, source_target_pairs={{0,4},{2,6},{4,0},{6,2},{1,5},{3,7},{5,1},{7,3},{8,12},{10,14},{12... | collective-permute-start | bytes 786440 | tf_op jit(solution)/shard_map/ppermute | solution.py:181
  112.0 8.5 %collective-permute-start.31 = (bf16[256,512]{1,0:T(8,128)(2,1)S(1)}, bf16[256,512]{1,0:T(8,128)(2,1)S(1)}, u32[]{:S(2)}, u32[]{:S(2)}) collective-permute-start(bf16[256,512]{1,0:T(8,128)(2,1)S(1)} %slice.76), channel_id=1, source_target_pairs={{0,2},{2,0},{4,6},{6,4},{1,3},{3,1},{5,7},{7,5},{8,10},{10,8},{12,... | collective-permute-start | bytes 786440 | tf_op jit(solution)/shard_map/ppermute | solution.py:181
  113.5 16.0 %collective-permute-start.33 = (bf16[1,512,512]{2,1,0:T(8,128)(2,1)}, bf16[1,512,512]{2,1,0:T(8,128)(2,1)S(1)}, u32[]{:S(2)}, u32[]{:S(2)}) collective-permute-start(bf16[1,512,512]{2,1,0:T(8,128)(2,1)} %collective-permute-done.25.refs_28_), channel_id=1, source_target_pairs={{0,16},{16,24},{24,8},{8,0},{1,17},{17,25},{25,9},{9,1},{2,18},{18... | collective-permute-start | bytes 1572872 | tf_op jit(solution)/shard_map/ppermute | solution.py:259
  120.5 9.0 %collective-permute-start.32 = (bf16[1,512,512]{2,1,0:T(8,128)(2,1)}, bf16[1,512,512]{2,1,0:T(8,128)(2,1)S(1)}, u32[]{:S(2)}, u32[]{:S(2)}) collective-permute-start(bf16[1,512,512]{2,1,0:T(8,128)(2,1)} %collective-permute-done.29.refs_36_), channel_id=1, source_target_pairs={{0,1},{1,0},{2,3},{3,2},{4,5},{5,4},{6,7},{7,6},{8,9},{9,8},{10,11... | collective-permute-start | bytes 1572872 | tf_op jit(solution)/shard_map/ppermute | solution.py:181
  120.6 14.3 %collective-permute-start.34 = (bf16[512,512]{1,0:T(8,128)(2,1)S(1)}, bf16[512,512]{1,0:T(8,128)(2,1)S(1)}, u32[]{:S(2)}, u32[]{:S(2)}) collective-permute-start(bf16[512,512]{1,0:T(8,128)(2,1)S(1)} %bitcast.73), channel_id=1, source_target_pairs={{0,2},{2,0},{4,6},{6,4},{1,3},{3,1},{5,7},{7,5},{8,10},{10,8},{12,... | collective-permute-start | bytes 1572872 | tf_op jit(solution)/shard_map/ppermute | solution.py:181
  121.8 14.0 %collective-permute-start.35 = (bf16[512,512]{1,0:T(8,128)(2,1)S(1)}, bf16[512,512]{1,0:T(8,128)(2,1)S(1)}, u32[]{:S(2)}, u32[]{:S(2)}) collective-permute-start(bf16[512,512]{1,0:T(8,128)(2,1)S(1)} %bitcast.74), channel_id=1, source_target_pairs={{0,4},{2,6},{4,0},{6,2},{1,5},{3,7},{5,1},{7,3},{8,12},{10,14},{12... | collective-permute-start | bytes 1572872 | tf_op jit(solution)/shard_map/ppermute | solution.py:181
  122.6 17.3 %collective-permute-start.37 = (bf16[1,512,512]{2,1,0:T(8,128)(2,1)}, bf16[1,512,512]{2,1,0:T(8,128)(2,1)}, u32[]{:S(2)}, u32[]{:S(2)}) collective-permute-start(bf16[1,512,512]{2,1,0:T(8,128)(2,1)} %collective-permute-done.29.refs_36_), channel_id=1, source_target_pairs={{0,16},{16,24},{24,8},{8,0},{1,17},{17,25},{25,9},{9,1},{2,18},{18... | collective-permute-start | bytes 1572872 | tf_op jit(solution)/shard_map/ppermute | solution.py:259
  135.8 9.5 %collective-permute-start.36 = (bf16[1,512,512]{2,1,0:T(8,128)(2,1)S(1)}, bf16[1,512,512]{2,1,0:T(8,128)(2,1)S(1)}, u32[]{:S(2)}, u32[]{:S(2)}) collective-permute-start(bf16[1,512,512]{2,1,0:T(8,128)(2,1)S(1)} %collective-permute-done.33.refs_34_), channel_id=1, source_target_pairs={{0,1},{1,0},{2,3},{3,2},{4,5},{5,4},{6,7},{7,6},{8,9},{9,8},{10,11... | collective-permute-start | bytes 1572872 | tf_op jit(solution)/shard_map/ppermute | solution.py:181
  135.8 8.8 %collective-permute-start.38 = (bf16[256,512]{1,0:T(8,128)(2,1)S(1)}, bf16[256,512]{1,0:T(8,128)(2,1)S(1)}, u32[]{:S(2)}, u32[]{:S(2)}) collective-permute-start(bf16[256,512]{1,0:T(8,128)(2,1)S(1)} %slice.77), channel_id=1, source_target_pairs={{0,4},{2,6},{4,0},{6,2},{1,5},{3,7},{5,1},{7,3},{8,12},{10,14},{12... | collective-permute-start | bytes 786440 | tf_op jit(solution)/shard_map/ppermute | solution.py:181
  137.9 15.8 %collective-permute-start.41 = (bf16[1,512,512]{2,1,0:T(8,128)(2,1)S(1)}, bf16[1,512,512]{2,1,0:T(8,128)(2,1)}, u32[]{:S(2)}, u32[]{:S(2)}) collective-permute-start(bf16[1,512,512]{2,1,0:T(8,128)(2,1)S(1)} %collective-permute-done.33.refs_34_), channel_id=1, source_target_pairs={{0,16},{16,24},{24,8},{8,0},{1,17},{17,25},{25,9},{9,1},{2,18},{18... | collective-permute-start | bytes 1572872 | tf_op jit(solution)/shard_map/ppermute | solution.py:259
  146.8 17.1 %collective-permute-start.43 = (bf16[1,512,512]{2,1,0:T(8,128)(2,1)S(1)}, bf16[1,512,512]{2,1,0:T(8,128)(2,1)}, u32[]{:S(2)}, u32[]{:S(2)}) collective-permute-start(bf16[1,512,512]{2,1,0:T(8,128)(2,1)S(1)} %collective-permute-done.17.refs_30_), channel_id=1, source_target_pairs={{0,16},{16,24},{24,8},{8,0},{1,17},{17,25},{25,9},{9,1},{2,18},{18... | collective-permute-start | bytes 1572872 | tf_op jit(solution)/shard_map/ppermute | solution.py:259
  153.7 10.2 %collective-permute-start.42 = (bf16[1,512,512]{2,1,0:T(8,128)(2,1)}, bf16[1,512,512]{2,1,0:T(8,128)(2,1)}, u32[]{:S(2)}, u32[]{:S(2)}) collective-permute-start(bf16[1,512,512]{2,1,0:T(8,128)(2,1)} %collective-permute-done.41.refs_40_), channel_id=1, source_target_pairs={{0,1},{1,0},{2,3},{3,2},{4,5},{5,4},{6,7},{7,6},{8,9},{9,8},{10,11... | collective-permute-start | bytes 1572872 | tf_op jit(solution)/shard_map/ppermute | solution.py:181
  209.8 47.2 %collective-permute-start.45 = (bf16[4,128,512]{2,1,0:T(8,128)(2,1)S(1)}, bf16[4,128,512]{2,1,0:T(8,128)(2,1)S(1)}, u32[]{:S(2)}, u32[]{:S(2)}) collective-permute-start(bf16[4,128,512]{2,1,0:T(8,128)(2,1)S(1)} %get-tuple-element.141), channel_id=1, source_target_pairs={{0,8},{8,16},{16,24},{24,0},{1,9},{9,17},{17,25},{25,1},{2,10},{10... | collective-permute-start | bytes 1572872 | tf_op jit(solution)/shard_map/ppermute | solution.py:185
  211.9 45.0 %collective-permute-start.46 = (bf16[4,128,512]{2,1,0:T(8,128)(2,1)S(1)}, bf16[4,128,512]{2,1,0:T(8,128)(2,1)S(1)}, u32[]{:S(2)}, u32[]{:S(2)}) collective-permute-start(bf16[4,128,512]{2,1,0:T(8,128)(2,1)S(1)} %get-tuple-element.142), channel_id=1, source_target_pairs={{0,16},{8,24},{16,0},{24,8},{1,17},{9,25},{17,1},{25,9},{2,18},{10... | collective-permute-start | bytes 1572872 | tf_op jit(solution)/shard_map/ppermute | solution.py:185
  256.7 13.6 %collective-permute-start.47 = (bf16[4,128,512]{2,1,0:T(8,128)(2,1)S(1)}, bf16[4,128,512]{2,1,0:T(8,128)(2,1)S(1)}, u32[]{:S(2)}, u32[]{:S(2)}) collective-permute-start(bf16[4,128,512]{2,1,0:T(8,128)(2,1)S(1)} %fusion.3), channel_id=1, source_target_pairs={{0,24},{8,0},{16,8},{24,16},{1,25},{9,1},{17,9},{25,17},{2,26},{10... | collective-permute-start | bytes 1572872 | tf_op jit(solution)/shard_map/ppermute | solution.py:185
  272.0 9.3 %collective-permute-start.48 = (f32[4,128,128]{2,1,0:T(8,128)S(1)}, f32[4,128,128]{2,1,0:T(8,128)S(1)}, u32[]{:S(2)}, u32[]{:S(2)}) collective-permute-start(f32[4,128,128]{2,1,0:T(8,128)S(1)} %get-tuple-element.140), channel_id=1, source_target_pairs={{0,2},{2,0},{4,6},{6,4},{1,3},{3,1},{5,7},{7,5},{8,10},{10,8},{12,... | collective-permute-start | bytes 786440 | tf_op jit(solution)/shard_map/ppermute | solution.py:181
  272.6 12.5 %collective-permute-start.49 = (f32[4,128,128]{2,1,0:T(8,128)S(1)}, f32[4,128,128]{2,1,0:T(8,128)S(1)}, u32[]{:S(2)}, u32[]{:S(2)}) collective-permute-start(f32[4,128,128]{2,1,0:T(8,128)S(1)} %get-tuple-element.139), channel_id=1, source_target_pairs={{0,4},{2,6},{4,0},{6,2},{1,5},{3,7},{5,1},{7,3},{8,12},{10,14},{12... | collective-permute-start | bytes 786440 | tf_op jit(solution)/shard_map/ppermute | solution.py:181
  273.8 11.3 %collective-permute-start.50 = (f32[4,128,128]{2,1,0:T(8,128)S(1)}, f32[4,128,128]{2,1,0:T(8,128)S(1)}, u32[]{:S(2)}, u32[]{:S(2)}) collective-permute-start(f32[4,128,128]{2,1,0:T(8,128)S(1)} %get-tuple-element.138), channel_id=1, source_target_pairs={{0,6},{2,4},{4,2},{6,0},{1,7},{3,5},{5,3},{7,1},{8,14},{10,12},{12... | collective-permute-start | bytes 786440 | tf_op jit(solution)/shard_map/ppermute | solution.py:181
  (44 other events, 1121.0 us)
Sparse Core Ops, SparseCore 0:
  67.6 14.0 all-gather.1

commit v5 on v4

--- a/solution.py
+++ b/solution.py
@@ -14,15 +14,16 @@
 GROUPS = 4
 
 
-def ladder_kernel(steps, count, half_ref, live_ref, pick_ref, tile_ref, *refs):
+def ladder_kernel(steps, count, tile_count, first, half_ref, live_ref, pick_ref, tile_ref, *refs):
     kinds = NTV + 1
     lefts = [refs[s * kinds:(s + 1) * kinds] for s in range(steps)]
     rest = refs[steps * kinds:]
     whole, rest = rest[:2], rest[2:]
-    tiles = [rest[2 * n:2 * n + 2] for n in range((steps - 1) * NTV)]
-    amp_ref, out_ref, total_ref, products, ready, left_buf, right_buf, left_sem, right_sem = rest[
-        2 * (steps - 1) * NTV:
-    ]
+    tiles = [rest[2 * n:2 * n + 2] for n in range((steps - 1) * tile_count)]
+    rest = rest[2 * (steps - 1) * tile_count:]
+    amp_ref = rest[0]
+    before_ref = None if first else rest[1]
+    out_ref, total_ref, products, ready, left_buf, right_buf, left_sem, right_sem = rest[-8:]
     d_tile, step = pl.program_id(0), pl.program_id(1)
     rows = left_buf.shape[0] // count
     depth = left_buf.shape[1] // steps
@@ -38,7 +39,7 @@
         copies = []
         for s in range(steps):
             for side in range(2):
-                source = whole[side].at[tile_ref[i]] if s == 0 else tiles[(s - 1) * NTV + i][side].at[0]
+                source = whole[side].at[tile_ref[i]] if s == 0 else tiles[(s - 1) * tile_count + i][side].at[0]
                 target = right_buf.at[i % 2, side, :, pl.ds(s * depth, depth)]
                 copies.append(pltpu.make_async_copy(source, target, right_sem.at[i % 2, s, side]))
         return copies
@@ -67,37 +68,48 @@
             for s in range(steps):
                 pltpu.make_async_copy(lefts[s][0], left_place(t, s, 0, rows), left_sem.at[t, s]).wait()
 
-    for i in range(NTV):
+    for i in range(tile_count):
 
         @pl.when((d_tile == i) & (step == 0))
         def _():
             for copy in right_copies(i):
                 copy.wait()
-            if i + 1 < NTV:
+            if i + 1 < tile_count:
                 for copy in right_copies(i + 1):
                     copy.start()
 
     @pl.when(step < GROUPS)
     def _():
-        half, p = step // half_blocks, step % half_blocks
-        side = jnp.where(half == 0, half_ref[0], 1 - half_ref[0])
-        result = lax.dot_general(
-            left_buf[...],
-            right_buf[slot, half, pl.ds(pl.multiple_of(p * wide, wide), wide), :],
-            (((1,), (1,)), ((), ())),
-            preferred_element_type=jnp.float32,
+        left = jnp.concatenate(
+            [
+                left_buf[pl.ds(pl.multiple_of(t * rows + step * group_rows, group_rows), group_rows), :]
+                for t in range(count)
+            ],
+            axis=0,
         )
-        lanes = GROUPS * TV
-        for j in range(GROUPS):
-            for t in range(count):
-                first = t * rows + j * group_rows
-                for b in range(2):
-                    piece = result[first:first + group_rows, b * lanes:(b + 1) * lanes]
-                    if j:
-                        piece = pltpu.roll(piece, lanes - j * TV, 1)
-                    products[
-                        j, side * half_blocks + p, t * group_rows:(t + 1) * group_rows, b * lanes:(b + 1) * lanes
-                    ] = piece.astype(jnp.bfloat16)
+        for half in range(2):
+            start = (half_ref[0] if half == 0 else 1 - half_ref[0]) * half_blocks
+            for p in range(half_blocks):
+                right = jnp.concatenate(
+                    [
+                        right_buf[
+                            slot,
+                            half,
+                            pl.ds(
+                                pl.multiple_of(
+                                    p * wide + (g // GROUPS * GROUPS + (g + step) % GROUPS) * TV, TV
+                                ),
+                                TV,
+                            ),
+                            :,
+                        ]
+                        for g in range(2 * GROUPS)
+                    ],
+                    axis=0,
+                )
+                products[step, start + p] = lax.dot_general(
+                    left, right, (((1,), (1,)), ((), ())), preferred_element_type=jnp.float32
+                ).astype(jnp.bfloat16)
 
     @pl.when(step >= GROUPS)
     def _():
@@ -129,37 +141,43 @@
 
             @pl.when(d_tile == 0)
             def _():
-                total_ref[t, k] = term
-
-            @pl.when((d_tile > 0) & (d_tile < NTV - 1))
+                total_ref[t, k] = term if first else before_ref[t, k] + term
+
+            @pl.when((d_tile > 0) & (d_tile < tile_count - 1))
             def _():
                 total_ref[t, k] += term
 
-            @pl.when(d_tile == NTV - 1)
+            @pl.when(d_tile == tile_count - 1)
             def _():
                 out_ref[t, k] = (total_ref[t, k] + term).astype(out_ref.dtype)
 
 
-def ladder(half, live, pick, tile, lefts, whole, tiles, amp, part, kind):
+def ladder(half, live, pick, tile, lefts, whole, tiles, amp, before, part, kind):
     steps = len(lefts)
     rows, depth = whole[0].shape[1:]
     columns = amp.shape[2]
     a_count = rows // TV
     b_blocks = TV // GROUPS
     wide = 2 * GROUPS * TV
-    count = NTV // 2
+    tile_count = live.shape[0]
+    first = before is None
+    count = NTV if first else NTV // 2
     base = part * count
     result = (count, GROUPS, b_blocks * a_count, columns)
-    flops = 2 * NTV * count * rows * 2 * rows * (steps * depth + columns)
+    flops = 2 * tile_count * count * rows * 2 * rows * (steps * depth + columns)
     anywhere = pl.BlockSpec(memory_space=pl.ANY)
     copied = [x for step in lefts for x in step] + [*whole] + [x for pair in tiles for x in pair]
     return pl.pallas_call(
-        functools.partial(ladder_kernel, steps, count),
+        functools.partial(ladder_kernel, steps, count, tile_count, first),
         grid_spec=pltpu.PrefetchScalarGridSpec(
             num_scalar_prefetch=4,
-            grid=(NTV, 2 * GROUPS),
+            grid=(tile_count, 2 * GROUPS),
             in_specs=[anywhere] * len(copied)
-            + [pl.BlockSpec((1, 2 * rows, columns), lambda i, j, h, v, k, d: (d[i], 0, 0))],
+            + [pl.BlockSpec((1, 2 * rows, columns), lambda i, j, h, v, k, d: (d[i], 0, 0))]
+            + [
+                pl.BlockSpec(result, lambda i, j, h, v, k, d: (part, 0, 0, 0), pipeline_mode=pl.Buffered(1))
+            ]
+            * (not first),
             out_specs=pl.BlockSpec(result, lambda i, j, h, v, k, d: (0, 0, 0, 0)),
             scratch_shapes=[
                 pltpu.VMEM(result, jnp.float32),
@@ -174,7 +192,7 @@
         out_shape=jax.ShapeDtypeStruct(result, kind),
         compiler_params=pltpu.CompilerParams(vmem_limit_bytes=60 * 2**20),
         cost_estimate=pl.CostEstimate(flops=flops, bytes_accessed=28 * 2**20, transcendentals=0),
-    )(half, live[:, base:base + count], pick[base:base + count], tile, *copied, amp)
+    )(half, live[:, base:base + count], pick[base:base + count], tile, *copied, amp, *([] if first else [before]))
 
 
 def partner(value, axis, size, flip):
@@ -234,6 +252,22 @@
         keys = list(dict.fromkeys(keys))
         for key, value in zip(keys, lax.optimization_barrier([held[key] for key in keys])):
             held[key] = value
+
+    def contract(chosen, before, part, kind):
+        d_order = jnp.stack([d_tiles[i] for i in chosen])
+        return ladder(
+            half,
+            live[:, d_order].T,
+            pick,
+            d_order,
+            [[held["left", s, piece] for piece in (0, 1, 2, "first", "second")] for s in range(NTV)],
+            (held["chol"], held["other", "chol"]),
+            [(held["block", s, i], held["other", s, i]) for s in range(1, NTV) for i in chosen],
+            held["amp"],
+            before,
+            part,
+            kind,
+        )
 
     for slot in range(last + 1):
         hops = [0, 1] if slot == 0 else [slot + 1] if slot + 1 < last else []
@@ -276,21 +310,12 @@
             every = [held["left", AMP, flip] for flip in range(3)] + [far]
             held["amp"] = lax.all_gather(jnp.concatenate(every, axis=2), "occ", axis=1, tiled=True)
             waiting[slot + 3].append("amp")
-    d_order = jnp.stack(d_tiles)
-    contract = functools.partial(
-        ladder,
-        half,
-        live[:, d_order].T,
-        pick,
-        d_order,
-        [[held["left", s, part] for part in (0, 1, 2, "first", "second")] for s in range(NTV)],
-        (held["chol"], held["other", "chol"]),
-        [(held["block", s, i], held["other", s, i]) for s in range(1, NTV) for i in range(NTV)],
-        held["amp"],
-    )
-    early = contract(0, jnp.bfloat16)
+        if slot == last - 1:
+            held["sum"] = contract((0, 2), None, 0, jnp.float32)
+            waiting[slot + 1].append("sum")
+    early = contract((1, 3), held["sum"], 0, jnp.bfloat16)
     moved = [shift(early[t], "left", NTV, t + 1) for t in range(NTV // 2)]
-    late = contract(1, jnp.float32)
+    late = contract((1, 3), held["sum"], 1, jnp.float32)
     moved += [
         shift(late[t].astype(jnp.bfloat16), "left", NTV, NTV // 2 + t + 1) for t in range(NTV // 2 - 1)
     ]

time: 298 us -> 296 us (level)
    ppermute x12, waiting for transfers between devices: 79.4 us -> 70.8 us  [on_square(): lax.ppermute(held['block', s - 1, (i + 1) % NTV], 'left', ring)]
    ppermute x3, waiting for transfers between devices: 13.4 us -> 20.4 us  [shift(): lax.ppermute(value, axis, [(i, (i + step) % size) for i in range(size)])]
    pallas_call x2 -> x3, Pallas kernels: 83.7 us -> 83.4 us  [ladder(): pl.pallas_call(functools.partial(ladder_kernel, steps, count, tile_count,...]
  transfers between devices with their start and end apart: 52 -> 52, of which waited for: 27 -> 27; matrix products, arithmetic and copies ran while one was open for 2% -> 3% of each run, Pallas kernels for 14% -> 20%
where the time goes in v5:
time: 296 us; the launch traced here: 294 us
  waiting for transfers between devices  125 us (42%)
  Pallas kernels  83.4 us (28%)
  starting transfers between devices  51.8 us (18%)
  local copies, waits for them, and re-layouts  14.7 us (5%)
  between operations  14 us (5%)
  other arithmetic  5.06 us (2%)
    pallas_call x3, Pallas kernels, ladder(): pl.pallas_call(functools.partial(ladder_kernel, steps, count, tile_count,...  83.4 us
    ppermute x12, waiting for transfers between devices, on_square(): lax.ppermute(held['block', s - 1, (i + 1) % NTV], 'left', ring)  70.8 us
    ppermute x36, waiting for transfers between devices, partner(): return lax.ppermute(value, axis, [(i, i ^ flip) for i in range(size)])  33.5 us
    ppermute x36, starting transfers between devices, partner(): return lax.ppermute(value, axis, [(i, i ^ flip) for i in range(size)])  26.5 us
    ppermute x12, starting transfers between devices, on_square(): lax.ppermute(held['block', s - 1, (i + 1) % NTV], 'left', ring)  21.6 us
    ppermute x3, waiting for transfers between devices, shift(): lax.ppermute(value, axis, [(i, (i + step) % size) for i in range(size)])  20.4 us
  transfers between devices with their start and end apart: 52, of which 27 were waited for; matrix products, arithmetic and copies ran while one was open for 3% of the time, Pallas kernels for 20%

profile of v5, /device:TPU:8, one launch (start us, length us, event | category | flops | bytes accessed | tf_op | source)
XLA Modules:
  0.0 293.6 jit_solution(17142205966027273121)
XLA Ops:
  6.5 1.8 constant_dynamic-slice_fusion
  8.7 1.9 collective-permute-start.1
  10.7 1.5 collective-permute-start.2
  12.2 11.1 %collective-permute-done.refs_24_ = bf16[1,512,512]{2,1,0:T(8,128)(2,1)S(1)} collective-permute-done((bf16[1,512,512]{2,1,0:T(8,128)(2,1)S(1)}, bf16[1,512,512]{2,1,0:T(8,128)(2,1)S(1)}, u32[]{:S(2)}, u32[]{:S(2)}) %collective-permute-start) | collective-permute-done | bytes 524320 | tf_op jit(solution)/shard_map/ppermute | solution.py:293
  23.8 2.6 collective-permute-start.5
  26.6 1.6 collective-permute-start.6
  28.8 10.3 %collective-permute-done.5.refs_22_ = bf16[1,512,512]{2,1,0:T(8,128)(2,1)} collective-permute-done((bf16[1,512,512]{2,1,0:T(8,128)(2,1)S(1)}, bf16[1,512,512]{2,1,0:T(8,128)(2,1)}, u32[]{:S(2)}, u32[]{:S(2)}) %collective-permute-start.5) | collective-permute-done | bytes 524320 | tf_op jit(solution)/shard_map/ppermute | solution.py:293
  39.1 1.7 collective-permute-start.9
  41.8 1.5 collective-permute-start.11
  43.3 2.5 collective-permute-start.13
  45.8 9.0 %collective-permute-done.9.refs_22_ = bf16[1,512,512]{2,1,0:T(8,128)(2,1)S(1)} collective-permute-done((bf16[1,512,512]{2,1,0:T(8,128)(2,1)S(1)}, bf16[1,512,512]{2,1,0:T(8,128)(2,1)S(1)}, u32[]{:S(2)}, u32[]{:S(2)}) %collective-permute-start.9) | collective-permute-done | bytes 524320 | tf_op jit(solution)/shard_map/ppermute | solution.py:293
  55.2 1.6 collective-permute-start.14
  58.1 6.8 %collective-permute-done.13.refs_26_ = bf16[1,512,512]{2,1,0:T(8,128)(2,1)} collective-permute-done((bf16[1,512,512]{2,1,0:T(8,128)(2,1)S(1)}, bf16[1,512,512]{2,1,0:T(8,128)(2,1)}, u32[]{:S(2)}, u32[]{:S(2)}) %collective-permute-start.13) | collective-permute-done | bytes 524320 | tf_op jit(solution)/shard_map/ppermute | solution.py:293
  66.1 1.6 maximum_maximum_fusion
  67.7 2.5 collective-permute-start.17
  71.6 2.0 collective-permute-start.21
  73.6 10.1 %collective-permute-done.17.refs_26_ = bf16[1,512,512]{2,1,0:T(8,128)(2,1)S(1)} collective-permute-done((bf16[1,512,512]{2,1,0:T(8,128)(2,1)}, bf16[1,512,512]{2,1,0:T(8,128)(2,1)S(1)}, u32[]{:S(2)}, u32[]{:S(2)}) %collective-permute-start.17) | collective-permute-done | bytes 524320 | tf_op jit(solution)/shard_map/ppermute | solution.py:293
  87.3 2.4 collective-permute-start.25
  89.7 5.3 %collective-permute-done.21.refs_30_ = bf16[1,512,512]{2,1,0:T(8,128)(2,1)S(1)} collective-permute-done((bf16[1,512,512]{2,1,0:T(8,128)(2,1)}, bf16[1,512,512]{2,1,0:T(8,128)(2,1)S(1)}, u32[]{:S(2)}, u32[]{:S(2)}) %collective-permute-start.21) | collective-permute-done | bytes 524320 | tf_op jit(solution)/shard_map/ppermute | solution.py:293
  97.1 1.5 collective-permute-start.29
  98.6 7.5 %collective-permute-done.25.refs_24_ = bf16[1,512,512]{2,1,0:T(8,128)(2,1)S(1)} collective-permute-done((bf16[1,512,512]{2,1,0:T(8,128)(2,1)S(1)}, bf16[1,512,512]{2,1,0:T(8,128)(2,1)S(1)}, u32[]{:S(2)}, u32[]{:S(2)}) %collective-permute-start.25) | collective-permute-done | bytes 524320 | tf_op jit(solution)/shard_map/ppermute | solution.py:293
  106.2 3.2 %collective-permute-done.26.refs_11_ = bf16[512,512]{1,0:T(8,128)(2,1)S(1)} collective-permute-done((bf16[512,512]{1,0:T(8,128)(2,1)S(1)}, bf16[512,512]{1,0:T(8,128)(2,1)S(1)}, u32[]{:S(2)}, u32[]{:S(2)}) %collective-permute-start.26) | collective-permute-done | bytes 524320 | tf_op jit(solution)/shard_map/ppermute | solution.py:199
  113.5 1.3 collective-permute-start.33
  116.0 3.0 %collective-permute-done.30.refs_13_ = bf16[256,512]{1,0:T(8,128)(2,1)S(1)} collective-permute-done((bf16[256,512]{1,0:T(8,128)(2,1)S(1)}, bf16[256,512]{1,0:T(8,128)(2,1)S(1)}, u32[]{:S(2)}, u32[]{:S(2)}) %collective-permute-start.30) | collective-permute-done | bytes 262176 | tf_op jit(solution)/shard_map/ppermute | solution.py:199
  119.0 1.8 collective-permute-done.31.refs_14_
  121.8 1.2 collective-permute-start.35
  123.0 1.6 collective-permute-start.37
  124.6 4.8 %collective-permute-done.33.refs_28_ = bf16[1,512,512]{2,1,0:T(8,128)(2,1)} collective-permute-done((bf16[1,512,512]{2,1,0:T(8,128)(2,1)S(1)}, bf16[1,512,512]{2,1,0:T(8,128)(2,1)}, u32[]{:S(2)}, u32[]{:S(2)}) %collective-permute-start.33) | collective-permute-done | bytes 524320 | tf_op jit(solution)/shard_map/ppermute | solution.py:293
  129.4 5.8 %collective-permute-done.34.refs_16_ = bf16[512,512]{1,0:T(8,128)(2,1)S(1)} collective-permute-done((bf16[512,512]{1,0:T(8,128)(2,1)S(1)}, bf16[512,512]{1,0:T(8,128)(2,1)S(1)}, u32[]{:S(2)}, u32[]{:S(2)}) %collective-permute-start.34) | collective-permute-done | bytes 524320 | tf_op jit(solution)/shard_map/ppermute | solution.py:199
  136.0 1.2 collective-permute-start.38
  139.0 1.8 collective-permute-start.41
  140.8 4.0 %collective-permute-done.38.refs_18_ = bf16[256,512]{1,0:T(8,128)(2,1)} collective-permute-done((bf16[256,512]{1,0:T(8,128)(2,1)S(1)}, bf16[256,512]{1,0:T(8,128)(2,1)}, u32[]{:S(2)}, u32[]{:S(2)}) %collective-permute-start.38) | collective-permute-done | bytes 262176 | tf_op jit(solution)/shard_map/ppermute | solution.py:199
  148.7 1.6 collective-permute-start.43
  150.2 4.8 %collective-permute-done.41.refs_30_ = bf16[1,512,512]{2,1,0:T(8,128)(2,1)} collective-permute-done((bf16[1,512,512]{2,1,0:T(8,128)(2,1)}, bf16[1,512,512]{2,1,0:T(8,128)(2,1)}, u32[]{:S(2)}, u32[]{:S(2)}) %collective-permute-start.41) | collective-permute-done | bytes 524320 | tf_op jit(solution)/shard_map/ppermute | solution.py:293
  155.1 36.1 %shard_map.37.refs_35_ = f32[4,4,128,512]{3,2,1,0:T(8,128)} custom-call(s32[1]{0:T(128)} %bitcast.half_ref, s32[2,4]{1,0:T(2,128)} %gather_fusion.2, s32[4]{0:T(128)} %fusion.4.pick_ref, s32[2]{0:T(128)} %pad_add_fusion.1.tile_ref, bf16[512,512]{1,0:T(8,128)(2,1)} %bitcast.62, bf16[512,512]{1,0:T(8,128)(2,1)} %copy-done.10, bf16[512,512]{1,0:T(8,128)(2,1)} %copy-done.11, ...), custom_call_target="tpu_custom_call" | custom-call | flops 21474836480 | bytes 29360128 | tf_op jit(solution)/shard_map/pallas_call | solution.py:170
  194.4 23.4 %shard_map.39 = bf16[2,4,128,512]{3,2,1,0:T(8,128)(2,1)} custom-call(s32[1]{0:T(128)} %bitcast.half_ref, s32[2,2]{1,0:T(2,128)} %get-tuple-element.145.live_ref, s32[2]{0:T(128)} %get-tuple-element.147.pick_ref, s32[2]{0:T(128)} %pad_add_fusion.tile_ref, bf16[512,512]{1,0:T(8,128)(2,1)} %bitcast.63, bf16[512,512]{1,0:T(8,128)(2,1)} %copy-done.10, ...), custom_call_target="tpu_custom_call" | custom-call | flops 10737418240 | bytes 29360128 | tf_op jit(solution)/shard_map/pallas_call | solution.py:170
  217.8 1.3 slice_bitcast_fusion.2
  219.1 2.0 collective-permute-start.45
  221.1 1.5 collective-permute-start.46
  222.6 23.9 %shard_map.38 = f32[2,4,128,512]{3,2,1,0:T(8,128)} custom-call(s32[1]{0:T(128)} %bitcast.half_ref, s32[2,2]{1,0:T(2,128)} %get-tuple-element.146.live_ref, s32[2]{0:T(128)} %get-tuple-element.148.pick_ref, s32[2]{0:T(128)} %pad_add_fusion.tile_ref, bf16[512,512]{1,0:T(8,128)(2,1)} %bitcast.64, bf16[512,512]{1,0:T(8,128)(2,1)} %copy-done.10, ...), custom_call_target="tpu_custom_call" | custom-call | flops 10737418240 | bytes 29360128 | tf_op jit(solution)/shard_map/pallas_call | solution.py:170
  246.5 1.3 fusion.3
  247.9 18.4 %collective-permute-done.46 = bf16[4,128,512]{2,1,0:T(8,128)(2,1)S(1)} collective-permute-done((bf16[4,128,512]{2,1,0:T(8,128)(2,1)S(1)}, bf16[4,128,512]{2,1,0:T(8,128)(2,1)S(1)}, u32[]{:S(2)}, u32[]{:S(2)}) %collective-permute-start.46) | collective-permute-done | bytes 524320 | tf_op jit(solution)/shard_map/ppermute | solution.py:203
  266.4 1.9 collective-permute-done.47
  268.3 1.5 fusion.2
  272.0 1.4 collective-permute-start.50
  273.5 5.7 %collective-permute-done.48 = f32[4,128,128]{2,1,0:T(8,128)S(1)} collective-permute-done((f32[4,128,128]{2,1,0:T(8,128)S(1)}, f32[4,128,128]{2,1,0:T(8,128)S(1)}, u32[]{:S(2)}, u32[]{:S(2)}) %collective-permute-start.48) | collective-permute-done | bytes 262176 | tf_op jit(solution)/shard_map/ppermute | solution.py:199
  279.2 5.2 %collective-permute-done.49 = f32[4,128,128]{2,1,0:T(8,128)S(1)} collective-permute-done((f32[4,128,128]{2,1,0:T(8,128)S(1)}, f32[4,128,128]{2,1,0:T(8,128)S(1)}, u32[]{:S(2)}, u32[]{:S(2)}) %collective-permute-start.49) | collective-permute-done | bytes 262176 | tf_op jit(solution)/shard_map/ppermute | solution.py:199
  285.1 1.6 copy.16
  (180 shorter events, 31.4 us)
Async XLA Ops:
  6.5 103.7 %all-gather.2.cloned.1.call-start = ((), (), s32[]{:S(2)}) async-start(), calls=%async_computation | async-start | bytes 6291456 | tf_op jit(solution)/shard_map/all_gather | solution.py:311
  8.7 14.6 %collective-permute-start = (bf16[1,512,512]{2,1,0:T(8,128)(2,1)S(1)}, bf16[1,512,512]{2,1,0:T(8,128)(2,1)S(1)}, u32[]{:S(2)}, u32[]{:S(2)}) collective-permute-start(bf16[1,512,512]{2,1,0:T(8,128)(2,1)S(1)} %get-tuple-element.70), channel_id=1, source_target_pairs={{0,16},{16,24},{24,8},{8,0},{1,17},{17,25},{25,9},{9,1},{2,18},{18... | collective-permute-start | bytes 1572872 | tf_op jit(solution)/shard_map/ppermute | solution.py:293
  8.7 14.6 %collective-permute-start.1 = (bf16[512,512]{1,0:T(8,128)(2,1)S(1)}, bf16[512,512]{1,0:T(8,128)(2,1)S(1)}, u32[]{:S(2)}, u32[]{:S(2)}) collective-permute-start(bf16[512,512]{1,0:T(8,128)(2,1)S(1)} %bitcast.60), channel_id=1, source_target_pairs={{0,2},{2,0},{4,6},{6,4},{1,3},{3,1},{5,7},{7,5},{8,10},{10,8},{12,... | collective-permute-start | bytes 1572872 | tf_op jit(solution)/shard_map/ppermute | solution.py:199
  10.7 13.1 %collective-permute-start.2 = (bf16[512,512]{1,0:T(8,128)(2,1)S(1)}, bf16[512,512]{1,0:T(8,128)(2,1)S(1)}, u32[]{:S(2)}, u32[]{:S(2)}) collective-permute-start(bf16[512,512]{1,0:T(8,128)(2,1)S(1)} %bitcast.61), channel_id=1, source_target_pairs={{0,4},{2,6},{4,0},{6,2},{1,5},{3,7},{5,1},{7,3},{8,12},{10,14},{12... | collective-permute-start | bytes 1572872 | tf_op jit(solution)/shard_map/ppermute | solution.py:199
  23.8 17.1 %collective-permute-start.3 = (bf16[4,512,512]{2,1,0:T(8,128)(2,1)S(1)}, bf16[4,512,512]{2,1,0:T(8,128)(2,1)S(1)}, u32[]{:S(2)}, u32[]{:S(2)}) collective-permute-start(bf16[4,512,512]{2,1,0:T(8,128)(2,1)S(1)} %copy-done.1), channel_id=1, source_target_pairs={{0,1},{1,0},{2,3},{3,2},{4,5},{5,4},{6,7},{7,6},{8,9},{9,8},{10,11... | collective-permute-start | bytes 6291464 | tf_op jit(solution)/shard_map/ppermute | solution.py:199
  23.8 15.3 %collective-permute-start.5 = (bf16[1,512,512]{2,1,0:T(8,128)(2,1)S(1)}, bf16[1,512,512]{2,1,0:T(8,128)(2,1)}, u32[]{:S(2)}, u32[]{:S(2)}) collective-permute-start(bf16[1,512,512]{2,1,0:T(8,128)(2,1)S(1)} %get-tuple-element.77), channel_id=1, source_target_pairs={{0,16},{16,24},{24,8},{8,0},{1,17},{17,25},{25,9},{9,1},{2,18},{18... | collective-permute-start | bytes 1572872 | tf_op jit(solution)/shard_map/ppermute | solution.py:293
  26.4 14.4 %collective-permute-start.4 = (bf16[1,512,512]{2,1,0:T(8,128)(2,1)S(1)}, bf16[1,512,512]{2,1,0:T(8,128)(2,1)S(1)}, u32[]{:S(2)}, u32[]{:S(2)}) collective-permute-start(bf16[1,512,512]{2,1,0:T(8,128)(2,1)S(1)} %collective-permute-done.refs_24_), channel_id=1, source_target_pairs={{0,1},{1,0},{2,3},{3,2},{4,5},{5,4},{6,7},{7,6},{8,9},{9,8},{10,11... | collective-permute-start | bytes 1572872 | tf_op jit(solution)/shard_map/ppermute | solution.py:199
  26.6 14.2 %collective-permute-start.6 = (bf16[256,512]{1,0:T(8,128)(2,1)S(1)}, bf16[256,512]{1,0:T(8,128)(2,1)S(1)}, u32[]{:S(2)}, u32[]{:S(2)}) collective-permute-start(bf16[256,512]{1,0:T(8,128)(2,1)S(1)} %slice.69), channel_id=1, source_target_pairs={{0,4},{2,6},{4,0},{6,2},{1,5},{3,7},{5,1},{7,3},{8,12},{10,14},{12... | collective-permute-start | bytes 786440 | tf_op jit(solution)/shard_map/ppermute | solution.py:199
  28.2 12.6 %collective-permute-start.7 = (bf16[256,512]{1,0:T(8,128)(2,1)S(1)}, bf16[256,512]{1,0:T(8,128)(2,1)S(1)}, u32[]{:S(2)}, u32[]{:S(2)}) collective-permute-start(bf16[256,512]{1,0:T(8,128)(2,1)S(1)} %slice.70), channel_id=1, source_target_pairs={{0,2},{2,0},{4,6},{6,4},{1,3},{3,1},{5,7},{7,5},{8,10},{10,8},{12,... | collective-permute-start | bytes 786440 | tf_op jit(solution)/shard_map/ppermute | solution.py:199
  39.1 15.7 %collective-permute-start.9 = (bf16[1,512,512]{2,1,0:T(8,128)(2,1)S(1)}, bf16[1,512,512]{2,1,0:T(8,128)(2,1)S(1)}, u32[]{:S(2)}, u32[]{:S(2)}) collective-permute-start(bf16[1,512,512]{2,1,0:T(8,128)(2,1)S(1)} %get-tuple-element.81), channel_id=1, source_target_pairs={{0,16},{16,24},{24,8},{8,0},{1,17},{17,25},{25,9},{9,1},{2,18},{18... | collective-permute-start | bytes 1572872 | tf_op jit(solution)/shard_map/ppermute | solution.py:293
  40.9 14.0 %collective-permute-start.10 = (bf16[4,512,128]{2,1,0:T(8,128)(2,1)S(1)}, bf16[4,512,128]{2,1,0:T(8,128)(2,1)S(1)}, u32[]{:S(2)}, u32[]{:S(2)}) collective-permute-start(bf16[4,512,128]{2,1,0:T(8,128)(2,1)S(1)} %bitcast.83), channel_id=1, source_target_pairs={{0,2},{2,0},{4,6},{6,4},{1,3},{3,1},{5,7},{7,5},{8,10},{10,8},{12,... | collective-permute-start | bytes 1572872 | tf_op jit(solution)/shard_map/ppermute | solution.py:199
  41.8 13.2 %collective-permute-start.11 = (bf16[4,512,128]{2,1,0:T(8,128)(2,1)S(1)}, bf16[4,512,128]{2,1,0:T(8,128)(2,1)S(1)}, u32[]{:S(2)}, u32[]{:S(2)}) collective-permute-start(bf16[4,512,128]{2,1,0:T(8,128)(2,1)S(1)} %bitcast.84), channel_id=1, source_target_pairs={{0,4},{2,6},{4,0},{6,2},{1,5},{3,7},{5,1},{7,3},{8,12},{10,14},{12... | collective-permute-start | bytes 1572872 | tf_op jit(solution)/shard_map/ppermute | solution.py:199
  43.3 11.7 %collective-permute-start.8 = (bf16[1,512,512]{2,1,0:T(8,128)(2,1)}, bf16[1,512,512]{2,1,0:T(8,128)(2,1)S(1)}, u32[]{:S(2)}, u32[]{:S(2)}) collective-permute-start(bf16[1,512,512]{2,1,0:T(8,128)(2,1)} %collective-permute-done.5.refs_22_), channel_id=1, source_target_pairs={{0,1},{1,0},{2,3},{3,2},{4,5},{5,4},{6,7},{7,6},{8,9},{9,8},{10,11... | collective-permute-start | bytes 1572872 | tf_op jit(solution)/shard_map/ppermute | solution.py:199
  43.3 21.5 %collective-permute-start.13 = (bf16[1,512,512]{2,1,0:T(8,128)(2,1)S(1)}, bf16[1,512,512]{2,1,0:T(8,128)(2,1)}, u32[]{:S(2)}, u32[]{:S(2)}) collective-permute-start(bf16[1,512,512]{2,1,0:T(8,128)(2,1)S(1)} %collective-permute-done.refs_24_), channel_id=1, source_target_pairs={{0,16},{16,24},{24,8},{8,0},{1,17},{17,25},{25,9},{9,1},{2,18},{18... | collective-permute-start | bytes 1572872 | tf_op jit(solution)/shard_map/ppermute | solution.py:293
  55.0 10.2 %collective-permute-start.12 = (bf16[1,512,512]{2,1,0:T(8,128)(2,1)S(1)}, bf16[1,512,512]{2,1,0:T(8,128)(2,1)S(1)}, u32[]{:S(2)}, u32[]{:S(2)}) collective-permute-start(bf16[1,512,512]{2,1,0:T(8,128)(2,1)S(1)} %collective-permute-done.9.refs_22_), channel_id=1, source_target_pairs={{0,1},{1,0},{2,3},{3,2},{4,5},{5,4},{6,7},{7,6},{8,9},{9,8},{10,11... | collective-permute-start | bytes 1572872 | tf_op jit(solution)/shard_map/ppermute | solution.py:199
  55.2 9.7 %collective-permute-start.14 = (bf16[2,512,128]{2,1,0:T(8,128)(2,1)S(1)}, bf16[2,512,128]{2,1,0:T(8,128)(2,1)S(1)}, u32[]{:S(2)}, u32[]{:S(2)}) collective-permute-start(bf16[2,512,128]{2,1,0:T(8,128)(2,1)S(1)} %slice.71), channel_id=1, source_target_pairs={{0,4},{2,6},{4,0},{6,2},{1,5},{3,7},{5,1},{7,3},{8,12},{10,14},{12... | collective-permute-start | bytes 786440 | tf_op jit(solution)/shard_map/ppermute | solution.py:199
  67.7 16.0 %collective-permute-start.17 = (bf16[1,512,512]{2,1,0:T(8,128)(2,1)}, bf16[1,512,512]{2,1,0:T(8,128)(2,1)S(1)}, u32[]{:S(2)}, u32[]{:S(2)}) collective-permute-start(bf16[1,512,512]{2,1,0:T(8,128)(2,1)} %collective-permute-done.5.refs_22_), channel_id=1, source_target_pairs={{0,16},{16,24},{24,8},{8,0},{1,17},{17,25},{25,9},{9,1},{2,18},{18... | collective-permute-start | bytes 1572872 | tf_op jit(solution)/shard_map/ppermute | solution.py:293
  70.2 13.5 %collective-permute-start.16 = (bf16[1,512,512]{2,1,0:T(8,128)(2,1)}, bf16[1,512,512]{2,1,0:T(8,128)(2,1)S(1)}, u32[]{:S(2)}, u32[]{:S(2)}) collective-permute-start(bf16[1,512,512]{2,1,0:T(8,128)(2,1)} %collective-permute-done.13.refs_26_), channel_id=1, source_target_pairs={{0,1},{1,0},{2,3},{3,2},{4,5},{5,4},{6,7},{7,6},{8,9},{9,8},{10,11... | collective-permute-start | bytes 1572872 | tf_op jit(solution)/shard_map/ppermute | solution.py:199
  70.2 14.3 %collective-permute-start.18 = (bf16[512,512]{1,0:T(8,128)(2,1)S(1)}, bf16[512,512]{1,0:T(8,128)(2,1)S(1)}, u32[]{:S(2)}, u32[]{:S(2)}) collective-permute-start(bf16[512,512]{1,0:T(8,128)(2,1)S(1)} %bitcast.65), channel_id=1, source_target_pairs={{0,2},{2,0},{4,6},{6,4},{1,3},{3,1},{5,7},{7,5},{8,10},{10,8},{12,... | collective-permute-start | bytes 1572872 | tf_op jit(solution)/shard_map/ppermute | solution.py:199
  71.1 14.1 %collective-permute-start.19 = (bf16[512,512]{1,0:T(8,128)(2,1)S(1)}, bf16[512,512]{1,0:T(8,128)(2,1)S(1)}, u32[]{:S(2)}, u32[]{:S(2)}) collective-permute-start(bf16[512,512]{1,0:T(8,128)(2,1)S(1)} %bitcast.66), channel_id=1, source_target_pairs={{0,4},{2,6},{4,0},{6,2},{1,5},{3,7},{5,1},{7,3},{8,12},{10,14},{12... | collective-permute-start | bytes 1572872 | tf_op jit(solution)/shard_map/ppermute | solution.py:199
  71.6 23.3 %collective-permute-start.21 = (bf16[1,512,512]{2,1,0:T(8,128)(2,1)}, bf16[1,512,512]{2,1,0:T(8,128)(2,1)S(1)}, u32[]{:S(2)}, u32[]{:S(2)}) collective-permute-start(bf16[1,512,512]{2,1,0:T(8,128)(2,1)} %collective-permute-done.13.refs_26_), channel_id=1, source_target_pairs={{0,16},{16,24},{24,8},{8,0},{1,17},{17,25},{25,9},{9,1},{2,18},{18... | collective-permute-start | bytes 1572872 | tf_op jit(solution)/shard_map/ppermute | solution.py:293
  85.2 9.8 %collective-permute-start.20 = (bf16[1,512,512]{2,1,0:T(8,128)(2,1)S(1)}, bf16[1,512,512]{2,1,0:T(8,128)(2,1)S(1)}, u32[]{:S(2)}, u32[]{:S(2)}) collective-permute-start(bf16[1,512,512]{2,1,0:T(8,128)(2,1)S(1)} %collective-permute-done.17.refs_26_), channel_id=1, source_target_pairs={{0,1},{1,0},{2,3},{3,2},{4,5},{5,4},{6,7},{7,6},{8,9},{9,8},{10,11... | collective-permute-start | bytes 1572872 | tf_op jit(solution)/shard_map/ppermute | solution.py:199
  85.2 9.8 %collective-permute-start.22 = (bf16[256,512]{1,0:T(8,128)(2,1)S(1)}, bf16[256,512]{1,0:T(8,128)(2,1)S(1)}, u32[]{:S(2)}, u32[]{:S(2)}) collective-permute-start(bf16[256,512]{1,0:T(8,128)(2,1)S(1)} %slice.73), channel_id=1, source_target_pairs={{0,4},{2,6},{4,0},{6,2},{1,5},{3,7},{5,1},{7,3},{8,12},{10,14},{12... | collective-permute-start | bytes 786440 | tf_op jit(solution)/shard_map/ppermute | solution.py:199
  85.8 9.1 %collective-permute-start.23 = (bf16[256,512]{1,0:T(8,128)(2,1)S(1)}, bf16[256,512]{1,0:T(8,128)(2,1)S(1)}, u32[]{:S(2)}, u32[]{:S(2)}) collective-permute-start(bf16[256,512]{1,0:T(8,128)(2,1)S(1)} %slice.74), channel_id=1, source_target_pairs={{0,2},{2,0},{4,6},{6,4},{1,3},{3,1},{5,7},{7,5},{8,10},{10,8},{12,... | collective-permute-start | bytes 786440 | tf_op jit(solution)/shard_map/ppermute | solution.py:199
  87.3 18.9 %collective-permute-start.25 = (bf16[1,512,512]{2,1,0:T(8,128)(2,1)S(1)}, bf16[1,512,512]{2,1,0:T(8,128)(2,1)S(1)}, u32[]{:S(2)}, u32[]{:S(2)}) collective-permute-start(bf16[1,512,512]{2,1,0:T(8,128)(2,1)S(1)} %get-tuple-element.100), channel_id=1, source_target_pairs={{0,16},{16,24},{24,8},{8,0},{1,17},{17,25},{25,9},{9,1},{2,18},{18... | collective-permute-start | bytes 1572872 | tf_op jit(solution)/shard_map/ppermute | solution.py:293
  95.0 11.2 %collective-permute-start.24 = (bf16[1,512,512]{2,1,0:T(8,128)(2,1)S(1)}, bf16[1,512,512]{2,1,0:T(8,128)(2,1)S(1)}, u32[]{:S(2)}, u32[]{:S(2)}) collective-permute-start(bf16[1,512,512]{2,1,0:T(8,128)(2,1)S(1)} %collective-permute-done.21.refs_30_), channel_id=1, source_target_pairs={{0,1},{1,0},{2,3},{3,2},{4,5},{5,4},{6,7},{7,6},{8,9},{9,8},{10,11... | collective-permute-start | bytes 1572872 | tf_op jit(solution)/shard_map/ppermute | solution.py:199
  95.1 14.3 %collective-permute-start.26 = (bf16[512,512]{1,0:T(8,128)(2,1)S(1)}, bf16[512,512]{1,0:T(8,128)(2,1)S(1)}, u32[]{:S(2)}, u32[]{:S(2)}) collective-permute-start(bf16[512,512]{1,0:T(8,128)(2,1)S(1)} %bitcast.71), channel_id=1, source_target_pairs={{0,2},{2,0},{4,6},{6,4},{1,3},{3,1},{5,7},{7,5},{8,10},{10,8},{12,... | collective-permute-start | bytes 1572872 | tf_op jit(solution)/shard_map/ppermute | solution.py:199
  96.1 14.1 %collective-permute-start.27 = (bf16[512,512]{1,0:T(8,128)(2,1)S(1)}, bf16[512,512]{1,0:T(8,128)(2,1)}, u32[]{:S(2)}, u32[]{:S(2)}) collective-permute-start(bf16[512,512]{1,0:T(8,128)(2,1)S(1)} %bitcast.72), channel_id=1, source_target_pairs={{0,4},{2,6},{4,0},{6,2},{1,5},{3,7},{5,1},{7,3},{8,12},{10,14},{12... | collective-permute-start | bytes 1572872 | tf_op jit(solution)/shard_map/ppermute | solution.py:199
  97.1 18.9 %collective-permute-start.29 = (bf16[1,512,512]{2,1,0:T(8,128)(2,1)S(1)}, bf16[1,512,512]{2,1,0:T(8,128)(2,1)}, u32[]{:S(2)}, u32[]{:S(2)}) collective-permute-start(bf16[1,512,512]{2,1,0:T(8,128)(2,1)S(1)} %collective-permute-done.9.refs_22_), channel_id=1, source_target_pairs={{0,16},{16,24},{24,8},{8,0},{1,17},{17,25},{25,9},{9,1},{2,18},{18... | collective-permute-start | bytes 1572872 | tf_op jit(solution)/shard_map/ppermute | solution.py:293
  110.2 10.6 %collective-permute-start.28 = (bf16[1,512,512]{2,1,0:T(8,128)(2,1)}, bf16[1,512,512]{2,1,0:T(8,128)(2,1)S(1)}, u32[]{:S(2)}, u32[]{:S(2)}) collective-permute-start(bf16[1,512,512]{2,1,0:T(8,128)(2,1)} %copy-done.24), channel_id=1, source_target_pairs={{0,1},{1,0},{2,3},{3,2},{4,5},{5,4},{6,7},{7,6},{8,9},{9,8},{10,11... | collective-permute-start | bytes 1572872 | tf_op jit(solution)/shard_map/ppermute | solution.py:199
  110.2 8.8 %collective-permute-start.30 = (bf16[256,512]{1,0:T(8,128)(2,1)S(1)}, bf16[256,512]{1,0:T(8,128)(2,1)S(1)}, u32[]{:S(2)}, u32[]{:S(2)}) collective-permute-start(bf16[256,512]{1,0:T(8,128)(2,1)S(1)} %slice.75), channel_id=1, source_target_pairs={{0,4},{2,6},{4,0},{6,2},{1,5},{3,7},{5,1},{7,3},{8,12},{10,14},{12... | collective-permute-start | bytes 786440 | tf_op jit(solution)/shard_map/ppermute | solution.py:199
  113.5 15.9 %collective-permute-start.33 = (bf16[1,512,512]{2,1,0:T(8,128)(2,1)S(1)}, bf16[1,512,512]{2,1,0:T(8,128)(2,1)}, u32[]{:S(2)}, u32[]{:S(2)}) collective-permute-start(bf16[1,512,512]{2,1,0:T(8,128)(2,1)S(1)} %copy-done.25), channel_id=1, source_target_pairs={{0,16},{16,24},{24,8},{8,0},{1,17},{17,25},{25,9},{9,1},{2,18},{18... | collective-permute-start | bytes 1572872 | tf_op jit(solution)/shard_map/ppermute | solution.py:293
  120.8 8.6 %collective-permute-start.32 = (bf16[1,512,512]{2,1,0:T(8,128)(2,1)}, bf16[1,512,512]{2,1,0:T(8,128)(2,1)S(1)}, u32[]{:S(2)}, u32[]{:S(2)}) collective-permute-start(bf16[1,512,512]{2,1,0:T(8,128)(2,1)} %collective-permute-done.29.refs_28_), channel_id=1, source_target_pairs={{0,1},{1,0},{2,3},{3,2},{4,5},{5,4},{6,7},{7,6},{8,9},{9,8},{10,11... | collective-permute-start | bytes 1572872 | tf_op jit(solution)/shard_map/ppermute | solution.py:199
  120.9 14.3 %collective-permute-start.34 = (bf16[512,512]{1,0:T(8,128)(2,1)S(1)}, bf16[512,512]{1,0:T(8,128)(2,1)S(1)}, u32[]{:S(2)}, u32[]{:S(2)}) collective-permute-start(bf16[512,512]{1,0:T(8,128)(2,1)S(1)} %bitcast.78), channel_id=1, source_target_pairs={{0,2},{2,0},{4,6},{6,4},{1,3},{3,1},{5,7},{7,5},{8,10},{10,8},{12,... | collective-permute-start | bytes 1572872 | tf_op jit(solution)/shard_map/ppermute | solution.py:199
  121.8 14.0 %collective-permute-start.35 = (bf16[512,512]{1,0:T(8,128)(2,1)S(1)}, bf16[512,512]{1,0:T(8,128)(2,1)S(1)}, u32[]{:S(2)}, u32[]{:S(2)}) collective-permute-start(bf16[512,512]{1,0:T(8,128)(2,1)S(1)} %bitcast.79), channel_id=1, source_target_pairs={{0,4},{2,6},{4,0},{6,2},{1,5},{3,7},{5,1},{7,3},{8,12},{10,14},{12... | collective-permute-start | bytes 1572872 | tf_op jit(solution)/shard_map/ppermute | solution.py:199
  123.0 17.8 %collective-permute-start.37 = (bf16[1,512,512]{2,1,0:T(8,128)(2,1)}, bf16[1,512,512]{2,1,0:T(8,128)(2,1)}, u32[]{:S(2)}, u32[]{:S(2)}) collective-permute-start(bf16[1,512,512]{2,1,0:T(8,128)(2,1)} %collective-permute-done.29.refs_28_), channel_id=1, source_target_pairs={{0,16},{16,24},{24,8},{8,0},{1,17},{17,25},{25,9},{9,1},{2,18},{18... | collective-permute-start | bytes 1572872 | tf_op jit(solution)/shard_map/ppermute | solution.py:293
  135.8 9.9 %collective-permute-start.36 = (bf16[1,512,512]{2,1,0:T(8,128)(2,1)}, bf16[1,512,512]{2,1,0:T(8,128)(2,1)}, u32[]{:S(2)}, u32[]{:S(2)}) collective-permute-start(bf16[1,512,512]{2,1,0:T(8,128)(2,1)} %collective-permute-done.33.refs_28_), channel_id=1, source_target_pairs={{0,1},{1,0},{2,3},{3,2},{4,5},{5,4},{6,7},{7,6},{8,9},{9,8},{10,11... | collective-permute-start | bytes 1572872 | tf_op jit(solution)/shard_map/ppermute | solution.py:199
  136.0 8.8 %collective-permute-start.38 = (bf16[256,512]{1,0:T(8,128)(2,1)S(1)}, bf16[256,512]{1,0:T(8,128)(2,1)}, u32[]{:S(2)}, u32[]{:S(2)}) collective-permute-start(bf16[256,512]{1,0:T(8,128)(2,1)S(1)} %slice.77), channel_id=1, source_target_pairs={{0,4},{2,6},{4,0},{6,2},{1,5},{3,7},{5,1},{7,3},{8,12},{10,14},{12... | collective-permute-start | bytes 786440 | tf_op jit(solution)/shard_map/ppermute | solution.py:199
  139.0 16.0 %collective-permute-start.41 = (bf16[1,512,512]{2,1,0:T(8,128)(2,1)}, bf16[1,512,512]{2,1,0:T(8,128)(2,1)}, u32[]{:S(2)}, u32[]{:S(2)}) collective-permute-start(bf16[1,512,512]{2,1,0:T(8,128)(2,1)} %collective-permute-done.33.refs_28_), channel_id=1, source_target_pairs={{0,16},{16,24},{24,8},{8,0},{1,17},{17,25},{25,9},{9,1},{2,18},{18... | collective-permute-start | bytes 1572872 | tf_op jit(solution)/shard_map/ppermute | solution.py:293
  145.7 9.3 %collective-permute-start.40 = (bf16[1,512,512]{2,1,0:T(8,128)(2,1)}, bf16[1,512,512]{2,1,0:T(8,128)(2,1)}, u32[]{:S(2)}, u32[]{:S(2)}) collective-permute-start(bf16[1,512,512]{2,1,0:T(8,128)(2,1)} %collective-permute-done.37.refs_32_), channel_id=1, source_target_pairs={{0,1},{1,0},{2,3},{3,2},{4,5},{5,4},{6,7},{7,6},{8,9},{9,8},{10,11... | collective-permute-start | bytes 1572872 | tf_op jit(solution)/shard_map/ppermute | solution.py:199
  148.7 42.5 %collective-permute-start.43 = (bf16[1,512,512]{2,1,0:T(8,128)(2,1)S(1)}, bf16[1,512,512]{2,1,0:T(8,128)(2,1)S(1)}, u32[]{:S(2)}, u32[]{:S(2)}) collective-permute-start(bf16[1,512,512]{2,1,0:T(8,128)(2,1)S(1)} %collective-permute-done.17.refs_26_), channel_id=1, source_target_pairs={{0,16},{16,24},{24,8},{8,0},{1,17},{17,25},{25,9},{9,1},{2,18},{18... | collective-permute-start | bytes 1572872 | tf_op jit(solution)/shard_map/ppermute | solution.py:293
  155.0 36.2 %collective-permute-start.42 = (bf16[1,512,512]{2,1,0:T(8,128)(2,1)}, bf16[1,512,512]{2,1,0:T(8,128)(2,1)S(1)}, u32[]{:S(2)}, u32[]{:S(2)}) collective-permute-start(bf16[1,512,512]{2,1,0:T(8,128)(2,1)} %collective-permute-done.41.refs_30_), channel_id=1, source_target_pairs={{0,1},{1,0},{2,3},{3,2},{4,5},{5,4},{6,7},{7,6},{8,9},{9,8},{10,11... | collective-permute-start | bytes 1572872 | tf_op jit(solution)/shard_map/ppermute | solution.py:199
  219.1 28.8 %collective-permute-start.45 = (bf16[4,128,512]{2,1,0:T(8,128)(2,1)S(1)}, bf16[4,128,512]{2,1,0:T(8,128)(2,1)S(1)}, u32[]{:S(2)}, u32[]{:S(2)}) collective-permute-start(bf16[4,128,512]{2,1,0:T(8,128)(2,1)S(1)} %get-tuple-element.143), channel_id=1, source_target_pairs={{0,8},{8,16},{16,24},{24,0},{1,9},{9,17},{17,25},{25,1},{2,10},{10... | collective-permute-start | bytes 1572872 | tf_op jit(solution)/shard_map/ppermute | solution.py:203
  221.1 45.2 %collective-permute-start.46 = (bf16[4,128,512]{2,1,0:T(8,128)(2,1)S(1)}, bf16[4,128,512]{2,1,0:T(8,128)(2,1)S(1)}, u32[]{:S(2)}, u32[]{:S(2)}) collective-permute-start(bf16[4,128,512]{2,1,0:T(8,128)(2,1)S(1)} %get-tuple-element.144), channel_id=1, source_target_pairs={{0,16},{8,24},{16,0},{24,8},{1,17},{9,25},{17,1},{25,9},{2,18},{10... | collective-permute-start | bytes 1572872 | tf_op jit(solution)/shard_map/ppermute | solution.py:203
  247.8 20.5 %collective-permute-start.47 = (bf16[4,128,512]{2,1,0:T(8,128)(2,1)S(1)}, bf16[4,128,512]{2,1,0:T(8,128)(2,1)S(1)}, u32[]{:S(2)}, u32[]{:S(2)}) collective-permute-start(bf16[4,128,512]{2,1,0:T(8,128)(2,1)S(1)} %fusion.3), channel_id=1, source_target_pairs={{0,24},{8,0},{16,8},{24,16},{1,25},{9,1},{17,9},{25,17},{2,26},{10... | collective-permute-start | bytes 1572872 | tf_op jit(solution)/shard_map/ppermute | solution.py:203
  269.9 9.2 %collective-permute-start.48 = (f32[4,128,128]{2,1,0:T(8,128)S(1)}, f32[4,128,128]{2,1,0:T(8,128)S(1)}, u32[]{:S(2)}, u32[]{:S(2)}) collective-permute-start(f32[4,128,128]{2,1,0:T(8,128)S(1)} %get-tuple-element.142), channel_id=1, source_target_pairs={{0,2},{2,0},{4,6},{6,4},{1,3},{3,1},{5,7},{7,5},{8,10},{10,8},{12,... | collective-permute-start | bytes 786440 | tf_op jit(solution)/shard_map/ppermute | solution.py:199
  270.8 13.6 %collective-permute-start.49 = (f32[4,128,128]{2,1,0:T(8,128)S(1)}, f32[4,128,128]{2,1,0:T(8,128)S(1)}, u32[]{:S(2)}, u32[]{:S(2)}) collective-permute-start(f32[4,128,128]{2,1,0:T(8,128)S(1)} %get-tuple-element.141), channel_id=1, source_target_pairs={{0,4},{2,6},{4,0},{6,2},{1,5},{3,7},{5,1},{7,3},{8,12},{10,14},{12... | collective-permute-start | bytes 786440 | tf_op jit(solution)/shard_map/ppermute | solution.py:199
  272.0 12.4 %collective-permute-start.50 = (f32[4,128,128]{2,1,0:T(8,128)S(1)}, f32[4,128,128]{2,1,0:T(8,128)S(1)}, u32[]{:S(2)}, u32[]{:S(2)}) collective-permute-start(f32[4,128,128]{2,1,0:T(8,128)S(1)} %get-tuple-element.140), channel_id=1, source_target_pairs={{0,6},{2,4},{4,2},{6,0},{1,7},{3,5},{5,3},{7,1},{8,14},{10,12},{12... | collective-permute-start | bytes 786440 | tf_op jit(solution)/shard_map/ppermute | solution.py:199
  (44 other events, 931.7 us)
Sparse Core Ops, SparseCore 0:
  67.8 13.8 all-gather.1

commit v6 on v5

--- a/solution.py
+++ b/solution.py
@@ -114,17 +114,18 @@
     @pl.when(step >= GROUPS)
     def _():
         k = step - GROUPS
-        lane_group = lax.broadcasted_iota(jnp.int32, (count * group_rows, wide), 1) // TV % GROUPS
+        lane_group = lax.broadcasted_iota(jnp.int32, (a_count, wide), 1) // TV % GROUPS
+        masks = [lane_group == g for g in range(GROUPS)]
+        lanes = GROUPS * TV
         for p in range(2 * half_blocks):
-            mixed = products[k, p]
-            for g in range(1, GROUPS):
-                mixed = jnp.where(lane_group == g, products[(k + GROUPS - g) % GROUPS, p], mixed)
-            mixed = mixed.reshape(count, c_part, a_count, wide)
-            for b in range(2):
+            for t in range(count):
                 for c in range(c_part):
-                    ready[:, 2 * p + b, :, c * GROUPS * TV:(c + 1) * GROUPS * TV] = mixed[
-                        :, c, :, b * GROUPS * TV:(b + 1) * GROUPS * TV
-                    ]
+                    place = pl.ds(t * group_rows + c * a_count, a_count)
+                    mixed = products[k, p, place, :]
+                    for g in range(1, GROUPS):
+                        mixed = jnp.where(masks[g], products[(k + GROUPS - g) % GROUPS, p, place, :], mixed)
+                    for b in range(2):
+                        ready[t, 2 * p + b, :, c * lanes:(c + 1) * lanes] = mixed[:, b * lanes:(b + 1) * lanes]
         amp = jnp.concatenate(
             [
                 amp_ref[0, pl.ds(pl.multiple_of(((k + GROUPS - g) % GROUPS * c_part + c) * TV, TV), TV), :]
@@ -325,7 +326,9 @@
     pieces = []
     for flip in range(NTV):
         piece = summed[:, :, flip * columns:(flip + 1) * columns]
-        pieces.append(partner(piece, "right", NTV, flip) if flip else piece)
+        if flip:
+            piece = partner(piece.astype(jnp.bfloat16), "right", NTV, flip).astype(jnp.float32)
+        pieces.append(piece)
     result = jnp.stack(pieces)[tiles ^ right_index]
     result = result.reshape(NTV, GROUPS, TV // GROUPS, a_count, columns).transpose(0, 3, 2, 1, 4)
     return result.reshape(1, NTV, row_count, columns)

time: 296 us -> 291 us (0.983)
  waiting for transfers between devices: 125 us -> 119 us
    ppermute x36, waiting for transfers between devices: 33.5 us -> 28.1 us  [partner(): return lax.ppermute(value, axis, [(i, i ^ flip) for i in range(size)])]
  transfers between devices with their start and end apart: 52 -> 52, of which waited for: 27 -> 27; matrix products, arithmetic and copies ran while one was open for 3% -> 3% of each run, Pallas kernels for 20% -> 21%
where the time goes in v6:
time: 291 us; the launch traced here: 288 us
  waiting for transfers between devices  119 us (41%)
  Pallas kernels  83.4 us (29%)
  starting transfers between devices  51.8 us (18%)
  local copies, waits for them, and re-layouts  14.8 us (5%)
  between operations  14 us (5%)
  other arithmetic  5.21 us (2%)
    pallas_call x3, Pallas kernels, ladder(): pl.pallas_call(functools.partial(ladder_kernel, steps, count, tile_count,...  83.4 us
    ppermute x12, waiting for transfers between devices, on_square(): lax.ppermute(held['block', s - 1, (i + 1) % NTV], 'left', ring)  70.8 us
    ppermute x36, waiting for transfers between devices, partner(): return lax.ppermute(value, axis, [(i, i ^ flip) for i in range(size)])  28.1 us
    ppermute x36, starting transfers between devices, partner(): return lax.ppermute(value, axis, [(i, i ^ flip) for i in range(size)])  26.5 us
    ppermute x12, starting transfers between devices, on_square(): lax.ppermute(held['block', s - 1, (i + 1) % NTV], 'left', ring)  21.6 us
    ppermute x3, waiting for transfers between devices, shift(): lax.ppermute(value, axis, [(i, (i + step) % size) for i in range(size)])  20.4 us
  transfers between devices with their start and end apart: 52, of which 27 were waited for; matrix products, arithmetic and copies ran while one was open for 3% of the time, Pallas kernels for 21%

profile of v6, /device:TPU:8, one launch (start us, length us, event | category | flops | bytes accessed | tf_op | source)
XLA Modules:
  0.0 288.5 jit_solution(10805690912820574437)
XLA Ops:
  6.5 1.8 constant_dynamic-slice_fusion
  8.7 1.9 collective-permute-start.1
  10.7 1.5 collective-permute-start.2
  12.2 11.1 %collective-permute-done.refs_24_ = bf16[1,512,512]{2,1,0:T(8,128)(2,1)S(1)} collective-permute-done((bf16[1,512,512]{2,1,0:T(8,128)(2,1)S(1)}, bf16[1,512,512]{2,1,0:T(8,128)(2,1)S(1)}, u32[]{:S(2)}, u32[]{:S(2)}) %collective-permute-start) | collective-permute-done | bytes 524320 | tf_op jit(solution)/shard_map/ppermute | solution.py:294
  23.8 2.6 collective-permute-start.5
  26.6 1.6 collective-permute-start.6
  28.8 10.3 %collective-permute-done.5.refs_22_ = bf16[1,512,512]{2,1,0:T(8,128)(2,1)} collective-permute-done((bf16[1,512,512]{2,1,0:T(8,128)(2,1)S(1)}, bf16[1,512,512]{2,1,0:T(8,128)(2,1)}, u32[]{:S(2)}, u32[]{:S(2)}) %collective-permute-start.5) | collective-permute-done | bytes 524320 | tf_op jit(solution)/shard_map/ppermute | solution.py:294
  39.1 1.7 collective-permute-start.9
  41.8 1.5 collective-permute-start.11
  43.3 2.5 collective-permute-start.13
  45.8 9.0 %collective-permute-done.9.refs_22_ = bf16[1,512,512]{2,1,0:T(8,128)(2,1)S(1)} collective-permute-done((bf16[1,512,512]{2,1,0:T(8,128)(2,1)S(1)}, bf16[1,512,512]{2,1,0:T(8,128)(2,1)S(1)}, u32[]{:S(2)}, u32[]{:S(2)}) %collective-permute-start.9) | collective-permute-done | bytes 524320 | tf_op jit(solution)/shard_map/ppermute | solution.py:294
  55.1 1.6 collective-permute-start.14
  58.1 6.8 %collective-permute-done.13.refs_26_ = bf16[1,512,512]{2,1,0:T(8,128)(2,1)} collective-permute-done((bf16[1,512,512]{2,1,0:T(8,128)(2,1)S(1)}, bf16[1,512,512]{2,1,0:T(8,128)(2,1)}, u32[]{:S(2)}, u32[]{:S(2)}) %collective-permute-start.13) | collective-permute-done | bytes 524320 | tf_op jit(solution)/shard_map/ppermute | solution.py:294
  66.1 1.6 maximum_maximum_fusion
  67.7 2.5 collective-permute-start.17
  71.6 2.0 collective-permute-start.21
  73.6 10.1 %collective-permute-done.17.refs_26_ = bf16[1,512,512]{2,1,0:T(8,128)(2,1)S(1)} collective-permute-done((bf16[1,512,512]{2,1,0:T(8,128)(2,1)}, bf16[1,512,512]{2,1,0:T(8,128)(2,1)S(1)}, u32[]{:S(2)}, u32[]{:S(2)}) %collective-permute-start.17) | collective-permute-done | bytes 524320 | tf_op jit(solution)/shard_map/ppermute | solution.py:294
  87.3 2.4 collective-permute-start.25
  89.7 5.2 %collective-permute-done.21.refs_30_ = bf16[1,512,512]{2,1,0:T(8,128)(2,1)S(1)} collective-permute-done((bf16[1,512,512]{2,1,0:T(8,128)(2,1)}, bf16[1,512,512]{2,1,0:T(8,128)(2,1)S(1)}, u32[]{:S(2)}, u32[]{:S(2)}) %collective-permute-start.21) | collective-permute-done | bytes 524320 | tf_op jit(solution)/shard_map/ppermute | solution.py:294
  97.1 1.5 collective-permute-start.29
  98.6 7.5 %collective-permute-done.25.refs_24_ = bf16[1,512,512]{2,1,0:T(8,128)(2,1)S(1)} collective-permute-done((bf16[1,512,512]{2,1,0:T(8,128)(2,1)S(1)}, bf16[1,512,512]{2,1,0:T(8,128)(2,1)S(1)}, u32[]{:S(2)}, u32[]{:S(2)}) %collective-permute-start.25) | collective-permute-done | bytes 524320 | tf_op jit(solution)/shard_map/ppermute | solution.py:294
  106.2 3.2 %collective-permute-done.26.refs_11_ = bf16[512,512]{1,0:T(8,128)(2,1)S(1)} collective-permute-done((bf16[512,512]{1,0:T(8,128)(2,1)S(1)}, bf16[512,512]{1,0:T(8,128)(2,1)S(1)}, u32[]{:S(2)}, u32[]{:S(2)}) %collective-permute-start.26) | collective-permute-done | bytes 524320 | tf_op jit(solution)/shard_map/ppermute | solution.py:200
  113.5 1.3 collective-permute-start.33
  116.0 3.0 %collective-permute-done.30.refs_13_ = bf16[256,512]{1,0:T(8,128)(2,1)S(1)} collective-permute-done((bf16[256,512]{1,0:T(8,128)(2,1)S(1)}, bf16[256,512]{1,0:T(8,128)(2,1)S(1)}, u32[]{:S(2)}, u32[]{:S(2)}) %collective-permute-start.30) | collective-permute-done | bytes 262176 | tf_op jit(solution)/shard_map/ppermute | solution.py:200
  119.0 1.8 collective-permute-done.31.refs_14_
  121.8 1.2 collective-permute-start.35
  123.0 1.6 collective-permute-start.37
  124.6 4.8 %collective-permute-done.33.refs_28_ = bf16[1,512,512]{2,1,0:T(8,128)(2,1)} collective-permute-done((bf16[1,512,512]{2,1,0:T(8,128)(2,1)S(1)}, bf16[1,512,512]{2,1,0:T(8,128)(2,1)}, u32[]{:S(2)}, u32[]{:S(2)}) %collective-permute-start.33) | collective-permute-done | bytes 524320 | tf_op jit(solution)/shard_map/ppermute | solution.py:294
  129.4 5.8 %collective-permute-done.34.refs_16_ = bf16[512,512]{1,0:T(8,128)(2,1)S(1)} collective-permute-done((bf16[512,512]{1,0:T(8,128)(2,1)S(1)}, bf16[512,512]{1,0:T(8,128)(2,1)S(1)}, u32[]{:S(2)}, u32[]{:S(2)}) %collective-permute-start.34) | collective-permute-done | bytes 524320 | tf_op jit(solution)/shard_map/ppermute | solution.py:200
  136.0 1.2 collective-permute-start.38
  139.0 1.8 collective-permute-start.41
  140.8 4.0 %collective-permute-done.38.refs_18_ = bf16[256,512]{1,0:T(8,128)(2,1)} collective-permute-done((bf16[256,512]{1,0:T(8,128)(2,1)S(1)}, bf16[256,512]{1,0:T(8,128)(2,1)}, u32[]{:S(2)}, u32[]{:S(2)}) %collective-permute-start.38) | collective-permute-done | bytes 262176 | tf_op jit(solution)/shard_map/ppermute | solution.py:200
  148.7 1.6 collective-permute-start.43
  150.3 4.7 %collective-permute-done.41.refs_30_ = bf16[1,512,512]{2,1,0:T(8,128)(2,1)} collective-permute-done((bf16[1,512,512]{2,1,0:T(8,128)(2,1)}, bf16[1,512,512]{2,1,0:T(8,128)(2,1)}, u32[]{:S(2)}, u32[]{:S(2)}) %collective-permute-start.41) | collective-permute-done | bytes 524320 | tf_op jit(solution)/shard_map/ppermute | solution.py:294
  155.0 36.1 %shard_map.37.refs_35_ = f32[4,4,128,512]{3,2,1,0:T(8,128)} custom-call(s32[1]{0:T(128)} %bitcast.half_ref, s32[2,4]{1,0:T(2,128)} %gather_fusion.2, s32[4]{0:T(128)} %fusion.4.pick_ref, s32[2]{0:T(128)} %pad_add_fusion.1.tile_ref, bf16[512,512]{1,0:T(8,128)(2,1)} %bitcast.69, bf16[512,512]{1,0:T(8,128)(2,1)} %copy-done.10, bf16[512,512]{1,0:T(8,128)(2,1)} %copy-done.11, ...), custom_call_target="tpu_custom_call" | custom-call | flops 21474836480 | bytes 29360128 | tf_op jit(solution)/shard_map/pallas_call | solution.py:171
  194.5 23.4 %shard_map.39 = bf16[2,4,128,512]{3,2,1,0:T(8,128)(2,1)} custom-call(s32[1]{0:T(128)} %bitcast.half_ref, s32[2,2]{1,0:T(2,128)} %get-tuple-element.146.live_ref, s32[2]{0:T(128)} %get-tuple-element.148.pick_ref, s32[2]{0:T(128)} %pad_add_fusion.tile_ref, bf16[512,512]{1,0:T(8,128)(2,1)} %bitcast.70, bf16[512,512]{1,0:T(8,128)(2,1)} %copy-done.10, ...), custom_call_target="tpu_custom_call" | custom-call | flops 10737418240 | bytes 29360128 | tf_op jit(solution)/shard_map/pallas_call | solution.py:171
  217.9 1.3 slice_bitcast_fusion.2
  219.1 2.0 collective-permute-start.45
  221.2 1.5 collective-permute-start.46
  222.7 23.9 %shard_map.38 = f32[2,4,128,512]{3,2,1,0:T(8,128)} custom-call(s32[1]{0:T(128)} %bitcast.half_ref, s32[2,2]{1,0:T(2,128)} %get-tuple-element.147.live_ref, s32[2]{0:T(128)} %get-tuple-element.149.pick_ref, s32[2]{0:T(128)} %pad_add_fusion.tile_ref, bf16[512,512]{1,0:T(8,128)(2,1)} %bitcast.71, bf16[512,512]{1,0:T(8,128)(2,1)} %copy-done.10, ...), custom_call_target="tpu_custom_call" | custom-call | flops 10737418240 | bytes 29360128 | tf_op jit(solution)/shard_map/pallas_call | solution.py:171
  246.6 1.3 fusion.3
  248.0 18.4 %collective-permute-done.46 = bf16[4,128,512]{2,1,0:T(8,128)(2,1)S(1)} collective-permute-done((bf16[4,128,512]{2,1,0:T(8,128)(2,1)S(1)}, bf16[4,128,512]{2,1,0:T(8,128)(2,1)S(1)}, u32[]{:S(2)}, u32[]{:S(2)}) %collective-permute-start.46) | collective-permute-done | bytes 524320 | tf_op jit(solution)/shard_map/ppermute | solution.py:204
  266.4 2.0 collective-permute-done.47
  268.4 1.6 fusion.11
  270.0 1.6 collective-permute-start.50
  273.6 3.7 %collective-permute-done.50 = bf16[4,128,128]{2,1,0:T(8,128)(2,1)S(1)} collective-permute-done((bf16[4,128,128]{2,1,0:T(8,128)(2,1)S(1)}, bf16[4,128,128]{2,1,0:T(8,128)(2,1)S(1)}, u32[]{:S(2)}, u32[]{:S(2)}) %collective-permute-start.50) | collective-permute-done | bytes 131104 | tf_op jit(solution)/shard_map/ppermute | solution.py:200
  277.4 1.8 collective-permute-done.49
  280.0 1.6 copy.16
  (184 shorter events, 31.4 us)
Async XLA Ops:
  6.5 103.6 %all-gather.2.cloned.1.call-start = ((), (), s32[]{:S(2)}) async-start(), calls=%async_computation | async-start | bytes 6291456 | tf_op jit(solution)/shard_map/all_gather | solution.py:312
  8.7 14.6 %collective-permute-start = (bf16[1,512,512]{2,1,0:T(8,128)(2,1)S(1)}, bf16[1,512,512]{2,1,0:T(8,128)(2,1)S(1)}, u32[]{:S(2)}, u32[]{:S(2)}) collective-permute-start(bf16[1,512,512]{2,1,0:T(8,128)(2,1)S(1)} %get-tuple-element.70), channel_id=1, source_target_pairs={{0,16},{16,24},{24,8},{8,0},{1,17},{17,25},{25,9},{9,1},{2,18},{18... | collective-permute-start | bytes 1572872 | tf_op jit(solution)/shard_map/ppermute | solution.py:294
  8.7 14.6 %collective-permute-start.1 = (bf16[512,512]{1,0:T(8,128)(2,1)S(1)}, bf16[512,512]{1,0:T(8,128)(2,1)S(1)}, u32[]{:S(2)}, u32[]{:S(2)}) collective-permute-start(bf16[512,512]{1,0:T(8,128)(2,1)S(1)} %bitcast.67), channel_id=1, source_target_pairs={{0,2},{2,0},{4,6},{6,4},{1,3},{3,1},{5,7},{7,5},{8,10},{10,8},{12,... | collective-permute-start | bytes 1572872 | tf_op jit(solution)/shard_map/ppermute | solution.py:200
  10.7 13.1 %collective-permute-start.2 = (bf16[512,512]{1,0:T(8,128)(2,1)S(1)}, bf16[512,512]{1,0:T(8,128)(2,1)S(1)}, u32[]{:S(2)}, u32[]{:S(2)}) collective-permute-start(bf16[512,512]{1,0:T(8,128)(2,1)S(1)} %bitcast.68), channel_id=1, source_target_pairs={{0,4},{2,6},{4,0},{6,2},{1,5},{3,7},{5,1},{7,3},{8,12},{10,14},{12... | collective-permute-start | bytes 1572872 | tf_op jit(solution)/shard_map/ppermute | solution.py:200
  23.8 17.1 %collective-permute-start.3 = (bf16[4,512,512]{2,1,0:T(8,128)(2,1)S(1)}, bf16[4,512,512]{2,1,0:T(8,128)(2,1)S(1)}, u32[]{:S(2)}, u32[]{:S(2)}) collective-permute-start(bf16[4,512,512]{2,1,0:T(8,128)(2,1)S(1)} %copy-done.1), channel_id=1, source_target_pairs={{0,1},{1,0},{2,3},{3,2},{4,5},{5,4},{6,7},{7,6},{8,9},{9,8},{10,11... | collective-permute-start | bytes 6291464 | tf_op jit(solution)/shard_map/ppermute | solution.py:200
  23.8 15.3 %collective-permute-start.5 = (bf16[1,512,512]{2,1,0:T(8,128)(2,1)S(1)}, bf16[1,512,512]{2,1,0:T(8,128)(2,1)}, u32[]{:S(2)}, u32[]{:S(2)}) collective-permute-start(bf16[1,512,512]{2,1,0:T(8,128)(2,1)S(1)} %get-tuple-element.77), channel_id=1, source_target_pairs={{0,16},{16,24},{24,8},{8,0},{1,17},{17,25},{25,9},{9,1},{2,18},{18... | collective-permute-start | bytes 1572872 | tf_op jit(solution)/shard_map/ppermute | solution.py:294
  26.4 14.4 %collective-permute-start.4 = (bf16[1,512,512]{2,1,0:T(8,128)(2,1)S(1)}, bf16[1,512,512]{2,1,0:T(8,128)(2,1)S(1)}, u32[]{:S(2)}, u32[]{:S(2)}) collective-permute-start(bf16[1,512,512]{2,1,0:T(8,128)(2,1)S(1)} %collective-permute-done.refs_24_), channel_id=1, source_target_pairs={{0,1},{1,0},{2,3},{3,2},{4,5},{5,4},{6,7},{7,6},{8,9},{9,8},{10,11... | collective-permute-start | bytes 1572872 | tf_op jit(solution)/shard_map/ppermute | solution.py:200
  26.6 14.2 %collective-permute-start.6 = (bf16[256,512]{1,0:T(8,128)(2,1)S(1)}, bf16[256,512]{1,0:T(8,128)(2,1)S(1)}, u32[]{:S(2)}, u32[]{:S(2)}) collective-permute-start(bf16[256,512]{1,0:T(8,128)(2,1)S(1)} %slice.72), channel_id=1, source_target_pairs={{0,4},{2,6},{4,0},{6,2},{1,5},{3,7},{5,1},{7,3},{8,12},{10,14},{12... | collective-permute-start | bytes 786440 | tf_op jit(solution)/shard_map/ppermute | solution.py:200
  28.2 12.6 %collective-permute-start.7 = (bf16[256,512]{1,0:T(8,128)(2,1)S(1)}, bf16[256,512]{1,0:T(8,128)(2,1)S(1)}, u32[]{:S(2)}, u32[]{:S(2)}) collective-permute-start(bf16[256,512]{1,0:T(8,128)(2,1)S(1)} %slice.73), channel_id=1, source_target_pairs={{0,2},{2,0},{4,6},{6,4},{1,3},{3,1},{5,7},{7,5},{8,10},{10,8},{12,... | collective-permute-start | bytes 786440 | tf_op jit(solution)/shard_map/ppermute | solution.py:200
  39.1 15.7 %collective-permute-start.9 = (bf16[1,512,512]{2,1,0:T(8,128)(2,1)S(1)}, bf16[1,512,512]{2,1,0:T(8,128)(2,1)S(1)}, u32[]{:S(2)}, u32[]{:S(2)}) collective-permute-start(bf16[1,512,512]{2,1,0:T(8,128)(2,1)S(1)} %get-tuple-element.81), channel_id=1, source_target_pairs={{0,16},{16,24},{24,8},{8,0},{1,17},{17,25},{25,9},{9,1},{2,18},{18... | collective-permute-start | bytes 1572872 | tf_op jit(solution)/shard_map/ppermute | solution.py:294
  40.9 14.0 %collective-permute-start.10 = (bf16[4,512,128]{2,1,0:T(8,128)(2,1)S(1)}, bf16[4,512,128]{2,1,0:T(8,128)(2,1)S(1)}, u32[]{:S(2)}, u32[]{:S(2)}) collective-permute-start(bf16[4,512,128]{2,1,0:T(8,128)(2,1)S(1)} %bitcast.90), channel_id=1, source_target_pairs={{0,2},{2,0},{4,6},{6,4},{1,3},{3,1},{5,7},{7,5},{8,10},{10,8},{12,... | collective-permute-start | bytes 1572872 | tf_op jit(solution)/shard_map/ppermute | solution.py:200
  41.8 13.2 %collective-permute-start.11 = (bf16[4,512,128]{2,1,0:T(8,128)(2,1)S(1)}, bf16[4,512,128]{2,1,0:T(8,128)(2,1)S(1)}, u32[]{:S(2)}, u32[]{:S(2)}) collective-permute-start(bf16[4,512,128]{2,1,0:T(8,128)(2,1)S(1)} %bitcast.91), channel_id=1, source_target_pairs={{0,4},{2,6},{4,0},{6,2},{1,5},{3,7},{5,1},{7,3},{8,12},{10,14},{12... | collective-permute-start | bytes 1572872 | tf_op jit(solution)/shard_map/ppermute | solution.py:200
  43.3 11.7 %collective-permute-start.8 = (bf16[1,512,512]{2,1,0:T(8,128)(2,1)}, bf16[1,512,512]{2,1,0:T(8,128)(2,1)S(1)}, u32[]{:S(2)}, u32[]{:S(2)}) collective-permute-start(bf16[1,512,512]{2,1,0:T(8,128)(2,1)} %collective-permute-done.5.refs_22_), channel_id=1, source_target_pairs={{0,1},{1,0},{2,3},{3,2},{4,5},{5,4},{6,7},{7,6},{8,9},{9,8},{10,11... | collective-permute-start | bytes 1572872 | tf_op jit(solution)/shard_map/ppermute | solution.py:200
  43.3 21.5 %collective-permute-start.13 = (bf16[1,512,512]{2,1,0:T(8,128)(2,1)S(1)}, bf16[1,512,512]{2,1,0:T(8,128)(2,1)}, u32[]{:S(2)}, u32[]{:S(2)}) collective-permute-start(bf16[1,512,512]{2,1,0:T(8,128)(2,1)S(1)} %collective-permute-done.refs_24_), channel_id=1, source_target_pairs={{0,16},{16,24},{24,8},{8,0},{1,17},{17,25},{25,9},{9,1},{2,18},{18... | collective-permute-start | bytes 1572872 | tf_op jit(solution)/shard_map/ppermute | solution.py:294
  55.0 10.2 %collective-permute-start.12 = (bf16[1,512,512]{2,1,0:T(8,128)(2,1)S(1)}, bf16[1,512,512]{2,1,0:T(8,128)(2,1)S(1)}, u32[]{:S(2)}, u32[]{:S(2)}) collective-permute-start(bf16[1,512,512]{2,1,0:T(8,128)(2,1)S(1)} %collective-permute-done.9.refs_22_), channel_id=1, source_target_pairs={{0,1},{1,0},{2,3},{3,2},{4,5},{5,4},{6,7},{7,6},{8,9},{9,8},{10,11... | collective-permute-start | bytes 1572872 | tf_op jit(solution)/shard_map/ppermute | solution.py:200
  55.1 9.7 %collective-permute-start.14 = (bf16[2,512,128]{2,1,0:T(8,128)(2,1)S(1)}, bf16[2,512,128]{2,1,0:T(8,128)(2,1)S(1)}, u32[]{:S(2)}, u32[]{:S(2)}) collective-permute-start(bf16[2,512,128]{2,1,0:T(8,128)(2,1)S(1)} %slice.74), channel_id=1, source_target_pairs={{0,4},{2,6},{4,0},{6,2},{1,5},{3,7},{5,1},{7,3},{8,12},{10,14},{12... | collective-permute-start | bytes 786440 | tf_op jit(solution)/shard_map/ppermute | solution.py:200
  56.8 8.5 %collective-permute-start.15 = (bf16[2,512,128]{2,1,0:T(8,128)(2,1)S(1)}, bf16[2,512,128]{2,1,0:T(8,128)(2,1)S(1)}, u32[]{:S(2)}, u32[]{:S(2)}) collective-permute-start(bf16[2,512,128]{2,1,0:T(8,128)(2,1)S(1)} %slice.75), channel_id=1, source_target_pairs={{0,2},{2,0},{4,6},{6,4},{1,3},{3,1},{5,7},{7,5},{8,10},{10,8},{12,... | collective-permute-start | bytes 786440 | tf_op jit(solution)/shard_map/ppermute | solution.py:200
  67.7 16.0 %collective-permute-start.17 = (bf16[1,512,512]{2,1,0:T(8,128)(2,1)}, bf16[1,512,512]{2,1,0:T(8,128)(2,1)S(1)}, u32[]{:S(2)}, u32[]{:S(2)}) collective-permute-start(bf16[1,512,512]{2,1,0:T(8,128)(2,1)} %collective-permute-done.5.refs_22_), channel_id=1, source_target_pairs={{0,16},{16,24},{24,8},{8,0},{1,17},{17,25},{25,9},{9,1},{2,18},{18... | collective-permute-start | bytes 1572872 | tf_op jit(solution)/shard_map/ppermute | solution.py:294
  70.2 13.5 %collective-permute-start.16 = (bf16[1,512,512]{2,1,0:T(8,128)(2,1)}, bf16[1,512,512]{2,1,0:T(8,128)(2,1)S(1)}, u32[]{:S(2)}, u32[]{:S(2)}) collective-permute-start(bf16[1,512,512]{2,1,0:T(8,128)(2,1)} %collective-permute-done.13.refs_26_), channel_id=1, source_target_pairs={{0,1},{1,0},{2,3},{3,2},{4,5},{5,4},{6,7},{7,6},{8,9},{9,8},{10,11... | collective-permute-start | bytes 1572872 | tf_op jit(solution)/shard_map/ppermute | solution.py:200
  70.2 14.3 %collective-permute-start.18 = (bf16[512,512]{1,0:T(8,128)(2,1)S(1)}, bf16[512,512]{1,0:T(8,128)(2,1)S(1)}, u32[]{:S(2)}, u32[]{:S(2)}) collective-permute-start(bf16[512,512]{1,0:T(8,128)(2,1)S(1)} %bitcast.72), channel_id=1, source_target_pairs={{0,2},{2,0},{4,6},{6,4},{1,3},{3,1},{5,7},{7,5},{8,10},{10,8},{12,... | collective-permute-start | bytes 1572872 | tf_op jit(solution)/shard_map/ppermute | solution.py:200
  71.1 14.1 %collective-permute-start.19 = (bf16[512,512]{1,0:T(8,128)(2,1)S(1)}, bf16[512,512]{1,0:T(8,128)(2,1)S(1)}, u32[]{:S(2)}, u32[]{:S(2)}) collective-permute-start(bf16[512,512]{1,0:T(8,128)(2,1)S(1)} %bitcast.73), channel_id=1, source_target_pairs={{0,4},{2,6},{4,0},{6,2},{1,5},{3,7},{5,1},{7,3},{8,12},{10,14},{12... | collective-permute-start | bytes 1572872 | tf_op jit(solution)/shard_map/ppermute | solution.py:200
  71.6 23.3 %collective-permute-start.21 = (bf16[1,512,512]{2,1,0:T(8,128)(2,1)}, bf16[1,512,512]{2,1,0:T(8,128)(2,1)S(1)}, u32[]{:S(2)}, u32[]{:S(2)}) collective-permute-start(bf16[1,512,512]{2,1,0:T(8,128)(2,1)} %collective-permute-done.13.refs_26_), channel_id=1, source_target_pairs={{0,16},{16,24},{24,8},{8,0},{1,17},{17,25},{25,9},{9,1},{2,18},{18... | collective-permute-start | bytes 1572872 | tf_op jit(solution)/shard_map/ppermute | solution.py:294
  85.2 9.8 %collective-permute-start.20 = (bf16[1,512,512]{2,1,0:T(8,128)(2,1)S(1)}, bf16[1,512,512]{2,1,0:T(8,128)(2,1)S(1)}, u32[]{:S(2)}, u32[]{:S(2)}) collective-permute-start(bf16[1,512,512]{2,1,0:T(8,128)(2,1)S(1)} %collective-permute-done.17.refs_26_), channel_id=1, source_target_pairs={{0,1},{1,0},{2,3},{3,2},{4,5},{5,4},{6,7},{7,6},{8,9},{9,8},{10,11... | collective-permute-start | bytes 1572872 | tf_op jit(solution)/shard_map/ppermute | solution.py:200
  85.2 9.8 %collective-permute-start.22 = (bf16[256,512]{1,0:T(8,128)(2,1)S(1)}, bf16[256,512]{1,0:T(8,128)(2,1)S(1)}, u32[]{:S(2)}, u32[]{:S(2)}) collective-permute-start(bf16[256,512]{1,0:T(8,128)(2,1)S(1)} %slice.76), channel_id=1, source_target_pairs={{0,4},{2,6},{4,0},{6,2},{1,5},{3,7},{5,1},{7,3},{8,12},{10,14},{12... | collective-permute-start | bytes 786440 | tf_op jit(solution)/shard_map/ppermute | solution.py:200
  85.8 9.1 %collective-permute-start.23 = (bf16[256,512]{1,0:T(8,128)(2,1)S(1)}, bf16[256,512]{1,0:T(8,128)(2,1)S(1)}, u32[]{:S(2)}, u32[]{:S(2)}) collective-permute-start(bf16[256,512]{1,0:T(8,128)(2,1)S(1)} %slice.77), channel_id=1, source_target_pairs={{0,2},{2,0},{4,6},{6,4},{1,3},{3,1},{5,7},{7,5},{8,10},{10,8},{12,... | collective-permute-start | bytes 786440 | tf_op jit(solution)/shard_map/ppermute | solution.py:200
  87.3 18.9 %collective-permute-start.25 = (bf16[1,512,512]{2,1,0:T(8,128)(2,1)S(1)}, bf16[1,512,512]{2,1,0:T(8,128)(2,1)S(1)}, u32[]{:S(2)}, u32[]{:S(2)}) collective-permute-start(bf16[1,512,512]{2,1,0:T(8,128)(2,1)S(1)} %get-tuple-element.100), channel_id=1, source_target_pairs={{0,16},{16,24},{24,8},{8,0},{1,17},{17,25},{25,9},{9,1},{2,18},{18... | collective-permute-start | bytes 1572872 | tf_op jit(solution)/shard_map/ppermute | solution.py:294
  95.0 11.2 %collective-permute-start.24 = (bf16[1,512,512]{2,1,0:T(8,128)(2,1)S(1)}, bf16[1,512,512]{2,1,0:T(8,128)(2,1)S(1)}, u32[]{:S(2)}, u32[]{:S(2)}) collective-permute-start(bf16[1,512,512]{2,1,0:T(8,128)(2,1)S(1)} %collective-permute-done.21.refs_30_), channel_id=1, source_target_pairs={{0,1},{1,0},{2,3},{3,2},{4,5},{5,4},{6,7},{7,6},{8,9},{9,8},{10,11... | collective-permute-start | bytes 1572872 | tf_op jit(solution)/shard_map/ppermute | solution.py:200
  95.1 14.3 %collective-permute-start.26 = (bf16[512,512]{1,0:T(8,128)(2,1)S(1)}, bf16[512,512]{1,0:T(8,128)(2,1)S(1)}, u32[]{:S(2)}, u32[]{:S(2)}) collective-permute-start(bf16[512,512]{1,0:T(8,128)(2,1)S(1)} %bitcast.78), channel_id=1, source_target_pairs={{0,2},{2,0},{4,6},{6,4},{1,3},{3,1},{5,7},{7,5},{8,10},{10,8},{12,... | collective-permute-start | bytes 1572872 | tf_op jit(solution)/shard_map/ppermute | solution.py:200
  96.1 14.1 %collective-permute-start.27 = (bf16[512,512]{1,0:T(8,128)(2,1)S(1)}, bf16[512,512]{1,0:T(8,128)(2,1)}, u32[]{:S(2)}, u32[]{:S(2)}) collective-permute-start(bf16[512,512]{1,0:T(8,128)(2,1)S(1)} %bitcast.79), channel_id=1, source_target_pairs={{0,4},{2,6},{4,0},{6,2},{1,5},{3,7},{5,1},{7,3},{8,12},{10,14},{12... | collective-permute-start | bytes 1572872 | tf_op jit(solution)/shard_map/ppermute | solution.py:200
  97.1 18.9 %collective-permute-start.29 = (bf16[1,512,512]{2,1,0:T(8,128)(2,1)S(1)}, bf16[1,512,512]{2,1,0:T(8,128)(2,1)}, u32[]{:S(2)}, u32[]{:S(2)}) collective-permute-start(bf16[1,512,512]{2,1,0:T(8,128)(2,1)S(1)} %collective-permute-done.9.refs_22_), channel_id=1, source_target_pairs={{0,16},{16,24},{24,8},{8,0},{1,17},{17,25},{25,9},{9,1},{2,18},{18... | collective-permute-start | bytes 1572872 | tf_op jit(solution)/shard_map/ppermute | solution.py:294
  110.2 10.6 %collective-permute-start.28 = (bf16[1,512,512]{2,1,0:T(8,128)(2,1)}, bf16[1,512,512]{2,1,0:T(8,128)(2,1)S(1)}, u32[]{:S(2)}, u32[]{:S(2)}) collective-permute-start(bf16[1,512,512]{2,1,0:T(8,128)(2,1)} %copy-done.24), channel_id=1, source_target_pairs={{0,1},{1,0},{2,3},{3,2},{4,5},{5,4},{6,7},{7,6},{8,9},{9,8},{10,11... | collective-permute-start | bytes 1572872 | tf_op jit(solution)/shard_map/ppermute | solution.py:200
  110.2 8.8 %collective-permute-start.30 = (bf16[256,512]{1,0:T(8,128)(2,1)S(1)}, bf16[256,512]{1,0:T(8,128)(2,1)S(1)}, u32[]{:S(2)}, u32[]{:S(2)}) collective-permute-start(bf16[256,512]{1,0:T(8,128)(2,1)S(1)} %slice.78), channel_id=1, source_target_pairs={{0,4},{2,6},{4,0},{6,2},{1,5},{3,7},{5,1},{7,3},{8,12},{10,14},{12... | collective-permute-start | bytes 786440 | tf_op jit(solution)/shard_map/ppermute | solution.py:200
  112.3 8.5 %collective-permute-start.31 = (bf16[256,512]{1,0:T(8,128)(2,1)S(1)}, bf16[256,512]{1,0:T(8,128)(2,1)S(1)}, u32[]{:S(2)}, u32[]{:S(2)}) collective-permute-start(bf16[256,512]{1,0:T(8,128)(2,1)S(1)} %slice.79), channel_id=1, source_target_pairs={{0,2},{2,0},{4,6},{6,4},{1,3},{3,1},{5,7},{7,5},{8,10},{10,8},{12,... | collective-permute-start | bytes 786440 | tf_op jit(solution)/shard_map/ppermute | solution.py:200
  113.5 15.9 %collective-permute-start.33 = (bf16[1,512,512]{2,1,0:T(8,128)(2,1)S(1)}, bf16[1,512,512]{2,1,0:T(8,128)(2,1)}, u32[]{:S(2)}, u32[]{:S(2)}) collective-permute-start(bf16[1,512,512]{2,1,0:T(8,128)(2,1)S(1)} %copy-done.25), channel_id=1, source_target_pairs={{0,16},{16,24},{24,8},{8,0},{1,17},{17,25},{25,9},{9,1},{2,18},{18... | collective-permute-start | bytes 1572872 | tf_op jit(solution)/shard_map/ppermute | solution.py:294
  120.8 8.6 %collective-permute-start.32 = (bf16[1,512,512]{2,1,0:T(8,128)(2,1)}, bf16[1,512,512]{2,1,0:T(8,128)(2,1)S(1)}, u32[]{:S(2)}, u32[]{:S(2)}) collective-permute-start(bf16[1,512,512]{2,1,0:T(8,128)(2,1)} %collective-permute-done.29.refs_28_), channel_id=1, source_target_pairs={{0,1},{1,0},{2,3},{3,2},{4,5},{5,4},{6,7},{7,6},{8,9},{9,8},{10,11... | collective-permute-start | bytes 1572872 | tf_op jit(solution)/shard_map/ppermute | solution.py:200
  120.8 14.3 %collective-permute-start.34 = (bf16[512,512]{1,0:T(8,128)(2,1)S(1)}, bf16[512,512]{1,0:T(8,128)(2,1)S(1)}, u32[]{:S(2)}, u32[]{:S(2)}) collective-permute-start(bf16[512,512]{1,0:T(8,128)(2,1)S(1)} %bitcast.85), channel_id=1, source_target_pairs={{0,2},{2,0},{4,6},{6,4},{1,3},{3,1},{5,7},{7,5},{8,10},{10,8},{12,... | collective-permute-start | bytes 1572872 | tf_op jit(solution)/shard_map/ppermute | solution.py:200
  121.8 14.0 %collective-permute-start.35 = (bf16[512,512]{1,0:T(8,128)(2,1)S(1)}, bf16[512,512]{1,0:T(8,128)(2,1)S(1)}, u32[]{:S(2)}, u32[]{:S(2)}) collective-permute-start(bf16[512,512]{1,0:T(8,128)(2,1)S(1)} %bitcast.86), channel_id=1, source_target_pairs={{0,4},{2,6},{4,0},{6,2},{1,5},{3,7},{5,1},{7,3},{8,12},{10,14},{12... | collective-permute-start | bytes 1572872 | tf_op jit(solution)/shard_map/ppermute | solution.py:200
  123.0 17.8 %collective-permute-start.37 = (bf16[1,512,512]{2,1,0:T(8,128)(2,1)}, bf16[1,512,512]{2,1,0:T(8,128)(2,1)}, u32[]{:S(2)}, u32[]{:S(2)}) collective-permute-start(bf16[1,512,512]{2,1,0:T(8,128)(2,1)} %collective-permute-done.29.refs_28_), channel_id=1, source_target_pairs={{0,16},{16,24},{24,8},{8,0},{1,17},{17,25},{25,9},{9,1},{2,18},{18... | collective-permute-start | bytes 1572872 | tf_op jit(solution)/shard_map/ppermute | solution.py:294
  135.8 9.9 %collective-permute-start.36 = (bf16[1,512,512]{2,1,0:T(8,128)(2,1)}, bf16[1,512,512]{2,1,0:T(8,128)(2,1)}, u32[]{:S(2)}, u32[]{:S(2)}) collective-permute-start(bf16[1,512,512]{2,1,0:T(8,128)(2,1)} %collective-permute-done.33.refs_28_), channel_id=1, source_target_pairs={{0,1},{1,0},{2,3},{3,2},{4,5},{5,4},{6,7},{7,6},{8,9},{9,8},{10,11... | collective-permute-start | bytes 1572872 | tf_op jit(solution)/shard_map/ppermute | solution.py:200
  136.0 8.8 %collective-permute-start.38 = (bf16[256,512]{1,0:T(8,128)(2,1)S(1)}, bf16[256,512]{1,0:T(8,128)(2,1)}, u32[]{:S(2)}, u32[]{:S(2)}) collective-permute-start(bf16[256,512]{1,0:T(8,128)(2,1)S(1)} %slice.80), channel_id=1, source_target_pairs={{0,4},{2,6},{4,0},{6,2},{1,5},{3,7},{5,1},{7,3},{8,12},{10,14},{12... | collective-permute-start | bytes 786440 | tf_op jit(solution)/shard_map/ppermute | solution.py:200
  137.2 8.5 %collective-permute-start.39 = (bf16[256,512]{1,0:T(8,128)(2,1)S(1)}, bf16[256,512]{1,0:T(8,128)(2,1)S(1)}, u32[]{:S(2)}, u32[]{:S(2)}) collective-permute-start(bf16[256,512]{1,0:T(8,128)(2,1)S(1)} %slice.81), channel_id=1, source_target_pairs={{0,2},{2,0},{4,6},{6,4},{1,3},{3,1},{5,7},{7,5},{8,10},{10,8},{12,... | collective-permute-start | bytes 786440 | tf_op jit(solution)/shard_map/ppermute | solution.py:200
  139.0 16.0 %collective-permute-start.41 = (bf16[1,512,512]{2,1,0:T(8,128)(2,1)}, bf16[1,512,512]{2,1,0:T(8,128)(2,1)}, u32[]{:S(2)}, u32[]{:S(2)}) collective-permute-start(bf16[1,512,512]{2,1,0:T(8,128)(2,1)} %collective-permute-done.33.refs_28_), channel_id=1, source_target_pairs={{0,16},{16,24},{24,8},{8,0},{1,17},{17,25},{25,9},{9,1},{2,18},{18... | collective-permute-start | bytes 1572872 | tf_op jit(solution)/shard_map/ppermute | solution.py:294
  145.7 9.3 %collective-permute-start.40 = (bf16[1,512,512]{2,1,0:T(8,128)(2,1)}, bf16[1,512,512]{2,1,0:T(8,128)(2,1)}, u32[]{:S(2)}, u32[]{:S(2)}) collective-permute-start(bf16[1,512,512]{2,1,0:T(8,128)(2,1)} %collective-permute-done.37.refs_32_), channel_id=1, source_target_pairs={{0,1},{1,0},{2,3},{3,2},{4,5},{5,4},{6,7},{7,6},{8,9},{9,8},{10,11... | collective-permute-start | bytes 1572872 | tf_op jit(solution)/shard_map/ppermute | solution.py:200
  148.7 42.5 %collective-permute-start.43 = (bf16[1,512,512]{2,1,0:T(8,128)(2,1)S(1)}, bf16[1,512,512]{2,1,0:T(8,128)(2,1)S(1)}, u32[]{:S(2)}, u32[]{:S(2)}) collective-permute-start(bf16[1,512,512]{2,1,0:T(8,128)(2,1)S(1)} %collective-permute-done.17.refs_26_), channel_id=1, source_target_pairs={{0,16},{16,24},{24,8},{8,0},{1,17},{17,25},{25,9},{9,1},{2,18},{18... | collective-permute-start | bytes 1572872 | tf_op jit(solution)/shard_map/ppermute | solution.py:294
  155.0 36.2 %collective-permute-start.42 = (bf16[1,512,512]{2,1,0:T(8,128)(2,1)}, bf16[1,512,512]{2,1,0:T(8,128)(2,1)S(1)}, u32[]{:S(2)}, u32[]{:S(2)}) collective-permute-start(bf16[1,512,512]{2,1,0:T(8,128)(2,1)} %collective-permute-done.41.refs_30_), channel_id=1, source_target_pairs={{0,1},{1,0},{2,3},{3,2},{4,5},{5,4},{6,7},{7,6},{8,9},{9,8},{10,11... | collective-permute-start | bytes 1572872 | tf_op jit(solution)/shard_map/ppermute | solution.py:200
  219.1 28.8 %collective-permute-start.45 = (bf16[4,128,512]{2,1,0:T(8,128)(2,1)S(1)}, bf16[4,128,512]{2,1,0:T(8,128)(2,1)S(1)}, u32[]{:S(2)}, u32[]{:S(2)}) collective-permute-start(bf16[4,128,512]{2,1,0:T(8,128)(2,1)S(1)} %get-tuple-element.141), channel_id=1, source_target_pairs={{0,8},{8,16},{16,24},{24,0},{1,9},{9,17},{17,25},{25,1},{2,10},{10... | collective-permute-start | bytes 1572872 | tf_op jit(solution)/shard_map/ppermute | solution.py:204
  221.2 45.2 %collective-permute-start.46 = (bf16[4,128,512]{2,1,0:T(8,128)(2,1)S(1)}, bf16[4,128,512]{2,1,0:T(8,128)(2,1)S(1)}, u32[]{:S(2)}, u32[]{:S(2)}) collective-permute-start(bf16[4,128,512]{2,1,0:T(8,128)(2,1)S(1)} %get-tuple-element.142), channel_id=1, source_target_pairs={{0,16},{8,24},{16,0},{24,8},{1,17},{9,25},{17,1},{25,9},{2,18},{10... | collective-permute-start | bytes 1572872 | tf_op jit(solution)/shard_map/ppermute | solution.py:204
  247.8 20.5 %collective-permute-start.47 = (bf16[4,128,512]{2,1,0:T(8,128)(2,1)S(1)}, bf16[4,128,512]{2,1,0:T(8,128)(2,1)S(1)}, u32[]{:S(2)}, u32[]{:S(2)}) collective-permute-start(bf16[4,128,512]{2,1,0:T(8,128)(2,1)S(1)} %fusion.3), channel_id=1, source_target_pairs={{0,24},{8,0},{16,8},{24,16},{1,25},{9,1},{17,9},{25,17},{2,26},{10... | collective-permute-start | bytes 1572872 | tf_op jit(solution)/shard_map/ppermute | solution.py:204
  (44 other events, 928.1 us)
Sparse Core Ops, SparseCore 0:
  67.8 13.8 all-gather.1

commit v7 on v6

--- a/solution.py
+++ b/solution.py
@@ -162,8 +162,7 @@
     wide = 2 * GROUPS * TV
     tile_count = live.shape[0]
     first = before is None
-    count = NTV if first else NTV // 2
-    base = part * count
+    base, count = part
     result = (count, GROUPS, b_blocks * a_count, columns)
     flops = 2 * tile_count * count * rows * 2 * rows * (steps * depth + columns)
     anywhere = pl.BlockSpec(memory_space=pl.ANY)
@@ -176,7 +175,7 @@
             in_specs=[anywhere] * len(copied)
             + [pl.BlockSpec((1, 2 * rows, columns), lambda i, j, h, v, k, d: (d[i], 0, 0))]
             + [
-                pl.BlockSpec(result, lambda i, j, h, v, k, d: (part, 0, 0, 0), pipeline_mode=pl.Buffered(1))
+                pl.BlockSpec(result, lambda i, j, h, v, k, d: (base // count, 0, 0, 0), pipeline_mode=pl.Buffered(1))
             ]
             * (not first),
             out_specs=pl.BlockSpec(result, lambda i, j, h, v, k, d: (0, 0, 0, 0)),
@@ -312,15 +311,12 @@
             held["amp"] = lax.all_gather(jnp.concatenate(every, axis=2), "occ", axis=1, tiled=True)
             waiting[slot + 3].append("amp")
         if slot == last - 1:
-            held["sum"] = contract((0, 2), None, 0, jnp.float32)
+            held["sum"] = contract((0, 2), None, (0, NTV), jnp.float32)
             waiting[slot + 1].append("sum")
-    early = contract((1, 3), held["sum"], 0, jnp.bfloat16)
-    moved = [shift(early[t], "left", NTV, t + 1) for t in range(NTV // 2)]
-    late = contract((1, 3), held["sum"], 1, jnp.float32)
-    moved += [
-        shift(late[t].astype(jnp.bfloat16), "left", NTV, NTV // 2 + t + 1) for t in range(NTV // 2 - 1)
-    ]
-    summed = late[NTV // 2 - 1]
+    early = contract((1, 3), held["sum"], (0, NTV - 1), jnp.bfloat16)
+    moved = [shift(early[t], "left", NTV, t + 1) for t in range(NTV - 1)]
+    late = contract((1, 3), held["sum"], (NTV - 1, 1), jnp.float32)
+    summed = late[0]
     for piece in moved:
         summed = summed + piece.astype(jnp.float32)
     pieces = []

time: 291 us -> 296 us (1.017)
  Pallas kernels: 83.4 us -> 89.8 us
  local copies, waits for them, and re-layouts: 14.8 us -> 18.1 us
    pallas_call x3, Pallas kernels: 83.4 us -> 89.8 us  [ladder(): pl.pallas_call(functools.partial(ladder_kernel, steps, count, tile_count,...]
  transfers between devices with their start and end apart: 52 -> 52, of which waited for: 27 -> 28; matrix products, arithmetic and copies ran while one was open for 3% -> 4% of each run, Pallas kernels for 21% -> 20%
where the time goes in v7:
time: 296 us; the launch traced here: 295 us
  waiting for transfers between devices  119 us (40%)
  Pallas kernels  89.8 us (30%)
  starting transfers between devices  49.1 us (17%)
  local copies, waits for them, and re-layouts  18.1 us (6%)
  between operations  13.9 us (5%)
  other arithmetic  5.23 us (2%)
    pallas_call x3, Pallas kernels, ladder(): pl.pallas_call(functools.partial(ladder_kernel, steps, count, tile_count,...  89.8 us
    ppermute x12, waiting for transfers between devices, on_square(): lax.ppermute(held['block', s - 1, (i + 1) % NTV], 'left', ring)  68.7 us
    ppermute x36, waiting for transfers between devices, partner(): return lax.ppermute(value, axis, [(i, i ^ flip) for i in range(size)])  29.1 us
    ppermute x36, starting transfers between devices, partner(): return lax.ppermute(value, axis, [(i, i ^ flip) for i in range(size)])  26.9 us
    ppermute x3, waiting for transfers between devices, shift(): lax.ppermute(value, axis, [(i, (i + step) % size) for i in range(size)])  21.1 us
    ppermute x12, starting transfers between devices, on_square(): lax.ppermute(held['block', s - 1, (i + 1) % NTV], 'left', ring)  19.1 us
  transfers between devices with their start and end apart: 52, of which 28 were waited for; matrix products, arithmetic and copies ran while one was open for 4% of the time, Pallas kernels for 20%

profile of v7, /device:TPU:8, one launch (start us, length us, event | category | flops | bytes accessed | tf_op | source)
XLA Modules:
  0.0 295.2 jit_solution(10376119444373624322)
XLA Ops:
  6.5 1.8 constant_dynamic-slice_fusion
  8.7 1.9 collective-permute-start.1
  10.7 1.5 collective-permute-start.2
  12.2 11.1 %collective-permute-done.refs_24_ = bf16[1,512,512]{2,1,0:T(8,128)(2,1)S(1)} collective-permute-done((bf16[1,512,512]{2,1,0:T(8,128)(2,1)S(1)}, bf16[1,512,512]{2,1,0:T(8,128)(2,1)S(1)}, u32[]{:S(2)}, u32[]{:S(2)}) %collective-permute-start) | collective-permute-done | bytes 524320 | tf_op jit(solution)/shard_map/ppermute | solution.py:293
  23.8 2.6 collective-permute-start.5
  26.6 1.6 collective-permute-start.6
  28.8 10.3 %collective-permute-done.5.refs_22_ = bf16[1,512,512]{2,1,0:T(8,128)(2,1)} collective-permute-done((bf16[1,512,512]{2,1,0:T(8,128)(2,1)S(1)}, bf16[1,512,512]{2,1,0:T(8,128)(2,1)}, u32[]{:S(2)}, u32[]{:S(2)}) %collective-permute-start.5) | collective-permute-done | bytes 524320 | tf_op jit(solution)/shard_map/ppermute | solution.py:293
  39.1 1.7 collective-permute-start.9
  40.9 1.4 copy-done.2
  42.8 1.5 collective-permute-start.11
  44.3 2.5 collective-permute-start.13
  46.8 8.2 %collective-permute-done.9.refs_22_ = bf16[1,512,512]{2,1,0:T(8,128)(2,1)} collective-permute-done((bf16[1,512,512]{2,1,0:T(8,128)(2,1)S(1)}, bf16[1,512,512]{2,1,0:T(8,128)(2,1)}, u32[]{:S(2)}, u32[]{:S(2)}) %collective-permute-start.9) | collective-permute-done | bytes 524320 | tf_op jit(solution)/shard_map/ppermute | solution.py:293
  55.7 1.6 collective-permute-start.14
  57.3 1.6 collective-permute-start.15
  60.2 4.6 %collective-permute-done.13.refs_26_ = bf16[1,512,512]{2,1,0:T(8,128)(2,1)} collective-permute-done((bf16[1,512,512]{2,1,0:T(8,128)(2,1)S(1)}, bf16[1,512,512]{2,1,0:T(8,128)(2,1)}, u32[]{:S(2)}, u32[]{:S(2)}) %collective-permute-start.13) | collective-permute-done | bytes 524320 | tf_op jit(solution)/shard_map/ppermute | solution.py:293
  66.7 1.6 maximum_maximum_fusion
  68.3 2.5 collective-permute-start.17
  70.9 1.5 collective-permute-start.18
  73.6 10.7 %collective-permute-done.17.refs_26_ = bf16[1,512,512]{2,1,0:T(8,128)(2,1)S(1)} collective-permute-done((bf16[1,512,512]{2,1,0:T(8,128)(2,1)}, bf16[1,512,512]{2,1,0:T(8,128)(2,1)S(1)}, u32[]{:S(2)}, u32[]{:S(2)}) %collective-permute-start.17) | collective-permute-done | bytes 524320 | tf_op jit(solution)/shard_map/ppermute | solution.py:293
  87.9 1.8 collective-permute-start.25
  89.7 6.0 %collective-permute-done.21.refs_30_ = bf16[1,512,512]{2,1,0:T(8,128)(2,1)} collective-permute-done((bf16[1,512,512]{2,1,0:T(8,128)(2,1)}, bf16[1,512,512]{2,1,0:T(8,128)(2,1)}, u32[]{:S(2)}, u32[]{:S(2)}) %collective-permute-start.21) | collective-permute-done | bytes 524320 | tf_op jit(solution)/shard_map/ppermute | solution.py:293
  95.8 1.6 collective-permute-start.26
  97.9 1.6 collective-permute-start.29
  99.5 7.5 %collective-permute-done.25.refs_24_ = bf16[1,512,512]{2,1,0:T(8,128)(2,1)} collective-permute-done((bf16[1,512,512]{2,1,0:T(8,128)(2,1)S(1)}, bf16[1,512,512]{2,1,0:T(8,128)(2,1)}, u32[]{:S(2)}, u32[]{:S(2)}) %collective-permute-start.25) | collective-permute-done | bytes 524320 | tf_op jit(solution)/shard_map/ppermute | solution.py:293
  106.9 3.2 %collective-permute-done.26.refs_11_ = bf16[512,512]{1,0:T(8,128)(2,1)S(1)} collective-permute-done((bf16[512,512]{1,0:T(8,128)(2,1)S(1)}, bf16[512,512]{1,0:T(8,128)(2,1)S(1)}, u32[]{:S(2)}, u32[]{:S(2)}) %collective-permute-start.26) | collective-permute-done | bytes 524320 | tf_op jit(solution)/shard_map/ppermute | solution.py:199
  113.0 1.4 collective-permute-start.31
  116.7 3.6 %collective-permute-done.30.refs_13_ = bf16[256,512]{1,0:T(8,128)(2,1)S(1)} collective-permute-done((bf16[256,512]{1,0:T(8,128)(2,1)S(1)}, bf16[256,512]{1,0:T(8,128)(2,1)S(1)}, u32[]{:S(2)}, u32[]{:S(2)}) %collective-permute-start.30) | collective-permute-done | bytes 262176 | tf_op jit(solution)/shard_map/ppermute | solution.py:199
  121.6 1.4 collective-permute-start.34
  123.8 1.6 collective-permute-start.37
  125.3 6.6 %collective-permute-done.33.refs_28_ = bf16[1,512,512]{2,1,0:T(8,128)(2,1)} collective-permute-done((bf16[1,512,512]{2,1,0:T(8,128)(2,1)}, bf16[1,512,512]{2,1,0:T(8,128)(2,1)}, u32[]{:S(2)}, u32[]{:S(2)}) %collective-permute-start.33) | collective-permute-done | bytes 524320 | tf_op jit(solution)/shard_map/ppermute | solution.py:293
  131.9 4.1 %collective-permute-done.34.refs_16_ = bf16[512,512]{1,0:T(8,128)(2,1)S(1)} collective-permute-done((bf16[512,512]{1,0:T(8,128)(2,1)S(1)}, bf16[512,512]{1,0:T(8,128)(2,1)S(1)}, u32[]{:S(2)}, u32[]{:S(2)}) %collective-permute-start.34) | collective-permute-done | bytes 524320 | tf_op jit(solution)/shard_map/ppermute | solution.py:199
  138.6 1.5 collective-permute-start.39
  140.1 1.6 collective-permute-start.41
  142.1 3.9 %collective-permute-done.38.refs_18_ = bf16[256,512]{1,0:T(8,128)(2,1)} collective-permute-done((bf16[256,512]{1,0:T(8,128)(2,1)S(1)}, bf16[256,512]{1,0:T(8,128)(2,1)}, u32[]{:S(2)}, u32[]{:S(2)}) %collective-permute-start.38) | collective-permute-done | bytes 262176 | tf_op jit(solution)/shard_map/ppermute | solution.py:199
  146.0 1.4 collective-permute-done.39.refs_19_
  150.5 1.6 collective-permute-start.43
  152.1 3.4 %collective-permute-done.41.refs_30_ = bf16[1,512,512]{2,1,0:T(8,128)(2,1)} collective-permute-done((bf16[1,512,512]{2,1,0:T(8,128)(2,1)}, bf16[1,512,512]{2,1,0:T(8,128)(2,1)}, u32[]{:S(2)}, u32[]{:S(2)}) %collective-permute-start.41) | collective-permute-done | bytes 524320 | tf_op jit(solution)/shard_map/ppermute | solution.py:293
  155.5 36.1 %shard_map.37.refs_35_ = f32[4,4,128,512]{3,2,1,0:T(8,128)} custom-call(s32[1]{0:T(128)} %bitcast.half_ref, s32[2,4]{1,0:T(2,128)} %gather_fusion.2, s32[4]{0:T(128)} %fusion.2.pick_ref, s32[2]{0:T(128)} %pad_add_fusion.1.tile_ref, bf16[512,512]{1,0:T(8,128)(2,1)} %bitcast.69, bf16[512,512]{1,0:T(8,128)(2,1)} %copy-done.7, bf16[512,512]{1,0:T(8,128)(2,1)} %copy-done.8, ...), custom_call_target="tpu_custom_call" | custom-call | flops 21474836480 | bytes 29360128 | tf_op jit(solution)/shard_map/pallas_call | solution.py:170
  194.8 30.2 %shard_map.39 = bf16[3,4,128,512]{3,2,1,0:T(8,128)(2,1)} custom-call(s32[1]{0:T(128)} %bitcast.half_ref, s32[2,3]{1,0:T(2,128)} %bitcast.92, s32[3]{0:T(128)} %bitcast.93, s32[2]{0:T(128)} %pad_add_fusion.tile_ref, bf16[512,512]{1,0:T(8,128)(2,1)} %bitcast.70, bf16[512,512]{1,0:T(8,128)(2,1)} %copy-done.7, bf16[512,512]{1,0:T(8,128)(2,1)} %copy-done.8, ...), custom_call_target="tpu_custom_call" | custom-call | flops 16106127360 | bytes 29360128 | tf_op jit(solution)/shard_map/pallas_call | solution.py:170
  225.1 1.5 slice_bitcast_fusion.2
  227.6 2.0 collective-permute-start.46
  230.9 23.5 %shard_map.38 = f32[1,4,128,512]{3,2,1,0:T(8,128)} custom-call(s32[1]{0:T(128)} %bitcast.half_ref, s32[2,1]{1,0:T(2,128)} %slice.66.live_ref, s32[1]{0:T(128)} %slice.67.pick_ref, s32[2]{0:T(128)} %pad_add_fusion.tile_ref, bf16[512,512]{1,0:T(8,128)(2,1)} %bitcast.71, bf16[512,512]{1,0:T(8,128)(2,1)} %copy-done.7, bf16[512,512]{1,0:T(8,128)(2,1)} %copy-done.8, ...), custom_call_target="tpu_custom_call" | custom-call | flops 5368709120 | bytes 29360128 | tf_op jit(solution)/shard_map/pallas_call | solution.py:170
  254.4 18.6 %collective-permute-done.46 = bf16[4,128,512]{2,1,0:T(8,128)(2,1)S(1)} collective-permute-done((bf16[4,128,512]{2,1,0:T(8,128)(2,1)S(1)}, bf16[4,128,512]{2,1,0:T(8,128)(2,1)S(1)}, u32[]{:S(2)}, u32[]{:S(2)}) %collective-permute-start.46) | collective-permute-done | bytes 524320 | tf_op jit(solution)/shard_map/ppermute | solution.py:203
  273.0 2.6 collective-permute-done.47
  275.6 1.6 fusion.9
  279.0 1.8 collective-permute-start.48
  280.8 3.8 %collective-permute-done.50 = bf16[4,128,128]{2,1,0:T(8,128)(2,1)S(1)} collective-permute-done((bf16[4,128,128]{2,1,0:T(8,128)(2,1)S(1)}, bf16[4,128,128]{2,1,0:T(8,128)(2,1)S(1)}, u32[]{:S(2)}, u32[]{:S(2)}) %collective-permute-start.50) | collective-permute-done | bytes 131104 | tf_op jit(solution)/shard_map/ppermute | solution.py:199
  286.7 1.6 copy.16
  (169 shorter events, 34.3 us)
Async XLA Ops:
  6.5 104.9 %all-gather.2.cloned.1.call-start = ((), (), s32[]{:S(2)}) async-start(), calls=%async_computation | async-start | bytes 6291456 | tf_op jit(solution)/shard_map/all_gather | solution.py:311
  8.7 14.6 %collective-permute-start = (bf16[1,512,512]{2,1,0:T(8,128)(2,1)S(1)}, bf16[1,512,512]{2,1,0:T(8,128)(2,1)S(1)}, u32[]{:S(2)}, u32[]{:S(2)}) collective-permute-start(bf16[1,512,512]{2,1,0:T(8,128)(2,1)S(1)} %get-tuple-element.70), channel_id=1, source_target_pairs={{0,16},{16,24},{24,8},{8,0},{1,17},{17,25},{25,9},{9,1},{2,18},{18... | collective-permute-start | bytes 1572872 | tf_op jit(solution)/shard_map/ppermute | solution.py:293
  8.7 14.6 %collective-permute-start.1 = (bf16[512,512]{1,0:T(8,128)(2,1)S(1)}, bf16[512,512]{1,0:T(8,128)(2,1)S(1)}, u32[]{:S(2)}, u32[]{:S(2)}) collective-permute-start(bf16[512,512]{1,0:T(8,128)(2,1)S(1)} %bitcast.67), channel_id=1, source_target_pairs={{0,2},{2,0},{4,6},{6,4},{1,3},{3,1},{5,7},{7,5},{8,10},{10,8},{12,... | collective-permute-start | bytes 1572872 | tf_op jit(solution)/shard_map/ppermute | solution.py:199
  10.7 13.1 %collective-permute-start.2 = (bf16[512,512]{1,0:T(8,128)(2,1)S(1)}, bf16[512,512]{1,0:T(8,128)(2,1)S(1)}, u32[]{:S(2)}, u32[]{:S(2)}) collective-permute-start(bf16[512,512]{1,0:T(8,128)(2,1)S(1)} %bitcast.68), channel_id=1, source_target_pairs={{0,4},{2,6},{4,0},{6,2},{1,5},{3,7},{5,1},{7,3},{8,12},{10,14},{12... | collective-permute-start | bytes 1572872 | tf_op jit(solution)/shard_map/ppermute | solution.py:199
  23.8 17.1 %collective-permute-start.3 = (bf16[4,512,512]{2,1,0:T(8,128)(2,1)S(1)}, bf16[4,512,512]{2,1,0:T(8,128)(2,1)S(1)}, u32[]{:S(2)}, u32[]{:S(2)}) collective-permute-start(bf16[4,512,512]{2,1,0:T(8,128)(2,1)S(1)} %copy-done.1), channel_id=1, source_target_pairs={{0,1},{1,0},{2,3},{3,2},{4,5},{5,4},{6,7},{7,6},{8,9},{9,8},{10,11... | collective-permute-start | bytes 6291464 | tf_op jit(solution)/shard_map/ppermute | solution.py:199
  23.8 15.3 %collective-permute-start.5 = (bf16[1,512,512]{2,1,0:T(8,128)(2,1)S(1)}, bf16[1,512,512]{2,1,0:T(8,128)(2,1)}, u32[]{:S(2)}, u32[]{:S(2)}) collective-permute-start(bf16[1,512,512]{2,1,0:T(8,128)(2,1)S(1)} %get-tuple-element.77), channel_id=1, source_target_pairs={{0,16},{16,24},{24,8},{8,0},{1,17},{17,25},{25,9},{9,1},{2,18},{18... | collective-permute-start | bytes 1572872 | tf_op jit(solution)/shard_map/ppermute | solution.py:293
  26.4 14.4 %collective-permute-start.4 = (bf16[1,512,512]{2,1,0:T(8,128)(2,1)S(1)}, bf16[1,512,512]{2,1,0:T(8,128)(2,1)S(1)}, u32[]{:S(2)}, u32[]{:S(2)}) collective-permute-start(bf16[1,512,512]{2,1,0:T(8,128)(2,1)S(1)} %collective-permute-done.refs_24_), channel_id=1, source_target_pairs={{0,1},{1,0},{2,3},{3,2},{4,5},{5,4},{6,7},{7,6},{8,9},{9,8},{10,11... | collective-permute-start | bytes 1572872 | tf_op jit(solution)/shard_map/ppermute | solution.py:199
  26.6 14.2 %collective-permute-start.6 = (bf16[256,512]{1,0:T(8,128)(2,1)S(1)}, bf16[256,512]{1,0:T(8,128)(2,1)S(1)}, u32[]{:S(2)}, u32[]{:S(2)}) collective-permute-start(bf16[256,512]{1,0:T(8,128)(2,1)S(1)} %slice.68), channel_id=1, source_target_pairs={{0,4},{2,6},{4,0},{6,2},{1,5},{3,7},{5,1},{7,3},{8,12},{10,14},{12... | collective-permute-start | bytes 786440 | tf_op jit(solution)/shard_map/ppermute | solution.py:199
  28.2 12.6 %collective-permute-start.7 = (bf16[256,512]{1,0:T(8,128)(2,1)S(1)}, bf16[256,512]{1,0:T(8,128)(2,1)S(1)}, u32[]{:S(2)}, u32[]{:S(2)}) collective-permute-start(bf16[256,512]{1,0:T(8,128)(2,1)S(1)} %slice.69), channel_id=1, source_target_pairs={{0,2},{2,0},{4,6},{6,4},{1,3},{3,1},{5,7},{7,5},{8,10},{10,8},{12,... | collective-permute-start | bytes 786440 | tf_op jit(solution)/shard_map/ppermute | solution.py:199
  39.1 15.8 %collective-permute-start.9 = (bf16[1,512,512]{2,1,0:T(8,128)(2,1)S(1)}, bf16[1,512,512]{2,1,0:T(8,128)(2,1)}, u32[]{:S(2)}, u32[]{:S(2)}) collective-permute-start(bf16[1,512,512]{2,1,0:T(8,128)(2,1)S(1)} %get-tuple-element.81), channel_id=1, source_target_pairs={{0,16},{16,24},{24,8},{8,0},{1,17},{17,25},{25,9},{9,1},{2,18},{18... | collective-permute-start | bytes 1572872 | tf_op jit(solution)/shard_map/ppermute | solution.py:293
  42.2 13.2 %collective-permute-start.10 = (bf16[4,512,128]{2,1,0:T(8,128)(2,1)S(1)}, bf16[4,512,128]{2,1,0:T(8,128)(2,1)S(1)}, u32[]{:S(2)}, u32[]{:S(2)}) collective-permute-start(bf16[4,512,128]{2,1,0:T(8,128)(2,1)S(1)} %bitcast.88), channel_id=1, source_target_pairs={{0,2},{2,0},{4,6},{6,4},{1,3},{3,1},{5,7},{7,5},{8,10},{10,8},{12,... | collective-permute-start | bytes 1572872 | tf_op jit(solution)/shard_map/ppermute | solution.py:199
  42.8 12.9 %collective-permute-start.11 = (bf16[4,512,128]{2,1,0:T(8,128)(2,1)S(1)}, bf16[4,512,128]{2,1,0:T(8,128)(2,1)S(1)}, u32[]{:S(2)}, u32[]{:S(2)}) collective-permute-start(bf16[4,512,128]{2,1,0:T(8,128)(2,1)S(1)} %bitcast.89), channel_id=1, source_target_pairs={{0,4},{2,6},{4,0},{6,2},{1,5},{3,7},{5,1},{7,3},{8,12},{10,14},{12... | collective-permute-start | bytes 1572872 | tf_op jit(solution)/shard_map/ppermute | solution.py:199
  44.3 11.4 %collective-permute-start.8 = (bf16[1,512,512]{2,1,0:T(8,128)(2,1)}, bf16[1,512,512]{2,1,0:T(8,128)(2,1)}, u32[]{:S(2)}, u32[]{:S(2)}) collective-permute-start(bf16[1,512,512]{2,1,0:T(8,128)(2,1)} %collective-permute-done.5.refs_22_), channel_id=1, source_target_pairs={{0,1},{1,0},{2,3},{3,2},{4,5},{5,4},{6,7},{7,6},{8,9},{9,8},{10,11... | collective-permute-start | bytes 1572872 | tf_op jit(solution)/shard_map/ppermute | solution.py:199
  44.3 20.6 %collective-permute-start.13 = (bf16[1,512,512]{2,1,0:T(8,128)(2,1)S(1)}, bf16[1,512,512]{2,1,0:T(8,128)(2,1)}, u32[]{:S(2)}, u32[]{:S(2)}) collective-permute-start(bf16[1,512,512]{2,1,0:T(8,128)(2,1)S(1)} %collective-permute-done.refs_24_), channel_id=1, source_target_pairs={{0,16},{16,24},{24,8},{8,0},{1,17},{17,25},{25,9},{9,1},{2,18},{18... | collective-permute-start | bytes 1572872 | tf_op jit(solution)/shard_map/ppermute | solution.py:293
  55.7 10.1 %collective-permute-start.12 = (bf16[1,512,512]{2,1,0:T(8,128)(2,1)}, bf16[1,512,512]{2,1,0:T(8,128)(2,1)S(1)}, u32[]{:S(2)}, u32[]{:S(2)}) collective-permute-start(bf16[1,512,512]{2,1,0:T(8,128)(2,1)} %collective-permute-done.9.refs_22_), channel_id=1, source_target_pairs={{0,1},{1,0},{2,3},{3,2},{4,5},{5,4},{6,7},{7,6},{8,9},{9,8},{10,11... | collective-permute-start | bytes 1572872 | tf_op jit(solution)/shard_map/ppermute | solution.py:199
  55.7 9.1 %collective-permute-start.14 = (bf16[2,512,128]{2,1,0:T(8,128)(2,1)S(1)}, bf16[2,512,128]{2,1,0:T(8,128)(2,1)S(1)}, u32[]{:S(2)}, u32[]{:S(2)}) collective-permute-start(bf16[2,512,128]{2,1,0:T(8,128)(2,1)S(1)} %slice.70), channel_id=1, source_target_pairs={{0,4},{2,6},{4,0},{6,2},{1,5},{3,7},{5,1},{7,3},{8,12},{10,14},{12... | collective-permute-start | bytes 786440 | tf_op jit(solution)/shard_map/ppermute | solution.py:199
  57.3 8.5 %collective-permute-start.15 = (bf16[2,512,128]{2,1,0:T(8,128)(2,1)S(1)}, bf16[2,512,128]{2,1,0:T(8,128)(2,1)S(1)}, u32[]{:S(2)}, u32[]{:S(2)}) collective-permute-start(bf16[2,512,128]{2,1,0:T(8,128)(2,1)S(1)} %slice.71), channel_id=1, source_target_pairs={{0,2},{2,0},{4,6},{6,4},{1,3},{3,1},{5,7},{7,5},{8,10},{10,8},{12,... | collective-permute-start | bytes 786440 | tf_op jit(solution)/shard_map/ppermute | solution.py:199
  68.3 16.0 %collective-permute-start.17 = (bf16[1,512,512]{2,1,0:T(8,128)(2,1)}, bf16[1,512,512]{2,1,0:T(8,128)(2,1)S(1)}, u32[]{:S(2)}, u32[]{:S(2)}) collective-permute-start(bf16[1,512,512]{2,1,0:T(8,128)(2,1)} %collective-permute-done.5.refs_22_), channel_id=1, source_target_pairs={{0,16},{16,24},{24,8},{8,0},{1,17},{17,25},{25,9},{9,1},{2,18},{18... | collective-permute-start | bytes 1572872 | tf_op jit(solution)/shard_map/ppermute | solution.py:293
  70.9 13.5 %collective-permute-start.16 = (bf16[1,512,512]{2,1,0:T(8,128)(2,1)}, bf16[1,512,512]{2,1,0:T(8,128)(2,1)S(1)}, u32[]{:S(2)}, u32[]{:S(2)}) collective-permute-start(bf16[1,512,512]{2,1,0:T(8,128)(2,1)} %collective-permute-done.13.refs_26_), channel_id=1, source_target_pairs={{0,1},{1,0},{2,3},{3,2},{4,5},{5,4},{6,7},{7,6},{8,9},{9,8},{10,11... | collective-permute-start | bytes 1572872 | tf_op jit(solution)/shard_map/ppermute | solution.py:199
  70.9 14.3 %collective-permute-start.18 = (bf16[512,512]{1,0:T(8,128)(2,1)S(1)}, bf16[512,512]{1,0:T(8,128)(2,1)S(1)}, u32[]{:S(2)}, u32[]{:S(2)}) collective-permute-start(bf16[512,512]{1,0:T(8,128)(2,1)S(1)} %bitcast.72), channel_id=1, source_target_pairs={{0,2},{2,0},{4,6},{6,4},{1,3},{3,1},{5,7},{7,5},{8,10},{10,8},{12,... | collective-permute-start | bytes 1572872 | tf_op jit(solution)/shard_map/ppermute | solution.py:199
  72.4 14.1 %collective-permute-start.19 = (bf16[512,512]{1,0:T(8,128)(2,1)S(1)}, bf16[512,512]{1,0:T(8,128)(2,1)S(1)}, u32[]{:S(2)}, u32[]{:S(2)}) collective-permute-start(bf16[512,512]{1,0:T(8,128)(2,1)S(1)} %bitcast.73), channel_id=1, source_target_pairs={{0,4},{2,6},{4,0},{6,2},{1,5},{3,7},{5,1},{7,3},{8,12},{10,14},{12... | collective-permute-start | bytes 1572872 | tf_op jit(solution)/shard_map/ppermute | solution.py:199
  72.9 22.8 %collective-permute-start.21 = (bf16[1,512,512]{2,1,0:T(8,128)(2,1)}, bf16[1,512,512]{2,1,0:T(8,128)(2,1)}, u32[]{:S(2)}, u32[]{:S(2)}) collective-permute-start(bf16[1,512,512]{2,1,0:T(8,128)(2,1)} %collective-permute-done.13.refs_26_), channel_id=1, source_target_pairs={{0,16},{16,24},{24,8},{8,0},{1,17},{17,25},{25,9},{9,1},{2,18},{18... | collective-permute-start | bytes 1572872 | tf_op jit(solution)/shard_map/ppermute | solution.py:293
  86.4 9.3 %collective-permute-start.20 = (bf16[1,512,512]{2,1,0:T(8,128)(2,1)S(1)}, bf16[1,512,512]{2,1,0:T(8,128)(2,1)S(1)}, u32[]{:S(2)}, u32[]{:S(2)}) collective-permute-start(bf16[1,512,512]{2,1,0:T(8,128)(2,1)S(1)} %collective-permute-done.17.refs_26_), channel_id=1, source_target_pairs={{0,1},{1,0},{2,3},{3,2},{4,5},{5,4},{6,7},{7,6},{8,9},{9,8},{10,11... | collective-permute-start | bytes 1572872 | tf_op jit(solution)/shard_map/ppermute | solution.py:199
  86.5 9.2 %collective-permute-start.22 = (bf16[256,512]{1,0:T(8,128)(2,1)S(1)}, bf16[256,512]{1,0:T(8,128)(2,1)S(1)}, u32[]{:S(2)}, u32[]{:S(2)}) collective-permute-start(bf16[256,512]{1,0:T(8,128)(2,1)S(1)} %slice.72), channel_id=1, source_target_pairs={{0,4},{2,6},{4,0},{6,2},{1,5},{3,7},{5,1},{7,3},{8,12},{10,14},{12... | collective-permute-start | bytes 786440 | tf_op jit(solution)/shard_map/ppermute | solution.py:199
  87.0 8.7 %collective-permute-start.23 = (bf16[256,512]{1,0:T(8,128)(2,1)S(1)}, bf16[256,512]{1,0:T(8,128)(2,1)S(1)}, u32[]{:S(2)}, u32[]{:S(2)}) collective-permute-start(bf16[256,512]{1,0:T(8,128)(2,1)S(1)} %slice.73), channel_id=1, source_target_pairs={{0,2},{2,0},{4,6},{6,4},{1,3},{3,1},{5,7},{7,5},{8,10},{10,8},{12,... | collective-permute-start | bytes 786440 | tf_op jit(solution)/shard_map/ppermute | solution.py:199
  87.9 19.0 %collective-permute-start.25 = (bf16[1,512,512]{2,1,0:T(8,128)(2,1)S(1)}, bf16[1,512,512]{2,1,0:T(8,128)(2,1)}, u32[]{:S(2)}, u32[]{:S(2)}) collective-permute-start(bf16[1,512,512]{2,1,0:T(8,128)(2,1)S(1)} %get-tuple-element.100), channel_id=1, source_target_pairs={{0,16},{16,24},{24,8},{8,0},{1,17},{17,25},{25,9},{9,1},{2,18},{18... | collective-permute-start | bytes 1572872 | tf_op jit(solution)/shard_map/ppermute | solution.py:293
  95.7 11.2 %collective-permute-start.24 = (bf16[1,512,512]{2,1,0:T(8,128)(2,1)}, bf16[1,512,512]{2,1,0:T(8,128)(2,1)S(1)}, u32[]{:S(2)}, u32[]{:S(2)}) collective-permute-start(bf16[1,512,512]{2,1,0:T(8,128)(2,1)} %collective-permute-done.21.refs_30_), channel_id=1, source_target_pairs={{0,1},{1,0},{2,3},{3,2},{4,5},{5,4},{6,7},{7,6},{8,9},{9,8},{10,11... | collective-permute-start | bytes 1572872 | tf_op jit(solution)/shard_map/ppermute | solution.py:199
  95.8 14.3 %collective-permute-start.26 = (bf16[512,512]{1,0:T(8,128)(2,1)S(1)}, bf16[512,512]{1,0:T(8,128)(2,1)S(1)}, u32[]{:S(2)}, u32[]{:S(2)}) collective-permute-start(bf16[512,512]{1,0:T(8,128)(2,1)S(1)} %bitcast.77), channel_id=1, source_target_pairs={{0,2},{2,0},{4,6},{6,4},{1,3},{3,1},{5,7},{7,5},{8,10},{10,8},{12,... | collective-permute-start | bytes 1572872 | tf_op jit(solution)/shard_map/ppermute | solution.py:199
  97.4 14.1 %collective-permute-start.27 = (bf16[512,512]{1,0:T(8,128)(2,1)S(1)}, bf16[512,512]{1,0:T(8,128)(2,1)}, u32[]{:S(2)}, u32[]{:S(2)}) collective-permute-start(bf16[512,512]{1,0:T(8,128)(2,1)S(1)} %bitcast.78), channel_id=1, source_target_pairs={{0,4},{2,6},{4,0},{6,2},{1,5},{3,7},{5,1},{7,3},{8,12},{10,14},{12... | collective-permute-start | bytes 1572872 | tf_op jit(solution)/shard_map/ppermute | solution.py:199
  97.9 18.8 %collective-permute-start.29 = (bf16[1,512,512]{2,1,0:T(8,128)(2,1)}, bf16[1,512,512]{2,1,0:T(8,128)(2,1)}, u32[]{:S(2)}, u32[]{:S(2)}) collective-permute-start(bf16[1,512,512]{2,1,0:T(8,128)(2,1)} %collective-permute-done.9.refs_22_), channel_id=1, source_target_pairs={{0,16},{16,24},{24,8},{8,0},{1,17},{17,25},{25,9},{9,1},{2,18},{18... | collective-permute-start | bytes 1572872 | tf_op jit(solution)/shard_map/ppermute | solution.py:293
  111.5 10.1 %collective-permute-start.28 = (bf16[1,512,512]{2,1,0:T(8,128)(2,1)}, bf16[1,512,512]{2,1,0:T(8,128)(2,1)S(1)}, u32[]{:S(2)}, u32[]{:S(2)}) collective-permute-start(bf16[1,512,512]{2,1,0:T(8,128)(2,1)} %collective-permute-done.25.refs_24_), channel_id=1, source_target_pairs={{0,1},{1,0},{2,3},{3,2},{4,5},{5,4},{6,7},{7,6},{8,9},{9,8},{10,11... | collective-permute-start | bytes 1572872 | tf_op jit(solution)/shard_map/ppermute | solution.py:199
  111.5 8.8 %collective-permute-start.30 = (bf16[256,512]{1,0:T(8,128)(2,1)S(1)}, bf16[256,512]{1,0:T(8,128)(2,1)S(1)}, u32[]{:S(2)}, u32[]{:S(2)}) collective-permute-start(bf16[256,512]{1,0:T(8,128)(2,1)S(1)} %slice.74), channel_id=1, source_target_pairs={{0,4},{2,6},{4,0},{6,2},{1,5},{3,7},{5,1},{7,3},{8,12},{10,14},{12... | collective-permute-start | bytes 786440 | tf_op jit(solution)/shard_map/ppermute | solution.py:199
  113.0 8.5 %collective-permute-start.31 = (bf16[256,512]{1,0:T(8,128)(2,1)S(1)}, bf16[256,512]{1,0:T(8,128)(2,1)S(1)}, u32[]{:S(2)}, u32[]{:S(2)}) collective-permute-start(bf16[256,512]{1,0:T(8,128)(2,1)S(1)} %slice.75), channel_id=1, source_target_pairs={{0,2},{2,0},{4,6},{6,4},{1,3},{3,1},{5,7},{7,5},{8,10},{10,8},{12,... | collective-permute-start | bytes 786440 | tf_op jit(solution)/shard_map/ppermute | solution.py:199
  115.8 16.1 %collective-permute-start.33 = (bf16[1,512,512]{2,1,0:T(8,128)(2,1)}, bf16[1,512,512]{2,1,0:T(8,128)(2,1)}, u32[]{:S(2)}, u32[]{:S(2)}) collective-permute-start(bf16[1,512,512]{2,1,0:T(8,128)(2,1)} %collective-permute-done.25.refs_24_), channel_id=1, source_target_pairs={{0,16},{16,24},{24,8},{8,0},{1,17},{17,25},{25,9},{9,1},{2,18},{18... | collective-permute-start | bytes 1572872 | tf_op jit(solution)/shard_map/ppermute | solution.py:293
  121.6 10.3 %collective-permute-start.32 = (bf16[1,512,512]{2,1,0:T(8,128)(2,1)}, bf16[1,512,512]{2,1,0:T(8,128)(2,1)S(1)}, u32[]{:S(2)}, u32[]{:S(2)}) collective-permute-start(bf16[1,512,512]{2,1,0:T(8,128)(2,1)} %collective-permute-done.29.refs_28_), channel_id=1, source_target_pairs={{0,1},{1,0},{2,3},{3,2},{4,5},{5,4},{6,7},{7,6},{8,9},{9,8},{10,11... | collective-permute-start | bytes 1572872 | tf_op jit(solution)/shard_map/ppermute | solution.py:199
  121.6 14.3 %collective-permute-start.34 = (bf16[512,512]{1,0:T(8,128)(2,1)S(1)}, bf16[512,512]{1,0:T(8,128)(2,1)S(1)}, u32[]{:S(2)}, u32[]{:S(2)}) collective-permute-start(bf16[512,512]{1,0:T(8,128)(2,1)S(1)} %bitcast.82), channel_id=1, source_target_pairs={{0,2},{2,0},{4,6},{6,4},{1,3},{3,1},{5,7},{7,5},{8,10},{10,8},{12,... | collective-permute-start | bytes 1572872 | tf_op jit(solution)/shard_map/ppermute | solution.py:199
  123.1 14.0 %collective-permute-start.35 = (bf16[512,512]{1,0:T(8,128)(2,1)S(1)}, bf16[512,512]{1,0:T(8,128)(2,1)S(1)}, u32[]{:S(2)}, u32[]{:S(2)}) collective-permute-start(bf16[512,512]{1,0:T(8,128)(2,1)S(1)} %bitcast.83), channel_id=1, source_target_pairs={{0,4},{2,6},{4,0},{6,2},{1,5},{3,7},{5,1},{7,3},{8,12},{10,14},{12... | collective-permute-start | bytes 1572872 | tf_op jit(solution)/shard_map/ppermute | solution.py:199
  123.8 18.4 %collective-permute-start.37 = (bf16[1,512,512]{2,1,0:T(8,128)(2,1)}, bf16[1,512,512]{2,1,0:T(8,128)(2,1)}, u32[]{:S(2)}, u32[]{:S(2)}) collective-permute-start(bf16[1,512,512]{2,1,0:T(8,128)(2,1)} %collective-permute-done.29.refs_28_), channel_id=1, source_target_pairs={{0,16},{16,24},{24,8},{8,0},{1,17},{17,25},{25,9},{9,1},{2,18},{18... | collective-permute-start | bytes 1572872 | tf_op jit(solution)/shard_map/ppermute | solution.py:293
  137.1 10.3 %collective-permute-start.36 = (bf16[1,512,512]{2,1,0:T(8,128)(2,1)}, bf16[1,512,512]{2,1,0:T(8,128)(2,1)}, u32[]{:S(2)}, u32[]{:S(2)}) collective-permute-start(bf16[1,512,512]{2,1,0:T(8,128)(2,1)} %collective-permute-done.33.refs_28_), channel_id=1, source_target_pairs={{0,1},{1,0},{2,3},{3,2},{4,5},{5,4},{6,7},{7,6},{8,9},{9,8},{10,11... | collective-permute-start | bytes 1572872 | tf_op jit(solution)/shard_map/ppermute | solution.py:199
  137.1 8.9 %collective-permute-start.38 = (bf16[256,512]{1,0:T(8,128)(2,1)S(1)}, bf16[256,512]{1,0:T(8,128)(2,1)}, u32[]{:S(2)}, u32[]{:S(2)}) collective-permute-start(bf16[256,512]{1,0:T(8,128)(2,1)S(1)} %slice.76), channel_id=1, source_target_pairs={{0,4},{2,6},{4,0},{6,2},{1,5},{3,7},{5,1},{7,3},{8,12},{10,14},{12... | collective-permute-start | bytes 786440 | tf_op jit(solution)/shard_map/ppermute | solution.py:199
  138.6 8.7 %collective-permute-start.39 = (bf16[256,512]{1,0:T(8,128)(2,1)}, bf16[256,512]{1,0:T(8,128)(2,1)}, u32[]{:S(2)}, u32[]{:S(2)}) collective-permute-start(bf16[256,512]{1,0:T(8,128)(2,1)} %slice.77), channel_id=1, source_target_pairs={{0,2},{2,0},{4,6},{6,4},{1,3},{3,1},{5,7},{7,5},{8,10},{10,8},{12,... | collective-permute-start | bytes 786440 | tf_op jit(solution)/shard_map/ppermute | solution.py:199
  140.1 15.3 %collective-permute-start.41 = (bf16[1,512,512]{2,1,0:T(8,128)(2,1)}, bf16[1,512,512]{2,1,0:T(8,128)(2,1)}, u32[]{:S(2)}, u32[]{:S(2)}) collective-permute-start(bf16[1,512,512]{2,1,0:T(8,128)(2,1)} %collective-permute-done.33.refs_28_), channel_id=1, source_target_pairs={{0,16},{16,24},{24,8},{8,0},{1,17},{17,25},{25,9},{9,1},{2,18},{18... | collective-permute-start | bytes 1572872 | tf_op jit(solution)/shard_map/ppermute | solution.py:293
  147.3 8.1 %collective-permute-start.40 = (bf16[1,512,512]{2,1,0:T(8,128)(2,1)}, bf16[1,512,512]{2,1,0:T(8,128)(2,1)}, u32[]{:S(2)}, u32[]{:S(2)}) collective-permute-start(bf16[1,512,512]{2,1,0:T(8,128)(2,1)} %collective-permute-done.37.refs_32_), channel_id=1, source_target_pairs={{0,1},{1,0},{2,3},{3,2},{4,5},{5,4},{6,7},{7,6},{8,9},{9,8},{10,11... | collective-permute-start | bytes 1572872 | tf_op jit(solution)/shard_map/ppermute | solution.py:199
  150.5 41.2 %collective-permute-start.43 = (bf16[1,512,512]{2,1,0:T(8,128)(2,1)}, bf16[1,512,512]{2,1,0:T(8,128)(2,1)}, u32[]{:S(2)}, u32[]{:S(2)}) collective-permute-start(bf16[1,512,512]{2,1,0:T(8,128)(2,1)} %copy-done.14), channel_id=1, source_target_pairs={{0,16},{16,24},{24,8},{8,0},{1,17},{17,25},{25,9},{9,1},{2,18},{18... | collective-permute-start | bytes 1572872 | tf_op jit(solution)/shard_map/ppermute | solution.py:293
  155.4 36.2 %collective-permute-start.42 = (bf16[1,512,512]{2,1,0:T(8,128)(2,1)}, bf16[1,512,512]{2,1,0:T(8,128)(2,1)}, u32[]{:S(2)}, u32[]{:S(2)}) collective-permute-start(bf16[1,512,512]{2,1,0:T(8,128)(2,1)} %collective-permute-done.41.refs_30_), channel_id=1, source_target_pairs={{0,1},{1,0},{2,3},{3,2},{4,5},{5,4},{6,7},{7,6},{8,9},{9,8},{10,11... | collective-permute-start | bytes 1572872 | tf_op jit(solution)/shard_map/ppermute | solution.py:199
  226.5 27.9 %collective-permute-start.45 = (bf16[4,128,512]{2,1,0:T(8,128)(2,1)S(1)}, bf16[4,128,512]{2,1,0:T(8,128)(2,1)S(1)}, u32[]{:S(2)}, u32[]{:S(2)}) collective-permute-start(bf16[4,128,512]{2,1,0:T(8,128)(2,1)S(1)} %get-tuple-element.141), channel_id=1, source_target_pairs={{0,8},{8,16},{16,24},{24,0},{1,9},{9,17},{17,25},{25,1},{2,10},{10... | collective-permute-start | bytes 1572872 | tf_op jit(solution)/shard_map/ppermute | solution.py:203
  227.6 45.4 %collective-permute-start.46 = (bf16[4,128,512]{2,1,0:T(8,128)(2,1)S(1)}, bf16[4,128,512]{2,1,0:T(8,128)(2,1)S(1)}, u32[]{:S(2)}, u32[]{:S(2)}) collective-permute-start(bf16[4,128,512]{2,1,0:T(8,128)(2,1)S(1)} %get-tuple-element.143), channel_id=1, source_target_pairs={{0,16},{8,24},{16,0},{24,8},{1,17},{9,25},{17,1},{25,9},{2,18},{10... | collective-permute-start | bytes 1572872 | tf_op jit(solution)/shard_map/ppermute | solution.py:203
  229.6 46.0 %collective-permute-start.47 = (bf16[4,128,512]{2,1,0:T(8,128)(2,1)S(1)}, bf16[4,128,512]{2,1,0:T(8,128)(2,1)S(1)}, u32[]{:S(2)}, u32[]{:S(2)}) collective-permute-start(bf16[4,128,512]{2,1,0:T(8,128)(2,1)S(1)} %get-tuple-element.142), channel_id=1, source_target_pairs={{0,24},{8,0},{16,8},{24,16},{1,25},{9,1},{17,9},{25,17},{2,26},{10... | collective-permute-start | bytes 1572872 | tf_op jit(solution)/shard_map/ppermute | solution.py:203
  (37 other events, 987.7 us)
Sparse Core Ops, SparseCore 0:
  68.5 13.2 all-gather.1

commit v8 on v6

--- a/solution.py
+++ b/solution.py
@@ -237,7 +237,12 @@
 
     d_tiles = [at_level(table) for table in near]
     tiles = jnp.arange(NTV)
-    targets = (left_index + 1 + tiles) % NTV
+    away = [NTV // 2] + [i for i in range(1, NTV) if i != NTV // 2] + [0]
+    targets = jnp.stack([d_tiles[i] for i in away])
+
+    def around(value, step):
+        return lax.ppermute(value, "left", [(order[p], order[(p + step) % NTV]) for p in range(NTV)])
+
     pick = (targets ^ right_index).astype(jnp.int32)
     own_c = lax.dynamic_index_in_dim(listed, left_index, 1, keepdims=False)
     live = lax.dynamic_index_in_dim(own_c, right_index, 1, keepdims=False)[targets]
@@ -315,11 +320,9 @@
             held["sum"] = contract((0, 2), None, 0, jnp.float32)
             waiting[slot + 1].append("sum")
     early = contract((1, 3), held["sum"], 0, jnp.bfloat16)
-    moved = [shift(early[t], "left", NTV, t + 1) for t in range(NTV // 2)]
+    moved = [around(early[t], away[t]) for t in range(NTV // 2)]
     late = contract((1, 3), held["sum"], 1, jnp.float32)
-    moved += [
-        shift(late[t].astype(jnp.bfloat16), "left", NTV, NTV // 2 + t + 1) for t in range(NTV // 2 - 1)
-    ]
+    moved += [around(late[t].astype(jnp.bfloat16), away[NTV // 2 + t]) for t in range(NTV // 2 - 1)]
     summed = late[NTV // 2 - 1]
     for piece in moved:
         summed = summed + piece.astype(jnp.float32)

time: 291 us -> 291 us (level)
  waiting for transfers between devices: 119 us -> 116 us
    ppermute x36, waiting for transfers between devices: 28.1 us -> 31.7 us  [partner(): return lax.ppermute(value, axis, [(i, i ^ flip) for i in range(size)])]
    ppermute x3, waiting for transfers between devices: 20.4 us -> 17.1 us  [around(): lax.ppermute(value, 'left', [(order[p], order[(p + step) % NTV]) for p in...]
    ppermute x12, waiting for transfers between devices: 70.8 us -> 67.7 us  [on_square(): lax.ppermute(held['block', s - 1, (i + 1) % NTV], 'left', ring)]
  transfers between devices with their start and end apart: 52 -> 52, of which waited for: 27 -> 28; matrix products, arithmetic and copies ran while one was open for 3% -> 3% of each run, Pallas kernels for 21% -> 21%
where the time goes in v8:
time: 291 us; the launch traced here: 286 us
  waiting for transfers between devices  116 us (40%)
  Pallas kernels  83.4 us (29%)
  starting transfers between devices  50.6 us (17%)
  local copies, waits for them, and re-layouts  16.7 us (6%)
  between operations  13.9 us (5%)
  other arithmetic  5.34 us (2%)
    pallas_call x3, Pallas kernels, ladder(): pl.pallas_call(functools.partial(ladder_kernel, steps, count, tile_count,...  83.4 us
    ppermute x12, waiting for transfers between devices, on_square(): lax.ppermute(held['block', s - 1, (i + 1) % NTV], 'left', ring)  67.7 us
    ppermute x36, waiting for transfers between devices, partner(): return lax.ppermute(value, axis, [(i, i ^ flip) for i in range(size)])  31.7 us
    ppermute x36, starting transfers between devices, partner(): return lax.ppermute(value, axis, [(i, i ^ flip) for i in range(size)])  26.8 us
    ppermute x12, starting transfers between devices, on_square(): lax.ppermute(held['block', s - 1, (i + 1) % NTV], 'left', ring)  20 us
    ppermute x3, waiting for transfers between devices, around(): lax.ppermute(value, 'left', [(order[p], order[(p + step) % NTV]) for p in...  17.1 us
  transfers between devices with their start and end apart: 52, of which 28 were waited for; matrix products, arithmetic and copies ran while one was open for 3% of the time, Pallas kernels for 21%

profile of v8, /device:TPU:8, one launch (start us, length us, event | category | flops | bytes accessed | tf_op | source)
XLA Modules:
  0.0 286.4 jit_solution(12840308468271503648)
XLA Ops:
  6.5 1.8 constant_dynamic-slice_fusion
  8.7 1.9 collective-permute-start.1
  10.7 1.5 collective-permute-start.2
  12.2 11.1 %collective-permute-done.refs_24_ = bf16[1,512,512]{2,1,0:T(8,128)(2,1)S(1)} collective-permute-done((bf16[1,512,512]{2,1,0:T(8,128)(2,1)S(1)}, bf16[1,512,512]{2,1,0:T(8,128)(2,1)S(1)}, u32[]{:S(2)}, u32[]{:S(2)}) %collective-permute-start) | collective-permute-done | bytes 524320 | tf_op jit(solution)/shard_map/ppermute | solution.py:299
  23.8 2.6 collective-permute-start.5
  26.6 1.6 collective-permute-start.6
  28.8 10.3 %collective-permute-done.5.refs_22_ = bf16[1,512,512]{2,1,0:T(8,128)(2,1)} collective-permute-done((bf16[1,512,512]{2,1,0:T(8,128)(2,1)S(1)}, bf16[1,512,512]{2,1,0:T(8,128)(2,1)}, u32[]{:S(2)}, u32[]{:S(2)}) %collective-permute-start.5) | collective-permute-done | bytes 524320 | tf_op jit(solution)/shard_map/ppermute | solution.py:299
  39.1 1.7 collective-permute-start.9
  42.3 1.5 collective-permute-start.11
  43.8 2.5 collective-permute-start.13
  46.3 8.6 %collective-permute-done.9.refs_22_ = bf16[1,512,512]{2,1,0:T(8,128)(2,1)S(1)} collective-permute-done((bf16[1,512,512]{2,1,0:T(8,128)(2,1)S(1)}, bf16[1,512,512]{2,1,0:T(8,128)(2,1)S(1)}, u32[]{:S(2)}, u32[]{:S(2)}) %collective-permute-start.9) | collective-permute-done | bytes 524320 | tf_op jit(solution)/shard_map/ppermute | solution.py:299
  56.0 1.5 collective-permute-start.14
  57.6 1.6 collective-permute-start.15
  59.4 5.4 %collective-permute-done.13.refs_26_ = bf16[1,512,512]{2,1,0:T(8,128)(2,1)} collective-permute-done((bf16[1,512,512]{2,1,0:T(8,128)(2,1)S(1)}, bf16[1,512,512]{2,1,0:T(8,128)(2,1)}, u32[]{:S(2)}, u32[]{:S(2)}) %collective-permute-start.13) | collective-permute-done | bytes 524320 | tf_op jit(solution)/shard_map/ppermute | solution.py:299
  66.3 1.6 maximum_maximum_fusion
  67.9 2.5 collective-permute-start.17
  70.4 1.5 collective-permute-start.18
  73.6 10.3 %collective-permute-done.17.refs_26_ = bf16[1,512,512]{2,1,0:T(8,128)(2,1)S(1)} collective-permute-done((bf16[1,512,512]{2,1,0:T(8,128)(2,1)}, bf16[1,512,512]{2,1,0:T(8,128)(2,1)S(1)}, u32[]{:S(2)}, u32[]{:S(2)}) %collective-permute-start.17) | collective-permute-done | bytes 524320 | tf_op jit(solution)/shard_map/ppermute | solution.py:299
  87.5 2.2 collective-permute-start.25
  89.7 5.1 %collective-permute-done.21.refs_30_ = bf16[1,512,512]{2,1,0:T(8,128)(2,1)S(1)} collective-permute-done((bf16[1,512,512]{2,1,0:T(8,128)(2,1)}, bf16[1,512,512]{2,1,0:T(8,128)(2,1)S(1)}, u32[]{:S(2)}, u32[]{:S(2)}) %collective-permute-start.21) | collective-permute-done | bytes 524320 | tf_op jit(solution)/shard_map/ppermute | solution.py:299
  95.8 1.3 collective-permute-start.26
  97.9 1.7 collective-permute-start.29
  99.6 6.4 %collective-permute-done.25.refs_24_ = bf16[1,512,512]{2,1,0:T(8,128)(2,1)S(1)} collective-permute-done((bf16[1,512,512]{2,1,0:T(8,128)(2,1)S(1)}, bf16[1,512,512]{2,1,0:T(8,128)(2,1)S(1)}, u32[]{:S(2)}, u32[]{:S(2)}) %collective-permute-start.25) | collective-permute-done | bytes 524320 | tf_op jit(solution)/shard_map/ppermute | solution.py:299
  106.0 4.2 %collective-permute-done.26.refs_11_ = bf16[512,512]{1,0:T(8,128)(2,1)S(1)} collective-permute-done((bf16[512,512]{1,0:T(8,128)(2,1)S(1)}, bf16[512,512]{1,0:T(8,128)(2,1)S(1)}, u32[]{:S(2)}, u32[]{:S(2)}) %collective-permute-start.26) | collective-permute-done | bytes 524320 | tf_op jit(solution)/shard_map/ppermute | solution.py:200
  113.1 1.6 collective-permute-start.31
  115.6 4.5 %collective-permute-done.30.refs_13_ = bf16[256,512]{1,0:T(8,128)(2,1)S(1)} collective-permute-done((bf16[256,512]{1,0:T(8,128)(2,1)S(1)}, bf16[256,512]{1,0:T(8,128)(2,1)S(1)}, u32[]{:S(2)}, u32[]{:S(2)}) %collective-permute-start.30) | collective-permute-done | bytes 262176 | tf_op jit(solution)/shard_map/ppermute | solution.py:200
  120.1 1.5 collective-permute-done.31.refs_14_
  121.7 1.6 collective-permute-start.34
  123.8 1.5 collective-permute-start.37
  125.3 5.6 %collective-permute-done.33.refs_28_ = bf16[1,512,512]{2,1,0:T(8,128)(2,1)} collective-permute-done((bf16[1,512,512]{2,1,0:T(8,128)(2,1)S(1)}, bf16[1,512,512]{2,1,0:T(8,128)(2,1)}, u32[]{:S(2)}, u32[]{:S(2)}) %collective-permute-start.33) | collective-permute-done | bytes 524320 | tf_op jit(solution)/shard_map/ppermute | solution.py:299
  130.8 5.2 %collective-permute-done.34.refs_16_ = bf16[512,512]{1,0:T(8,128)(2,1)S(1)} collective-permute-done((bf16[512,512]{1,0:T(8,128)(2,1)S(1)}, bf16[512,512]{1,0:T(8,128)(2,1)S(1)}, u32[]{:S(2)}, u32[]{:S(2)}) %collective-permute-start.34) | collective-permute-done | bytes 524320 | tf_op jit(solution)/shard_map/ppermute | solution.py:200
  140.0 2.0 collective-permute-start.41
  141.9 4.1 %collective-permute-done.38.refs_18_ = bf16[256,512]{1,0:T(8,128)(2,1)S(1)} collective-permute-done((bf16[256,512]{1,0:T(8,128)(2,1)S(1)}, bf16[256,512]{1,0:T(8,128)(2,1)S(1)}, u32[]{:S(2)}, u32[]{:S(2)}) %collective-permute-start.38) | collective-permute-done | bytes 262176 | tf_op jit(solution)/shard_map/ppermute | solution.py:200
  149.5 1.6 collective-permute-start.43
  151.1 4.9 %collective-permute-done.41.refs_30_ = bf16[1,512,512]{2,1,0:T(8,128)(2,1)} collective-permute-done((bf16[1,512,512]{2,1,0:T(8,128)(2,1)}, bf16[1,512,512]{2,1,0:T(8,128)(2,1)}, u32[]{:S(2)}, u32[]{:S(2)}) %collective-permute-start.41) | collective-permute-done | bytes 524320 | tf_op jit(solution)/shard_map/ppermute | solution.py:299
  156.0 36.1 %shard_map.37.refs_35_ = f32[4,4,128,512]{3,2,1,0:T(8,128)} custom-call(s32[1]{0:T(128)} %bitcast.half_ref, s32[2,4]{1,0:T(2,128)} %gather_fusion.2, s32[4]{0:T(128)} %add_xor_fusion.pick_ref, s32[2]{0:T(128)} %pad_add_fusion.1.tile_ref, bf16[512,512]{1,0:T(8,128)(2,1)} %bitcast.69, bf16[512,512]{1,0:T(8,128)(2,1)} %copy-done.10, ...), custom_call_target="tpu_custom_call" | custom-call | flops 21474836480 | bytes 29360128 | tf_op jit(solution)/shard_map/pallas_call | solution.py:171
  195.5 23.4 %shard_map.39 = bf16[2,4,128,512]{3,2,1,0:T(8,128)(2,1)} custom-call(s32[1]{0:T(128)} %bitcast.half_ref, s32[2,2]{1,0:T(2,128)} %get-tuple-element.146.live_ref, s32[2]{0:T(128)} %get-tuple-element.148.pick_ref, s32[2]{0:T(128)} %pad_add_fusion.tile_ref, bf16[512,512]{1,0:T(8,128)(2,1)} %bitcast.70, bf16[512,512]{1,0:T(8,128)(2,1)} %copy-done.10, ...), custom_call_target="tpu_custom_call" | custom-call | flops 10737418240 | bytes 29360128 | tf_op jit(solution)/shard_map/pallas_call | solution.py:171
  218.9 1.3 slice_bitcast_fusion.2
  221.5 23.9 %shard_map.38 = f32[2,4,128,512]{3,2,1,0:T(8,128)} custom-call(s32[1]{0:T(128)} %bitcast.half_ref, s32[2,2]{1,0:T(2,128)} %get-tuple-element.147.live_ref, s32[2]{0:T(128)} %get-tuple-element.149.pick_ref, s32[2]{0:T(128)} %pad_add_fusion.tile_ref, bf16[512,512]{1,0:T(8,128)(2,1)} %bitcast.71, bf16[512,512]{1,0:T(8,128)(2,1)} %copy-done.10, ...), custom_call_target="tpu_custom_call" | custom-call | flops 10737418240 | bytes 29360128 | tf_op jit(solution)/shard_map/pallas_call | solution.py:171
  245.4 1.3 fusion.3
  246.7 2.5 collective-permute-start.47
  249.2 8.3 %collective-permute-done.45 = bf16[4,128,512]{2,1,0:T(8,128)(2,1)S(1)} collective-permute-done((bf16[4,128,512]{2,1,0:T(8,128)(2,1)S(1)}, bf16[4,128,512]{2,1,0:T(8,128)(2,1)S(1)}, u32[]{:S(2)}, u32[]{:S(2)}) %collective-permute-start.45) | collective-permute-done | bytes 524320 | tf_op jit(solution)/shard_map/ppermute | solution.py:244
  257.5 8.8 %collective-permute-done.47 = bf16[4,128,512]{2,1,0:T(8,128)(2,1)S(1)} collective-permute-done((bf16[4,128,512]{2,1,0:T(8,128)(2,1)S(1)}, bf16[4,128,512]{2,1,0:T(8,128)(2,1)S(1)}, u32[]{:S(2)}, u32[]{:S(2)}) %collective-permute-start.47) | collective-permute-done | bytes 524320 | tf_op jit(solution)/shard_map/ppermute | solution.py:244
  266.3 1.6 fusion.8
  267.9 2.7 collective-permute-start.50
  271.5 3.0 %collective-permute-done.50 = bf16[4,128,128]{2,1,0:T(8,128)(2,1)S(1)} collective-permute-done((bf16[4,128,128]{2,1,0:T(8,128)(2,1)S(1)}, bf16[4,128,128]{2,1,0:T(8,128)(2,1)S(1)}, u32[]{:S(2)}, u32[]{:S(2)}) %collective-permute-start.50) | collective-permute-done | bytes 131104 | tf_op jit(solution)/shard_map/ppermute | solution.py:200
  274.6 2.6 collective-permute-done.49
  277.9 1.6 copy.16
  (184 shorter events, 31.3 us)
Async XLA Ops:
  6.5 104.7 %all-gather.2.cloned.1.call-start = ((), (), s32[]{:S(2)}) async-start(), calls=%async_computation | async-start | bytes 6291456 | tf_op jit(solution)/shard_map/all_gather | solution.py:317
  8.7 14.6 %collective-permute-start = (bf16[1,512,512]{2,1,0:T(8,128)(2,1)S(1)}, bf16[1,512,512]{2,1,0:T(8,128)(2,1)S(1)}, u32[]{:S(2)}, u32[]{:S(2)}) collective-permute-start(bf16[1,512,512]{2,1,0:T(8,128)(2,1)S(1)} %get-tuple-element.70), channel_id=1, source_target_pairs={{0,16},{16,24},{24,8},{8,0},{1,17},{17,25},{25,9},{9,1},{2,18},{18... | collective-permute-start | bytes 1572872 | tf_op jit(solution)/shard_map/ppermute | solution.py:299
  8.7 14.6 %collective-permute-start.1 = (bf16[512,512]{1,0:T(8,128)(2,1)S(1)}, bf16[512,512]{1,0:T(8,128)(2,1)S(1)}, u32[]{:S(2)}, u32[]{:S(2)}) collective-permute-start(bf16[512,512]{1,0:T(8,128)(2,1)S(1)} %bitcast.67), channel_id=1, source_target_pairs={{0,2},{2,0},{4,6},{6,4},{1,3},{3,1},{5,7},{7,5},{8,10},{10,8},{12,... | collective-permute-start | bytes 1572872 | tf_op jit(solution)/shard_map/ppermute | solution.py:200
  10.7 13.1 %collective-permute-start.2 = (bf16[512,512]{1,0:T(8,128)(2,1)S(1)}, bf16[512,512]{1,0:T(8,128)(2,1)S(1)}, u32[]{:S(2)}, u32[]{:S(2)}) collective-permute-start(bf16[512,512]{1,0:T(8,128)(2,1)S(1)} %bitcast.68), channel_id=1, source_target_pairs={{0,4},{2,6},{4,0},{6,2},{1,5},{3,7},{5,1},{7,3},{8,12},{10,14},{12... | collective-permute-start | bytes 1572872 | tf_op jit(solution)/shard_map/ppermute | solution.py:200
  23.8 17.1 %collective-permute-start.3 = (bf16[4,512,512]{2,1,0:T(8,128)(2,1)S(1)}, bf16[4,512,512]{2,1,0:T(8,128)(2,1)S(1)}, u32[]{:S(2)}, u32[]{:S(2)}) collective-permute-start(bf16[4,512,512]{2,1,0:T(8,128)(2,1)S(1)} %copy-done.1), channel_id=1, source_target_pairs={{0,1},{1,0},{2,3},{3,2},{4,5},{5,4},{6,7},{7,6},{8,9},{9,8},{10,11... | collective-permute-start | bytes 6291464 | tf_op jit(solution)/shard_map/ppermute | solution.py:200
  23.8 15.3 %collective-permute-start.5 = (bf16[1,512,512]{2,1,0:T(8,128)(2,1)S(1)}, bf16[1,512,512]{2,1,0:T(8,128)(2,1)}, u32[]{:S(2)}, u32[]{:S(2)}) collective-permute-start(bf16[1,512,512]{2,1,0:T(8,128)(2,1)S(1)} %get-tuple-element.77), channel_id=1, source_target_pairs={{0,16},{16,24},{24,8},{8,0},{1,17},{17,25},{25,9},{9,1},{2,18},{18... | collective-permute-start | bytes 1572872 | tf_op jit(solution)/shard_map/ppermute | solution.py:299
  26.4 14.4 %collective-permute-start.4 = (bf16[1,512,512]{2,1,0:T(8,128)(2,1)S(1)}, bf16[1,512,512]{2,1,0:T(8,128)(2,1)S(1)}, u32[]{:S(2)}, u32[]{:S(2)}) collective-permute-start(bf16[1,512,512]{2,1,0:T(8,128)(2,1)S(1)} %collective-permute-done.refs_24_), channel_id=1, source_target_pairs={{0,1},{1,0},{2,3},{3,2},{4,5},{5,4},{6,7},{7,6},{8,9},{9,8},{10,11... | collective-permute-start | bytes 1572872 | tf_op jit(solution)/shard_map/ppermute | solution.py:200
  26.6 14.2 %collective-permute-start.6 = (bf16[256,512]{1,0:T(8,128)(2,1)S(1)}, bf16[256,512]{1,0:T(8,128)(2,1)S(1)}, u32[]{:S(2)}, u32[]{:S(2)}) collective-permute-start(bf16[256,512]{1,0:T(8,128)(2,1)S(1)} %slice.72), channel_id=1, source_target_pairs={{0,4},{2,6},{4,0},{6,2},{1,5},{3,7},{5,1},{7,3},{8,12},{10,14},{12... | collective-permute-start | bytes 786440 | tf_op jit(solution)/shard_map/ppermute | solution.py:200
  28.2 12.6 %collective-permute-start.7 = (bf16[256,512]{1,0:T(8,128)(2,1)S(1)}, bf16[256,512]{1,0:T(8,128)(2,1)S(1)}, u32[]{:S(2)}, u32[]{:S(2)}) collective-permute-start(bf16[256,512]{1,0:T(8,128)(2,1)S(1)} %slice.73), channel_id=1, source_target_pairs={{0,2},{2,0},{4,6},{6,4},{1,3},{3,1},{5,7},{7,5},{8,10},{10,8},{12,... | collective-permute-start | bytes 786440 | tf_op jit(solution)/shard_map/ppermute | solution.py:200
  39.1 15.7 %collective-permute-start.9 = (bf16[1,512,512]{2,1,0:T(8,128)(2,1)S(1)}, bf16[1,512,512]{2,1,0:T(8,128)(2,1)S(1)}, u32[]{:S(2)}, u32[]{:S(2)}) collective-permute-start(bf16[1,512,512]{2,1,0:T(8,128)(2,1)S(1)} %get-tuple-element.81), channel_id=1, source_target_pairs={{0,16},{16,24},{24,8},{8,0},{1,17},{17,25},{25,9},{9,1},{2,18},{18... | collective-permute-start | bytes 1572872 | tf_op jit(solution)/shard_map/ppermute | solution.py:299
  41.8 13.2 %collective-permute-start.10 = (bf16[4,512,128]{2,1,0:T(8,128)(2,1)S(1)}, bf16[4,512,128]{2,1,0:T(8,128)(2,1)S(1)}, u32[]{:S(2)}, u32[]{:S(2)}) collective-permute-start(bf16[4,512,128]{2,1,0:T(8,128)(2,1)S(1)} %bitcast.90), channel_id=1, source_target_pairs={{0,2},{2,0},{4,6},{6,4},{1,3},{3,1},{5,7},{7,5},{8,10},{10,8},{12,... | collective-permute-start | bytes 1572872 | tf_op jit(solution)/shard_map/ppermute | solution.py:200
  42.3 12.9 %collective-permute-start.11 = (bf16[4,512,128]{2,1,0:T(8,128)(2,1)S(1)}, bf16[4,512,128]{2,1,0:T(8,128)(2,1)S(1)}, u32[]{:S(2)}, u32[]{:S(2)}) collective-permute-start(bf16[4,512,128]{2,1,0:T(8,128)(2,1)S(1)} %bitcast.91), channel_id=1, source_target_pairs={{0,4},{2,6},{4,0},{6,2},{1,5},{3,7},{5,1},{7,3},{8,12},{10,14},{12... | collective-permute-start | bytes 1572872 | tf_op jit(solution)/shard_map/ppermute | solution.py:200
  43.8 11.4 %collective-permute-start.8 = (bf16[1,512,512]{2,1,0:T(8,128)(2,1)}, bf16[1,512,512]{2,1,0:T(8,128)(2,1)S(1)}, u32[]{:S(2)}, u32[]{:S(2)}) collective-permute-start(bf16[1,512,512]{2,1,0:T(8,128)(2,1)} %collective-permute-done.5.refs_22_), channel_id=1, source_target_pairs={{0,1},{1,0},{2,3},{3,2},{4,5},{5,4},{6,7},{7,6},{8,9},{9,8},{10,11... | collective-permute-start | bytes 1572872 | tf_op jit(solution)/shard_map/ppermute | solution.py:200
  43.8 21.0 %collective-permute-start.13 = (bf16[1,512,512]{2,1,0:T(8,128)(2,1)S(1)}, bf16[1,512,512]{2,1,0:T(8,128)(2,1)}, u32[]{:S(2)}, u32[]{:S(2)}) collective-permute-start(bf16[1,512,512]{2,1,0:T(8,128)(2,1)S(1)} %collective-permute-done.refs_24_), channel_id=1, source_target_pairs={{0,16},{16,24},{24,8},{8,0},{1,17},{17,25},{25,9},{9,1},{2,18},{18... | collective-permute-start | bytes 1572872 | tf_op jit(solution)/shard_map/ppermute | solution.py:299
  55.2 10.2 %collective-permute-start.12 = (bf16[1,512,512]{2,1,0:T(8,128)(2,1)S(1)}, bf16[1,512,512]{2,1,0:T(8,128)(2,1)S(1)}, u32[]{:S(2)}, u32[]{:S(2)}) collective-permute-start(bf16[1,512,512]{2,1,0:T(8,128)(2,1)S(1)} %collective-permute-done.9.refs_22_), channel_id=1, source_target_pairs={{0,1},{1,0},{2,3},{3,2},{4,5},{5,4},{6,7},{7,6},{8,9},{9,8},{10,11... | collective-permute-start | bytes 1572872 | tf_op jit(solution)/shard_map/ppermute | solution.py:200
  56.0 8.8 %collective-permute-start.14 = (bf16[2,512,128]{2,1,0:T(8,128)(2,1)S(1)}, bf16[2,512,128]{2,1,0:T(8,128)(2,1)S(1)}, u32[]{:S(2)}, u32[]{:S(2)}) collective-permute-start(bf16[2,512,128]{2,1,0:T(8,128)(2,1)S(1)} %slice.74), channel_id=1, source_target_pairs={{0,4},{2,6},{4,0},{6,2},{1,5},{3,7},{5,1},{7,3},{8,12},{10,14},{12... | collective-permute-start | bytes 786440 | tf_op jit(solution)/shard_map/ppermute | solution.py:200
  57.6 7.9 %collective-permute-start.15 = (bf16[2,512,128]{2,1,0:T(8,128)(2,1)S(1)}, bf16[2,512,128]{2,1,0:T(8,128)(2,1)S(1)}, u32[]{:S(2)}, u32[]{:S(2)}) collective-permute-start(bf16[2,512,128]{2,1,0:T(8,128)(2,1)S(1)} %slice.75), channel_id=1, source_target_pairs={{0,2},{2,0},{4,6},{6,4},{1,3},{3,1},{5,7},{7,5},{8,10},{10,8},{12,... | collective-permute-start | bytes 786440 | tf_op jit(solution)/shard_map/ppermute | solution.py:200
  67.9 16.0 %collective-permute-start.17 = (bf16[1,512,512]{2,1,0:T(8,128)(2,1)}, bf16[1,512,512]{2,1,0:T(8,128)(2,1)S(1)}, u32[]{:S(2)}, u32[]{:S(2)}) collective-permute-start(bf16[1,512,512]{2,1,0:T(8,128)(2,1)} %collective-permute-done.5.refs_22_), channel_id=1, source_target_pairs={{0,16},{16,24},{24,8},{8,0},{1,17},{17,25},{25,9},{9,1},{2,18},{18... | collective-permute-start | bytes 1572872 | tf_op jit(solution)/shard_map/ppermute | solution.py:299
  70.4 13.5 %collective-permute-start.16 = (bf16[1,512,512]{2,1,0:T(8,128)(2,1)}, bf16[1,512,512]{2,1,0:T(8,128)(2,1)S(1)}, u32[]{:S(2)}, u32[]{:S(2)}) collective-permute-start(bf16[1,512,512]{2,1,0:T(8,128)(2,1)} %collective-permute-done.13.refs_26_), channel_id=1, source_target_pairs={{0,1},{1,0},{2,3},{3,2},{4,5},{5,4},{6,7},{7,6},{8,9},{9,8},{10,11... | collective-permute-start | bytes 1572872 | tf_op jit(solution)/shard_map/ppermute | solution.py:200
  70.4 14.3 %collective-permute-start.18 = (bf16[512,512]{1,0:T(8,128)(2,1)S(1)}, bf16[512,512]{1,0:T(8,128)(2,1)S(1)}, u32[]{:S(2)}, u32[]{:S(2)}) collective-permute-start(bf16[512,512]{1,0:T(8,128)(2,1)S(1)} %bitcast.72), channel_id=1, source_target_pairs={{0,2},{2,0},{4,6},{6,4},{1,3},{3,1},{5,7},{7,5},{8,10},{10,8},{12,... | collective-permute-start | bytes 1572872 | tf_op jit(solution)/shard_map/ppermute | solution.py:200
  71.9 14.1 %collective-permute-start.19 = (bf16[512,512]{1,0:T(8,128)(2,1)S(1)}, bf16[512,512]{1,0:T(8,128)(2,1)S(1)}, u32[]{:S(2)}, u32[]{:S(2)}) collective-permute-start(bf16[512,512]{1,0:T(8,128)(2,1)S(1)} %bitcast.73), channel_id=1, source_target_pairs={{0,4},{2,6},{4,0},{6,2},{1,5},{3,7},{5,1},{7,3},{8,12},{10,14},{12... | collective-permute-start | bytes 1572872 | tf_op jit(solution)/shard_map/ppermute | solution.py:200
  72.4 22.3 %collective-permute-start.21 = (bf16[1,512,512]{2,1,0:T(8,128)(2,1)}, bf16[1,512,512]{2,1,0:T(8,128)(2,1)S(1)}, u32[]{:S(2)}, u32[]{:S(2)}) collective-permute-start(bf16[1,512,512]{2,1,0:T(8,128)(2,1)} %collective-permute-done.13.refs_26_), channel_id=1, source_target_pairs={{0,16},{16,24},{24,8},{8,0},{1,17},{17,25},{25,9},{9,1},{2,18},{18... | collective-permute-start | bytes 1572872 | tf_op jit(solution)/shard_map/ppermute | solution.py:299
  86.0 9.1 %collective-permute-start.20 = (bf16[1,512,512]{2,1,0:T(8,128)(2,1)S(1)}, bf16[1,512,512]{2,1,0:T(8,128)(2,1)S(1)}, u32[]{:S(2)}, u32[]{:S(2)}) collective-permute-start(bf16[1,512,512]{2,1,0:T(8,128)(2,1)S(1)} %collective-permute-done.17.refs_26_), channel_id=1, source_target_pairs={{0,1},{1,0},{2,3},{3,2},{4,5},{5,4},{6,7},{7,6},{8,9},{9,8},{10,11... | collective-permute-start | bytes 1572872 | tf_op jit(solution)/shard_map/ppermute | solution.py:200
  86.0 8.8 %collective-permute-start.22 = (bf16[256,512]{1,0:T(8,128)(2,1)S(1)}, bf16[256,512]{1,0:T(8,128)(2,1)S(1)}, u32[]{:S(2)}, u32[]{:S(2)}) collective-permute-start(bf16[256,512]{1,0:T(8,128)(2,1)S(1)} %slice.76), channel_id=1, source_target_pairs={{0,4},{2,6},{4,0},{6,2},{1,5},{3,7},{5,1},{7,3},{8,12},{10,14},{12... | collective-permute-start | bytes 786440 | tf_op jit(solution)/shard_map/ppermute | solution.py:200
  86.6 8.5 %collective-permute-start.23 = (bf16[256,512]{1,0:T(8,128)(2,1)S(1)}, bf16[256,512]{1,0:T(8,128)(2,1)S(1)}, u32[]{:S(2)}, u32[]{:S(2)}) collective-permute-start(bf16[256,512]{1,0:T(8,128)(2,1)S(1)} %slice.77), channel_id=1, source_target_pairs={{0,2},{2,0},{4,6},{6,4},{1,3},{3,1},{5,7},{7,5},{8,10},{10,8},{12,... | collective-permute-start | bytes 786440 | tf_op jit(solution)/shard_map/ppermute | solution.py:200
  87.5 18.5 %collective-permute-start.25 = (bf16[1,512,512]{2,1,0:T(8,128)(2,1)S(1)}, bf16[1,512,512]{2,1,0:T(8,128)(2,1)S(1)}, u32[]{:S(2)}, u32[]{:S(2)}) collective-permute-start(bf16[1,512,512]{2,1,0:T(8,128)(2,1)S(1)} %get-tuple-element.100), channel_id=1, source_target_pairs={{0,16},{16,24},{24,8},{8,0},{1,17},{17,25},{25,9},{9,1},{2,18},{18... | collective-permute-start | bytes 1572872 | tf_op jit(solution)/shard_map/ppermute | solution.py:299
  95.8 10.2 %collective-permute-start.24 = (bf16[1,512,512]{2,1,0:T(8,128)(2,1)S(1)}, bf16[1,512,512]{2,1,0:T(8,128)(2,1)S(1)}, u32[]{:S(2)}, u32[]{:S(2)}) collective-permute-start(bf16[1,512,512]{2,1,0:T(8,128)(2,1)S(1)} %collective-permute-done.21.refs_30_), channel_id=1, source_target_pairs={{0,1},{1,0},{2,3},{3,2},{4,5},{5,4},{6,7},{7,6},{8,9},{9,8},{10,11... | collective-permute-start | bytes 1572872 | tf_op jit(solution)/shard_map/ppermute | solution.py:200
  95.8 14.3 %collective-permute-start.26 = (bf16[512,512]{1,0:T(8,128)(2,1)S(1)}, bf16[512,512]{1,0:T(8,128)(2,1)S(1)}, u32[]{:S(2)}, u32[]{:S(2)}) collective-permute-start(bf16[512,512]{1,0:T(8,128)(2,1)S(1)} %bitcast.78), channel_id=1, source_target_pairs={{0,2},{2,0},{4,6},{6,4},{1,3},{3,1},{5,7},{7,5},{8,10},{10,8},{12,... | collective-permute-start | bytes 1572872 | tf_op jit(solution)/shard_map/ppermute | solution.py:200
  97.1 14.2 %collective-permute-start.27 = (bf16[512,512]{1,0:T(8,128)(2,1)S(1)}, bf16[512,512]{1,0:T(8,128)(2,1)}, u32[]{:S(2)}, u32[]{:S(2)}) collective-permute-start(bf16[512,512]{1,0:T(8,128)(2,1)S(1)} %bitcast.79), channel_id=1, source_target_pairs={{0,4},{2,6},{4,0},{6,2},{1,5},{3,7},{5,1},{7,3},{8,12},{10,14},{12... | collective-permute-start | bytes 1572872 | tf_op jit(solution)/shard_map/ppermute | solution.py:200
  97.9 17.7 %collective-permute-start.29 = (bf16[1,512,512]{2,1,0:T(8,128)(2,1)S(1)}, bf16[1,512,512]{2,1,0:T(8,128)(2,1)}, u32[]{:S(2)}, u32[]{:S(2)}) collective-permute-start(bf16[1,512,512]{2,1,0:T(8,128)(2,1)S(1)} %collective-permute-done.9.refs_22_), channel_id=1, source_target_pairs={{0,16},{16,24},{24,8},{8,0},{1,17},{17,25},{25,9},{9,1},{2,18},{18... | collective-permute-start | bytes 1572872 | tf_op jit(solution)/shard_map/ppermute | solution.py:299
  111.2 10.4 %collective-permute-start.28 = (bf16[1,512,512]{2,1,0:T(8,128)(2,1)}, bf16[1,512,512]{2,1,0:T(8,128)(2,1)S(1)}, u32[]{:S(2)}, u32[]{:S(2)}) collective-permute-start(bf16[1,512,512]{2,1,0:T(8,128)(2,1)} %copy-done.24), channel_id=1, source_target_pairs={{0,1},{1,0},{2,3},{3,2},{4,5},{5,4},{6,7},{7,6},{8,9},{9,8},{10,11... | collective-permute-start | bytes 1572872 | tf_op jit(solution)/shard_map/ppermute | solution.py:200
  111.3 8.8 %collective-permute-start.30 = (bf16[256,512]{1,0:T(8,128)(2,1)S(1)}, bf16[256,512]{1,0:T(8,128)(2,1)S(1)}, u32[]{:S(2)}, u32[]{:S(2)}) collective-permute-start(bf16[256,512]{1,0:T(8,128)(2,1)S(1)} %slice.78), channel_id=1, source_target_pairs={{0,4},{2,6},{4,0},{6,2},{1,5},{3,7},{5,1},{7,3},{8,12},{10,14},{12... | collective-permute-start | bytes 786440 | tf_op jit(solution)/shard_map/ppermute | solution.py:200
  113.1 8.5 %collective-permute-start.31 = (bf16[256,512]{1,0:T(8,128)(2,1)S(1)}, bf16[256,512]{1,0:T(8,128)(2,1)S(1)}, u32[]{:S(2)}, u32[]{:S(2)}) collective-permute-start(bf16[256,512]{1,0:T(8,128)(2,1)S(1)} %slice.79), channel_id=1, source_target_pairs={{0,2},{2,0},{4,6},{6,4},{1,3},{3,1},{5,7},{7,5},{8,10},{10,8},{12,... | collective-permute-start | bytes 786440 | tf_op jit(solution)/shard_map/ppermute | solution.py:200
  115.0 15.9 %collective-permute-start.33 = (bf16[1,512,512]{2,1,0:T(8,128)(2,1)S(1)}, bf16[1,512,512]{2,1,0:T(8,128)(2,1)}, u32[]{:S(2)}, u32[]{:S(2)}) collective-permute-start(bf16[1,512,512]{2,1,0:T(8,128)(2,1)S(1)} %copy-done.25), channel_id=1, source_target_pairs={{0,16},{16,24},{24,8},{8,0},{1,17},{17,25},{25,9},{9,1},{2,18},{18... | collective-permute-start | bytes 1572872 | tf_op jit(solution)/shard_map/ppermute | solution.py:299
  121.6 9.2 %collective-permute-start.32 = (bf16[1,512,512]{2,1,0:T(8,128)(2,1)}, bf16[1,512,512]{2,1,0:T(8,128)(2,1)S(1)}, u32[]{:S(2)}, u32[]{:S(2)}) collective-permute-start(bf16[1,512,512]{2,1,0:T(8,128)(2,1)} %collective-permute-done.29.refs_28_), channel_id=1, source_target_pairs={{0,1},{1,0},{2,3},{3,2},{4,5},{5,4},{6,7},{7,6},{8,9},{9,8},{10,11... | collective-permute-start | bytes 1572872 | tf_op jit(solution)/shard_map/ppermute | solution.py:200
  121.7 14.3 %collective-permute-start.34 = (bf16[512,512]{1,0:T(8,128)(2,1)S(1)}, bf16[512,512]{1,0:T(8,128)(2,1)S(1)}, u32[]{:S(2)}, u32[]{:S(2)}) collective-permute-start(bf16[512,512]{1,0:T(8,128)(2,1)S(1)} %bitcast.85), channel_id=1, source_target_pairs={{0,2},{2,0},{4,6},{6,4},{1,3},{3,1},{5,7},{7,5},{8,10},{10,8},{12,... | collective-permute-start | bytes 1572872 | tf_op jit(solution)/shard_map/ppermute | solution.py:200
  123.2 14.0 %collective-permute-start.35 = (bf16[512,512]{1,0:T(8,128)(2,1)S(1)}, bf16[512,512]{1,0:T(8,128)(2,1)S(1)}, u32[]{:S(2)}, u32[]{:S(2)}) collective-permute-start(bf16[512,512]{1,0:T(8,128)(2,1)S(1)} %bitcast.86), channel_id=1, source_target_pairs={{0,4},{2,6},{4,0},{6,2},{1,5},{3,7},{5,1},{7,3},{8,12},{10,14},{12... | collective-permute-start | bytes 1572872 | tf_op jit(solution)/shard_map/ppermute | solution.py:200
  123.8 18.2 %collective-permute-start.37 = (bf16[1,512,512]{2,1,0:T(8,128)(2,1)}, bf16[1,512,512]{2,1,0:T(8,128)(2,1)}, u32[]{:S(2)}, u32[]{:S(2)}) collective-permute-start(bf16[1,512,512]{2,1,0:T(8,128)(2,1)} %collective-permute-done.29.refs_28_), channel_id=1, source_target_pairs={{0,16},{16,24},{24,8},{8,0},{1,17},{17,25},{25,9},{9,1},{2,18},{18... | collective-permute-start | bytes 1572872 | tf_op jit(solution)/shard_map/ppermute | solution.py:299
  137.2 9.2 %collective-permute-start.36 = (bf16[1,512,512]{2,1,0:T(8,128)(2,1)}, bf16[1,512,512]{2,1,0:T(8,128)(2,1)}, u32[]{:S(2)}, u32[]{:S(2)}) collective-permute-start(bf16[1,512,512]{2,1,0:T(8,128)(2,1)} %collective-permute-done.33.refs_28_), channel_id=1, source_target_pairs={{0,1},{1,0},{2,3},{3,2},{4,5},{5,4},{6,7},{7,6},{8,9},{9,8},{10,11... | collective-permute-start | bytes 1572872 | tf_op jit(solution)/shard_map/ppermute | solution.py:200
  137.3 8.8 %collective-permute-start.38 = (bf16[256,512]{1,0:T(8,128)(2,1)S(1)}, bf16[256,512]{1,0:T(8,128)(2,1)S(1)}, u32[]{:S(2)}, u32[]{:S(2)}) collective-permute-start(bf16[256,512]{1,0:T(8,128)(2,1)S(1)} %slice.80), channel_id=1, source_target_pairs={{0,4},{2,6},{4,0},{6,2},{1,5},{3,7},{5,1},{7,3},{8,12},{10,14},{12... | collective-permute-start | bytes 786440 | tf_op jit(solution)/shard_map/ppermute | solution.py:200
  138.1 8.4 %collective-permute-start.39 = (bf16[256,512]{1,0:T(8,128)(2,1)S(1)}, bf16[256,512]{1,0:T(8,128)(2,1)}, u32[]{:S(2)}, u32[]{:S(2)}) collective-permute-start(bf16[256,512]{1,0:T(8,128)(2,1)S(1)} %slice.81), channel_id=1, source_target_pairs={{0,2},{2,0},{4,6},{6,4},{1,3},{3,1},{5,7},{7,5},{8,10},{10,8},{12,... | collective-permute-start | bytes 786440 | tf_op jit(solution)/shard_map/ppermute | solution.py:200
  140.0 16.0 %collective-permute-start.41 = (bf16[1,512,512]{2,1,0:T(8,128)(2,1)}, bf16[1,512,512]{2,1,0:T(8,128)(2,1)}, u32[]{:S(2)}, u32[]{:S(2)}) collective-permute-start(bf16[1,512,512]{2,1,0:T(8,128)(2,1)} %collective-permute-done.33.refs_28_), channel_id=1, source_target_pairs={{0,16},{16,24},{24,8},{8,0},{1,17},{17,25},{25,9},{9,1},{2,18},{18... | collective-permute-start | bytes 1572872 | tf_op jit(solution)/shard_map/ppermute | solution.py:299
  146.5 9.5 %collective-permute-start.40 = (bf16[1,512,512]{2,1,0:T(8,128)(2,1)}, bf16[1,512,512]{2,1,0:T(8,128)(2,1)}, u32[]{:S(2)}, u32[]{:S(2)}) collective-permute-start(bf16[1,512,512]{2,1,0:T(8,128)(2,1)} %collective-permute-done.37.refs_32_), channel_id=1, source_target_pairs={{0,1},{1,0},{2,3},{3,2},{4,5},{5,4},{6,7},{7,6},{8,9},{9,8},{10,11... | collective-permute-start | bytes 1572872 | tf_op jit(solution)/shard_map/ppermute | solution.py:200
  149.5 42.7 %collective-permute-start.43 = (bf16[1,512,512]{2,1,0:T(8,128)(2,1)S(1)}, bf16[1,512,512]{2,1,0:T(8,128)(2,1)S(1)}, u32[]{:S(2)}, u32[]{:S(2)}) collective-permute-start(bf16[1,512,512]{2,1,0:T(8,128)(2,1)S(1)} %collective-permute-done.17.refs_26_), channel_id=1, source_target_pairs={{0,16},{16,24},{24,8},{8,0},{1,17},{17,25},{25,9},{9,1},{2,18},{18... | collective-permute-start | bytes 1572872 | tf_op jit(solution)/shard_map/ppermute | solution.py:299
  156.0 36.2 %collective-permute-start.42 = (bf16[1,512,512]{2,1,0:T(8,128)(2,1)}, bf16[1,512,512]{2,1,0:T(8,128)(2,1)S(1)}, u32[]{:S(2)}, u32[]{:S(2)}) collective-permute-start(bf16[1,512,512]{2,1,0:T(8,128)(2,1)} %collective-permute-done.41.refs_30_), channel_id=1, source_target_pairs={{0,1},{1,0},{2,3},{3,2},{4,5},{5,4},{6,7},{7,6},{8,9},{9,8},{10,11... | collective-permute-start | bytes 1572872 | tf_op jit(solution)/shard_map/ppermute | solution.py:200
  220.2 37.3 %collective-permute-start.45 = (bf16[4,128,512]{2,1,0:T(8,128)(2,1)S(1)}, bf16[4,128,512]{2,1,0:T(8,128)(2,1)S(1)}, u32[]{:S(2)}, u32[]{:S(2)}) collective-permute-start(bf16[4,128,512]{2,1,0:T(8,128)(2,1)S(1)} %get-tuple-element.141), channel_id=1, source_target_pairs={{0,24},{16,8},{24,0},{8,16},{1,25},{17,9},{25,1},{9,17},{2,26},{18... | collective-permute-start | bytes 1572872 | tf_op jit(solution)/shard_map/ppermute | solution.py:244
  221.1 36.4 %collective-permute-start.46 = (bf16[4,128,512]{2,1,0:T(8,128)(2,1)S(1)}, bf16[4,128,512]{2,1,0:T(8,128)(2,1)S(1)}, u32[]{:S(2)}, u32[]{:S(2)}) collective-permute-start(bf16[4,128,512]{2,1,0:T(8,128)(2,1)S(1)} %get-tuple-element.142), channel_id=1, source_target_pairs={{0,16},{16,24},{24,8},{8,0},{1,17},{17,25},{25,9},{9,1},{2,18},{18... | collective-permute-start | bytes 1572872 | tf_op jit(solution)/shard_map/ppermute | solution.py:244
  246.7 19.6 %collective-permute-start.47 = (bf16[4,128,512]{2,1,0:T(8,128)(2,1)S(1)}, bf16[4,128,512]{2,1,0:T(8,128)(2,1)S(1)}, u32[]{:S(2)}, u32[]{:S(2)}) collective-permute-start(bf16[4,128,512]{2,1,0:T(8,128)(2,1)S(1)} %fusion.3), channel_id=1, source_target_pairs={{0,8},{16,0},{24,16},{8,24},{1,9},{17,1},{25,17},{9,25},{2,10},{18... | collective-permute-start | bytes 1572872 | tf_op jit(solution)/shard_map/ppermute | solution.py:244
  (44 other events, 1001.4 us)
Sparse Core Ops, SparseCore 0:
  68.0 13.6 all-gather.1

commit v9 on v8

--- a/solution.py
+++ b/solution.py
@@ -307,8 +307,9 @@
         if slot == 1:
             held["other", "chol"] = partner(held["chol"], "occ", 2, 1)
             waiting[slot + 1].append(("other", "chol"))
-        if slot >= 1:
-            unit = HOPS[slot - 1]
+        late_hop = near_block is not None
+        for u in [] if slot == 0 or late_hop else [slot - 2, slot - 1] if slot - 1 in NEAR and slot > 1 else [slot - 1]:
+            unit = HOPS[u]
             held["other", *unit] = partner(held["block", *unit], "occ", 2, 1)
             waiting[slot + 1].append(("other", *unit))
         if done_block == AMP:

time: 291 us -> 287 us (0.986)
  waiting for transfers between devices: 116 us -> 112 us
    ppermute x36, waiting for transfers between devices: 31.7 us -> 24 us  [partner(): return lax.ppermute(value, axis, [(i, i ^ flip) for i in range(size)])]
    ppermute x12, waiting for transfers between devices: 67.7 us -> 70.7 us  [on_square(): lax.ppermute(held['block', s - 1, (i + 1) % NTV], 'left', ring)]
  transfers between devices with their start and end apart: 52 -> 52, of which waited for: 28 -> 27; matrix products, arithmetic and copies ran while one was open for 3% -> 3% of each run, Pallas kernels for 21% -> 21%
where the time goes in v9:
time: 287 us; the launch traced here: 284 us
  waiting for transfers between devices  112 us (39%)
  Pallas kernels  83.4 us (29%)
  starting transfers between devices  53 us (18%)
  local copies, waits for them, and re-layouts  16.8 us (6%)
  between operations  13.9 us (5%)
  other arithmetic  5.31 us (2%)
    pallas_call x3, Pallas kernels, ladder(): pl.pallas_call(functools.partial(ladder_kernel, steps, count, tile_count,...  83.4 us
    ppermute x12, waiting for transfers between devices, on_square(): lax.ppermute(held['block', s - 1, (i + 1) % NTV], 'left', ring)  70.7 us
    ppermute x36, starting transfers between devices, partner(): return lax.ppermute(value, axis, [(i, i ^ flip) for i in range(size)])  27.8 us
    ppermute x36, waiting for transfers between devices, partner(): return lax.ppermute(value, axis, [(i, i ^ flip) for i in range(size)])  24 us
    ppermute x12, starting transfers between devices, on_square(): lax.ppermute(held['block', s - 1, (i + 1) % NTV], 'left', ring)  20 us
    ppermute x3, waiting for transfers between devices, around(): lax.ppermute(value, 'left', [(order[p], order[(p + step) % NTV]) for p in...  16.9 us
  transfers between devices with their start and end apart: 52, of which 27 were waited for; matrix products, arithmetic and copies ran while one was open for 3% of the time, Pallas kernels for 21%

profile of v9, /device:TPU:8, one launch (start us, length us, event | category | flops | bytes accessed | tf_op | source)
XLA Modules:
  0.0 283.9 jit_solution(9076652549599204894)
XLA Ops:
  6.5 1.8 constant_dynamic-slice_fusion
  8.7 1.9 collective-permute-start.1
  10.7 1.5 collective-permute-start.2
  12.2 11.1 %collective-permute-done.refs_24_ = bf16[1,512,512]{2,1,0:T(8,128)(2,1)S(1)} collective-permute-done((bf16[1,512,512]{2,1,0:T(8,128)(2,1)S(1)}, bf16[1,512,512]{2,1,0:T(8,128)(2,1)S(1)}, u32[]{:S(2)}, u32[]{:S(2)}) %collective-permute-start) | collective-permute-done | bytes 524320 | tf_op jit(solution)/shard_map/ppermute | solution.py:299
  23.8 2.6 collective-permute-start.5
  26.6 1.6 collective-permute-start.6
  28.8 10.3 %collective-permute-done.5.refs_22_ = bf16[1,512,512]{2,1,0:T(8,128)(2,1)} collective-permute-done((bf16[1,512,512]{2,1,0:T(8,128)(2,1)S(1)}, bf16[1,512,512]{2,1,0:T(8,128)(2,1)}, u32[]{:S(2)}, u32[]{:S(2)}) %collective-permute-start.5) | collective-permute-done | bytes 524320 | tf_op jit(solution)/shard_map/ppermute | solution.py:299
  39.1 1.7 collective-permute-start.8
  41.8 1.5 collective-permute-start.10
  43.8 2.5 collective-permute-start.14
  46.3 8.6 %collective-permute-done.8.refs_22_ = bf16[1,512,512]{2,1,0:T(8,128)(2,1)S(1)} collective-permute-done((bf16[1,512,512]{2,1,0:T(8,128)(2,1)S(1)}, bf16[1,512,512]{2,1,0:T(8,128)(2,1)S(1)}, u32[]{:S(2)}, u32[]{:S(2)}) %collective-permute-start.8) | collective-permute-done | bytes 524320 | tf_op jit(solution)/shard_map/ppermute | solution.py:299
  58.5 6.3 %collective-permute-done.14.refs_26_ = bf16[1,512,512]{2,1,0:T(8,128)(2,1)} collective-permute-done((bf16[1,512,512]{2,1,0:T(8,128)(2,1)S(1)}, bf16[1,512,512]{2,1,0:T(8,128)(2,1)}, u32[]{:S(2)}, u32[]{:S(2)}) %collective-permute-start.14) | collective-permute-done | bytes 524320 | tf_op jit(solution)/shard_map/ppermute | solution.py:299
  67.0 1.6 maximum_maximum_fusion
  68.6 2.5 collective-permute-start.11
  71.6 1.5 collective-permute-start.18
  74.3 10.2 %collective-permute-done.11.refs_26_ = bf16[1,512,512]{2,1,0:T(8,128)(2,1)S(1)} collective-permute-done((bf16[1,512,512]{2,1,0:T(8,128)(2,1)}, bf16[1,512,512]{2,1,0:T(8,128)(2,1)S(1)}, u32[]{:S(2)}, u32[]{:S(2)}) %collective-permute-start.11) | collective-permute-done | bytes 524320 | tf_op jit(solution)/shard_map/ppermute | solution.py:299
  84.7 1.6 collective-permute-start.22
  87.3 1.6 collective-permute-start.24
  88.9 6.9 %collective-permute-done.21.refs_30_ = bf16[1,512,512]{2,1,0:T(8,128)(2,1)S(1)} collective-permute-done((bf16[1,512,512]{2,1,0:T(8,128)(2,1)}, bf16[1,512,512]{2,1,0:T(8,128)(2,1)S(1)}, u32[]{:S(2)}, u32[]{:S(2)}) %collective-permute-start.21) | collective-permute-done | bytes 524320 | tf_op jit(solution)/shard_map/ppermute | solution.py:299
  98.8 1.5 collective-permute-start.29
  100.3 6.7 %collective-permute-done.24.refs_24_ = bf16[1,512,512]{2,1,0:T(8,128)(2,1)S(1)} collective-permute-done((bf16[1,512,512]{2,1,0:T(8,128)(2,1)S(1)}, bf16[1,512,512]{2,1,0:T(8,128)(2,1)S(1)}, u32[]{:S(2)}, u32[]{:S(2)}) %collective-permute-start.24) | collective-permute-done | bytes 524320 | tf_op jit(solution)/shard_map/ppermute | solution.py:299
  107.0 1.7 collective-permute-done.25.refs_11_
  112.7 1.6 collective-permute-start.32
  114.3 2.0 collective-permute-done.29.refs_28_
  116.3 1.7 collective-permute-done.30.refs_13_
  118.0 1.6 collective-permute-done.31.refs_14_
  120.8 1.4 collective-permute-start.34
  122.3 1.6 collective-permute-start.37
  123.8 4.6 %collective-permute-done.32.refs_28_ = bf16[1,512,512]{2,1,0:T(8,128)(2,1)} collective-permute-done((bf16[1,512,512]{2,1,0:T(8,128)(2,1)S(1)}, bf16[1,512,512]{2,1,0:T(8,128)(2,1)}, u32[]{:S(2)}, u32[]{:S(2)}) %collective-permute-start.32) | collective-permute-done | bytes 524320 | tf_op jit(solution)/shard_map/ppermute | solution.py:299
  128.4 4.5 %collective-permute-done.33.refs_16_ = bf16[512,512]{1,0:T(8,128)(2,1)S(1)} collective-permute-done((bf16[512,512]{1,0:T(8,128)(2,1)S(1)}, bf16[512,512]{1,0:T(8,128)(2,1)S(1)}, u32[]{:S(2)}, u32[]{:S(2)}) %collective-permute-start.33) | collective-permute-done | bytes 524320 | tf_op jit(solution)/shard_map/ppermute | solution.py:200
  133.9 1.5 collective-permute-start.38
  137.3 1.6 collective-permute-start.41
  138.9 3.9 %collective-permute-done.38.refs_18_ = bf16[256,512]{1,0:T(8,128)(2,1)S(1)} collective-permute-done((bf16[256,512]{1,0:T(8,128)(2,1)S(1)}, bf16[256,512]{1,0:T(8,128)(2,1)S(1)}, u32[]{:S(2)}, u32[]{:S(2)}) %collective-permute-start.38) | collective-permute-done | bytes 262176 | tf_op jit(solution)/shard_map/ppermute | solution.py:200
  142.7 1.3 collective-permute-done.39.refs_19_
  147.0 1.6 collective-permute-start.43
  148.6 4.0 %collective-permute-done.41.refs_30_ = bf16[1,512,512]{2,1,0:T(8,128)(2,1)} collective-permute-done((bf16[1,512,512]{2,1,0:T(8,128)(2,1)}, bf16[1,512,512]{2,1,0:T(8,128)(2,1)}, u32[]{:S(2)}, u32[]{:S(2)}) %collective-permute-start.41) | collective-permute-done | bytes 524320 | tf_op jit(solution)/shard_map/ppermute | solution.py:299
  152.6 36.1 %shard_map.37.refs_35_ = f32[4,4,128,512]{3,2,1,0:T(8,128)} custom-call(s32[1]{0:T(128)} %bitcast.half_ref, s32[2,4]{1,0:T(2,128)} %gather_fusion.2, s32[4]{0:T(128)} %add_xor_fusion.pick_ref, s32[2]{0:T(128)} %pad_add_fusion.1.tile_ref, bf16[512,512]{1,0:T(8,128)(2,1)} %bitcast.69, bf16[512,512]{1,0:T(8,128)(2,1)} %copy-done.10, ...), custom_call_target="tpu_custom_call" | custom-call | flops 21474836480 | bytes 29360128 | tf_op jit(solution)/shard_map/pallas_call | solution.py:171
  192.0 23.4 %shard_map.39 = bf16[2,4,128,512]{3,2,1,0:T(8,128)(2,1)} custom-call(s32[1]{0:T(128)} %bitcast.half_ref, s32[2,2]{1,0:T(2,128)} %get-tuple-element.146.live_ref, s32[2]{0:T(128)} %get-tuple-element.148.pick_ref, s32[2]{0:T(128)} %pad_add_fusion.tile_ref, bf16[512,512]{1,0:T(8,128)(2,1)} %bitcast.70, bf16[512,512]{1,0:T(8,128)(2,1)} %copy-done.10, ...), custom_call_target="tpu_custom_call" | custom-call | flops 10737418240 | bytes 29360128 | tf_op jit(solution)/shard_map/pallas_call | solution.py:171
  216.7 2.1 collective-permute-start.45
  219.1 23.8 %shard_map.38 = f32[2,4,128,512]{3,2,1,0:T(8,128)} custom-call(s32[1]{0:T(128)} %bitcast.half_ref, s32[2,2]{1,0:T(2,128)} %get-tuple-element.147.live_ref, s32[2]{0:T(128)} %get-tuple-element.149.pick_ref, s32[2]{0:T(128)} %pad_add_fusion.tile_ref, bf16[512,512]{1,0:T(8,128)(2,1)} %bitcast.71, bf16[512,512]{1,0:T(8,128)(2,1)} %copy-done.10, ...), custom_call_target="tpu_custom_call" | custom-call | flops 10737418240 | bytes 29360128 | tf_op jit(solution)/shard_map/pallas_call | solution.py:171
  244.2 2.7 collective-permute-start.47
  247.0 7.1 %collective-permute-done.45 = bf16[4,128,512]{2,1,0:T(8,128)(2,1)S(1)} collective-permute-done((bf16[4,128,512]{2,1,0:T(8,128)(2,1)S(1)}, bf16[4,128,512]{2,1,0:T(8,128)(2,1)S(1)}, u32[]{:S(2)}, u32[]{:S(2)}) %collective-permute-start.45) | collective-permute-done | bytes 524320 | tf_op jit(solution)/shard_map/ppermute | solution.py:244
  254.0 9.8 %collective-permute-done.47 = bf16[4,128,512]{2,1,0:T(8,128)(2,1)S(1)} collective-permute-done((bf16[4,128,512]{2,1,0:T(8,128)(2,1)S(1)}, bf16[4,128,512]{2,1,0:T(8,128)(2,1)S(1)}, u32[]{:S(2)}, u32[]{:S(2)}) %collective-permute-start.47) | collective-permute-done | bytes 524320 | tf_op jit(solution)/shard_map/ppermute | solution.py:244
  263.8 1.6 fusion.8
  265.5 1.9 collective-permute-start.50
  269.1 3.7 %collective-permute-done.50 = bf16[4,128,128]{2,1,0:T(8,128)(2,1)S(1)} collective-permute-done((bf16[4,128,128]{2,1,0:T(8,128)(2,1)S(1)}, bf16[4,128,128]{2,1,0:T(8,128)(2,1)S(1)}, u32[]{:S(2)}, u32[]{:S(2)}) %collective-permute-start.50) | collective-permute-done | bytes 131104 | tf_op jit(solution)/shard_map/ppermute | solution.py:200
  272.8 1.9 collective-permute-done.49
  275.4 1.6 copy.16
  (182 shorter events, 34.2 us)
Async XLA Ops:
  6.5 102.6 %all-gather.2.cloned.1.call-start = ((), (), s32[]{:S(2)}) async-start(), calls=%async_computation | async-start | bytes 6291456 | tf_op jit(solution)/shard_map/all_gather | solution.py:318
  8.7 14.6 %collective-permute-start = (bf16[1,512,512]{2,1,0:T(8,128)(2,1)S(1)}, bf16[1,512,512]{2,1,0:T(8,128)(2,1)S(1)}, u32[]{:S(2)}, u32[]{:S(2)}) collective-permute-start(bf16[1,512,512]{2,1,0:T(8,128)(2,1)S(1)} %get-tuple-element.70), channel_id=1, source_target_pairs={{0,16},{16,24},{24,8},{8,0},{1,17},{17,25},{25,9},{9,1},{2,18},{18... | collective-permute-start | bytes 1572872 | tf_op jit(solution)/shard_map/ppermute | solution.py:299
  8.7 14.6 %collective-permute-start.1 = (bf16[512,512]{1,0:T(8,128)(2,1)S(1)}, bf16[512,512]{1,0:T(8,128)(2,1)S(1)}, u32[]{:S(2)}, u32[]{:S(2)}) collective-permute-start(bf16[512,512]{1,0:T(8,128)(2,1)S(1)} %bitcast.67), channel_id=1, source_target_pairs={{0,2},{2,0},{4,6},{6,4},{1,3},{3,1},{5,7},{7,5},{8,10},{10,8},{12,... | collective-permute-start | bytes 1572872 | tf_op jit(solution)/shard_map/ppermute | solution.py:200
  10.7 13.1 %collective-permute-start.2 = (bf16[512,512]{1,0:T(8,128)(2,1)S(1)}, bf16[512,512]{1,0:T(8,128)(2,1)S(1)}, u32[]{:S(2)}, u32[]{:S(2)}) collective-permute-start(bf16[512,512]{1,0:T(8,128)(2,1)S(1)} %bitcast.68), channel_id=1, source_target_pairs={{0,4},{2,6},{4,0},{6,2},{1,5},{3,7},{5,1},{7,3},{8,12},{10,14},{12... | collective-permute-start | bytes 1572872 | tf_op jit(solution)/shard_map/ppermute | solution.py:200
  23.8 17.1 %collective-permute-start.3 = (bf16[4,512,512]{2,1,0:T(8,128)(2,1)S(1)}, bf16[4,512,512]{2,1,0:T(8,128)(2,1)S(1)}, u32[]{:S(2)}, u32[]{:S(2)}) collective-permute-start(bf16[4,512,512]{2,1,0:T(8,128)(2,1)S(1)} %copy-done.1), channel_id=1, source_target_pairs={{0,1},{1,0},{2,3},{3,2},{4,5},{5,4},{6,7},{7,6},{8,9},{9,8},{10,11... | collective-permute-start | bytes 6291464 | tf_op jit(solution)/shard_map/ppermute | solution.py:200
  23.8 15.3 %collective-permute-start.5 = (bf16[1,512,512]{2,1,0:T(8,128)(2,1)S(1)}, bf16[1,512,512]{2,1,0:T(8,128)(2,1)}, u32[]{:S(2)}, u32[]{:S(2)}) collective-permute-start(bf16[1,512,512]{2,1,0:T(8,128)(2,1)S(1)} %get-tuple-element.77), channel_id=1, source_target_pairs={{0,16},{16,24},{24,8},{8,0},{1,17},{17,25},{25,9},{9,1},{2,18},{18... | collective-permute-start | bytes 1572872 | tf_op jit(solution)/shard_map/ppermute | solution.py:299
  26.4 14.4 %collective-permute-start.4 = (bf16[1,512,512]{2,1,0:T(8,128)(2,1)S(1)}, bf16[1,512,512]{2,1,0:T(8,128)(2,1)S(1)}, u32[]{:S(2)}, u32[]{:S(2)}) collective-permute-start(bf16[1,512,512]{2,1,0:T(8,128)(2,1)S(1)} %collective-permute-done.refs_24_), channel_id=1, source_target_pairs={{0,1},{1,0},{2,3},{3,2},{4,5},{5,4},{6,7},{7,6},{8,9},{9,8},{10,11... | collective-permute-start | bytes 1572872 | tf_op jit(solution)/shard_map/ppermute | solution.py:200
  26.6 14.2 %collective-permute-start.6 = (bf16[256,512]{1,0:T(8,128)(2,1)S(1)}, bf16[256,512]{1,0:T(8,128)(2,1)S(1)}, u32[]{:S(2)}, u32[]{:S(2)}) collective-permute-start(bf16[256,512]{1,0:T(8,128)(2,1)S(1)} %slice.72), channel_id=1, source_target_pairs={{0,4},{2,6},{4,0},{6,2},{1,5},{3,7},{5,1},{7,3},{8,12},{10,14},{12... | collective-permute-start | bytes 786440 | tf_op jit(solution)/shard_map/ppermute | solution.py:200
  28.2 12.6 %collective-permute-start.7 = (bf16[256,512]{1,0:T(8,128)(2,1)S(1)}, bf16[256,512]{1,0:T(8,128)(2,1)S(1)}, u32[]{:S(2)}, u32[]{:S(2)}) collective-permute-start(bf16[256,512]{1,0:T(8,128)(2,1)S(1)} %slice.73), channel_id=1, source_target_pairs={{0,2},{2,0},{4,6},{6,4},{1,3},{3,1},{5,7},{7,5},{8,10},{10,8},{12,... | collective-permute-start | bytes 786440 | tf_op jit(solution)/shard_map/ppermute | solution.py:200
  39.1 15.7 %collective-permute-start.8 = (bf16[1,512,512]{2,1,0:T(8,128)(2,1)S(1)}, bf16[1,512,512]{2,1,0:T(8,128)(2,1)S(1)}, u32[]{:S(2)}, u32[]{:S(2)}) collective-permute-start(bf16[1,512,512]{2,1,0:T(8,128)(2,1)S(1)} %get-tuple-element.80), channel_id=1, source_target_pairs={{0,16},{16,24},{24,8},{8,0},{1,17},{17,25},{25,9},{9,1},{2,18},{18... | collective-permute-start | bytes 1572872 | tf_op jit(solution)/shard_map/ppermute | solution.py:299
  41.8 13.2 %collective-permute-start.10 = (bf16[4,512,128]{2,1,0:T(8,128)(2,1)S(1)}, bf16[4,512,128]{2,1,0:T(8,128)(2,1)S(1)}, u32[]{:S(2)}, u32[]{:S(2)}) collective-permute-start(bf16[4,512,128]{2,1,0:T(8,128)(2,1)S(1)} %bitcast.90), channel_id=1, source_target_pairs={{0,4},{2,6},{4,0},{6,2},{1,5},{3,7},{5,1},{7,3},{8,12},{10,14},{12... | collective-permute-start | bytes 1572872 | tf_op jit(solution)/shard_map/ppermute | solution.py:200
  43.3 12.9 %collective-permute-start.9 = (bf16[4,512,128]{2,1,0:T(8,128)(2,1)S(1)}, bf16[4,512,128]{2,1,0:T(8,128)(2,1)S(1)}, u32[]{:S(2)}, u32[]{:S(2)}) collective-permute-start(bf16[4,512,128]{2,1,0:T(8,128)(2,1)S(1)} %bitcast.91), channel_id=1, source_target_pairs={{0,2},{2,0},{4,6},{6,4},{1,3},{3,1},{5,7},{7,5},{8,10},{10,8},{12,... | collective-permute-start | bytes 1572872 | tf_op jit(solution)/shard_map/ppermute | solution.py:200
  43.8 21.0 %collective-permute-start.14 = (bf16[1,512,512]{2,1,0:T(8,128)(2,1)S(1)}, bf16[1,512,512]{2,1,0:T(8,128)(2,1)}, u32[]{:S(2)}, u32[]{:S(2)}) collective-permute-start(bf16[1,512,512]{2,1,0:T(8,128)(2,1)S(1)} %collective-permute-done.refs_24_), channel_id=1, source_target_pairs={{0,16},{16,24},{24,8},{8,0},{1,17},{17,25},{25,9},{9,1},{2,18},{18... | collective-permute-start | bytes 1572872 | tf_op jit(solution)/shard_map/ppermute | solution.py:299
  56.2 9.1 %collective-permute-start.12 = (bf16[1,512,512]{2,1,0:T(8,128)(2,1)}, bf16[1,512,512]{2,1,0:T(8,128)(2,1)S(1)}, u32[]{:S(2)}, u32[]{:S(2)}) collective-permute-start(bf16[1,512,512]{2,1,0:T(8,128)(2,1)} %collective-permute-done.5.refs_22_), channel_id=1, source_target_pairs={{0,1},{1,0},{2,3},{3,2},{4,5},{5,4},{6,7},{7,6},{8,9},{9,8},{10,11... | collective-permute-start | bytes 1572872 | tf_op jit(solution)/shard_map/ppermute | solution.py:200
  56.2 9.1 %collective-permute-start.13 = (bf16[1,512,512]{2,1,0:T(8,128)(2,1)S(1)}, bf16[1,512,512]{2,1,0:T(8,128)(2,1)S(1)}, u32[]{:S(2)}, u32[]{:S(2)}) collective-permute-start(bf16[1,512,512]{2,1,0:T(8,128)(2,1)S(1)} %collective-permute-done.8.refs_22_), channel_id=1, source_target_pairs={{0,1},{1,0},{2,3},{3,2},{4,5},{5,4},{6,7},{7,6},{8,9},{9,8},{10,11... | collective-permute-start | bytes 1572872 | tf_op jit(solution)/shard_map/ppermute | solution.py:200
  56.8 8.3 %collective-permute-start.15 = (bf16[2,512,128]{2,1,0:T(8,128)(2,1)S(1)}, bf16[2,512,128]{2,1,0:T(8,128)(2,1)S(1)}, u32[]{:S(2)}, u32[]{:S(2)}) collective-permute-start(bf16[2,512,128]{2,1,0:T(8,128)(2,1)S(1)} %slice.74), channel_id=1, source_target_pairs={{0,4},{2,6},{4,0},{6,2},{1,5},{3,7},{5,1},{7,3},{8,12},{10,14},{12... | collective-permute-start | bytes 786440 | tf_op jit(solution)/shard_map/ppermute | solution.py:200
  57.3 8.0 %collective-permute-start.16 = (bf16[2,512,128]{2,1,0:T(8,128)(2,1)S(1)}, bf16[2,512,128]{2,1,0:T(8,128)(2,1)S(1)}, u32[]{:S(2)}, u32[]{:S(2)}) collective-permute-start(bf16[2,512,128]{2,1,0:T(8,128)(2,1)S(1)} %slice.75), channel_id=1, source_target_pairs={{0,2},{2,0},{4,6},{6,4},{1,3},{3,1},{5,7},{7,5},{8,10},{10,8},{12,... | collective-permute-start | bytes 786440 | tf_op jit(solution)/shard_map/ppermute | solution.py:200
  68.6 16.0 %collective-permute-start.11 = (bf16[1,512,512]{2,1,0:T(8,128)(2,1)}, bf16[1,512,512]{2,1,0:T(8,128)(2,1)S(1)}, u32[]{:S(2)}, u32[]{:S(2)}) collective-permute-start(bf16[1,512,512]{2,1,0:T(8,128)(2,1)} %collective-permute-done.5.refs_22_), channel_id=1, source_target_pairs={{0,16},{16,24},{24,8},{8,0},{1,17},{17,25},{25,9},{9,1},{2,18},{18... | collective-permute-start | bytes 1572872 | tf_op jit(solution)/shard_map/ppermute | solution.py:299
  71.1 13.5 %collective-permute-start.17 = (bf16[512,512]{1,0:T(8,128)(2,1)S(1)}, bf16[512,512]{1,0:T(8,128)(2,1)S(1)}, u32[]{:S(2)}, u32[]{:S(2)}) collective-permute-start(bf16[512,512]{1,0:T(8,128)(2,1)S(1)} %bitcast.72), channel_id=1, source_target_pairs={{0,2},{2,0},{4,6},{6,4},{1,3},{3,1},{5,7},{7,5},{8,10},{10,8},{12,... | collective-permute-start | bytes 1572872 | tf_op jit(solution)/shard_map/ppermute | solution.py:200
  71.6 13.0 %collective-permute-start.18 = (bf16[512,512]{1,0:T(8,128)(2,1)S(1)}, bf16[512,512]{1,0:T(8,128)(2,1)S(1)}, u32[]{:S(2)}, u32[]{:S(2)}) collective-permute-start(bf16[512,512]{1,0:T(8,128)(2,1)S(1)} %bitcast.73), channel_id=1, source_target_pairs={{0,4},{2,6},{4,0},{6,2},{1,5},{3,7},{5,1},{7,3},{8,12},{10,14},{12... | collective-permute-start | bytes 1572872 | tf_op jit(solution)/shard_map/ppermute | solution.py:200
  73.1 14.2 %collective-permute-start.19 = (bf16[1,512,512]{2,1,0:T(8,128)(2,1)}, bf16[1,512,512]{2,1,0:T(8,128)(2,1)S(1)}, u32[]{:S(2)}, u32[]{:S(2)}) collective-permute-start(bf16[1,512,512]{2,1,0:T(8,128)(2,1)} %collective-permute-done.14.refs_26_), channel_id=1, source_target_pairs={{0,1},{1,0},{2,3},{3,2},{4,5},{5,4},{6,7},{7,6},{8,9},{9,8},{10,11... | collective-permute-start | bytes 1572872 | tf_op jit(solution)/shard_map/ppermute | solution.py:200
  73.1 22.7 %collective-permute-start.21 = (bf16[1,512,512]{2,1,0:T(8,128)(2,1)}, bf16[1,512,512]{2,1,0:T(8,128)(2,1)S(1)}, u32[]{:S(2)}, u32[]{:S(2)}) collective-permute-start(bf16[1,512,512]{2,1,0:T(8,128)(2,1)} %collective-permute-done.14.refs_26_), channel_id=1, source_target_pairs={{0,16},{16,24},{24,8},{8,0},{1,17},{17,25},{25,9},{9,1},{2,18},{18... | collective-permute-start | bytes 1572872 | tf_op jit(solution)/shard_map/ppermute | solution.py:299
  84.6 11.2 %collective-permute-start.20 = (bf16[1,512,512]{2,1,0:T(8,128)(2,1)S(1)}, bf16[1,512,512]{2,1,0:T(8,128)(2,1)S(1)}, u32[]{:S(2)}, u32[]{:S(2)}) collective-permute-start(bf16[1,512,512]{2,1,0:T(8,128)(2,1)S(1)} %collective-permute-done.11.refs_26_), channel_id=1, source_target_pairs={{0,1},{1,0},{2,3},{3,2},{4,5},{5,4},{6,7},{7,6},{8,9},{9,8},{10,11... | collective-permute-start | bytes 1572872 | tf_op jit(solution)/shard_map/ppermute | solution.py:200
  84.7 11.1 %collective-permute-start.22 = (bf16[256,512]{1,0:T(8,128)(2,1)S(1)}, bf16[256,512]{1,0:T(8,128)(2,1)S(1)}, u32[]{:S(2)}, u32[]{:S(2)}) collective-permute-start(bf16[256,512]{1,0:T(8,128)(2,1)S(1)} %slice.76), channel_id=1, source_target_pairs={{0,4},{2,6},{4,0},{6,2},{1,5},{3,7},{5,1},{7,3},{8,12},{10,14},{12... | collective-permute-start | bytes 786440 | tf_op jit(solution)/shard_map/ppermute | solution.py:200
  86.3 9.5 %collective-permute-start.23 = (bf16[256,512]{1,0:T(8,128)(2,1)S(1)}, bf16[256,512]{1,0:T(8,128)(2,1)S(1)}, u32[]{:S(2)}, u32[]{:S(2)}) collective-permute-start(bf16[256,512]{1,0:T(8,128)(2,1)S(1)} %slice.77), channel_id=1, source_target_pairs={{0,2},{2,0},{4,6},{6,4},{1,3},{3,1},{5,7},{7,5},{8,10},{10,8},{12,... | collective-permute-start | bytes 786440 | tf_op jit(solution)/shard_map/ppermute | solution.py:200
  87.3 19.7 %collective-permute-start.24 = (bf16[1,512,512]{2,1,0:T(8,128)(2,1)S(1)}, bf16[1,512,512]{2,1,0:T(8,128)(2,1)S(1)}, u32[]{:S(2)}, u32[]{:S(2)}) collective-permute-start(bf16[1,512,512]{2,1,0:T(8,128)(2,1)S(1)} %get-tuple-element.99), channel_id=1, source_target_pairs={{0,16},{16,24},{24,8},{8,0},{1,17},{17,25},{25,9},{9,1},{2,18},{18... | collective-permute-start | bytes 1572872 | tf_op jit(solution)/shard_map/ppermute | solution.py:299
  96.7 12.1 %collective-permute-start.25 = (bf16[512,512]{1,0:T(8,128)(2,1)S(1)}, bf16[512,512]{1,0:T(8,128)(2,1)S(1)}, u32[]{:S(2)}, u32[]{:S(2)}) collective-permute-start(bf16[512,512]{1,0:T(8,128)(2,1)S(1)} %bitcast.78), channel_id=1, source_target_pairs={{0,2},{2,0},{4,6},{6,4},{1,3},{3,1},{5,7},{7,5},{8,10},{10,8},{12,... | collective-permute-start | bytes 1572872 | tf_op jit(solution)/shard_map/ppermute | solution.py:200
  97.6 11.6 %collective-permute-start.26 = (bf16[512,512]{1,0:T(8,128)(2,1)S(1)}, bf16[512,512]{1,0:T(8,128)(2,1)}, u32[]{:S(2)}, u32[]{:S(2)}) collective-permute-start(bf16[512,512]{1,0:T(8,128)(2,1)S(1)} %bitcast.79), channel_id=1, source_target_pairs={{0,4},{2,6},{4,0},{6,2},{1,5},{3,7},{5,1},{7,3},{8,12},{10,14},{12... | collective-permute-start | bytes 1572872 | tf_op jit(solution)/shard_map/ppermute | solution.py:200
  98.8 13.9 %collective-permute-start.27 = (bf16[1,512,512]{2,1,0:T(8,128)(2,1)S(1)}, bf16[1,512,512]{2,1,0:T(8,128)(2,1)}, u32[]{:S(2)}, u32[]{:S(2)}) collective-permute-start(bf16[1,512,512]{2,1,0:T(8,128)(2,1)S(1)} %collective-permute-done.21.refs_30_), channel_id=1, source_target_pairs={{0,1},{1,0},{2,3},{3,2},{4,5},{5,4},{6,7},{7,6},{8,9},{9,8},{10,11... | collective-permute-start | bytes 1572872 | tf_op jit(solution)/shard_map/ppermute | solution.py:200
  98.8 17.5 %collective-permute-start.29 = (bf16[1,512,512]{2,1,0:T(8,128)(2,1)S(1)}, bf16[1,512,512]{2,1,0:T(8,128)(2,1)}, u32[]{:S(2)}, u32[]{:S(2)}) collective-permute-start(bf16[1,512,512]{2,1,0:T(8,128)(2,1)S(1)} %collective-permute-done.8.refs_22_), channel_id=1, source_target_pairs={{0,16},{16,24},{24,8},{8,0},{1,17},{17,25},{25,9},{9,1},{2,18},{18... | collective-permute-start | bytes 1572872 | tf_op jit(solution)/shard_map/ppermute | solution.py:299
  109.2 10.4 %collective-permute-start.28 = (bf16[1,512,512]{2,1,0:T(8,128)(2,1)}, bf16[1,512,512]{2,1,0:T(8,128)(2,1)S(1)}, u32[]{:S(2)}, u32[]{:S(2)}) collective-permute-start(bf16[1,512,512]{2,1,0:T(8,128)(2,1)} %copy-done.24), channel_id=1, source_target_pairs={{0,1},{1,0},{2,3},{3,2},{4,5},{5,4},{6,7},{7,6},{8,9},{9,8},{10,11... | collective-permute-start | bytes 1572872 | tf_op jit(solution)/shard_map/ppermute | solution.py:200
  109.2 8.8 %collective-permute-start.30 = (bf16[256,512]{1,0:T(8,128)(2,1)S(1)}, bf16[256,512]{1,0:T(8,128)(2,1)S(1)}, u32[]{:S(2)}, u32[]{:S(2)}) collective-permute-start(bf16[256,512]{1,0:T(8,128)(2,1)S(1)} %slice.78), channel_id=1, source_target_pairs={{0,4},{2,6},{4,0},{6,2},{1,5},{3,7},{5,1},{7,3},{8,12},{10,14},{12... | collective-permute-start | bytes 786440 | tf_op jit(solution)/shard_map/ppermute | solution.py:200
  111.0 8.5 %collective-permute-start.31 = (bf16[256,512]{1,0:T(8,128)(2,1)S(1)}, bf16[256,512]{1,0:T(8,128)(2,1)S(1)}, u32[]{:S(2)}, u32[]{:S(2)}) collective-permute-start(bf16[256,512]{1,0:T(8,128)(2,1)S(1)} %slice.79), channel_id=1, source_target_pairs={{0,2},{2,0},{4,6},{6,4},{1,3},{3,1},{5,7},{7,5},{8,10},{10,8},{12,... | collective-permute-start | bytes 786440 | tf_op jit(solution)/shard_map/ppermute | solution.py:200
  112.7 15.8 %collective-permute-start.32 = (bf16[1,512,512]{2,1,0:T(8,128)(2,1)S(1)}, bf16[1,512,512]{2,1,0:T(8,128)(2,1)}, u32[]{:S(2)}, u32[]{:S(2)}) collective-permute-start(bf16[1,512,512]{2,1,0:T(8,128)(2,1)S(1)} %copy-done.25), channel_id=1, source_target_pairs={{0,16},{16,24},{24,8},{8,0},{1,17},{17,25},{25,9},{9,1},{2,18},{18... | collective-permute-start | bytes 1572872 | tf_op jit(solution)/shard_map/ppermute | solution.py:299
  119.6 13.4 %collective-permute-start.33 = (bf16[512,512]{1,0:T(8,128)(2,1)S(1)}, bf16[512,512]{1,0:T(8,128)(2,1)S(1)}, u32[]{:S(2)}, u32[]{:S(2)}) collective-permute-start(bf16[512,512]{1,0:T(8,128)(2,1)S(1)} %bitcast.85), channel_id=1, source_target_pairs={{0,2},{2,0},{4,6},{6,4},{1,3},{3,1},{5,7},{7,5},{8,10},{10,8},{12,... | collective-permute-start | bytes 1572872 | tf_op jit(solution)/shard_map/ppermute | solution.py:200
  120.8 13.1 %collective-permute-start.34 = (bf16[512,512]{1,0:T(8,128)(2,1)S(1)}, bf16[512,512]{1,0:T(8,128)(2,1)S(1)}, u32[]{:S(2)}, u32[]{:S(2)}) collective-permute-start(bf16[512,512]{1,0:T(8,128)(2,1)S(1)} %bitcast.86), channel_id=1, source_target_pairs={{0,4},{2,6},{4,0},{6,2},{1,5},{3,7},{5,1},{7,3},{8,12},{10,14},{12... | collective-permute-start | bytes 1572872 | tf_op jit(solution)/shard_map/ppermute | solution.py:200
  122.3 15.0 %collective-permute-start.35 = (bf16[1,512,512]{2,1,0:T(8,128)(2,1)}, bf16[1,512,512]{2,1,0:T(8,128)(2,1)S(1)}, u32[]{:S(2)}, u32[]{:S(2)}) collective-permute-start(bf16[1,512,512]{2,1,0:T(8,128)(2,1)} %collective-permute-done.29.refs_28_), channel_id=1, source_target_pairs={{0,1},{1,0},{2,3},{3,2},{4,5},{5,4},{6,7},{7,6},{8,9},{9,8},{10,11... | collective-permute-start | bytes 1572872 | tf_op jit(solution)/shard_map/ppermute | solution.py:200
  122.3 16.6 %collective-permute-start.37 = (bf16[1,512,512]{2,1,0:T(8,128)(2,1)}, bf16[1,512,512]{2,1,0:T(8,128)(2,1)}, u32[]{:S(2)}, u32[]{:S(2)}) collective-permute-start(bf16[1,512,512]{2,1,0:T(8,128)(2,1)} %collective-permute-done.29.refs_28_), channel_id=1, source_target_pairs={{0,16},{16,24},{24,8},{8,0},{1,17},{17,25},{25,9},{9,1},{2,18},{18... | collective-permute-start | bytes 1572872 | tf_op jit(solution)/shard_map/ppermute | solution.py:299
  133.9 10.2 %collective-permute-start.36 = (bf16[1,512,512]{2,1,0:T(8,128)(2,1)}, bf16[1,512,512]{2,1,0:T(8,128)(2,1)}, u32[]{:S(2)}, u32[]{:S(2)}) collective-permute-start(bf16[1,512,512]{2,1,0:T(8,128)(2,1)} %collective-permute-done.32.refs_28_), channel_id=1, source_target_pairs={{0,1},{1,0},{2,3},{3,2},{4,5},{5,4},{6,7},{7,6},{8,9},{9,8},{10,11... | collective-permute-start | bytes 1572872 | tf_op jit(solution)/shard_map/ppermute | solution.py:200
  133.9 8.8 %collective-permute-start.38 = (bf16[256,512]{1,0:T(8,128)(2,1)S(1)}, bf16[256,512]{1,0:T(8,128)(2,1)S(1)}, u32[]{:S(2)}, u32[]{:S(2)}) collective-permute-start(bf16[256,512]{1,0:T(8,128)(2,1)S(1)} %slice.80), channel_id=1, source_target_pairs={{0,4},{2,6},{4,0},{6,2},{1,5},{3,7},{5,1},{7,3},{8,12},{10,14},{12... | collective-permute-start | bytes 786440 | tf_op jit(solution)/shard_map/ppermute | solution.py:200
  135.4 8.6 %collective-permute-start.39 = (bf16[256,512]{1,0:T(8,128)(2,1)S(1)}, bf16[256,512]{1,0:T(8,128)(2,1)}, u32[]{:S(2)}, u32[]{:S(2)}) collective-permute-start(bf16[256,512]{1,0:T(8,128)(2,1)S(1)} %slice.81), channel_id=1, source_target_pairs={{0,2},{2,0},{4,6},{6,4},{1,3},{3,1},{5,7},{7,5},{8,10},{10,8},{12,... | collective-permute-start | bytes 786440 | tf_op jit(solution)/shard_map/ppermute | solution.py:200
  137.3 15.3 %collective-permute-start.41 = (bf16[1,512,512]{2,1,0:T(8,128)(2,1)}, bf16[1,512,512]{2,1,0:T(8,128)(2,1)}, u32[]{:S(2)}, u32[]{:S(2)}) collective-permute-start(bf16[1,512,512]{2,1,0:T(8,128)(2,1)} %collective-permute-done.32.refs_28_), channel_id=1, source_target_pairs={{0,16},{16,24},{24,8},{8,0},{1,17},{17,25},{25,9},{9,1},{2,18},{18... | collective-permute-start | bytes 1572872 | tf_op jit(solution)/shard_map/ppermute | solution.py:299
  144.1 8.5 %collective-permute-start.40 = (bf16[1,512,512]{2,1,0:T(8,128)(2,1)}, bf16[1,512,512]{2,1,0:T(8,128)(2,1)}, u32[]{:S(2)}, u32[]{:S(2)}) collective-permute-start(bf16[1,512,512]{2,1,0:T(8,128)(2,1)} %collective-permute-done.37.refs_32_), channel_id=1, source_target_pairs={{0,1},{1,0},{2,3},{3,2},{4,5},{5,4},{6,7},{7,6},{8,9},{9,8},{10,11... | collective-permute-start | bytes 1572872 | tf_op jit(solution)/shard_map/ppermute | solution.py:200
  147.0 41.8 %collective-permute-start.43 = (bf16[1,512,512]{2,1,0:T(8,128)(2,1)S(1)}, bf16[1,512,512]{2,1,0:T(8,128)(2,1)S(1)}, u32[]{:S(2)}, u32[]{:S(2)}) collective-permute-start(bf16[1,512,512]{2,1,0:T(8,128)(2,1)S(1)} %collective-permute-done.11.refs_26_), channel_id=1, source_target_pairs={{0,16},{16,24},{24,8},{8,0},{1,17},{17,25},{25,9},{9,1},{2,18},{18... | collective-permute-start | bytes 1572872 | tf_op jit(solution)/shard_map/ppermute | solution.py:299
  152.6 36.2 %collective-permute-start.42 = (bf16[1,512,512]{2,1,0:T(8,128)(2,1)}, bf16[1,512,512]{2,1,0:T(8,128)(2,1)S(1)}, u32[]{:S(2)}, u32[]{:S(2)}) collective-permute-start(bf16[1,512,512]{2,1,0:T(8,128)(2,1)} %collective-permute-done.41.refs_30_), channel_id=1, source_target_pairs={{0,1},{1,0},{2,3},{3,2},{4,5},{5,4},{6,7},{7,6},{8,9},{9,8},{10,11... | collective-permute-start | bytes 1572872 | tf_op jit(solution)/shard_map/ppermute | solution.py:200
  216.7 37.3 %collective-permute-start.45 = (bf16[4,128,512]{2,1,0:T(8,128)(2,1)S(1)}, bf16[4,128,512]{2,1,0:T(8,128)(2,1)S(1)}, u32[]{:S(2)}, u32[]{:S(2)}) collective-permute-start(bf16[4,128,512]{2,1,0:T(8,128)(2,1)S(1)} %get-tuple-element.141), channel_id=1, source_target_pairs={{0,24},{16,8},{24,0},{8,16},{1,25},{17,9},{25,1},{9,17},{2,26},{18... | collective-permute-start | bytes 1572872 | tf_op jit(solution)/shard_map/ppermute | solution.py:244
  218.8 35.2 %collective-permute-start.46 = (bf16[4,128,512]{2,1,0:T(8,128)(2,1)S(1)}, bf16[4,128,512]{2,1,0:T(8,128)(2,1)S(1)}, u32[]{:S(2)}, u32[]{:S(2)}) collective-permute-start(bf16[4,128,512]{2,1,0:T(8,128)(2,1)S(1)} %get-tuple-element.142), channel_id=1, source_target_pairs={{0,16},{16,24},{24,8},{8,0},{1,17},{17,25},{25,9},{9,1},{2,18},{18... | collective-permute-start | bytes 1572872 | tf_op jit(solution)/shard_map/ppermute | solution.py:244
  244.2 19.6 %collective-permute-start.47 = (bf16[4,128,512]{2,1,0:T(8,128)(2,1)S(1)}, bf16[4,128,512]{2,1,0:T(8,128)(2,1)S(1)}, u32[]{:S(2)}, u32[]{:S(2)}) collective-permute-start(bf16[4,128,512]{2,1,0:T(8,128)(2,1)S(1)} %fusion.3), channel_id=1, source_target_pairs={{0,8},{16,0},{24,16},{8,24},{1,9},{17,1},{25,17},{9,25},{2,10},{18... | collective-permute-start | bytes 1572872 | tf_op jit(solution)/shard_map/ppermute | solution.py:244
  (43 other events, 986.4 us)
Sparse Core Ops, SparseCore 0:
  68.7 13.7 all-gather.1
